TPU v7x, 32 devices: a whole 2x2x4 slice. The times are simulated.
32 devices in a mesh: gx: 4 (over y, x), gy: 2 (over core), gz: 4 (over z).
Axes of the slice: x: 2, y: 2, z: 4, core: 2. Of those that a mesh axis runs over, the one named last changes fastest.
Arguments:
- starting_warmth: float32 [32, 1024, 256], P('gz', 'gx', 'gy'), may hold values from -6 to 6
- sheet_stratum_number: int32 [32], replicated, may hold values from 0 to 15
- stratum_heat_conduction: float32 [16], replicated, may hold values from 1 to 16
- substance_kind: int32 [32, 1024, 256], P('gz', 'gx', 'gy'), may hold values from 0 to 3
- substance_kind_scaling: float32 [4], replicated, may hold values from 0.5 to 1.5
- wire_piece_amperes: float32 [131072], P(('gx', 'gy', 'gz')), may hold values from -6 to 6
- wire_piece_ohms_base: float32 [131072], P(('gx', 'gy', 'gz')), may hold values from 0.5 to 2
- wire_piece_tile: int32 [131072, 1], P(('gx', 'gy', 'gz')), may hold values from 0 to 31; in each aligned block of 4096 rows (0 to 4095, 4096 to 8191, ...) at most 256 rows name the same one
- wire_piece_voxel: int32 [131072], P(('gx', 'gy', 'gz')), may hold values from 0 to 262143
Outputs:
- warmed: float32 [32, 1024, 256], P('gz', 'gx', 'gy')
- ohmic_power_final: float32 [32, 1024, 256], P('gz', 'gx', 'gy')
Inputs may be any that keep to these rules, and one draw needn't show every extreme that they name: `wire_piece_tile`: among the 4096 segments of one device, at most 256 name the same block, and some block is named by exactly 256 of them.
All inputs are finite; a program needn't handle non-finite values.
Results may differ from a plain program's by a relative error of at most 0.0029.
Values sent between devices are 32-bit elements; how exact they have to be, the bound alone decides.
No kernel may reach another device: no remote copies, remote signals or barrier semaphores. Data moves between devices by JAX's collectives and lax.ppermute only.
A program may use at most 128 MiB of HBM per device.

v0:
```python
import jax
import jax.numpy as jnp
from jax import lax
from jax.sharding import PartitionSpec as P

STEPS = 2


HEAT_SPREADING = 1000.0
STIFF = 1.5
WARMING_SLOPE = 0.1
OHMIC_POWER = 8.0
EXACT = lax.Precision.HIGHEST


def carried_in(array, axis, combine, identity, reverse):
    count, mine = (lax.axis_size(axis), lax.axis_index(axis))
    everything = jax.tree.map(lambda part: lax.all_gather(part, axis), array)
    start = jax.tree.map(
        lambda part, zero: jnp.broadcast_to(jnp.asarray(zero, part.dtype), part.shape),
        array,
        identity,
    )

    def hop(k, before):
        at = count - 1 - k if reverse else k
        reached = at > mine if reverse else at < mine
        new = combine(before, jax.tree.map(lambda part: part[at], everything))
        return jax.tree.map(lambda a, b: jnp.where(reached, a, b), new, before)

    return lax.fori_loop(0, count, hop, start)


def padded_2(array, sides, width):
    for axis, dim in sides:
        count, length = (lax.axis_size(axis), array.shape[dim])
        up = [(i, (i + 1) % count) for i in range(count - 1)]
        down = [(j, i) for i, j in up]
        last = lax.slice_in_dim(array, length - width, length, axis=dim)
        initial = lax.slice_in_dim(array, 0, width, axis=dim)
        before = lax.ppermute(last, axis, up)
        after = lax.ppermute(initial, axis, down)
        array = jnp.concatenate([before, array, after], axis=dim)
    return array


def band_inverse(conductance, couple_low):
    length = conductance.shape[-1] - 1
    diagonal = 1.0 + HEAT_SPREADING * (conductance[..., :-1] + conductance[..., 1:])
    couplings = jnp.concatenate(
        [-HEAT_SPREADING * conductance[..., 1:-1], jnp.zeros_like(conductance[..., :1])], axis=-1
    )
    unit_matrix = jnp.eye(length, dtype=jnp.float32)
    above_band = jnp.eye(length, k=1, dtype=jnp.float32)
    below_band = jnp.eye(length, k=-1, dtype=jnp.float32)
    matrix = (
        diagonal[..., :, None] * unit_matrix
        + couplings[..., :, None] * above_band
        + couplings[..., None, :] * below_band
    )
    factor = jnp.linalg.cholesky(matrix)
    inverse = jax.scipy.linalg.cho_solve(
        (factor, True), jnp.broadcast_to(unit_matrix, matrix.shape)
    )
    spike_low = (-HEAT_SPREADING * couple_low)[..., None] * inverse[..., :, 0]
    spike_high = (-HEAT_SPREADING * conductance[..., -1])[..., None] * inverse[..., :, -1]
    return (inverse, spike_low, spike_high)


def join(earlier, later):
    divisor = 1.0 - earlier[5] * later[2]
    tail_base = (earlier[1] - earlier[5] * later[0]) / divisor
    tail_left = earlier[3] / divisor
    tail_right = -earlier[5] * later[4] / divisor
    head_base = (later[0] - later[2] * earlier[1]) / divisor
    head_left = -later[2] * earlier[3] / divisor
    head_right = later[4] / divisor
    return (
        earlier[0] - earlier[4] * head_base,
        later[1] - later[3] * tail_base,
        earlier[2] - earlier[4] * head_left,
        -later[3] * tail_left,
        -earlier[4] * head_right,
        later[5] - later[3] * tail_right,
    )


def flipped(earlier, later):
    return join(later, earlier)


def identity_of(own):
    return (
        jnp.zeros_like(own[0]),
        jnp.zeros_like(own[1]),
        jnp.zeros_like(own[2]),
        -jnp.ones_like(own[3]),
        -jnp.ones_like(own[4]),
        jnp.zeros_like(own[5]),
    )


def settle(own, before, after):
    left_base, left_slope = (before[1], before[5])
    right_base, right_slope = (after[0], after[2])
    head_rhs = own[0] - own[2] * left_base - own[4] * right_base
    tail_rhs = own[1] - own[3] * left_base - own[5] * right_base
    upper_left = 1.0 - own[2] * left_slope
    upper_right = -own[4] * right_slope
    lower_left = -own[3] * left_slope
    lower_right = 1.0 - own[5] * right_slope
    divisor = upper_left * lower_right - upper_right * lower_left
    head_value = (head_rhs * lower_right - upper_right * tail_rhs) / divisor
    tail_value = (upper_left * tail_rhs - lower_left * head_rhs) / divisor
    return (left_base - left_slope * head_value, right_base - right_slope * tail_value)


def flow(padded, conduct, along, at_low, at_high, to_sink):
    length = padded.shape[along] - 2
    lead_field = lax.slice_in_dim(padded, 0, length + 1, axis=along)
    next_field = lax.slice_in_dim(padded, 1, length + 2, axis=along)
    lead_cond = lax.slice_in_dim(conduct, 0, length + 1, axis=along)
    next_cond = lax.slice_in_dim(conduct, 1, length + 2, axis=along)
    fluxes = 0.5 * (lead_cond + next_cond) * (next_field - lead_field)
    bottom = lax.slice_in_dim(fluxes, 0, 1, axis=along)
    if to_sink:
        grounded = lax.slice_in_dim(next_cond, 0, 1, axis=along) * lax.slice_in_dim(
            next_field, 0, 1, axis=along
        )
    else:
        grounded = jnp.zeros_like(bottom)
    bottom = jnp.where(at_low, grounded, bottom)
    summit = jnp.where(at_high, 0.0, lax.slice_in_dim(fluxes, length, length + 1, axis=along))
    fluxes = jnp.concatenate(
        [bottom, lax.slice_in_dim(fluxes, 1, length, axis=along), summit], axis=along
    )
    return lax.slice_in_dim(fluxes, 1, length + 1, axis=along) - lax.slice_in_dim(
        fluxes, 0, length, axis=along
    )


def lateral_faces(plane_own, cells, place, parts):
    position = jnp.arange(cells + 1, dtype=jnp.int32)
    blocked = (position == 0) & (place == 0) | (position == cells) & (place == parts - 1)
    keep = jnp.where(blocked, 0.0, 1.0).astype(jnp.float32)
    return STIFF * plane_own[:, None] * keep[None, :]


def per_device(
    starting_warmth,
    sheet_stratum_number,
    stratum_heat_conduction,
    substance_kind,
    substance_kind_scaling,
    wire_piece_amperes,
    wire_piece_ohms_base,
    wire_piece_tile,
    wire_piece_voxel,
):
    sheet_voxel_total, horizontal_voxel_total, vertical_voxel_total = starting_warmth.shape
    row_parts = lax.axis_size("gx")
    column_parts = lax.axis_size("gy")
    slab_parts = lax.axis_size("gz")
    row_place = lax.axis_index("gx")
    column_place = lax.axis_index("gy")
    slab_place = lax.axis_index("gz")
    matches = (
        sheet_stratum_number[:, None]
        == jnp.arange(stratum_heat_conduction.shape[0], dtype=jnp.int32)[None, :]
    )
    plane_all = jnp.sum(jnp.where(matches, stratum_heat_conduction[None, :], 0.0), axis=1)
    plane_own = lax.dynamic_slice_in_dim(
        plane_all, slab_place * sheet_voxel_total, sheet_voxel_total
    )
    factor_cell = jnp.zeros(substance_kind.shape, jnp.float32)
    for category in range(substance_kind_scaling.shape[0]):
        factor_cell = factor_cell + jnp.where(
            substance_kind == category, substance_kind_scaling[category], 0.0
        )
    voxel_conductance = plane_own[:, None, None] * factor_cell
    count = wire_piece_amperes.shape[0]
    devices = row_parts * column_parts * slab_parts
    capacity = 2 * count // devices
    power = wire_piece_amperes * wire_piece_amperes * wire_piece_ohms_base
    target = wire_piece_tile[:, 0]
    onehot = (target[:, None] == jnp.arange(devices, dtype=jnp.int32)[None, :]).astype(jnp.int32)
    rank = jnp.sum((jnp.cumsum(onehot, axis=0) - onehot) * onehot, axis=1)
    slot = target * capacity + rank
    send_power = (
        jnp.zeros((devices * capacity,), jnp.float32).at[slot].set(power).reshape(devices, capacity)
    )
    send_cell = (
        jnp.zeros((devices * capacity,), jnp.int32)
        .at[slot]
        .set(wire_piece_voxel)
        .reshape(devices, capacity)
    )
    got_power, got_cell = (
        lax.all_to_all(send_power, ("gx", "gy", "gz"), split_axis=0, concat_axis=0, tiled=True),
        lax.all_to_all(send_cell, ("gx", "gy", "gz"), split_axis=0, concat_axis=0, tiled=True),
    )
    ohmic_loss = jnp.zeros(
        (sheet_voxel_total * horizontal_voxel_total * vertical_voxel_total,), jnp.float32
    )
    ohmic_loss = (
        ohmic_loss.at[got_cell.reshape(-1)]
        .add(got_power.reshape(-1))
        .reshape(sheet_voxel_total, horizontal_voxel_total, vertical_voxel_total)
    )
    row_faces = lateral_faces(plane_own, horizontal_voxel_total, row_place, row_parts)
    row_inverse, row_low, row_high = band_inverse(row_faces, row_faces[:, 0])
    column_faces = lateral_faces(plane_own, vertical_voxel_total, column_place, column_parts)
    column_inverse, column_low, column_high = band_inverse(column_faces, column_faces[:, 0])
    plane_faces = STIFF * jnp.concatenate(
        [plane_all[:1], 0.5 * (plane_all[:-1] + plane_all[1:]), jnp.zeros((1,), jnp.float32)]
    )
    slab_faces = lax.dynamic_slice_in_dim(
        plane_faces, slab_place * sheet_voxel_total, sheet_voxel_total + 1
    )
    slab_inverse, slab_low, slab_high = band_inverse(
        slab_faces, jnp.where(slab_place > 0, slab_faces[0], 0.0)
    )
    warmth_excess = starting_warmth
    for repeat in range(STEPS):
        padded_warm, padded_cond = (
            padded_2(warmth_excess, (("gx", 1), ("gy", 2), ("gz", 0)), 1),
            padded_2(voxel_conductance, (("gx", 1), ("gy", 2), ("gz", 0)), 1),
        )
        diffusion_term = flow(
            padded_warm[:, 1:-1, 1:-1],
            padded_cond[:, 1:-1, 1:-1],
            0,
            slab_place == 0,
            slab_place == slab_parts - 1,
            True,
        )
        diffusion_term = diffusion_term + flow(
            padded_warm[1:-1, :, 1:-1],
            padded_cond[1:-1, :, 1:-1],
            1,
            row_place == 0,
            row_place == row_parts - 1,
            False,
        )
        diffusion_term = diffusion_term + flow(
            padded_warm[1:-1, 1:-1, :],
            padded_cond[1:-1, 1:-1, :],
            2,
            column_place == 0,
            column_place == column_parts - 1,
            False,
        )
        power_input = HEAT_SPREADING * diffusion_term + OHMIC_POWER * (
            (1.0 + WARMING_SLOPE * warmth_excess) * ohmic_loss
        )
        local_rows = jnp.einsum("zij,zjy->ziy", row_inverse, power_input, precision=EXACT)
        own_rows = (
            local_rows[:, 0, :],
            local_rows[:, -1, :],
            row_low[:, 0:1],
            row_low[:, -1:],
            row_high[:, 0:1],
            row_high[:, -1:],
        )
        rows_neutral = identity_of(own_rows)
        rows_before = carried_in(
            (own_rows[0], own_rows[1], own_rows[2], own_rows[3], own_rows[4], own_rows[5]),
            "gx",
            join,
            rows_neutral,
            False,
        )
        rows_after = carried_in(
            (own_rows[0], own_rows[1], own_rows[2], own_rows[3], own_rows[4], own_rows[5]),
            "gx",
            flipped,
            rows_neutral,
            True,
        )
        before, after = settle(own_rows, rows_before, rows_after)
        first_pass = (
            local_rows
            - row_low[:, :, None] * before[:, None, :]
            - row_high[:, :, None] * after[:, None, :]
        )
        local_columns = jnp.einsum("zxj,zij->zxi", first_pass, column_inverse, precision=EXACT)
        own_columns = (
            local_columns[:, :, 0],
            local_columns[:, :, -1],
            column_low[:, 0:1],
            column_low[:, -1:],
            column_high[:, 0:1],
            column_high[:, -1:],
        )
        columns_neutral = identity_of(own_columns)
        columns_before = carried_in(
            (
                own_columns[0],
                own_columns[1],
                own_columns[2],
                own_columns[3],
                own_columns[4],
                own_columns[5],
            ),
            "gy",
            join,
            columns_neutral,
            False,
        )
        columns_after = carried_in(
            (
                own_columns[0],
                own_columns[1],
                own_columns[2],
                own_columns[3],
                own_columns[4],
                own_columns[5],
            ),
            "gy",
            flipped,
            columns_neutral,
            True,
        )
        before, after = settle(own_columns, columns_before, columns_after)
        second_pass = (
            local_columns
            - column_low[:, None, :] * before[:, :, None]
            - column_high[:, None, :] * after[:, :, None]
        )
        local_slabs = jnp.dot(
            slab_inverse, second_pass.reshape(sheet_voxel_total, -1), precision=EXACT
        ).reshape(sheet_voxel_total, horizontal_voxel_total, vertical_voxel_total)
        own_slabs = (
            local_slabs[0],
            local_slabs[-1],
            slab_low[0].reshape(1, 1),
            slab_low[-1].reshape(1, 1),
            slab_high[0].reshape(1, 1),
            slab_high[-1].reshape(1, 1),
        )
        neutral = identity_of(own_slabs)
        slabs_before = carried_in(
            (own_slabs[0], own_slabs[1], own_slabs[2], own_slabs[3], own_slabs[4], own_slabs[5]),
            "gz",
            join,
            neutral,
            False,
        )
        slabs_after = carried_in(
            (own_slabs[0], own_slabs[1], own_slabs[2], own_slabs[3], own_slabs[4], own_slabs[5]),
            "gz",
            flipped,
            neutral,
            True,
        )
        before, after = settle(own_slabs, slabs_before, slabs_after)
        vertical_sweep_final = (
            local_slabs
            - slab_low[:, None, None] * before[None]
            - slab_high[:, None, None] * after[None]
        )
        warmth_excess = warmth_excess + vertical_sweep_final
    ohmic_power_final = (1.0 + WARMING_SLOPE * warmth_excess) * ohmic_loss
    return (warmth_excess, ohmic_power_final)


def solution(mesh):
    return jax.shard_map(
        per_device,
        mesh=mesh,
        in_specs=(
            P("gz", "gx", "gy"),
            P(),
            P(),
            P("gz", "gx", "gy"),
            P(),
            P(("gx", "gy", "gz")),
            P(("gx", "gy", "gz")),
            P(("gx", "gy", "gz"), None),
            P(("gx", "gy", "gz")),
        ),
        out_specs=(P("gz", "gx", "gy"), P("gz", "gx", "gy")),
        check_vma=False,
    )
```

profile of v0, /device:TPU:0, one launch (start us, length us, event | category | flops | bytes accessed | tf_op | source)
XLA Modules:
  0.0 1163.5 jit_solution(14618857172319072211)
XLA Ops:
  2.9 4.2 add_multiply_fusion.2
  7.8 4.8 collective-permute-start
  14.5 5.1 collective-permute-start.6
  21.0 9.2 reduce-window.6
  31.9 16.3 %scatter_custom_fusion = s32[8192]{0:T(1024)} fusion(s32[4096]{0:T(1024)S(1)} %bitcast.959, s32[4096]{0:T(1024)} %param.41, s32[]{:T(128)} %constant.722.clone.1), kind=kCustom, calls=%fused_computation.512 | custom fusion | bytes 33280 | tf_op jit(solution)/shard_map/scatter | solution.py:195
  48.1 8.0 all-to-all-start
  67.3 93.8 %custom-call.42 = f32[8,128,128]{2,1,0:T(8,128)S(1)} custom-call(f32[8,128,128]{2,1,0:T(8,128)S(1)} %cholesky.242), custom_call_target="Cholesky" | custom-call | tf_op jit(solution)/shard_map/jit(cholesky)/cholesky | solution.py:61
  161.9 79.2 %custom-call.43 = f32[8,1,128,128]{2,3,1,0:T(8,128)} custom-call(f32[8,1,128,128]{3,2,1,0:T(8,128)S(1)} %select_bitcast_fusion.1), custom_call_target="InvertDiagBlocksLowerTriangular" | custom-call | tf_op jit(solution)/shard_map/jit(cholesky)/cholesky | solution.py:61
  246.2 94.6 %custom-call.44 = f32[8,128,128]{2,1,0:T(8,128)} custom-call(f32[8,128,128]{2,1,0:T(8,128)S(1)} %convolution_subtract_fusion.2), custom_call_target="Cholesky" | custom-call | tf_op jit(solution)/shard_map/jit(cholesky)/cholesky | solution.py:61
  342.4 2.0 add_multiply_fusion.3
  344.4 94.6 %custom-call.46 = f32[8,128,128]{2,1,0:T(8,128)S(1)} custom-call(f32[8,128,128]{2,1,0:T(8,128)} %add_multiply_fusion.3), custom_call_target="Cholesky" | custom-call | tf_op jit(solution)/shard_map/jit(cholesky)/cholesky | solution.py:61
  438.9 2.6 select_reduce_fusion.1
  442.6 79.4 %custom-call.47 = f32[8,1,128,128]{2,3,1,0:T(8,128)S(1)} custom-call(f32[8,1,128,128]{3,2,1,0:T(8,128)} %select_bitcast_fusion), custom_call_target="InvertDiagBlocksLowerTriangular" | custom-call | tf_op jit(solution)/shard_map/jit(_cho_solve)/vmap()/triangular_solve | solution.py:62
  525.9 3.3 select_select_fusion
  529.3 7.9 while.205
  529.9 3.5 bitcast_dynamic-update-slice_fusion.6
  533.9 3.3 bitcast_dynamic-update-slice_fusion.6
  537.2 158.2 %custom-call.45 = f32[8,2,128,128]{2,3,1,0:T(8,128)S(1)} custom-call(f32[8,2,128,128]{3,2,1,0:T(8,128)} %bitcast.972), custom_call_target="InvertDiagBlocksLowerTriangular" | custom-call | tf_op jit(solution)/shard_map/jit(_cho_solve)/vmap()/triangular_solve | solution.py:62
  696.4 2.1 convolution_subtract_fusion.1
  700.6 2.5 convolution_subtract_fusion
  704.3 2.1 multiply_reduce_fusion.1
  718.6 12.1 %all-reduce.15 = (f32[4]{0:T(128)S(1)}, f32[4]{0:T(128)S(1)}, f32[4]{0:T(128)S(1)}, f32[4]{0:T(128)S(1)}) all-reduce(f32[4]{0:T(128)S(1)} %bitcast_dynamic-update-slice_fusion.1, f32[4]{0:T(128)S(1)} %bitcast_dynamic-update-slice_fusion.2, f32[4]{0:T(128)S(1)} %bitcast_dynamic-update-slice_fusion.3, ...), channel_id=17, replica_groups=mesh['gx'=4,'gy'=2,'gz'=4] {'gz'}, use_global_device_ids=true, to_apply=%add.14 | all-reduce | flops 16 | bytes 128
  734.2 2.4 all-reduce.17
  739.0 10.2 all-reduce.16
  754.5 16.2 %scatter_custom_fusion.1 = f32[8192]{0:T(1024)} fusion(s32[4096]{0:T(1024)} %bitcast.960, f32[4096]{0:T(1024)S(1)} %multiply_multiply_fusion, f32[]{:T(128)} %constant.716.clone.1), kind=kCustom, calls=%fused_computation.510 | custom fusion | bytes 33280 | tf_op jit(solution)/shard_map/scatter | solution.py:190
  774.0 1.9 collective-permute-start.2
  780.3 2.3 copy.802
  782.6 4.2 collective-permute-start.8
  792.4 2.1 copy.801
  794.5 2.1 copy.804
  796.6 2.1 copy.805
  798.7 3.2 fusion.147
  806.1 2.0 collective-permute-start.4
  812.5 5.9 collective-permute-start.11
  818.4 3.3 all-to-all-start.1
  823.1 5.9 all-to-all-done.1
  828.9 53.5 %scatter_custom_fusion.2 = f32[262144]{0:T(1024)} fusion(s32[8192]{0:T(1024)} %bitcast.950, f32[8192]{0:T(1024)} %bitcast.21, f32[]{:T(128)} %constant.716.clone.1), kind=kCustom, calls=%fused_computation.429 | custom fusion | flops 8192 | bytes 1049088 | tf_op jit(solution)/shard_map/scatter-add | solution.py:207
  882.5 4.9 fusion.155
  889.1 2.7 fusion.151
  892.8 7.6 all-gather
  900.4 7.7 all-gather.2
  908.1 5.8 while.207
  914.0 5.6 while.206
  920.1 3.0 fusion.222
  931.8 2.7 fusion.166
  934.7 16.0 %all_gather.84 = f32[4,256,128]{2,1,0:T(8,128)S(1)} all-gather(f32[1,256,128]{2,1,0:T(8,128)S(1)} %bitcast.919), channel_id=1, replica_groups=mesh['gx'=4,'gy'=2,'gz'=4] {'gz'}, dimensions={0}, use_global_device_ids=true | all-gather | bytes 655360 | tf_op jit(solution)/shard_map/all_gather | solution.py:18
  950.7 15.0 %all_gather.86 = f32[4,256,128]{2,1,0:T(8,128)S(1)} all-gather(f32[1,256,128]{2,1,0:T(8,128)S(1)} %bitcast.921), channel_id=1, replica_groups=mesh['gx'=4,'gy'=2,'gz'=4] {'gz'}, dimensions={0}, use_global_device_ids=true | all-gather | bytes 655360 | tf_op jit(solution)/shard_map/all_gather | solution.py:18
  965.7 23.5 %while.210 = (s32[]{:T(128)}, f32[256,128]{1,0:T(8,128)S(1)}, f32[1,1]{1,0:T(1,128)}, s32[]{:T(128)}, f32[4,256,128]{2,1,0:T(8,128)S(1)}, /*index=5*/f32[4,1,1]{...) while((s32[]{:T(128)}, f32[256,128]{1,0:T(8,128)S(1)}, ...), condition=%wide.region_24.25_spmd.clone, body=%wide.region_23.24_spmd.clone.sunk | while | flops 229388 | bytes 524590 | solution.py:31
  989.9 23.3 %while.211 = (s32[]{:T(128)}, f32[256,128]{1,0:T(8,128)S(1)}, f32[1,1]{1,0:T(1,128)}, s32[]{:T(128)}, f32[4,256,128]{2,1,0:T(8,128)S(1)}, /*index=5*/f32[4,1,1]{...) while((s32[]{:T(128)}, f32[256,128]{1,0:T(8,128)S(1)}, ...), condition=%wide.region_26.27_spmd.clone, body=%wide.region_25.26_spmd.clone.sunk | while | flops 229392 | bytes 524644 | solution.py:31
  1013.8 3.5 multiply_subtract_fusion.7
  1019.0 3.4 collective-permute-start.12
  1023.7 4.1 collective-permute-done.13
  1042.8 4.8 collective-permute-start.17
  1047.6 3.0 fusion.145
  1056.6 2.8 fusion.150
  1060.3 9.0 all-gather.16
  1069.3 6.6 all-gather.17
  1077.6 3.0 fusion.213
  1089.9 15.3 %all_gather.94 = f32[4,256,128]{2,1,0:T(8,128)S(1)} all-gather(f32[1,256,128]{2,1,0:T(8,128)S(1)} %bitcast.915), channel_id=1, replica_groups=mesh['gx'=4,'gy'=2,'gz'=4] {'gz'}, dimensions={0}, use_global_device_ids=true | all-gather | bytes 655360 | tf_op jit(solution)/shard_map/all_gather | solution.py:18
  1105.2 16.2 %all_gather.95 = f32[4,256,128]{2,1,0:T(8,128)S(1)} all-gather(f32[1,256,128]{2,1,0:T(8,128)S(1)} %bitcast.917), channel_id=1, replica_groups=mesh['gx'=4,'gy'=2,'gz'=4] {'gz'}, dimensions={0}, use_global_device_ids=true | all-gather | bytes 655360 | tf_op jit(solution)/shard_map/all_gather | solution.py:18
  1121.4 16.6 %while.217 = (s32[]{:T(128)}, f32[256,128]{1,0:T(8,128)S(1)}, f32[1,1]{1,0:T(1,128)}, s32[]{:T(128)}, f32[4,256,128]{2,1,0:T(8,128)S(1)}, /*index=5*/f32[4,1,1]{...) while((s32[]{:T(128)}, f32[256,128]{1,0:T(8,128)S(1)}, ...), condition=%wide.region_38.39_spmd.clone, body=%wide.region_37.38_spmd.clone.sunk | while | flops 229392 | bytes 524644 | solution.py:31
  1138.5 17.6 %while.216 = (s32[]{:T(128)}, f32[256,128]{1,0:T(8,128)S(1)}, f32[1,1]{1,0:T(1,128)}, s32[]{:T(128)}, f32[4,256,128]{2,1,0:T(8,128)S(1)}, /*index=5*/f32[4,1,1]{...) while((s32[]{:T(128)}, f32[256,128]{1,0:T(8,128)S(1)}, ...), condition=%wide.region_36.37_spmd.clone, body=%wide.region_35.36_spmd.clone.sunk | while | flops 229388 | bytes 524590 | solution.py:31
  1156.8 3.5 multiply_subtract_fusion.3
  1160.3 3.0 add_multiply_fusion.1
  (588 shorter events, 178.8 us)
Async XLA Ops:
  0.6 20.3 %copy-start.39 = (s32[4096,1]{0,1:T(1,128)S(1)}, s32[4096,1]{0,1:T(1,128)}, u32[]{:S(2)}) copy-start(s32[4096,1]{0,1:T(1,128)} %param.40) | copy-start | bytes 49156
  7.8 763.0 %collective-permute-start = (f32[8,1,128]{2,1,0:T(1,128)}, f32[8,1,128]{2,1,0:T(1,128)S(1)}, u32[]{:S(2)}, u32[]{:S(2)}) collective-permute-start(f32[8,1,128]{2,1,0:T(1,128)} %get-tuple-element.4255), channel_id=1, source_target_pairs={{0,8},{8,16},{16,24},{1,9},{9,17},{17,25},{2,10},{10,18},{18,26},{... | collective-permute-start | bytes 12296 | tf_op jit(solution)/shard_map/ppermute | solution.py:41
  12.6 758.1 %collective-permute-start.1 = (f32[8,1,128]{2,1,0:T(1,128)}, f32[8,1,128]{2,1,0:T(1,128)S(1)}, u32[]{:S(2)}, u32[]{:S(2)}) collective-permute-start(f32[8,1,128]{2,1,0:T(1,128)} %get-tuple-element.4256), channel_id=1, source_target_pairs={{8,0},{16,8},{24,16},{9,1},{17,9},{25,17},{10,2},{18,10},{26,18},{... | collective-permute-start | bytes 12296 | tf_op jit(solution)/shard_map/ppermute | solution.py:42
  14.5 763.7 %collective-permute-start.6 = (f32[8,1,128]{2,1,0:T(1,128)}, f32[8,1,128]{2,1,0:T(1,128)}, u32[]{:S(2)}, u32[]{:S(2)}) collective-permute-start(f32[8,1,128]{2,1,0:T(1,128)} %get-tuple-element.4257), channel_id=1, source_target_pairs={{0,8},{8,16},{16,24},{1,9},{9,17},{17,25},{2,10},{10,18},{18,26},{... | collective-permute-start | bytes 12296 | tf_op jit(solution)/shard_map/ppermute | solution.py:41
  19.7 758.6 %collective-permute-start.7 = (f32[8,1,128]{2,1,0:T(1,128)}, f32[8,1,128]{2,1,0:T(1,128)}, u32[]{:S(2)}, u32[]{:S(2)}) collective-permute-start(f32[8,1,128]{2,1,0:T(1,128)} %get-tuple-element.4258), channel_id=1, source_target_pairs={{8,0},{16,8},{24,16},{9,1},{17,9},{25,17},{10,2},{18,10},{26,18},{... | collective-permute-start | bytes 12296 | tf_op jit(solution)/shard_map/ppermute | solution.py:42
  31.9 27.1 %copy-start.67 = (s32[4096,1]{0,1:T(1,128)}, s32[4096,1]{0,1:T(1,128)S(1)}, u32[]{:S(2)}) copy-start(s32[4096,1]{0,1:T(1,128)S(1)} %compare_select_fusion.1) | copy-start | bytes 49156
  48.1 770.2 %all-to-all-start = ((s32[32,1,256]{2,1,0:T(1,128)}), s32[32,1,256]{2,1,0:T(1,128)}, u32[]{:S(2)}, u32[]{:S(2)}) async-start(s32[32,1,256]{2,1,0:T(1,128)} %bitcast.17), calls=%async_computation | async-start | bytes 65536 | tf_op jit(solution)/shard_map/all_to_all | solution.py:200
  245.0 97.4 %copy-start.54 = (f32[8,128]{1,0:T(8,128)S(1)}, f32[8,128]{1,0:T(8,128)}, u32[]{:S(2)}) copy-start(f32[8,128]{1,0:T(8,128)} %fusion.296) | copy-start | bytes 12292
  525.4 207.9 %copy-start.74 = (f32[8]{0:T(128)}, f32[8]{0:T(128)S(1)}, u32[]{:S(2)}) copy-start(f32[8]{0:T(128)S(1)} %get-tuple-element.3905) | copy-start | bytes 100
  525.4 208.1 %copy-start.77 = (f32[8]{0:T(128)}, f32[8]{0:T(128)S(1)}, u32[]{:S(2)}) copy-start(f32[8]{0:T(128)S(1)} %get-tuple-element.3906) | copy-start | bytes 100
  525.7 208.1 %copy-start.80 = (f32[8]{0:T(128)}, f32[8]{0:T(128)S(1)}, u32[]{:S(2)}) copy-start(f32[8]{0:T(128)S(1)} %get-tuple-element.3907) | copy-start | bytes 100
  525.7 208.3 %copy-start.83 = (f32[8]{0:T(128)}, f32[8]{0:T(128)S(1)}, u32[]{:S(2)}) copy-start(f32[8]{0:T(128)S(1)} %get-tuple-element.3908) | copy-start | bytes 100
  704.2 27.7 %copy-start.106 = (u32[32]{0:T(128)S(1)}, u32[32]{0:T(128)}, u32[]{:S(2)}) copy-start(u32[32]{0:T(128)} %constant.788) | copy-start | bytes 388
  704.3 32.7 %copy-start.105 = (u32[32]{0:T(128)S(1)}, u32[32]{0:T(128)}, u32[]{:S(2)}) copy-start(u32[32]{0:T(128)} %constant.768) | copy-start | bytes 388
  706.6 64.2 %copy-start.86 = (f32[8]{0:T(128)}, f32[8]{0:T(128)S(1)}, u32[]{:S(2)}) copy-start(f32[8]{0:T(128)S(1)} %get-tuple-element.3901) | copy-start | bytes 100
  706.6 64.2 %copy-start.89 = (f32[8]{0:T(128)}, f32[8]{0:T(128)S(1)}, u32[]{:S(2)}) copy-start(f32[8]{0:T(128)S(1)} %get-tuple-element.3902) | copy-start | bytes 100
  706.9 63.9 %copy-start.92 = (f32[8]{0:T(128)}, f32[8]{0:T(128)S(1)}, u32[]{:S(2)}) copy-start(f32[8]{0:T(128)S(1)} %get-tuple-element.3903) | copy-start | bytes 100
  706.9 63.9 %copy-start.95 = (f32[8]{0:T(128)}, f32[8]{0:T(128)S(1)}, u32[]{:S(2)}) copy-start(f32[8]{0:T(128)S(1)} %get-tuple-element.3904) | copy-start | bytes 100
  710.1 26.5 %copy-start.51 = (f32[8,8]{0,1:T(8,128)}, f32[8,8]{0,1:T(8,128)S(1)}, u32[]{:S(2)}) copy-start(f32[8,8]{0,1:T(8,128)S(1)} %fusion.301) | copy-start | bytes 772
  711.5 59.4 %copy-start.68 = (f32[8,1]{0,1:T(1,128)}, f32[8,1]{0,1:T(1,128)S(1)}, u32[]{:S(2)}) copy-start(f32[8,1]{0,1:T(1,128)S(1)} %get-tuple-element.4276) | copy-start | bytes 100
  774.0 17.3 %collective-permute-start.2 = (f32[8,258,1]{1,0,2:T(8,128)S(1)}, f32[8,258,1]{1,0,2:T(8,128)}, u32[]{:S(2)}, u32[]{:S(2)}) collective-permute-start(f32[8,258,1]{1,0,2:T(8,128)S(1)} %copy.798), channel_id=1, source_target_pairs={{0,4},{1,5},{2,6},{3,7},{8,12},{9,13},{10,14},{11,15},{16,20},{17,... | collective-permute-start | bytes 24776 | tf_op jit(solution)/shard_map/ppermute | solution.py:41
  776.9 15.5 %collective-permute-start.3 = (f32[8,258,1]{1,0,2:T(8,128)}, f32[8,258,1]{1,0,2:T(8,128)}, u32[]{:S(2)}, u32[]{:S(2)}) collective-permute-start(f32[8,258,1]{1,0,2:T(8,128)} %copy.799), channel_id=1, source_target_pairs={{4,0},{5,1},{6,2},{7,3},{12,8},{13,9},{14,10},{15,11},{20,16},{21,... | collective-permute-start | bytes 24776 | tf_op jit(solution)/shard_map/ppermute | solution.py:42
  782.6 11.9 %collective-permute-start.8 = (f32[8,258,1]{1,0,2:T(8,128)}, f32[8,258,1]{1,0,2:T(8,128)}, u32[]{:S(2)}, u32[]{:S(2)}) collective-permute-start(f32[8,258,1]{1,0,2:T(8,128)} %copy.802), channel_id=1, source_target_pairs={{0,4},{1,5},{2,6},{3,7},{8,12},{9,13},{10,14},{11,15},{16,20},{17,... | collective-permute-start | bytes 24776 | tf_op jit(solution)/shard_map/ppermute | solution.py:41
  787.9 8.7 collective-permute-start.9
  792.4 90.1 %copy-start.1 = (f32[8,258,1]{2,1,0:T(8,128)}, f32[8,258,1]{2,1,0:T(8,128)S(1)}, u32[]{:S(2)}) copy-start(f32[8,258,1]{2,1,0:T(8,128)S(1)} %copy.800) | copy-start | bytes 24772
  806.1 76.4 %collective-permute-start.4 = (f32[1,258,130]{2,1,0:T(8,128)}, f32[1,258,130]{2,1,0:T(8,128)}, u32[]{:S(2)}, u32[]{:S(2)}) collective-permute-start(f32[1,258,130]{2,1,0:T(8,128)} %get-tuple-element.4219), channel_id=1, source_target_pairs={{0,1},{1,2},{2,3},{4,5},{5,6},{6,7},{8,9},{9,10},{10,11},{12,13},{... | collective-permute-start | bytes 402488 | tf_op jit(solution)/shard_map/ppermute | solution.py:41
  808.1 74.4 %collective-permute-start.5 = (f32[1,258,130]{2,1,0:T(8,128)}, f32[1,258,130]{2,1,0:T(8,128)}, u32[]{:S(2)}, u32[]{:S(2)}) collective-permute-start(f32[1,258,130]{2,1,0:T(8,128)} %get-tuple-element.4220), channel_id=1, source_target_pairs={{1,0},{2,1},{3,2},{5,4},{6,5},{7,6},{9,8},{10,9},{11,10},{13,12},{... | collective-permute-start | bytes 402488 | tf_op jit(solution)/shard_map/ppermute | solution.py:42
  811.2 71.3 %collective-permute-start.10 = (f32[1,258,130]{2,1,0:T(8,128)}, f32[1,258,130]{2,1,0:T(8,128)}, u32[]{:S(2)}, u32[]{:S(2)}) collective-permute-start(f32[1,258,130]{2,1,0:T(8,128)} %get-tuple-element.4221), channel_id=1, source_target_pairs={{1,0},{2,1},{3,2},{5,4},{6,5},{7,6},{9,8},{10,9},{11,10},{13,12},{... | collective-permute-start | bytes 402488 | tf_op jit(solution)/shard_map/ppermute | solution.py:42
  812.5 70.0 %collective-permute-start.11 = (f32[1,258,130]{2,1,0:T(8,128)}, f32[1,258,130]{2,1,0:T(8,128)}, u32[]{:S(2)}, u32[]{:S(2)}) collective-permute-start(f32[1,258,130]{2,1,0:T(8,128)} %get-tuple-element.4222), channel_id=1, source_target_pairs={{0,1},{1,2},{2,3},{4,5},{5,6},{6,7},{8,9},{9,10},{10,11},{12,13},{... | collective-permute-start | bytes 402488 | tf_op jit(solution)/shard_map/ppermute | solution.py:41
  818.4 10.6 all-to-all-start.1
  889.0 19.1 %copy-start.40 = (f32[8,128]{1,0:T(8,128)S(1)}, f32[8,128]{1,0:T(8,128)}, u32[]{:S(2)}) copy-start(f32[8,128]{1,0:T(8,128)} %custom-call.50) | copy-start | bytes 12292
  889.0 19.1 %copy-start.60 = (f32[8,1]{0,1:T(1,128)S(1)}, f32[8,1]{0,1:T(1,128)}, u32[]{:S(2)}) copy-start(f32[8,1]{0,1:T(1,128)} %custom-call.51) | copy-start | bytes 100
  889.0 25.0 %copy-start.58 = (f32[8,1]{0,1:T(1,128)S(1)}, f32[8,1]{0,1:T(1,128)}, u32[]{:S(2)}) copy-start(f32[8,1]{0,1:T(1,128)} %custom-call.49) | copy-start | bytes 100
  889.0 30.9 %copy-start.87 = (f32[8]{0:T(128)S(1)}, f32[8]{0:T(128)}, u32[]{:S(2)}) copy-start(f32[8]{0:T(128)} %copy-done.86) | copy-start | bytes 100
  889.0 30.9 %copy-start.90 = (f32[8]{0:T(128)S(1)}, f32[8]{0:T(128)}, u32[]{:S(2)}) copy-start(f32[8]{0:T(128)} %copy-done.89) | copy-start | bytes 100
  889.0 30.9 %copy-start.93 = (f32[8]{0:T(128)S(1)}, f32[8]{0:T(128)}, u32[]{:S(2)}) copy-start(f32[8]{0:T(128)} %copy-done.92) | copy-start | bytes 100
  889.0 30.9 %copy-start.96 = (f32[8]{0:T(128)S(1)}, f32[8]{0:T(128)}, u32[]{:S(2)}) copy-start(f32[8]{0:T(128)} %copy-done.95) | copy-start | bytes 100
  889.0 31.0 %copy-start.23 = (f32[8,128,128]{1,2,0:T(8,128)S(1)}, f32[8,128,128]{1,2,0:T(8,128)}, u32[]{:S(2)}) copy-start(f32[8,128,128]{1,2,0:T(8,128)} %copy-done.22) | copy-start | bytes 1572868
  889.0 31.0 %copy-start.41 = (f32[8,256]{1,0:T(8,128)S(1)}, f32[8,256]{1,0:T(8,128)}, u32[]{:S(2)}) copy-start(f32[8,256]{1,0:T(8,128)} %get-tuple-element.3872) | copy-start | bytes 24580
  989.9 27.5 %copy-start.69 = (f32[8,1]{0,1:T(1,128)S(1)}, f32[8,1]{0,1:T(1,128)}, u32[]{:S(2)}) copy-start(f32[8,1]{0,1:T(1,128)} %copy-done.68) | copy-start | bytes 100
  989.9 27.5 %copy-start.71 = (f32[8,1]{0,1:T(1,128)S(1)}, f32[8,1]{0,1:T(1,128)}, u32[]{:S(2)}) copy-start(f32[8,1]{0,1:T(1,128)} %copy-done.70) | copy-start | bytes 100
  1019.0 4.8 collective-permute-start.12
  1022.3 5.5 collective-permute-start.13
  1031.4 5.7 collective-permute-start.14
  1034.4 4.2 collective-permute-start.15
  1041.5 11.1 collective-permute-start.16
  1042.8 11.3 collective-permute-start.17
  1056.5 19.4 %copy-start.47 = (f32[4,8,1]{1,2,0:T(1,128)S(1)}, f32[4,8,1]{1,2,0:T(1,128)}, u32[]{:S(2)}) copy-start(f32[4,8,1]{1,2,0:T(1,128)} %get-tuple-element.5684) | copy-start | bytes 388
  1056.5 19.4 %copy-start.48 = (f32[4,8,1]{1,2,0:T(1,128)S(1)}, f32[4,8,1]{1,2,0:T(1,128)}, u32[]{:S(2)}) copy-start(f32[4,8,1]{1,2,0:T(1,128)} %get-tuple-element.5687) | copy-start | bytes 388
  1056.5 19.4 %copy-start.49 = (f32[4,8,1]{1,2,0:T(1,128)S(1)}, f32[4,8,1]{1,2,0:T(1,128)}, u32[]{:S(2)}) copy-start(f32[4,8,1]{1,2,0:T(1,128)} %get-tuple-element.5690) | copy-start | bytes 388
  1056.5 19.4 %copy-start.50 = (f32[4,8,1]{1,2,0:T(1,128)S(1)}, f32[4,8,1]{1,2,0:T(1,128)}, u32[]{:S(2)}) copy-start(f32[4,8,1]{1,2,0:T(1,128)} %get-tuple-element.5693) | copy-start | bytes 388
  1056.5 19.4 %copy-start.62 = (f32[8,1]{0,1:T(1,128)S(1)}, f32[8,1]{0,1:T(1,128)}, u32[]{:S(2)}) copy-start(f32[8,1]{0,1:T(1,128)} %custom-call.61) | copy-start | bytes 100
  1056.5 20.0 %copy-start.61 = (f32[8,1]{0,1:T(1,128)S(1)}, f32[8,1]{0,1:T(1,128)}, u32[]{:S(2)}) copy-start(f32[8,1]{0,1:T(1,128)} %custom-call.59) | copy-start | bytes 100
  1056.5 20.8 %copy-start.88 = (f32[8]{0:T(128)S(1)}, f32[8]{0:T(128)}, u32[]{:S(2)}) copy-start(f32[8]{0:T(128)} %copy-done.86) | copy-start | bytes 100
  1056.5 20.8 %copy-start.91 = (f32[8]{0:T(128)S(1)}, f32[8]{0:T(128)}, u32[]{:S(2)}) copy-start(f32[8]{0:T(128)} %copy-done.89) | copy-start | bytes 100
  1056.5 20.8 %copy-start.94 = (f32[8]{0:T(128)S(1)}, f32[8]{0:T(128)}, u32[]{:S(2)}) copy-start(f32[8]{0:T(128)} %copy-done.92) | copy-start | bytes 100
  1056.6 20.8 %copy-start.97 = (f32[8]{0:T(128)S(1)}, f32[8]{0:T(128)}, u32[]{:S(2)}) copy-start(f32[8]{0:T(128)} %copy-done.95) | copy-start | bytes 100
  1056.6 20.9 %copy-start.24 = (f32[8,128,128]{1,2,0:T(8,128)S(1)}, f32[8,128,128]{1,2,0:T(8,128)}, u32[]{:S(2)}) copy-start(f32[8,128,128]{1,2,0:T(8,128)} %copy-done.22) | copy-start | bytes 1572868
  1056.6 20.9 %copy-start.42 = (f32[8,256]{1,0:T(8,128)S(1)}, f32[8,256]{1,0:T(8,128)}, u32[]{:S(2)}) copy-start(f32[8,256]{1,0:T(8,128)} %get-tuple-element.3872) | copy-start | bytes 24580
  1089.6 31.7 %copy-start.43 = (f32[4,1,1]{2,1,0:T(1,128)S(1)}, f32[4,1,1]{2,1,0:T(1,128)}, u32[]{:S(2)}) copy-start(f32[4,1,1]{2,1,0:T(1,128)} %get-tuple-element.5672) | copy-start | bytes 52
  1089.7 31.7 %copy-start.44 = (f32[4,1,1]{2,1,0:T(1,128)S(1)}, f32[4,1,1]{2,1,0:T(1,128)}, u32[]{:S(2)}) copy-start(f32[4,1,1]{2,1,0:T(1,128)} %get-tuple-element.5675) | copy-start | bytes 52
  1089.7 31.7 %copy-start.45 = (f32[4,1,1]{2,1,0:T(1,128)S(1)}, f32[4,1,1]{2,1,0:T(1,128)}, u32[]{:S(2)}) copy-start(f32[4,1,1]{2,1,0:T(1,128)} %get-tuple-element.5678) | copy-start | bytes 52
  1089.7 31.7 %copy-start.46 = (f32[4,1,1]{2,1,0:T(1,128)S(1)}, f32[4,1,1]{2,1,0:T(1,128)}, u32[]{:S(2)}) copy-start(f32[4,1,1]{2,1,0:T(1,128)} %get-tuple-element.5681) | copy-start | bytes 52
  1138.5 21.8 %copy-start.17 = (f32[262144]{0:T(1024)S(1)}, f32[262144]{0:T(1024)}, u32[]{:S(2)}) copy-start(f32[262144]{0:T(1024)} %scatter_custom_fusion.2) | copy-start | bytes 3145732
  (65 other events, 347.1 us)
where the time goes:
time: 1180 us; the launch traced here: 1160 us
  other arithmetic  750 us (64%)
  local copies, waits for them, and re-layouts  139 us (12%)
  blocking collectives  125 us (11%)
  starting transfers between devices  56.2 us (5%)
  loops' own time  41.3 us (4%)
  matrix products  29.6 us (3%)
  waiting for transfers between devices  12.9 us (1%)
    another operation x15, other arithmetic, band_inverse(): factor = jnp.linalg.cholesky(matrix)  369 us
    another operation x8, other arithmetic, band_inverse(): jax.scipy.linalg.cho_solve((factor, True), jnp.broadcast_to(unit_matrix,...  244 us
    all_gather x12, blocking collectives, carried_in(): everything = jax.tree.map(lambda part: lax.all_gather(part, axis), array)  101 us
    scatter-add x1, other arithmetic, per_device(): ohmic_loss = ohmic_loss.at[got_cell.reshape(-1)].add(got_power.reshape(-1...  53.5 us
    another operation x12, loops' own time, carried_in(): return lax.fori_loop(0, count, hop, start)  41.3 us
    ppermute x9, starting transfers between devices, padded_2(): before = lax.ppermute(last, axis, up)  33.4 us
    dynamic_slice x32, local copies, waits for them, and re-layouts, hop(): new = combine(before, jax.tree.map(lambda part: part[at], everything))  28.7 us
    unnamed x3, blocking collectives  24.8 us
  transfers between devices with their start and end apart: 20, of which 4 were waited for; matrix products, arithmetic and copies ran while one was open for 69% of the time, Pallas kernels for 0%

commit v1 on v0

v1 whole, which is shorter than its diff:
```python
import functools

import jax
import jax.numpy as jnp
from jax import lax
from jax.experimental import pallas as pl
from jax.experimental.pallas import tpu as pltpu
from jax.sharding import PartitionSpec as P

STEPS = 2
HEAT_SPREADING = 1000.0
STIFF = 1.5
WARMING_SLOPE = 0.1
OHMIC_POWER = 8.0

F32 = jnp.float32
BF16 = jnp.bfloat16
EXTRA = 16
SLOT = 8
EXACT = lax.Precision.HIGHEST


def call(kernel, out_shapes, args, smem=0, vmem=48, flops=0):
    nbytes = sum(a.size * a.dtype.itemsize for a in args)
    nbytes += sum(o.size * o.dtype.itemsize for o in out_shapes)
    specs = [pl.BlockSpec(memory_space=pltpu.SMEM)] * smem
    specs += [pl.BlockSpec(memory_space=pltpu.VMEM)] * (len(args) - smem)
    return pl.pallas_call(
        kernel,
        out_shape=out_shapes,
        in_specs=specs,
        out_specs=[pl.BlockSpec(memory_space=pltpu.VMEM)] * len(out_shapes),
        compiler_params=pltpu.CompilerParams(vmem_limit_bytes=vmem * 2**20),
        cost_estimate=pl.CostEstimate(flops=flops, bytes_accessed=nbytes, transcendentals=0),
    )(*args)


def shaped(*shape, dtype=F32):
    return jax.ShapeDtypeStruct(shape, dtype)


def split(x):
    high = x.astype(BF16)
    return high, (x - high.astype(F32)).astype(BF16)


def iota(shape, dim):
    return lax.broadcasted_iota(jnp.int32, shape, dim)


def mm(a, b):
    return jnp.dot(a, b, preferred_element_type=F32)


def mm_nt(a, b):
    return lax.dot_general(a, b, (((1,), (1,)), ((), ())), preferred_element_type=F32)


def partner(me, k, n):
    return me ^ k if n & (n - 1) == 0 else lax.rem(me + k, n)


def groups(n):
    return [k.bit_length() - 1 for k in range(1, n)]


def all_pairs(arrays, axis):
    n = lax.axis_size(axis)
    return [
        lax.ppermute(arrays[b], axis, [(i, i ^ k) for i in range(n)])
        for k, b in zip(range(1, n), groups(n))
    ]


def next_pairs(even, odd, axis):
    n = lax.axis_size(axis)
    first = lax.ppermute(even, axis, [(i, i ^ 1) for i in range(n)])
    if n == 2:
        return first, first
    other = {i: (i + 1) % n if i % 2 else (i - 1) % n for i in range(n)}
    return first, lax.ppermute(odd, axis, list(other.items()))


def faces_kernel(
    idx, sheet, table, scaling, u_ref, kind_ref, c_ref, xs0, xs1, ys0, ys1, zs0, zs1
):
    planes, rows, columns = u_ref.shape
    even = [idx[d] % 2 == 0 for d in range(3)]
    lane = iota((rows, columns), 1)
    low = jnp.zeros((rows, columns), F32)
    high = jnp.zeros((rows, columns), F32)
    for z in range(planes):
        u, kind = u_ref[z], kind_ref[z]
        factor = jnp.zeros((rows, columns), F32)
        for category in range(scaling.shape[0]):
            factor = jnp.where(kind == category, scaling[category], factor)
        c = table[sheet[idx[2] * planes + z]] * factor
        c_ref[z] = c
        for slot, values in ((0, u), (1, c)):
            at = z * SLOT + slot
            low = jnp.where(lane == at, pltpu.roll(values, at, 1) if at else values, low)
            high = jnp.where(lane == at, pltpu.roll(values, at + 1, 1), high)
            first, last = values[0:1, :], values[rows - 1 : rows, :]
            xs0[slot, z : z + 1, :] = jnp.where(even[0], last, first)
            xs1[slot, z : z + 1, :] = jnp.where(even[0], first, last)
    ys0[...] = jnp.where(even[1], high, low)
    ys1[...] = jnp.where(even[1], low, high)
    for slot, ref in ((0, u_ref), (1, c_ref)):
        zs0[slot] = jnp.where(even[2], ref[planes - 1], ref[0])
        zs1[slot] = jnp.where(even[2], ref[0], ref[planes - 1])


def dispatch_kernel(blocks, capacity, amps, ohms, tile, voxel, send, a_scr, b_scr, o_scr):
    chunks, lanes = amps.shape
    block_row = iota((blocks, lanes), 0)
    for c in range(chunks):
        hit = block_row == tile[c : c + 1, :]
        o_scr[c * blocks : (c + 1) * blocks, :] = jnp.where(hit, 1.0, 0.0).astype(BF16)
    ahead = jnp.where(iota((lanes, lanes), 0) < iota((lanes, lanes), 1), 1.0, 0.0)
    both = jnp.concatenate([ahead, jnp.ones((lanes, lanes), F32)], axis=1).astype(BF16)
    counted = mm(o_scr[...], both)
    base = jnp.zeros((blocks, lanes), F32)
    ranks = iota((capacity, lanes), 0)
    power = amps[...] * amps[...] * ohms[...]
    cell = voxel[...]
    p_high, p_mid = split(power)
    p_low = (power - p_high.astype(F32) - p_mid.astype(F32))
    pieces = [
        p_high.astype(F32),
        p_mid.astype(F32),
        p_low,
        (cell >> 16).astype(F32),
        ((cell >> 8) & 255).astype(F32),
        (cell & 255).astype(F32),
    ]
    for c in range(chunks):
        part = slice(c * blocks, (c + 1) * blocks)
        cols = slice(c * lanes, (c + 1) * lanes)
        hit = block_row == tile[c : c + 1, :]
        order = jnp.where(hit, counted[part, :lanes] + base, 0.0)
        base = base + counted[part, lanes:]
        rank = jnp.sum(order, axis=0, keepdims=True).astype(jnp.int32)
        b_scr[:, cols] = jnp.where(ranks == rank, 1.0, 0.0).astype(BF16)
        for k, piece in enumerate(pieces):
            a_scr[k * blocks : (k + 1) * blocks, cols] = jnp.where(
                hit, piece[c : c + 1, :], 0.0
            ).astype(BF16)
    out = mm_nt(a_scr[...], b_scr[...])
    r = [out[k * blocks : (k + 1) * blocks] for k in range(6)]
    send[...] = jnp.concatenate(
        [r[0] + r[1] + r[2], r[3] * 65536.0 + r[4] * 256.0 + r[5]], axis=1
    )


def joule_into(got, joule, r_scr, k_scr):
    planes, rows, columns = joule.shape
    sources, capacity = got.shape[0], got.shape[1] // 2
    column = iota((columns, capacity), 0)
    for s in range(sources):
        power = got[s : s + 1, :capacity]
        cell = got[s : s + 1, capacity:].astype(jnp.int32)
        part = slice(s * capacity, (s + 1) * capacity)
        high, low = split(power)
        hit = column == cell % columns
        r_scr[:columns, part] = jnp.where(hit, high.astype(F32), 0.0).astype(BF16)
        r_scr[columns:, part] = jnp.where(hit, low.astype(F32), 0.0).astype(BF16)
        k_scr[:, part] = jnp.broadcast_to(cell // columns, (8, capacity))
    total = sources * capacity
    step = min(total, 2048)
    row = iota((rows, step), 0)

    def plane(z, carry):
        sums = jnp.zeros((rows, 2 * columns), F32)
        for at in range(0, total, step):
            hit = row == k_scr[0:1, at : at + step] - z * rows
            onehot = jnp.where(hit, 1.0, 0.0).astype(BF16)
            sums = sums + mm_nt(onehot, r_scr[:, at : at + step])
        joule[z] = sums[:, :columns] + sums[:, columns:]
        return carry

    lax.fori_loop(0, planes, plane, 0)


def line_parts(position, theta, start, cells):
    growing = jnp.exp(position * theta)
    lower = growing * (1.0 + jnp.exp(-(2.0 * (start + position) + 1.0) * theta))
    upper = (1.0 + jnp.exp(-(2.0 * (cells - start - position) - 1.0) * theta)) / growing
    return lower, upper


def prep_kernel(
    sizes, idx, sheet, table, gx_ref, psx, phx, dx, gyh, gyl, dy, cyh, cyl, phz, psz, mz, wz,
    low_scr, high_scr,
):
    planes, rows, columns, nx, ny, nz = sizes
    lanes = 128
    extent = rows + EXTRA
    gx, gy, gz = idx[0], idx[1], idx[2]
    x0, xn = (gx * rows).astype(F32), float(nx * rows)
    y0, yn = (gy * columns).astype(F32), float(ny * columns)

    def line(conduct, cells):
        lead = HEAT_SPREADING * STIFF * conduct
        t = 0.5 / jnp.sqrt(lead)
        theta = 2.0 * jnp.log1p(t + t * t / (1.0 + jnp.sqrt(1.0 + t * t)))
        scale = 1.0 / (jnp.sqrt(4.0 * lead + 1.0) * (1.0 - jnp.exp(-2.0 * cells * theta)))
        return theta, scale

    lane_plane = iota((8, lanes), 1) // SLOT
    row8 = iota((8, lanes), 0)
    by_lane = jnp.ones((8, lanes), F32)
    by_row = jnp.ones((planes, lanes), F32)
    own = []
    for z in range(planes):
        value = table[sheet[gz * planes + z]]
        own.append(value)
        by_lane = jnp.where(lane_plane == z, value, by_lane)
        by_row = jnp.where(iota((planes, lanes), 0) == z, value, by_row)
    theta_rows, _ = line(by_row, 1.0)
    theta_lane, _ = line(by_lane, 1.0)
    for k in range(nx):
        dx[k] = jnp.exp(-float(k * rows) * theta_rows)
    for k in range(ny):
        dy[k] = jnp.exp(-float(k * columns) * theta_lane)

    order = iota((extent, lanes), 0)
    wide = jnp.where(order == rows, -1, jnp.where(order == rows + 1, rows, order))
    position = wide.astype(F32)
    real = order < rows + 2
    j = iota((8, rows), 1)
    wide2 = jnp.concatenate([wide] * (rows // lanes), axis=1)
    order2 = jnp.concatenate([order] * (rows // lanes), axis=1)
    jj = iota((extent, rows), 1)
    y_lane = iota((8, columns), 1).astype(F32)
    y_col = iota((columns, columns), 0).astype(F32)
    y_i, y_j = iota((columns, columns), 0), iota((columns, columns), 1)
    for z in range(planes):
        theta, k_x = line(jnp.full((8, lanes), own[z], F32), xn)
        theta1, k1 = theta[0:1, :], k_x[0:1, :]
        low_c, high_c = line_parts(position, theta1, x0, xn)
        phx[z] = jnp.where(real, low_c * k1, 0.0)
        psx[z] = jnp.where(real, high_c * k1, 0.0)
        theta2 = jnp.concatenate([theta1] * (rows // lanes), axis=1)
        low_r, high_r = line_parts(j.astype(F32), jnp.broadcast_to(theta2, (8, rows)), x0, xn)
        low_r, high_r = low_r[0:1, :], high_r[0:1, :]
        low_k = jnp.concatenate([phx[z]] * (rows // lanes), axis=1)
        high_k = jnp.concatenate([psx[z]] * (rows // lanes), axis=1)
        g = jnp.where(wide2 >= jj, high_k * low_r, low_k * high_r)
        g = jnp.where(order2 == rows + 2, low_r, jnp.where(order2 == rows + 3, high_r, g))
        gx_ref[z, :extent, :], gx_ref[z, extent:, :] = split(g)

        theta, k_y = line(jnp.full((8, lanes), own[z], F32), yn)
        theta1, k1 = theta[0:1, :], k_y[0:1, :]
        low_r, high_r = line_parts(y_lane[0:1, :], theta1, y0, yn)
        low_c, high_c = line_parts(y_col, theta1, y0, yn)
        low_b, high_b = line_parts(jnp.full((1, lanes), -1.0, F32), theta1, y0, yn)
        low_t, high_t = line_parts(jnp.full((1, lanes), float(columns), F32), theta1, y0, yn)
        g = k1 * jnp.where(y_j >= y_i, high_r * low_c, low_r * high_c)
        ext = jnp.zeros((columns, lanes), F32)
        for slot, values in enumerate((low_b * high_c * k1, high_t * low_c * k1, low_c, high_c)):
            ext = jnp.where(y_j == z * SLOT + slot, values, ext)
        gyh[z, :, :lanes], gyl[z, :, :lanes] = split(g)
        gyh[z, :, lanes:], gyl[z, :, lanes:] = split(ext)
        add = jnp.where(
            y_i == z * SLOT + 2, high_r * k1, jnp.where(y_i == z * SLOT + 3, low_r * k1, 0.0)
        )
        cyh[:, z * lanes : (z + 1) * lanes], cyl[:, z * lanes : (z + 1) * lanes] = split(add)
        ghost_low = jnp.where(
            y_i == z * SLOT + 2, high_b * k1, jnp.where(y_i == z * SLOT + 3, low_b * k1, 0.0)
        )
        ghost_high = jnp.where(
            y_i == z * SLOT + 2, high_t * k1, jnp.where(y_i == z * SLOT + 3, low_t * k1, 0.0)
        )
        low_scr[z] = jnp.where(
            y_j == z * SLOT, ghost_low, jnp.where(y_j == z * SLOT + 1, ghost_high, 0.0)
        )
    ghosts = low_scr[0]
    for z in range(1, planes):
        ghosts = ghosts + low_scr[z]
    cyh[:, planes * lanes :], cyl[:, planes * lanes :] = split(ghosts)

    total = planes * nz
    cond = [jnp.full((8, lanes), table[sheet[z]], F32) for z in range(total)]
    lead = [HEAT_SPREADING * STIFF * 0.5 * (cond[z] + cond[z + 1]) for z in range(total - 1)]
    lower = [jnp.ones((8, lanes), F32)]
    flux = HEAT_SPREADING * STIFF * cond[0]
    resist = [1.0 / value for value in lead]
    for z in range(total - 1):
        flux = flux + lower[z]
        lower.append(lower[z] + flux * resist[z])
    weight = 1.0 / (flux + lower[total - 1])
    upper = [None] * total
    upper[total - 1] = weight
    flux = jnp.zeros((8, lanes), F32)
    for z in range(total - 2, -1, -1):
        flux = flux + upper[z + 1]
        upper[z] = upper[z + 1] + flux * resist[z]
    zero = jnp.zeros((8, lanes), F32)
    high_scr[0], high_scr[total + 3] = zero, zero
    high_scr[total + 1], high_scr[total + 2] = zero, zero
    for z in range(total):
        high_scr[1 + z] = lower[z]
        high_scr[total + 3 + z] = upper[z]
    high_scr[2 * total + 3] = zero
    mine = gz * planes
    for z in range(planes + 2):
        phz[z] = high_scr[mine + z]
        psz[z] = jnp.where(mine + z == 0, zero, high_scr[total + 2 + mine + z])

    lower_lane, upper_lane = zero, zero
    for z in range(planes):
        lower_lane = jnp.where(lane_plane == z, phz[z + 1], lower_lane)
        upper_lane = jnp.where(lane_plane == z, psz[z + 1], upper_lane)
    lane8 = iota((8, lanes), 1)
    slot = lane8 % SLOT
    mz[...] = jnp.zeros(mz.shape, F32)
    for z in range(planes):
        part = slice(z * SLOT, (z + 1) * SLOT)
        g = jnp.where(lane_plane >= z, phz[z + 1] * upper_lane, psz[z + 1] * lower_lane)
        keep = (slot == row8) & (row8 < 2) & (lane_plane < planes)
        mz[part, :lanes] = jnp.where(keep, g, 0.0)
        mz[part, lanes:] = jnp.where(
            (lane8 == row8) & (row8 < 2),
            phz[z + 1],
            jnp.where((lane8 == row8 + 2) & (row8 < 2), psz[z + 1], 0.0),
        )
    wz[...] = jnp.where(
        (row8 < 2) & (slot == row8),
        upper_lane,
        jnp.where((row8 >= 2) & (row8 < 4) & (slot == row8 - 2), lower_lane, 0.0),
    )


def outflow(z, idx, counts, u_ref, c_ref, ux, cx, uy, cy, uz, cz):
    planes, rows, columns = u_ref.shape
    at_low = [idx[d] == 0 for d in range(3)]
    at_high = [idx[d] == counts[d] - 1 for d in range(3)]
    u, c = u_ref[z], c_ref[z]
    row, lane = iota((rows, columns), 0), iota((rows, columns), 1)

    def pair(other_u, other_c):
        return (c + other_c) * (other_u - u)

    lo_u = jnp.where(at_low[0], u[0:1, :], ux[z, 0:1, :])
    hi_u = jnp.where(at_high[0], u[rows - 1 : rows, :], ux[z, 1:2, :])
    total = pair(
        jnp.where(row == 0, lo_u, pltpu.roll(u, 1, 0)),
        jnp.where(row == 0, cx[z, 0:1, :], pltpu.roll(c, 1, 0)),
    )
    total += pair(
        jnp.where(row == rows - 1, hi_u, pltpu.roll(u, rows - 1, 0)),
        jnp.where(row == rows - 1, cx[z, 1:2, :], pltpu.roll(c, rows - 1, 0)),
    )
    low = (columns - z * SLOT) % columns
    high = columns - 2 - z * SLOT

    def moved(values, by):
        return pltpu.roll(values, by, 1) if by else values

    lo_u = jnp.where(at_low[1], u, moved(uy[:rows, :], low))
    hi_u = jnp.where(at_high[1], u, moved(uy[:rows, :], high))
    total += pair(
        jnp.where(lane == 0, lo_u, pltpu.roll(u, 1, 1)),
        jnp.where(lane == 0, moved(cy[...], low), pltpu.roll(c, 1, 1)),
    )
    total += pair(
        jnp.where(lane == columns - 1, hi_u, pltpu.roll(u, columns - 1, 1)),
        jnp.where(lane == columns - 1, moved(cy[...], high), pltpu.roll(c, columns - 1, 1)),
    )
    if z == 0:
        total += pair(jnp.where(at_low[2], 0.0, uz[0]), jnp.where(at_low[2], c, cz[0]))
    else:
        total += pair(u_ref[z - 1], c_ref[z - 1])
    if z == planes - 1:
        total += pair(jnp.where(at_high[2], u, uz[1]), cz[1])
    else:
        total += pair(u_ref[z + 1], c_ref[z + 1])
    return (0.5 * HEAT_SPREADING) * total


def slope_kernel(
    counts, idx, u_ref, c_ref, xr0, xr1, yr0, yr1, zr0, zr1, d_ref, ux, cx, uy, cy, uz, cz
):
    planes, rows, columns = u_ref.shape
    even = [idx[d] % 2 == 0 for d in range(3)]

    def ends(first, second, d):
        return jnp.where(even[d], second, first), jnp.where(even[d], first, second)

    for slot, out in ((0, ux), (1, cx)):
        low, high = ends(xr0[slot], xr1[slot], 0)
        out[...] = jnp.zeros(out.shape, F32)
        for z in range(planes):
            out[z, 0:1, :] = low[z : z + 1, :]
            out[z, 1:2, :] = high[z : z + 1, :]
    low, high = ends(yr0[...], yr1[...], 1)
    slot = iota((rows, 128), 1) % SLOT
    uy[...] = jnp.zeros(uy.shape, F32)
    uy[:rows, :] = jnp.where(slot == 0, low, jnp.where(slot == 1, pltpu.roll(high, 1, 1), 0.0))
    cy[...] = jnp.where(slot == 0, pltpu.roll(low, 127, 1), jnp.where(slot == 1, high, 0.0))
    for slot, out in ((0, uz), (1, cz)):
        out[0], out[1] = ends(zr0[slot], zr1[slot], 2)
    for z in range(planes):
        d_ref[z] = outflow(z, idx, counts, u_ref, c_ref, ux, cx, uy, cy, uz, cz)


def rows_solve(z, idx, source, gx_ref, t_ref, sends):
    rows = source.shape[0]
    columns = source.shape[1]
    extent = rows + EXTRA
    high, low = split(source)
    out = mm(gx_ref[z], jnp.concatenate([high, low], axis=1))
    t = out[:extent, :columns] + (out[:extent, columns:] + out[extent:, :columns])
    t_ref[z] = t
    for b, send in enumerate(sends):
        below = (idx[0] >> b) % 2 == 0
        send[z : z + 1, :] = jnp.where(
            below, t[rows + 2 : rows + 3, :], t[rows + 3 : rows + 4, :]
        )


def start_kernel(idx, got, d_ref, u_ref, gx_ref, joule, t_ref, *rest):
    sends, (r_scr, k_scr) = rest[:-2], rest[-2:]
    joule_into(got, joule, r_scr, k_scr)
    for z in range(u_ref.shape[0]):
        source = d_ref[z] + OHMIC_POWER * ((1.0 + WARMING_SLOPE * u_ref[z]) * joule[z])
        rows_solve(z, idx, source, gx_ref, t_ref, sends)


def columns_kernel(nx, idx, t_ref, dx, psx, phx, gyh, gyl, *rest):
    gots, (first_ref, y_ref) = rest[:-2], rest[-2:]
    planes, extent, columns = t_ref.shape
    me = idx[0]
    below = jnp.zeros(gots[0].shape, F32)
    above = jnp.zeros(gots[0].shape, F32)
    for k, got in zip(range(1, nx), gots):
        other = me ^ k
        value = got[...] * dx[jnp.abs(me - other)]
        below += jnp.where(other < me, value, 0.0)
        above += jnp.where(other > me, value, 0.0)
    sums = jnp.zeros((extent, 128), F32)
    for z in range(planes):
        first = t_ref[z] + psx[z] * below[z : z + 1, :] + phx[z] * above[z : z + 1, :]
        high, low = split(first)
        out = mm(jnp.concatenate([high, low], axis=0), gyh[z])
        out = out[:extent] + out[extent:] + mm(high, gyl[z])
        first_ref[z] = out[:, :columns]
        sums = sums + out[:, columns:]
    y_ref[...] = sums


def planes_kernel(ny, idx, t_ref, y_ref, dy, cyh, cyl, phz, psz, mz, *rest):
    gots, rest = rest[: ny - 1], rest[ny - 1 :]
    second_ref, q_ref = rest[:2]
    sends = rest[2:]
    planes, extent, columns = t_ref.shape
    rows = extent - EXTRA
    me = idx[1]
    slot = iota((8, 128), 1) % SLOT
    others = jnp.zeros((extent, 128), F32)
    for k, got in zip(range(1, ny), gots):
        other = me ^ k
        keep = jnp.where(other < me, 2, 3)
        factor = jnp.where(slot == keep, dy[jnp.abs(me - other)], 0.0)
        others += got[...] * factor[0:1, :]
    high, low = split(others)
    pair = jnp.concatenate([high, low], axis=0)
    below = jnp.zeros((extent, columns), F32)
    above = jnp.zeros((extent, columns), F32)

    def added(part):
        out = mm(pair, cyh[:, part])
        return out[:extent] + out[extent:] + mm(high, cyl[:, part])

    for z in range(planes):
        second = t_ref[z] + added(slice(z * 128, (z + 1) * 128))
        second_ref[z] = second
        below += phz[z + 1, 0:1, :] * second
        above += psz[z + 1, 0:1, :] * second
    slots = iota((extent, 128), 1) % SLOT
    q = y_ref[...] + added(slice(planes * 128, (planes + 1) * 128))
    q = jnp.where(slots < 2, q, 0.0)
    q_ref[...] = q
    edge = jnp.dot(q[:rows], mz[:, 128:], precision=EXACT, preferred_element_type=F32).T
    for b, send in enumerate(sends):
        lower = (idx[2] >> b) % 2 == 0
        send[: rows + 8, :] = jnp.where(lower, below[: rows + 8], above[: rows + 8])
        for part in range(rows // 128):
            at = rows + 8 + 8 * part
            send[at : at + 8, :] = edge[0:8, part * 128 : (part + 1) * 128]


def carried(nz, idx, gots, rows):
    me = idx[2]
    below, above = None, None
    for k, got in zip(range(1, nz), gots):
        other = me ^ k
        value = got[:rows]
        lower = jnp.where(other < me, value, 0.0)
        higher = jnp.where(other < me, 0.0, value)
        below = lower if below is None else below + lower
        above = higher if above is None else above + higher
    return below, above


def change(z_range, second_ref, phz, psz, below, above, rows, emit):
    planes = second_ref.shape[0]
    tails = [above]
    for z in range(planes - 1, -1, -1):
        tails.append(tails[-1] + psz[z + 1, 0:1, :] * second_ref[z, :rows, :])
    tails = tails[::-1]
    if z_range:
        emit(-1, psz[0, 0:1, :] * below + phz[0, 0:1, :] * tails[0])
    head = below
    for z in range(planes):
        head = head + phz[z + 1, 0:1, :] * second_ref[z, :rows, :]
        emit(z, psz[z + 1, 0:1, :] * head + phz[z + 1, 0:1, :] * tails[z + 1])
    if z_range:
        emit(planes, psz[planes + 1, 0:1, :] * head + phz[planes + 1, 0:1, :] * above)


def rise_kernel(counts, idx, second_ref, q_ref, phz, psz, mz, wz, u_ref, ux, uy, uz,
                c_ref, cx, cy, cz, joule, gx_ref, *rest):
    nz = counts[2]
    gots, rest = rest[: nz - 1], rest[nz - 1 :]
    u_out, ux_out, uy_out, uz_out, t_ref = rest[:5]
    sends = rest[5:]
    planes, rows, columns = u_ref.shape
    below, above = carried(nz, idx, gots, rows + 8)

    def emit(z, value):
        if z == -1:
            uz_out[0] = uz[0] + value[:rows]
        elif z == planes:
            uz_out[1] = uz[1] + value[:rows]
        else:
            u_out[z] = u_ref[z] + value[:rows]
            ux_out[z] = ux[z] + value[rows:]

    change(True, second_ref, phz, psz, below, above, rows + 8, emit)
    edges = jnp.zeros((8, rows), F32)
    sub = iota((8, rows), 0)
    me = idx[2]
    for k, got in zip(range(1, nz), gots):
        other = me ^ k
        value = jnp.concatenate(
            [got[rows + 8 + 8 * p : rows + 16 + 8 * p, :] for p in range(rows // 128)], axis=1
        )
        keep = jnp.where(other < me, 0, 1)
        edges += jnp.where(sub // 2 == keep, value, 0.0)
    q = q_ref[:rows, :]
    grown = jnp.dot(q, mz[:, :128], precision=EXACT, preferred_element_type=F32)
    grown += jnp.dot(edges.T, wz[...], precision=EXACT, preferred_element_type=F32)
    uy_out[...] = uy[...]
    uy_out[:rows, :] = uy[:rows, :] + grown
    for z in range(planes):
        source = outflow(
            z, idx, counts, u_out, c_ref, ux_out, cx, uy_out, cy, uz_out, cz
        ) + OHMIC_POWER * ((1.0 + WARMING_SLOPE * u_out[z]) * joule[z])
        rows_solve(z, idx, source, gx_ref, t_ref, sends)


def finish_kernel(counts, idx, second_ref, phz, psz, u_ref, joule, *rest):
    nz = counts[2]
    gots, (u_out, heat_out) = rest[: nz - 1], rest[nz - 1 :]
    rows = u_ref.shape[1]
    below, above = carried(nz, idx, gots, rows)

    def emit(z, value):
        u = u_ref[z] + value
        u_out[z] = u
        heat_out[z] = (1.0 + WARMING_SLOPE * u) * joule[z]

    change(False, second_ref, phz, psz, below, above, rows, emit)


def per_device(
    starting_warmth,
    sheet_stratum_number,
    stratum_heat_conduction,
    substance_kind,
    substance_kind_scaling,
    wire_piece_amperes,
    wire_piece_ohms_base,
    wire_piece_tile,
    wire_piece_voxel,
):
    planes, rows, columns = starting_warmth.shape
    counts = tuple(lax.axis_size(axis) for axis in ("gx", "gy", "gz"))
    nx, ny, nz = counts
    bits = [(n - 1).bit_length() for n in counts]
    devices = nx * ny * nz
    extent = rows + EXTRA
    idx = jnp.stack([lax.axis_index(axis) for axis in ("gx", "gy", "gz")]).astype(jnp.int32)
    block = shaped(planes, rows, columns)
    number, table = sheet_stratum_number, stratum_heat_conduction

    count = wire_piece_amperes.shape[0]
    capacity = 2 * count // devices
    lanes = 128
    chunks = count // lanes
    send = pl.pallas_call(
        functools.partial(dispatch_kernel, devices, capacity),
        out_shape=shaped(devices, 2 * capacity),
        in_specs=[pl.BlockSpec(memory_space=pltpu.VMEM)] * 4,
        out_specs=pl.BlockSpec(memory_space=pltpu.VMEM),
        scratch_shapes=[
            pltpu.VMEM((6 * devices, count), BF16),
            pltpu.VMEM((capacity, count), BF16),
            pltpu.VMEM((chunks * devices, lanes), BF16),
        ],
        compiler_params=pltpu.CompilerParams(vmem_limit_bytes=48 * 2**20),
    )(
        wire_piece_amperes.reshape(chunks, lanes),
        wire_piece_ohms_base.reshape(chunks, lanes),
        wire_piece_tile.reshape(chunks, lanes),
        wire_piece_voxel.reshape(chunks, lanes),
    )
    got = lax.all_to_all(send, ("gx", "gy", "gz"), split_axis=0, concat_axis=0, tiled=True)

    c, xs0, xs1, ys0, ys1, zs0, zs1 = call(
        faces_kernel,
        [block]
        + [shaped(2, planes, columns)] * 2
        + [shaped(rows, 128)] * 2
        + [shaped(2, rows, columns)] * 2,
        (idx, number, table, substance_kind_scaling, starting_warmth, substance_kind),
        smem=4,
    )
    zr = next_pairs(zs0, zs1, "gz")
    xr = next_pairs(xs0, xs1, "gx")
    yr = next_pairs(ys0, ys1, "gy")
    sizes = (planes, rows, columns, nx, ny, nz)
    prep_out = [
        shaped(planes, 2 * extent, rows, dtype=BF16),
        shaped(planes, extent, columns),
        shaped(planes, extent, columns),
        shaped(nx, planes, lanes),
        shaped(planes, columns, 256, dtype=BF16),
        shaped(planes, columns, 256, dtype=BF16),
        shaped(ny, 8, lanes),
        shaped(lanes, (planes + 1) * lanes, dtype=BF16),
        shaped(lanes, (planes + 1) * lanes, dtype=BF16),
        shaped(planes + 2, 8, lanes),
        shaped(planes + 2, 8, lanes),
        shaped(lanes, 256),
        shaped(8, lanes),
    ]
    gx_m, psx, phx, dx, gyh, gyl, dy, cyh, cyl, phz, psz, mz, wz = pl.pallas_call(
        functools.partial(prep_kernel, sizes),
        out_shape=prep_out,
        in_specs=[pl.BlockSpec(memory_space=pltpu.SMEM)] * 3,
        out_specs=[pl.BlockSpec(memory_space=pltpu.VMEM)] * len(prep_out),
        scratch_shapes=[
            pltpu.VMEM((planes, lanes, lanes), F32),
            pltpu.VMEM((2 * planes * nz + 4, 8, lanes), F32),
        ],
        compiler_params=pltpu.CompilerParams(vmem_limit_bytes=48 * 2**20),
    )(idx, number, table)
    d0, ux, cx, uy, cy, uz, cz = call(
        functools.partial(slope_kernel, counts),
        [block]
        + [shaped(planes, 8, columns)] * 2
        + [shaped(extent, 128), shaped(rows, 128)]
        + [shaped(2, rows, columns)] * 2,
        (idx, starting_warmth, c, *xr, *yr, *zr),
        smem=1,
    )
    x_sends = [shaped(planes, columns)] * bits[0]
    total = devices * capacity
    outs = [block, shaped(planes, extent, columns)] + x_sends
    joule, t, *sends = pl.pallas_call(
        start_kernel,
        out_shape=outs,
        in_specs=[pl.BlockSpec(memory_space=pltpu.SMEM)]
        + [pl.BlockSpec(memory_space=pltpu.VMEM)] * 4,
        out_specs=[pl.BlockSpec(memory_space=pltpu.VMEM)] * len(outs),
        scratch_shapes=[
            pltpu.VMEM((2 * columns, total), BF16),
            pltpu.VMEM((8, total), jnp.int32),
        ],
        compiler_params=pltpu.CompilerParams(vmem_limit_bytes=48 * 2**20),
    )(idx, got, d0, starting_warmth, gx_m)
    u = starting_warmth
    for repeat in range(STEPS):
        gots = all_pairs(sends, "gx")
        first, y_own = call(
            functools.partial(columns_kernel, nx),
            [shaped(planes, extent, columns), shaped(extent, 128)],
            (idx, t, dx, psx, phx, gyh, gyl, *gots),
            smem=1,
        )
        gots = all_pairs([y_own] * bits[1], "gy")
        z_rows = rows + 8 + 8 * (rows // 128)
        second, q, *sends = call(
            functools.partial(planes_kernel, ny),
            [shaped(planes, extent, columns), shaped(extent, 128)]
            + [shaped(z_rows, 128)] * bits[2],
            (idx, first, y_own, dy, cyh, cyl, phz, psz, mz, *gots),
            smem=1,
        )
        gots = all_pairs(sends, "gz")
        if repeat < STEPS - 1:
            u, ux, uy, uz, t, *sends = call(
                functools.partial(rise_kernel, counts),
                [block, shaped(planes, 8, columns), shaped(extent, 128)]
                + [shaped(2, rows, columns), shaped(planes, extent, columns)]
                + x_sends,
                (idx, second, q, phz, psz, mz, wz, u, ux, uy, uz, c, cx, cy, cz, joule, gx_m)
                + tuple(gots),
                smem=1,
            )
    return tuple(
        call(
            functools.partial(finish_kernel, counts),
            [block, block],
            (idx, second, phz, psz, u, joule, *gots),
            smem=1,
        )
    )


def solution(mesh):
    return jax.shard_map(
        per_device,
        mesh=mesh,
        in_specs=(
            P("gz", "gx", "gy"),
            P(),
            P(),
            P("gz", "gx", "gy"),
            P(),
            P(("gx", "gy", "gz")),
            P(("gx", "gy", "gz")),
            P(("gx", "gy", "gz"), None),
            P(("gx", "gy", "gz")),
        ),
        out_specs=(P("gz", "gx", "gy"), P("gz", "gx", "gy")),
        check_vma=False,
    )
```

time: 1180 us -> 119 us (0.10); the launches traced: 1160 us -> 119 us
  other arithmetic: 750 us -> 0.08 us
  local copies, waits for them, and re-layouts: 139 us -> 13.5 us
  blocking collectives: 125 us -> 0 us
  Pallas kernels: 0 us -> 43.7 us
  loops' own time: 41.3 us -> 0 us
  matrix products: 29.6 us -> 0 us
  starting transfers between devices: 56.2 us -> 27.1 us
  waiting for transfers between devices: 12.9 us -> 33.6 us
    another operation x26 -> x1, other arithmetic: 622 us -> 0.08 us  [per_device(): jnp.stack([lax.axis_index(axis) for axis in ('gx', 'gy', 'gz')])]
    all_gather x12 -> x0, blocking collectives: 101 us -> none  [carried_in(): everything = jax.tree.map(lambda part: lax.all_gather(part, axis), array)]
    scatter-add x1 -> x0, other arithmetic: 53.5 us -> none  [per_device(): ohmic_loss = ohmic_loss.at[got_cell.reshape(-1)].add(got_power.reshape(-1...]
    pallas_call x0 -> x11, Pallas kernels: none -> 43.7 us  [the longest x8 23.3 us: call(): pl.pallas_call(kernel, out_shape=out_shapes, in_specs=specs, out_specs=[p...]
    another operation x13 -> x0, loops' own time: 41.3 us -> none  [the longest x12 41.3 us: carried_in(): return lax.fori_loop(0, count, hop, start)]
    scatter x2 -> x0, local copies, waits for them, and re-layouts: 32.5 us -> none  [the longest x1 16.3 us: per_device(): send_cell = jnp.zeros((devices * capacity,), jnp.int32).at[slot].set(wire...]
    dynamic_slice x33 -> x0, local copies, waits for them, and re-layouts: 28.8 us -> none  [the longest x32 28.7 us: hop(): new = combine(before, jax.tree.map(lambda part: part[at], everything))]
    ppermute x18 -> x19, waiting for transfers between devices: 7.06 us -> 33.6 us  [the longest x14 33.6 us: all_pairs(): lax.ppermute(arrays[b], axis, [(i, i ^ k) for i in range(n)])]
  transfers between devices with their start and end apart: 20 -> 20, of which waited for: 4 -> 13; matrix products, arithmetic and copies ran while one was open for 69% -> 1% of each run, Pallas kernels for 0% -> 5%
where the time goes in v1:
time: 119 us
  Pallas kernels  43.7 us (37%)
  waiting for transfers between devices  33.6 us (28%)
  starting transfers between devices  27.1 us (23%)
  local copies, waits for them, and re-layouts  13.5 us (11%)
    ppermute x14, waiting for transfers between devices, all_pairs(): lax.ppermute(arrays[b], axis, [(i, i ^ k) for i in range(n)])  33.6 us
    pallas_call x8, Pallas kernels, call(): pl.pallas_call(kernel, out_shape=out_shapes, in_specs=specs, out_specs=[p...  23.3 us
    ppermute x14, starting transfers between devices, all_pairs(): lax.ppermute(arrays[b], axis, [(i, i ^ k) for i in range(n)])  14.6 us
    pallas_call x1, Pallas kernels, per_device(): pl.pallas_call(start_kernel, out_shape=outs, in_specs=[pl.BlockSpec(memor...  14 us
    unnamed x55, local copies, waits for them, and re-layouts  12.8 us
    ppermute x3, starting transfers between devices, next_pairs(): first = lax.ppermute(even, axis, [(i, i ^ 1) for i in range(n)])  4.79 us
    pallas_call x1, Pallas kernels, per_device(): pl.pallas_call(functools.partial(prep_kernel, sizes), out_shape=prep_out,...  4.54 us
    ppermute x2, starting transfers between devices, next_pairs(): return (first, lax.ppermute(odd, axis, list(other.items())))  3.94 us
  transfers between devices with their start and end apart: 20, of which 13 were waited for; matrix products, arithmetic and copies ran while one was open for 1% of the time, Pallas kernels for 5%

profile of v1, /device:TPU:0, one launch (start us, length us, event | category | flops | bytes accessed | tf_op | source)
XLA Modules:
  0.0 118.9 jit_solution(10400540372663537109)
XLA Ops:
  0.6 0.1 pad_add_fusion.idx
  0.7 1.2 %copy-done = f32[8,256,128]{2,1,0:T(8,128)S(1)} copy-done((f32[8,256,128]{2,1,0:T(8,128)S(1)}, f32[8,256,128]{2,1,0:T(8,128)}, u32[]{:S(2)}) %copy-start) | copy-done | bytes 1048600
  2.0 1.2 %copy-done.17 = s32[8,256,128]{2,1,0:T(8,128)S(1)} copy-done((s32[8,256,128]{2,1,0:T(8,128)S(1)}, s32[8,256,128]{2,1,0:T(8,128)}, u32[]{:S(2)}) %copy-start.17) | copy-done | bytes 1048600
  3.2 0.7 copy-done.22
  3.8 0.7 copy-done.23
  4.5 0.7 copy-done.25
  5.2 2.6 %shard_map.105 = (f32[8,256,128]{2,1,0:T(8,128)S(1)}, f32[2,8,128]{2,1,0:T(8,128)}, f32[2,8,128]{2,1,0:T(8,128)S(1)}, f32[256,128]{1,0:T(8,128)}, f32[256,128]{1...) custom-call(s32[3]{0:T(128)S(1)} %pad_add_fusion.idx, s32[32]{0:T(128)S(1)} %copy-done.23, f32[16]{0:T(128)S(1)} %copy-done.25, ...), custom_call_target="tpu_custom_call" | custom-call | bytes 3948764 | tf_op jit(solution)/shard_map/pallas_call | solution.py:28
  7.8 1.0 copy-done.4
  8.7 3.0 %collective-permute-start.3 = (f32[2,256,128]{2,1,0:T(8,128)}, f32[2,256,128]{2,1,0:T(8,128)}, u32[]{:S(2)}, u32[]{:S(2)}) collective-permute-start(f32[2,256,128]{2,1,0:T(8,128)} %get-tuple-element.51), channel_id=1, source_target_pairs={{0,1},{1,0},{2,3},{3,2},{4,5},{5,4},{6,7},{7,6},{8,9},{9,8},{10,11... | collective-permute-start | bytes 786440 | tf_op jit(solution)/shard_map/ppermute | solution.py:77
  11.7 2.5 %collective-permute-start.4 = (f32[2,256,128]{2,1,0:T(8,128)}, f32[2,256,128]{2,1,0:T(8,128)}, u32[]{:S(2)}, u32[]{:S(2)}) collective-permute-start(f32[2,256,128]{2,1,0:T(8,128)} %get-tuple-element.52), channel_id=1, source_target_pairs={{0,3},{1,2},{2,1},{3,0},{4,7},{5,6},{6,5},{7,4},{8,11},{9,10},{10,... | collective-permute-start | bytes 786440 | tf_op jit(solution)/shard_map/ppermute | solution.py:81
  14.2 1.8 %shard_map.104 = f32[32,512]{1,0:T(8,128)S(1)} custom-call(f32[32,128]{1,0:T(8,128)S(1)} %bitcast.13, f32[32,128]{1,0:T(8,128)S(1)} %bitcast.14, s32[32,128]{1,0:T(8,128)S(1)} %bitcast.15, s32[32,128]{1,0:T(8,128)S(1)} %bitcast.16), custom_call_target="tpu_custom_call" | custom-call | tf_op jit(solution)/shard_map/pallas_call | solution.py:602
  16.0 0.7 copy.11
  16.7 3.8 %all-to-all-start = ((f32[32,1,512]{2,1,0:T(1,128)}), f32[32,1,512]{2,1,0:T(1,128)}, u32[]{:S(2)}, u32[]{:S(2)}) async-start(f32[32,1,512]{2,1,0:T(1,128)} %copy.11), calls=%async_computation | async-start | bytes 131072 | tf_op jit(solution)/shard_map/all_to_all | solution.py:619
  20.6 1.8 %collective-permute-start = (f32[2,8,128]{2,1,0:T(8,128)}, f32[2,8,128]{2,1,0:T(8,128)S(1)}, u32[]{:S(2)}, u32[]{:S(2)}) collective-permute-start(f32[2,8,128]{2,1,0:T(8,128)} %get-tuple-element.48), channel_id=1, source_target_pairs={{0,8},{8,0},{16,24},{24,16},{1,9},{9,1},{17,25},{25,17},{2,10},{10... | collective-permute-start | bytes 24584 | tf_op jit(solution)/shard_map/ppermute | solution.py:77
  22.3 1.5 %collective-permute-start.1 = (f32[2,8,128]{2,1,0:T(8,128)S(1)}, f32[2,8,128]{2,1,0:T(8,128)S(1)}, u32[]{:S(2)}, u32[]{:S(2)}) collective-permute-start(f32[2,8,128]{2,1,0:T(8,128)S(1)} %get-tuple-element.49), channel_id=1, source_target_pairs={{0,24},{8,16},{16,8},{24,0},{1,25},{9,17},{17,9},{25,1},{2,26},{10... | collective-permute-start | bytes 24584 | tf_op jit(solution)/shard_map/ppermute | solution.py:81
  23.8 4.5 %shard_map.107 = (bf16[8,544,256]{2,1,0:T(8,128)(2,1)}, f32[8,272,128]{2,1,0:T(8,128)S(1)}, f32[8,272,128]{2,1,0:T(8,128)S(1)}, f32[4,8,128]{2,1,0:T(8,128)S(1)}...) custom-call(s32[3]{0:T(128)S(1)} %pad_add_fusion.idx, ...), custom_call_target="tpu_custom_call" | custom-call | tf_op jit(solution)/shard_map/pallas_call | solution.py:649
  28.3 0.8 copy-done.7
  29.1 0.8 copy-done.9
  29.9 0.7 copy-done.11
  30.6 0.7 copy-done.13
  31.4 0.8 copy.14
  32.2 0.0 collective-permute-done.xr0
  32.2 0.0 collective-permute-done.2.yr0.yr1
  32.2 0.0 collective-permute-done.4.zr1
  32.3 0.0 copy-start.5
  32.3 1.2 %copy-done.5 = f32[8,256,128]{2,1,0:T(8,128)S(1)} copy-done((f32[8,256,128]{2,1,0:T(8,128)S(1)}, f32[8,256,128]{2,1,0:T(8,128)}, u32[]{:S(2)}) %copy-start.5) | copy-done | bytes 1048600
  33.5 4.2 %shard_map.106 = (f32[8,256,128]{2,1,0:T(8,128)S(1)}, f32[8,8,128]{2,1,0:T(8,128)S(1)}, f32[8,8,128]{2,1,0:T(8,128)S(1)}, f32[272,128]{1,0:T(8,128)S(1)}, f32[25...) custom-call(s32[3]{0:T(128)S(1)} %pad_add_fusion.idx, f32[8,256,128]{2,1,0:T(8,128)S(1)} %copy-done.1, ...), custom_call_target="tpu_custom_call" | custom-call | bytes 4808716 | tf_op jit(solution)/shard_map/pallas_call | solution.py:28
  37.7 14.0 %shard_map.108 = (f32[8,256,128]{2,1,0:T(8,128)S(1)}, f32[8,272,128]{2,1,0:T(8,128)S(1)}, f32[8,128]{1,0:T(8,128)S(1)}, f32[8,128]{1,0:T(8,128)S(1)}) custom-call(s32[3]{0:T(128)S(1)} %pad_add_fusion.idx, f32[32,512]{1,0:T(8,128)S(1)} %bitcast.11, f32[8,256,128]{2,1,0:T(8,128)S(1)} %get-tuple-element.53.d_ref, f32[8,256,128]{2,1,0:T(8,128)S(1)} %copy-done.1, ...), custom_call_target="tpu_custom_call" | custom-call | tf_op jit(solution)/shard_map/pallas_call | solution.py:672
  51.8 0.0 copy-start.2
  51.8 1.5 %collective-permute-start.5 = (f32[8,128]{1,0:T(8,128)S(1)}, f32[8,128]{1,0:T(8,128)S(1)}, u32[]{:S(2)}, u32[]{:S(2)}) collective-permute-start(f32[8,128]{1,0:T(8,128)S(1)} %get-tuple-element.61), channel_id=1, source_target_pairs={{0,8},{8,0},{16,24},{24,16},{1,9},{9,1},{17,25},{25,17},{2,10},{10... | collective-permute-start | bytes 12296 | tf_op jit(solution)/shard_map/ppermute | solution.py:70
  53.3 0.3 collective-permute-start.7
  53.6 1.7 %collective-permute-start.6 = (f32[8,128]{1,0:T(8,128)S(1)}, f32[8,128]{1,0:T(8,128)S(1)}, u32[]{:S(2)}, u32[]{:S(2)}) collective-permute-start(f32[8,128]{1,0:T(8,128)S(1)} %get-tuple-element.62), channel_id=1, source_target_pairs={{0,16},{8,24},{16,0},{24,8},{1,17},{9,25},{17,1},{25,9},{2,18},{10... | collective-permute-start | bytes 12296 | tf_op jit(solution)/shard_map/ppermute | solution.py:70
  55.3 0.1 collective-permute-done.5.rest_0_
  55.4 2.4 %collective-permute-done.7.rest_2_ = f32[8,128]{1,0:T(8,128)S(1)} collective-permute-done((f32[8,128]{1,0:T(8,128)S(1)}, f32[8,128]{1,0:T(8,128)S(1)}, u32[]{:S(2)}, u32[]{:S(2)}) %collective-permute-start.7) | collective-permute-done | bytes 4128 | tf_op jit(solution)/shard_map/ppermute | solution.py:70
  57.8 1.6 %shard_map.109 = (f32[8,272,128]{2,1,0:T(8,128)S(1)}, f32[272,128]{1,0:T(8,128)S(1)}) custom-call(s32[3]{0:T(128)S(1)} %pad_add_fusion.idx, f32[8,272,128]{2,1,0:T(8,128)S(1)} %get-tuple-element.55.t_ref, f32[4,8,128]{2,1,0:T(8,128)S(1)} %get-tuple-element.56.dx, f32[8,272,128]{2,1,0:T(8,128)S(1)} %get-tuple-element.57.psx, ...), custom_call_target="tpu_custom_call" | custom-call | bytes 5672972 | tf_op jit(solution)/shard_map/pallas_call | solution.py:28
  59.4 0.1 collective-permute-start.8
  59.5 1.3 %collective-permute-done.8.rest_0_ = f32[272,128]{1,0:T(8,128)S(1)} collective-permute-done((f32[272,128]{1,0:T(8,128)S(1)}, f32[272,128]{1,0:T(8,128)S(1)}, u32[]{:S(2)}, u32[]{:S(2)}) %collective-permute-start.8) | collective-permute-done | bytes 139296 | tf_op jit(solution)/shard_map/ppermute | solution.py:70
  60.9 1.8 %shard_map.110 = (f32[8,272,128]{2,1,0:T(8,128)S(1)}, f32[272,128]{1,0:T(8,128)S(1)}, f32[280,128]{1,0:T(8,128)S(1)}, f32[280,128]{1,0:T(8,128)S(1)}) custom-call(s32[3]{0:T(128)S(1)} %pad_add_fusion.idx, f32[8,272,128]{2,1,0:T(8,128)S(1)} %get-tuple-element.63.t_ref, f32[272,128]{1,0:T(8,128)S(1)} %get-tuple-element.64.y_ref, ...), custom_call_target="tpu_custom_call" | custom-call | bytes 3743756 | tf_op jit(solution)/shard_map/pallas_call | solution.py:28
  62.7 1.0 copy-done.15
  63.7 1.5 %collective-permute-start.9 = (f32[280,128]{1,0:T(8,128)S(1)}, f32[280,128]{1,0:T(8,128)S(1)}, u32[]{:S(2)}, u32[]{:S(2)}) collective-permute-start(f32[280,128]{1,0:T(8,128)S(1)} %get-tuple-element.81), channel_id=1, source_target_pairs={{0,1},{1,0},{2,3},{3,2},{4,5},{5,4},{6,7},{7,6},{8,9},{9,8},{10,11... | collective-permute-start | bytes 430088 | tf_op jit(solution)/shard_map/ppermute | solution.py:70
  65.2 2.4 %collective-permute-start.11 = (f32[280,128]{1,0:T(8,128)S(1)}, f32[280,128]{1,0:T(8,128)S(1)}, u32[]{:S(2)}, u32[]{:S(2)}) collective-permute-start(f32[280,128]{1,0:T(8,128)S(1)} %get-tuple-element.82), channel_id=1, source_target_pairs={{0,3},{1,2},{2,1},{3,0},{4,7},{5,6},{6,5},{7,4},{8,11},{9,10},{10,... | collective-permute-start | bytes 430088 | tf_op jit(solution)/shard_map/ppermute | solution.py:70
  67.5 0.1 collective-permute-start.10
  67.6 1.9 %collective-permute-done.9.rest_0_ = f32[280,128]{1,0:T(8,128)S(1)} collective-permute-done((f32[280,128]{1,0:T(8,128)S(1)}, f32[280,128]{1,0:T(8,128)S(1)}, u32[]{:S(2)}, u32[]{:S(2)}) %collective-permute-start.9) | collective-permute-done | bytes 143392 | tf_op jit(solution)/shard_map/ppermute | solution.py:70
  69.5 5.8 %collective-permute-done.11.rest_2_ = f32[280,128]{1,0:T(8,128)S(1)} collective-permute-done((f32[280,128]{1,0:T(8,128)S(1)}, f32[280,128]{1,0:T(8,128)S(1)}, u32[]{:S(2)}, u32[]{:S(2)}) %collective-permute-start.11) | collective-permute-done | bytes 143392 | tf_op jit(solution)/shard_map/ppermute | solution.py:70
  75.3 5.3 %collective-permute-done.10.rest_1_ = f32[280,128]{1,0:T(8,128)S(1)} collective-permute-done((f32[280,128]{1,0:T(8,128)S(1)}, f32[280,128]{1,0:T(8,128)S(1)}, u32[]{:S(2)}, u32[]{:S(2)}) %collective-permute-start.10) | collective-permute-done | bytes 143392 | tf_op jit(solution)/shard_map/ppermute | solution.py:70
  80.6 7.1 %shard_map.111 = (f32[8,256,128]{2,1,0:T(8,128)S(1)}, f32[8,8,128]{2,1,0:T(8,128)}, f32[272,128]{1,0:T(8,128)}, f32[2,256,128]{2,1,0:T(8,128)}, f32[8,272,128]{2...) custom-call(s32[3]{0:T(128)S(1)} %pad_add_fusion.idx, f32[8,272,128]{2,1,0:T(8,128)} %copy-done.15, ...), custom_call_target="tpu_custom_call" | custom-call | bytes 10739724 | tf_op jit(solution)/shard_map/pallas_call | solution.py:28
  87.7 1.1 collective-permute-start.12
  88.8 1.5 %collective-permute-start.14 = (f32[8,128]{1,0:T(8,128)S(1)}, f32[8,128]{1,0:T(8,128)S(1)}, u32[]{:S(2)}, u32[]{:S(2)}) collective-permute-start(f32[8,128]{1,0:T(8,128)S(1)} %get-tuple-element.85), channel_id=1, source_target_pairs={{0,24},{8,16},{16,8},{24,0},{1,25},{9,17},{17,9},{25,1},{2,26},{10... | collective-permute-start | bytes 12296 | tf_op jit(solution)/shard_map/ppermute | solution.py:70
  90.3 0.9 collective-permute-start.13
  91.2 0.1 collective-permute-done.12.rest_0_
  91.4 2.0 %collective-permute-done.14.rest_2_ = f32[8,128]{1,0:T(8,128)S(1)} collective-permute-done((f32[8,128]{1,0:T(8,128)S(1)}, f32[8,128]{1,0:T(8,128)S(1)}, u32[]{:S(2)}, u32[]{:S(2)}) %collective-permute-start.14) | collective-permute-done | bytes 4128 | tf_op jit(solution)/shard_map/ppermute | solution.py:70
  93.3 0.6 collective-permute-done.13.rest_1_
  93.9 1.2 %copy-done.16 = f32[8,272,128]{2,1,0:T(8,128)S(1)} copy-done((f32[8,272,128]{2,1,0:T(8,128)S(1)}, f32[8,272,128]{2,1,0:T(8,128)}, u32[]{:S(2)}) %copy-start.16) | copy-done | bytes 1114136
  95.2 1.6 %shard_map.112 = (f32[8,272,128]{2,1,0:T(8,128)S(1)}, f32[272,128]{1,0:T(8,128)S(1)}) custom-call(s32[3]{0:T(128)S(1)} %pad_add_fusion.idx, f32[8,272,128]{2,1,0:T(8,128)S(1)} %copy-done.16, f32[4,8,128]{2,1,0:T(8,128)S(1)} %get-tuple-element.56.dx, f32[8,272,128]{2,1,0:T(8,128)S(1)} %get-tuple-element.57.psx, f32[8,272,128]{2,1,0:T(8,128)S(1)} %get-tuple-element.58.phx, ...), custom_call_target="tpu_custom_call" | custom-call | bytes 5672972 | tf_op jit(solution)/shard_map/pallas_call | solution.py:28
  96.8 0.0 copy-start.3
  96.8 0.1 collective-permute-start.15
  96.8 1.3 %collective-permute-done.15.rest_0_ = f32[272,128]{1,0:T(8,128)S(1)} collective-permute-done((f32[272,128]{1,0:T(8,128)S(1)}, f32[272,128]{1,0:T(8,128)S(1)}, u32[]{:S(2)}, u32[]{:S(2)}) %collective-permute-start.15) | collective-permute-done | bytes 139296 | tf_op jit(solution)/shard_map/ppermute | solution.py:70
  98.2 2.1 %shard_map.113 = (f32[8,272,128]{2,1,0:T(8,128)S(1)}, f32[272,128]{1,0:T(8,128)}, f32[280,128]{1,0:T(8,128)S(1)}, f32[280,128]{1,0:T(8,128)S(1)}) custom-call(s32[3]{0:T(128)S(1)} %pad_add_fusion.idx, f32[8,272,128]{2,1,0:T(8,128)S(1)} %get-tuple-element.86.t_ref, f32[272,128]{1,0:T(8,128)S(1)} %get-tuple-element.87.y_ref, ...), custom_call_target="tpu_custom_call" | custom-call | bytes 3743756 | tf_op jit(solution)/shard_map/pallas_call | solution.py:28
  100.3 2.6 %collective-permute-start.18 = (f32[280,128]{1,0:T(8,128)S(1)}, f32[280,128]{1,0:T(8,128)S(1)}, u32[]{:S(2)}, u32[]{:S(2)}) collective-permute-start(f32[280,128]{1,0:T(8,128)S(1)} %get-tuple-element.91), channel_id=1, source_target_pairs={{0,3},{1,2},{2,1},{3,0},{4,7},{5,6},{6,5},{7,4},{8,11},{9,10},{10,... | collective-permute-start | bytes 430088 | tf_op jit(solution)/shard_map/ppermute | solution.py:70
  103.0 0.8 collective-permute-start.17
  103.8 2.3 %collective-permute-done.16.rest_0_ = f32[280,128]{1,0:T(8,128)S(1)} collective-permute-done((f32[280,128]{1,0:T(8,128)S(1)}, f32[280,128]{1,0:T(8,128)S(1)}, u32[]{:S(2)}, u32[]{:S(2)}) %collective-permute-start.16) | collective-permute-done | bytes 143392 | tf_op jit(solution)/shard_map/ppermute | solution.py:70
  106.1 4.5 %collective-permute-done.18.rest_2_ = f32[280,128]{1,0:T(8,128)S(1)} collective-permute-done((f32[280,128]{1,0:T(8,128)S(1)}, f32[280,128]{1,0:T(8,128)S(1)}, u32[]{:S(2)}, u32[]{:S(2)}) %collective-permute-start.18) | collective-permute-done | bytes 143392 | tf_op jit(solution)/shard_map/ppermute | solution.py:70
  110.7 5.9 %collective-permute-done.17.rest_1_ = f32[280,128]{1,0:T(8,128)S(1)} collective-permute-done((f32[280,128]{1,0:T(8,128)S(1)}, f32[280,128]{1,0:T(8,128)S(1)}, u32[]{:S(2)}, u32[]{:S(2)}) %collective-permute-start.17) | collective-permute-done | bytes 143392 | tf_op jit(solution)/shard_map/ppermute | solution.py:70
  116.5 2.3 %shard_map.114 = (f32[8,256,128]{2,1,0:T(8,128)}, f32[8,256,128]{2,1,0:T(8,128)}) custom-call(s32[3]{0:T(128)S(1)} %pad_add_fusion.idx, f32[8,272,128]{2,1,0:T(8,128)S(1)} %get-tuple-element.88.second_ref, f32[10,8,128]{2,1,0:T(8,128)S(1)} %get-tuple-element.68.phz, f32[10,8,128]{2,1,0:T(8,128)S(1)} %get-tuple-element.69.psz, ...), custom_call_target="tpu_custom_call" | custom-call | bytes 5820428 | tf_op jit(solution)/shard_map/pallas_call | solution.py:28
  (44 shorter events, 0.1 us)
Async XLA Ops:
  0.6 13.6 %copy-start.18 = (f32[4096]{0:T(1024)S(1)}, f32[4096]{0:T(1024)}, u32[]{:S(2)}) copy-start(f32[4096]{0:T(1024)} %param.14) | copy-start | bytes 49156
  0.7 1.2 %copy-start = (f32[8,256,128]{2,1,0:T(8,128)S(1)}, f32[8,256,128]{2,1,0:T(8,128)}, u32[]{:S(2)}) copy-start(f32[8,256,128]{2,1,0:T(8,128)} %u_ref.7) | copy-start | bytes 3145732
  1.9 1.2 %copy-start.17 = (s32[8,256,128]{2,1,0:T(8,128)S(1)}, s32[8,256,128]{2,1,0:T(8,128)}, u32[]{:S(2)}) copy-start(s32[8,256,128]{2,1,0:T(8,128)} %kind_ref.1) | copy-start | bytes 3145732
  3.2 0.7 copy-start.22
  3.8 0.7 copy-start.23
  4.5 0.7 copy-start.25
  5.1 9.1 %copy-start.19 = (f32[4096]{0:T(1024)S(1)}, f32[4096]{0:T(1024)}, u32[]{:S(2)}) copy-start(f32[4096]{0:T(1024)} %param.15) | copy-start | bytes 49156
  5.1 9.1 %copy-start.20 = (s32[4096,1]{0,1:T(1,128)S(1)}, s32[4096,1]{0,1:T(1,128)}, u32[]{:S(2)}) copy-start(s32[4096,1]{0,1:T(1,128)} %param.16) | copy-start | bytes 49156
  5.1 9.1 %copy-start.21 = (s32[4096]{0:T(1024)S(1)}, s32[4096]{0:T(1024)}, u32[]{:S(2)}) copy-start(s32[4096]{0:T(1024)} %param.17) | copy-start | bytes 49156
  5.1 18.6 %copy-start.24 = (s32[32]{0:T(128)S(1)}, s32[32]{0:T(128)}, u32[]{:S(2)}) copy-start(s32[32]{0:T(128)} %sheet.3) | copy-start | bytes 388
  5.2 18.6 %copy-start.26 = (f32[16]{0:T(128)S(1)}, f32[16]{0:T(128)}, u32[]{:S(2)}) copy-start(f32[16]{0:T(128)} %table.3) | copy-start | bytes 196
  5.2 27.1 %copy-start.1 = (f32[8,256,128]{2,1,0:T(8,128)S(1)}, f32[8,256,128]{2,1,0:T(8,128)}, u32[]{:S(2)}) copy-start(f32[8,256,128]{2,1,0:T(8,128)} %u_ref.7) | copy-start | bytes 3145732
  7.7 1.0 copy-start.4
  8.7 23.5 %collective-permute-start.3 = (f32[2,256,128]{2,1,0:T(8,128)}, f32[2,256,128]{2,1,0:T(8,128)}, u32[]{:S(2)}, u32[]{:S(2)}) collective-permute-start(f32[2,256,128]{2,1,0:T(8,128)} %get-tuple-element.51), channel_id=1, source_target_pairs={{0,1},{1,0},{2,3},{3,2},{4,5},{5,4},{6,7},{7,6},{8,9},{9,8},{10,11... | collective-permute-start | bytes 786440 | tf_op jit(solution)/shard_map/ppermute | solution.py:77
  11.7 20.5 %collective-permute-start.4 = (f32[2,256,128]{2,1,0:T(8,128)}, f32[2,256,128]{2,1,0:T(8,128)}, u32[]{:S(2)}, u32[]{:S(2)}) collective-permute-start(f32[2,256,128]{2,1,0:T(8,128)} %get-tuple-element.52), channel_id=1, source_target_pairs={{0,3},{1,2},{2,1},{3,0},{4,7},{5,6},{6,5},{7,4},{8,11},{9,10},{10,... | collective-permute-start | bytes 786440 | tf_op jit(solution)/shard_map/ppermute | solution.py:81
  14.2 18.0 %collective-permute-start.2 = (f32[256,128]{1,0:T(8,128)}, f32[256,128]{1,0:T(8,128)}, u32[]{:S(2)}, u32[]{:S(2)}) collective-permute-start(f32[256,128]{1,0:T(8,128)} %get-tuple-element.50), channel_id=1, source_target_pairs={{0,4},{4,0},{1,5},{5,1},{2,6},{6,2},{3,7},{7,3},{8,12},{12,8},{9,1... | collective-permute-start | bytes 393224 | tf_op jit(solution)/shard_map/ppermute | solution.py:77
  16.7 14.6 %all-to-all-start = ((f32[32,1,512]{2,1,0:T(1,128)}), f32[32,1,512]{2,1,0:T(1,128)}, u32[]{:S(2)}, u32[]{:S(2)}) async-start(f32[32,1,512]{2,1,0:T(1,128)} %copy.11), calls=%async_computation | async-start | bytes 131072 | tf_op jit(solution)/shard_map/all_to_all | solution.py:619
  20.6 11.7 %collective-permute-start = (f32[2,8,128]{2,1,0:T(8,128)}, f32[2,8,128]{2,1,0:T(8,128)S(1)}, u32[]{:S(2)}, u32[]{:S(2)}) collective-permute-start(f32[2,8,128]{2,1,0:T(8,128)} %get-tuple-element.48), channel_id=1, source_target_pairs={{0,8},{8,0},{16,24},{24,16},{1,9},{9,1},{17,25},{25,17},{2,10},{10... | collective-permute-start | bytes 24584 | tf_op jit(solution)/shard_map/ppermute | solution.py:77
  22.3 9.9 %collective-permute-start.1 = (f32[2,8,128]{2,1,0:T(8,128)S(1)}, f32[2,8,128]{2,1,0:T(8,128)S(1)}, u32[]{:S(2)}, u32[]{:S(2)}) collective-permute-start(f32[2,8,128]{2,1,0:T(8,128)S(1)} %get-tuple-element.49), channel_id=1, source_target_pairs={{0,24},{8,16},{16,8},{24,0},{1,25},{9,17},{17,9},{25,1},{2,26},{10... | collective-permute-start | bytes 24584 | tf_op jit(solution)/shard_map/ppermute | solution.py:81
  28.3 0.8 copy-start.7
  29.1 0.8 copy-start.9
  29.9 0.7 copy-start.11
  30.6 0.7 copy-start.13
  32.3 1.2 %copy-start.5 = (f32[8,256,128]{2,1,0:T(8,128)S(1)}, f32[8,256,128]{2,1,0:T(8,128)}, u32[]{:S(2)}) copy-start(f32[8,256,128]{2,1,0:T(8,128)} %copy-done.4) | copy-start | bytes 3145732
  37.7 20.1 %copy-start.8 = (bf16[8,128,256]{2,1,0:T(8,128)(2,1)S(1)}, bf16[8,128,256]{2,1,0:T(8,128)(2,1)}, u32[]{:S(2)}) copy-start(bf16[8,128,256]{2,1,0:T(8,128)(2,1)} %copy-done.7) | copy-start | bytes 1572868
  37.7 20.1 %copy-start.10 = (bf16[8,128,256]{2,1,0:T(8,128)(2,1)S(1)}, bf16[8,128,256]{2,1,0:T(8,128)(2,1)}, u32[]{:S(2)}) copy-start(bf16[8,128,256]{2,1,0:T(8,128)(2,1)} %copy-done.9) | copy-start | bytes 1572868
  51.8 7.7 %copy-start.2 = (f32[8,256,128]{2,1,0:T(8,128)}, f32[8,256,128]{2,1,0:T(8,128)S(1)}, u32[]{:S(2)}) copy-start(f32[8,256,128]{2,1,0:T(8,128)S(1)} %get-tuple-element.80.joule) | copy-start | bytes 3145732
  51.8 3.7 %collective-permute-start.5 = (f32[8,128]{1,0:T(8,128)S(1)}, f32[8,128]{1,0:T(8,128)S(1)}, u32[]{:S(2)}, u32[]{:S(2)}) collective-permute-start(f32[8,128]{1,0:T(8,128)S(1)} %get-tuple-element.61), channel_id=1, source_target_pairs={{0,8},{8,0},{16,24},{24,16},{1,9},{9,1},{17,25},{25,17},{2,10},{10... | collective-permute-start | bytes 12296 | tf_op jit(solution)/shard_map/ppermute | solution.py:70
  53.3 4.5 %collective-permute-start.7 = (f32[8,128]{1,0:T(8,128)S(1)}, f32[8,128]{1,0:T(8,128)S(1)}, u32[]{:S(2)}, u32[]{:S(2)}) collective-permute-start(f32[8,128]{1,0:T(8,128)S(1)} %get-tuple-element.62), channel_id=1, source_target_pairs={{0,24},{8,16},{16,8},{24,0},{1,25},{9,17},{17,9},{25,1},{2,26},{10... | collective-permute-start | bytes 12296 | tf_op jit(solution)/shard_map/ppermute | solution.py:70
  53.6 4.2 %collective-permute-start.6 = (f32[8,128]{1,0:T(8,128)S(1)}, f32[8,128]{1,0:T(8,128)S(1)}, u32[]{:S(2)}, u32[]{:S(2)}) collective-permute-start(f32[8,128]{1,0:T(8,128)S(1)} %get-tuple-element.62), channel_id=1, source_target_pairs={{0,16},{8,24},{16,0},{24,8},{1,17},{9,25},{17,1},{25,9},{2,18},{10... | collective-permute-start | bytes 12296 | tf_op jit(solution)/shard_map/ppermute | solution.py:70
  57.8 3.1 %copy-start.12 = (bf16[128,1152]{1,0:T(8,128)(2,1)S(1)}, bf16[128,1152]{1,0:T(8,128)(2,1)}, u32[]{:S(2)}) copy-start(bf16[128,1152]{1,0:T(8,128)(2,1)} %copy-done.11) | copy-start | bytes 884740
  57.8 3.0 %copy-start.14 = (bf16[128,1152]{1,0:T(8,128)(2,1)S(1)}, bf16[128,1152]{1,0:T(8,128)(2,1)}, u32[]{:S(2)}) copy-start(bf16[128,1152]{1,0:T(8,128)(2,1)} %copy-done.13) | copy-start | bytes 884740
  59.4 1.4 %collective-permute-start.8 = (f32[272,128]{1,0:T(8,128)S(1)}, f32[272,128]{1,0:T(8,128)S(1)}, u32[]{:S(2)}, u32[]{:S(2)}) collective-permute-start(f32[272,128]{1,0:T(8,128)S(1)} %get-tuple-element.64.y_ref), channel_id=1, source_target_pairs={{0,4},{4,0},{1,5},{5,1},{2,6},{6,2},{3,7},{7,3},{8,12},{12,8},{9,1... | collective-permute-start | bytes 417800 | tf_op jit(solution)/shard_map/ppermute | solution.py:70
  60.9 19.7 %copy-start.6 = (f32[8,256,128]{2,1,0:T(8,128)S(1)}, f32[8,256,128]{2,1,0:T(8,128)}, u32[]{:S(2)}) copy-start(f32[8,256,128]{2,1,0:T(8,128)} %copy-done.4) | copy-start | bytes 3145732
  62.7 1.0 copy-start.15
  63.7 5.8 %collective-permute-start.9 = (f32[280,128]{1,0:T(8,128)S(1)}, f32[280,128]{1,0:T(8,128)S(1)}, u32[]{:S(2)}, u32[]{:S(2)}) collective-permute-start(f32[280,128]{1,0:T(8,128)S(1)} %get-tuple-element.81), channel_id=1, source_target_pairs={{0,1},{1,0},{2,3},{3,2},{4,5},{5,4},{6,7},{7,6},{8,9},{9,8},{10,11... | collective-permute-start | bytes 430088 | tf_op jit(solution)/shard_map/ppermute | solution.py:70
  65.2 10.1 %collective-permute-start.11 = (f32[280,128]{1,0:T(8,128)S(1)}, f32[280,128]{1,0:T(8,128)S(1)}, u32[]{:S(2)}, u32[]{:S(2)}) collective-permute-start(f32[280,128]{1,0:T(8,128)S(1)} %get-tuple-element.82), channel_id=1, source_target_pairs={{0,3},{1,2},{2,1},{3,0},{4,7},{5,6},{6,5},{7,4},{8,11},{9,10},{10,... | collective-permute-start | bytes 430088 | tf_op jit(solution)/shard_map/ppermute | solution.py:70
  67.5 13.1 %collective-permute-start.10 = (f32[280,128]{1,0:T(8,128)S(1)}, f32[280,128]{1,0:T(8,128)S(1)}, u32[]{:S(2)}, u32[]{:S(2)}) collective-permute-start(f32[280,128]{1,0:T(8,128)S(1)} %get-tuple-element.82), channel_id=1, source_target_pairs={{0,2},{1,3},{2,0},{3,1},{4,6},{5,7},{6,4},{7,5},{8,10},{9,11},{10,... | collective-permute-start | bytes 430088 | tf_op jit(solution)/shard_map/ppermute | solution.py:70
  87.7 3.6 %collective-permute-start.12 = (f32[8,128]{1,0:T(8,128)S(1)}, f32[8,128]{1,0:T(8,128)S(1)}, u32[]{:S(2)}, u32[]{:S(2)}) collective-permute-start(f32[8,128]{1,0:T(8,128)S(1)} %get-tuple-element.84), channel_id=1, source_target_pairs={{0,8},{8,0},{16,24},{24,16},{1,9},{9,1},{17,25},{25,17},{2,10},{10... | collective-permute-start | bytes 12296 | tf_op jit(solution)/shard_map/ppermute | solution.py:70
  88.8 4.5 %collective-permute-start.14 = (f32[8,128]{1,0:T(8,128)S(1)}, f32[8,128]{1,0:T(8,128)S(1)}, u32[]{:S(2)}, u32[]{:S(2)}) collective-permute-start(f32[8,128]{1,0:T(8,128)S(1)} %get-tuple-element.85), channel_id=1, source_target_pairs={{0,24},{8,16},{16,8},{24,0},{1,25},{9,17},{17,9},{25,1},{2,26},{10... | collective-permute-start | bytes 12296 | tf_op jit(solution)/shard_map/ppermute | solution.py:70
  90.3 3.6 %collective-permute-start.13 = (f32[8,128]{1,0:T(8,128)S(1)}, f32[8,128]{1,0:T(8,128)S(1)}, u32[]{:S(2)}, u32[]{:S(2)}) collective-permute-start(f32[8,128]{1,0:T(8,128)S(1)} %get-tuple-element.85), channel_id=1, source_target_pairs={{0,16},{8,24},{16,0},{24,8},{1,17},{9,25},{17,1},{25,9},{2,18},{10... | collective-permute-start | bytes 12296 | tf_op jit(solution)/shard_map/ppermute | solution.py:70
  93.9 1.2 %copy-start.16 = (f32[8,272,128]{2,1,0:T(8,128)S(1)}, f32[8,272,128]{2,1,0:T(8,128)}, u32[]{:S(2)}) copy-start(f32[8,272,128]{2,1,0:T(8,128)} %get-tuple-element.83.t_ref) | copy-start | bytes 3342340
  96.8 19.8 %copy-start.3 = (f32[8,256,128]{2,1,0:T(8,128)S(1)}, f32[8,256,128]{2,1,0:T(8,128)}, u32[]{:S(2)}) copy-start(f32[8,256,128]{2,1,0:T(8,128)} %copy-done.2) | copy-start | bytes 3145732
  96.8 1.4 %collective-permute-start.15 = (f32[272,128]{1,0:T(8,128)S(1)}, f32[272,128]{1,0:T(8,128)S(1)}, u32[]{:S(2)}, u32[]{:S(2)}) collective-permute-start(f32[272,128]{1,0:T(8,128)S(1)} %get-tuple-element.87.y_ref), channel_id=1, source_target_pairs={{0,4},{4,0},{1,5},{5,1},{2,6},{6,2},{3,7},{7,3},{8,12},{12,8},{9,1... | collective-permute-start | bytes 417800 | tf_op jit(solution)/shard_map/ppermute | solution.py:70
  100.3 5.8 %collective-permute-start.16 = (f32[280,128]{1,0:T(8,128)S(1)}, f32[280,128]{1,0:T(8,128)S(1)}, u32[]{:S(2)}, u32[]{:S(2)}) collective-permute-start(f32[280,128]{1,0:T(8,128)S(1)} %get-tuple-element.90), channel_id=1, source_target_pairs={{0,1},{1,0},{2,3},{3,2},{4,5},{5,4},{6,7},{7,6},{8,9},{9,8},{10,11... | collective-permute-start | bytes 430088 | tf_op jit(solution)/shard_map/ppermute | solution.py:70
  100.3 10.4 %collective-permute-start.18 = (f32[280,128]{1,0:T(8,128)S(1)}, f32[280,128]{1,0:T(8,128)S(1)}, u32[]{:S(2)}, u32[]{:S(2)}) collective-permute-start(f32[280,128]{1,0:T(8,128)S(1)} %get-tuple-element.91), channel_id=1, source_target_pairs={{0,3},{1,2},{2,1},{3,0},{4,7},{5,6},{6,5},{7,4},{8,11},{9,10},{10,... | collective-permute-start | bytes 430088 | tf_op jit(solution)/shard_map/ppermute | solution.py:70
  103.0 13.6 %collective-permute-start.17 = (f32[280,128]{1,0:T(8,128)S(1)}, f32[280,128]{1,0:T(8,128)S(1)}, u32[]{:S(2)}, u32[]{:S(2)}) collective-permute-start(f32[280,128]{1,0:T(8,128)S(1)} %get-tuple-element.91), channel_id=1, source_target_pairs={{0,2},{1,3},{2,0},{3,1},{4,6},{5,7},{6,4},{7,5},{8,10},{9,11},{10,... | collective-permute-start | bytes 430088 | tf_op jit(solution)/shard_map/ppermute | solution.py:70

commit v2 on v1

v2 whole, which is shorter than its diff:
```python
import functools

import jax
import jax.numpy as jnp
from jax import lax
from jax.experimental import pallas as pl
from jax.experimental.pallas import tpu as pltpu
from jax.sharding import PartitionSpec as P

STEPS = 2
HEAT_SPREADING = 1000.0
STIFF = 1.5
WARMING_SLOPE = 0.1
OHMIC_POWER = 8.0

F32 = jnp.float32
BF16 = jnp.bfloat16
EXTRA = 16
EXACT = lax.Precision.HIGHEST


def call(kernel, out_shapes, args, smem=0, scratch=(), vmem=24):
    specs = [pl.BlockSpec(memory_space=pltpu.SMEM)] * smem
    specs += [pl.BlockSpec(memory_space=pltpu.VMEM)] * (len(args) - smem)
    return pl.pallas_call(
        kernel,
        out_shape=out_shapes,
        in_specs=specs,
        out_specs=[pl.BlockSpec(memory_space=pltpu.VMEM)] * len(out_shapes),
        scratch_shapes=list(scratch),
        compiler_params=pltpu.CompilerParams(vmem_limit_bytes=vmem * 2**20),
        cost_estimate=pl.CostEstimate(flops=0, bytes_accessed=1, transcendentals=0),
    )(*args)


def shaped(*shape, dtype=F32):
    return jax.ShapeDtypeStruct(shape, dtype)


def split(x):
    high = x.astype(BF16)
    return high, (x - high.astype(F32)).astype(BF16)


def iota(shape, dim):
    return lax.broadcasted_iota(jnp.int32, shape, dim)


def mm(a, b):
    return jnp.dot(a, b, preferred_element_type=F32)


def exact(a, b, dims=((1,), (0,))):
    return lax.dot_general(a, b, (dims, ((), ())), precision=EXACT, preferred_element_type=F32)


def mm_nt(a, b):
    return lax.dot_general(a, b, (((1,), (1,)), ((), ())), preferred_element_type=F32)


def table_rows(planes, rows, columns, nx, ny, nz):
    at, places = 0, {}
    for name, items, each in (
        ("lx", 1, rows + EXTRA),
        ("ax", nz * (rows // 128), 2 * planes),
        ("by", nz, 2 * planes),
        ("dx", nx, planes),
        ("dxl", nx, 8),
        ("dy", ny, planes),
        ("cg", 1, 128),
        ("phz", planes + 2, 8),
        ("psz", planes + 2, 8),
        ("mz", 2, 128),
        ("wz", 1, 8),
    ):
        places[name] = (at, each)
        at += items * each
    return places, at


class Group:
    def __init__(self, ref, place):
        self.ref, (self.at, self.each) = ref, place

    def rows(self, k):
        at = self.at + k * self.each
        return pl.ds(at if isinstance(at, int) else pl.multiple_of(at, 8), self.each)

    def __getitem__(self, k):
        return self.ref[self.rows(k), :]

    def __setitem__(self, k, value):
        self.ref[self.rows(k), :] = value


def groups_of(sizes, ref, *names):
    places, _ = table_rows(*sizes)
    return [Group(ref, places[name]) for name in names]


def partner(me, k, n):
    return me ^ k


def groups(n):
    return [k.bit_length() - 1 for k in range(1, n)]


def all_pairs(arrays, axis):
    n = lax.axis_size(axis)
    return [
        lax.ppermute(arrays[b], axis, [(i, i ^ k) for i in range(n)])
        for k, b in zip(range(1, n), groups(n))
    ]


def next_pairs(even, odd, axis):
    n = lax.axis_size(axis)
    first = lax.ppermute(even, axis, [(i, i ^ 1) for i in range(n)])
    if n == 2:
        return first, first
    other = {i: (i + 1) % n if i % 2 else (i - 1) % n for i in range(n)}
    return first, lax.ppermute(odd, axis, list(other.items()))


def conductance(z, idx, scalars, kind_ref, n_planes):
    factor = jnp.zeros(kind_ref.shape[1:], F32)
    for category in range(scalars.shape[0] - n_planes):
        factor = jnp.where(kind_ref[z] == category, scalars[n_planes + category], factor)
    return scalars[idx[2] * kind_ref.shape[0] + z] * factor


def faces_kernel(
    n_planes, idx, scalars, u_ref, kind_ref, xs0, xs1, ys0, ys1, zs0, zs1
):
    planes, rows, columns = u_ref.shape
    even = [idx[d] % 2 == 0 for d in range(3)]
    lane = iota((rows, columns), 1)
    low = jnp.zeros((rows, columns), F32)
    high = jnp.zeros((rows, columns), F32)
    for z in range(planes):
        u, c = u_ref[z], conductance(z, idx, scalars, kind_ref, n_planes)
        if z == 0:
            zs0[1], zs1[1] = c, c
        elif z == planes - 1:
            zs0[1] = jnp.where(even[2], c, zs0[1])
            zs1[1] = jnp.where(even[2], zs1[1], c)
        for slot, values in ((0, u), (1, c)):
            at = slot * planes + z
            low = jnp.where(lane == at, pltpu.roll(values, at, 1) if at else values, low)
            high = jnp.where(lane == at, pltpu.roll(values, at + 1, 1), high)
            first, last = values[0:1, :], values[rows - 1 : rows, :]
            xs0[slot, z : z + 1, :] = jnp.where(even[0], last, first)
            xs1[slot, z : z + 1, :] = jnp.where(even[0], first, last)
    ys0[...] = jnp.where(even[1], high, low)
    ys1[...] = jnp.where(even[1], low, high)
    zs0[0] = jnp.where(even[2], u_ref[planes - 1], u_ref[0])
    zs1[0] = jnp.where(even[2], u_ref[0], u_ref[planes - 1])


def dispatch_kernel(blocks, capacity, segments, send, a_scr, b_scr, o_scr):
    _, chunks, lanes = segments.shape
    power, tile, cell = segments[0], segments[1].astype(jnp.int32), segments[2].astype(jnp.int32)
    block_row = iota((blocks, lanes), 0)
    for c in range(chunks):
        hit = block_row == tile[c : c + 1, :]
        o_scr[c * blocks : (c + 1) * blocks, :] = jnp.where(hit, 1.0, 0.0).astype(BF16)
    ahead = jnp.where(iota((lanes, lanes), 0) < iota((lanes, lanes), 1), 1.0, 0.0)
    both = jnp.concatenate([ahead, jnp.ones((lanes, lanes), F32)], axis=1).astype(BF16)
    counted = mm(o_scr[...], both)
    base = jnp.zeros((blocks, lanes), F32)
    ranks = iota((capacity, lanes), 0)
    p_high, p_mid = split(power)
    p_low = (power - p_high.astype(F32) - p_mid.astype(F32))
    pieces = [
        p_high.astype(F32),
        p_mid.astype(F32),
        p_low,
        (cell >> 16).astype(F32),
        ((cell >> 8) & 255).astype(F32),
        (cell & 255).astype(F32),
    ]
    for c in range(chunks):
        part = slice(c * blocks, (c + 1) * blocks)
        cols = slice(c * lanes, (c + 1) * lanes)
        hit = block_row == tile[c : c + 1, :]
        order = jnp.where(hit, counted[part, :lanes] + base, 0.0)
        base = base + counted[part, lanes:]
        rank = jnp.sum(order, axis=0, keepdims=True).astype(jnp.int32)
        b_scr[:, cols] = jnp.where(ranks == rank, 1.0, 0.0).astype(BF16)
        for k, piece in enumerate(pieces):
            a_scr[k * blocks : (k + 1) * blocks, cols] = jnp.where(
                hit, piece[c : c + 1, :], 0.0
            ).astype(BF16)
    out = mm_nt(a_scr[...], b_scr[...])
    r = [out[k * blocks : (k + 1) * blocks] for k in range(6)]
    send[...] = jnp.concatenate(
        [r[0] + r[1] + r[2], r[3] * 65536.0 + r[4] * 256.0 + r[5]], axis=1
    )


def joule_into(got, joule, r_scr, k_scr):
    planes, rows, columns = joule.shape
    sources, capacity = got.shape[0], got.shape[1] // 2
    column = iota((columns, capacity), 0)
    for s in range(sources):
        power = got[s : s + 1, :capacity]
        cell = got[s : s + 1, capacity:].astype(jnp.int32)
        part = slice(s * capacity, (s + 1) * capacity)
        high, low = split(power)
        hit = column == cell % columns
        r_scr[:columns, part] = jnp.where(hit, high.astype(F32), 0.0).astype(BF16)
        r_scr[columns:, part] = jnp.where(hit, low.astype(F32), 0.0).astype(BF16)
        k_scr[:, part] = jnp.broadcast_to(cell // columns, (8, capacity))
    total = sources * capacity
    step = min(total, 2048)
    row = iota((rows, step), 0)

    def plane(z, carry):
        sums = jnp.zeros((rows, 2 * columns), F32)
        for at in range(0, total, step):
            hit = row == k_scr[0:1, at : at + step] - z * rows
            onehot = jnp.where(hit, 1.0, 0.0).astype(BF16)
            sums = sums + mm_nt(onehot, r_scr[:, at : at + step])
        joule[z] = sums[:, :columns] + sums[:, columns:]
        return carry

    lax.fori_loop(0, planes, plane, 0)


def line_parts(position, theta, start, cells):
    growing, falling = jnp.exp(position * theta), jnp.exp(-position * theta)
    lower = growing + falling * jnp.exp(-(2.0 * start + 1.0) * theta)
    upper = falling + growing * jnp.exp(-(2.0 * (cells - start) - 1.0) * theta)
    return lower, upper


def line(conduct, cells):
    lead = HEAT_SPREADING * STIFF * conduct
    t = 0.5 / jnp.sqrt(lead)
    theta = 2.0 * jnp.log1p(t + t * t / (1.0 + jnp.sqrt(1.0 + t * t)))
    scale = 1.0 / (jnp.sqrt(4.0 * lead + 1.0) * (1.0 - jnp.exp(-2.0 * cells * theta)))
    return theta, scale


def prep_kernel(
    sizes, idx, scalars, gx_ref, gy_ref, co, z_scr,
):
    planes, rows, columns, nx, ny, nz = sizes
    lanes = 128
    extent = rows + EXTRA
    lx, ax, by, dx, dxl, dy, cg, phz, psz, mz, wz = groups_of(
        sizes, co, "lx", "ax", "by", "dx", "dxl", "dy", "cg", "phz", "psz", "mz", "wz"
    )
    gx, gy, gz = idx[0], idx[1], idx[2]
    x0, xn = (gx * rows).astype(F32), float(nx * rows)
    y0, yn = (gy * columns).astype(F32), float(ny * columns)

    def wide(array, width):
        return jnp.concatenate([array] * (width // lanes), axis=1)

    def rows_of(first):
        value = jnp.ones((planes, lanes), F32)
        for z in range(planes):
            one = scalars[first + z]
            value = jnp.where(iota((planes, lanes), 0) == z, one, value)
        return value

    lane_z = iota((8, lanes), 1) % planes
    lane_e = iota((8, lanes), 1) // planes
    by_lane = jnp.ones((8, lanes), F32)
    own = []
    for z in range(planes):
        value = scalars[gz * planes + z]
        own.append(value)
        by_lane = jnp.where(lane_z == z, value, by_lane)
    theta_lane, scale_lane = line(by_lane, yn)
    theta_rows, _ = line(rows_of(gz * planes), 1.0)
    for k in range(nx):
        dx[k] = jnp.exp(-float(k * rows) * theta_rows)
        dxl[k] = jnp.exp(-float(k * rows) * theta_lane)
    for k in range(ny):
        dy[k] = jnp.exp(-float(k * columns) * theta_rows)

    for part in range(nz):
        conduct = rows_of(part * planes)
        theta, scale = line(conduct, xn)
        low, high = line_parts(
            iota((planes, rows), 1).astype(F32), wide(theta, rows), x0, xn
        )
        both = jnp.concatenate([high * wide(scale, rows), low * wide(scale, rows)], axis=0)
        for half in range(rows // lanes):
            ax[part * (rows // lanes) + half] = both[:, half * lanes : (half + 1) * lanes]
        theta, scale = line(conduct, yn)
        low, high = line_parts(iota((planes, columns), 1).astype(F32), theta, y0, yn)
        by[part] = jnp.concatenate([high * scale, low * scale], axis=0)

    minus, plus = jnp.full((8, lanes), -1.0, F32), jnp.full((8, lanes), float(columns), F32)
    low_b, high_b = line_parts(minus, theta_lane, y0, yn)
    low_t, high_t = line_parts(plus, theta_lane, y0, yn)
    r, n = iota((lanes, lanes), 0), iota((lanes, lanes), 1)
    same = r % planes == n % planes
    kind = jnp.where(same, (r // planes) * 4 + n // planes, -1)
    cg[0] = jnp.where(
        kind == 8, (high_b * scale_lane)[0:1, :],
        jnp.where(
            kind == 9, (high_t * scale_lane)[0:1, :],
            jnp.where(
                kind == 12, (low_b * scale_lane)[0:1, :],
                jnp.where(kind == 13, (low_t * scale_lane)[0:1, :], 0.0),
            ),
        ),
    )

    order = iota((extent, lanes), 0)
    index = jnp.where(order == rows, -1, jnp.where(order == rows + 1, rows, order))
    position = index.astype(F32)
    real = order < rows + 2
    index_w, order_w = wide(index, rows), wide(order, rows)
    at_or_past = index_w >= iota((extent, rows), 1)
    lane = iota((extent, lanes), 1)
    packed = jnp.zeros((extent, lanes), F32)
    y_col = iota((columns, columns), 0).astype(F32)
    y_i, y_j = iota((columns, columns), 0), iota((columns, columns), 1)
    y_past = y_j >= y_i
    for z in range(planes):
        theta, k_x = line(jnp.full((8, lanes), own[z], F32), xn)
        theta1, k1 = theta[0:1, :], k_x[0:1, :]
        low_c, high_c = line_parts(position, theta1, x0, xn)
        low_c = jnp.where(real, low_c * k1, 0.0)
        high_c = jnp.where(real, high_c * k1, 0.0)
        packed = jnp.where(lane == z, high_c, jnp.where(lane == planes + z, low_c, packed))
        low_r, high_r = line_parts(
            iota((8, rows), 1).astype(F32), wide(theta, rows), x0, xn
        )
        low_r, high_r = low_r[0:1, :], high_r[0:1, :]
        g = jnp.where(at_or_past, wide(high_c, rows) * low_r, wide(low_c, rows) * high_r)
        g = jnp.where(order_w == rows + 2, low_r, jnp.where(order_w == rows + 3, high_r, g))
        gx_ref[z, :extent, :], gx_ref[z, extent:, :] = split(g)

        theta, k_y = line(jnp.full((8, lanes), own[z], F32), yn)
        theta1, k1 = theta[0:1, :], k_y[0:1, :]
        low_r, high_r = line_parts(iota((8, columns), 1).astype(F32), theta, y0, yn)
        low_r, high_r = low_r[0:1, :], high_r[0:1, :]
        low_c, high_c = line_parts(y_col, theta1, y0, yn)
        low_b, _ = line_parts(minus[0:1, :], theta1, y0, yn)
        _, high_t = line_parts(plus[0:1, :], theta1, y0, yn)
        g = k1 * jnp.where(y_past, high_r * low_c, low_r * high_c)
        ext = jnp.zeros((columns, lanes), F32)
        for e, values in enumerate((low_b * high_c * k1, high_t * low_c * k1, low_c, high_c)):
            ext = jnp.where(y_j == e * planes + z, values, ext)
        gy_ref[z, :, :lanes], gy_ref[planes + z, :, :lanes] = split(g)
        gy_ref[z, :, lanes:], gy_ref[planes + z, :, lanes:] = split(ext)
    lx[0] = packed

    total = planes * nz
    cond = [jnp.full((8, lanes), scalars[z], F32) for z in range(total)]
    lead = [HEAT_SPREADING * STIFF * 0.5 * (cond[z] + cond[z + 1]) for z in range(total - 1)]
    lower = [jnp.ones((8, lanes), F32)]
    flux = HEAT_SPREADING * STIFF * cond[0]
    resist = [1.0 / value for value in lead]
    for z in range(total - 1):
        flux = flux + lower[z]
        lower.append(lower[z] + flux * resist[z])
    weight = 1.0 / (flux + lower[total - 1])
    upper = [None] * total
    upper[total - 1] = weight
    flux = jnp.zeros((8, lanes), F32)
    for z in range(total - 2, -1, -1):
        flux = flux + upper[z + 1]
        upper[z] = upper[z + 1] + flux * resist[z]
    zero = jnp.zeros((8, lanes), F32)
    z_scr[0], z_scr[total + 3] = zero, zero
    z_scr[total + 1], z_scr[total + 2] = zero, zero
    for z in range(total):
        z_scr[1 + z] = lower[z]
        z_scr[total + 3 + z] = upper[z]
    z_scr[2 * total + 3] = zero
    mine = gz * planes
    for z in range(planes + 2):
        phz[z] = z_scr[mine + z]
        psz[z] = jnp.where(mine + z == 0, zero, z_scr[total + 2 + mine + z])

    low_lane, high_lane = zero, zero
    for z in range(planes):
        low_lane = jnp.where(lane_z == z, phz[z + 1], low_lane)
        high_lane = jnp.where(lane_z == z, psz[z + 1], high_lane)
    row_p, lane_p = iota((planes, lanes), 0), iota((planes, lanes), 1)
    low_rows, high_rows = jnp.zeros((planes, lanes), F32), jnp.zeros((planes, lanes), F32)
    for z in range(planes):
        low_rows = jnp.where(row_p == z, phz[z + 1][0:1, :], low_rows)
        high_rows = jnp.where(row_p == z, psz[z + 1][0:1, :], high_rows)
    blocks, ends = [], []
    for e in range(2):
        g = jnp.where(
            lane_p % planes >= row_p,
            low_rows * high_lane[0:1, :],
            high_rows * low_lane[0:1, :],
        )
        blocks.append(jnp.where(lane_p // planes == e, g, 0.0))
        ends.append(
            jnp.where(lane_p == e, low_rows, jnp.where(lane_p == 2 + e, high_rows, 0.0))
        )
    rest = jnp.zeros((lanes - 2 * planes, lanes), F32)
    mz[0] = jnp.concatenate(blocks + [rest], axis=0)
    mz[1] = jnp.concatenate(ends + [rest], axis=0)
    row8 = iota((8, lanes), 0)
    wz[0] = jnp.where(
        (row8 < 2) & (lane_e == row8),
        high_lane,
        jnp.where((row8 >= 2) & (row8 < 4) & (lane_e == row8 - 2), low_lane, 0.0),
    )


def slope_kernel(
    counts, n_planes, idx, scalars, u_ref, kind_ref, xr0, xr1, yr0, yr1, zr0, zr1,
    d_ref, ux, uy, uz, kx0, kx1, ky0, ky1, kz,
):
    planes, rows, columns = u_ref.shape
    even = [idx[d] % 2 == 0 for d in range(3)]
    at_low = [idx[d] == 0 for d in range(3)]
    at_high = [idx[d] == counts[d] - 1 for d in range(3)]
    row, lane = iota((rows, columns), 0), iota((rows, columns), 1)

    def ends(first, second, d):
        return jnp.where(even[d], second, first), jnp.where(even[d], first, second)

    low, high = ends(xr0[0], xr1[0], 0)
    ux[...] = jnp.zeros(ux.shape, F32)
    for z in range(planes):
        ux[z, 0:1, :] = low[z : z + 1, :]
        ux[z, 1:2, :] = high[z : z + 1, :]
    x_low, x_high = ends(xr0[1], xr1[1], 0)
    low, high = ends(yr0[...], yr1[...], 1)
    kind = iota((rows, 128), 1) // planes
    uy[...] = jnp.zeros(uy.shape, F32)
    uy[:rows, :] = jnp.where(
        kind == 0, low, jnp.where(kind == 1, pltpu.roll(high, planes, 1), 0.0)
    )
    low, high = ends(zr0[0], zr1[0], 2)
    uz[0] = jnp.where(at_low[2], 0.0, low)
    uz[1] = high
    z_low, z_high = ends(zr0[1], zr1[1], 2)
    half = 0.5 * HEAT_SPREADING
    y_low, y_high = ends(yr0[...], yr1[...], 1)
    c_before = None
    for z in range(planes):
        c = conductance(z, idx, scalars, kind_ref, n_planes)
        first = jnp.where(at_low[0], -c[0:1, :], x_low[z : z + 1, :])
        final = jnp.where(at_high[0], -c[rows - 1 :, :], x_high[z : z + 1, :])
        kx0[z] = half * (c + jnp.where(row == 0, first, pltpu.roll(c, 1, 0)))
        kx1[z] = half * (c + jnp.where(row == rows - 1, final, pltpu.roll(c, rows - 1, 0)))
        first = jnp.where(at_low[1], -c, pltpu.roll(y_low, columns - planes - z, 1))
        final = jnp.where(at_high[1], -c, pltpu.roll(y_high, columns - 1 - planes - z, 1))
        ky0[z] = half * (c + jnp.where(lane == 0, first, pltpu.roll(c, 1, 1)))
        ky1[z] = half * (c + jnp.where(lane == columns - 1, final, pltpu.roll(c, columns - 1, 1)))
        if z == 0:
            kz[z] = half * (c + jnp.where(at_low[2], c, z_low))
        else:
            kz[z] = half * (c + c_before)
        c_before = c
        if z == planes - 1:
            kz[planes] = half * jnp.where(at_high[2], 0.0, c + z_high)
    for z in range(planes):
        d_ref[z] = outflow(z, u_ref, ux, uy, uz, kx0, kx1, ky0, ky1, kz)


def outflow(z, u_ref, ux, uy, uz, kx0, kx1, ky0, ky1, kz):
    planes, rows, columns = u_ref.shape
    u = u_ref[z]
    row, lane = iota((rows, columns), 0), iota((rows, columns), 1)
    edge = uy[:rows, :]
    edge_low = pltpu.roll(edge, columns - z, 1) if z else edge
    edge_high = pltpu.roll(edge, columns - 1 - planes - z, 1)
    below = uz[0] if z == 0 else u_ref[z - 1]
    above = uz[1] if z == planes - 1 else u_ref[z + 1]
    total = kx0[z] * (jnp.where(row == 0, ux[z, 0:1, :], pltpu.roll(u, 1, 0)) - u)
    total += kx1[z] * (
        jnp.where(row == rows - 1, ux[z, 1:2, :], pltpu.roll(u, rows - 1, 0)) - u
    )
    total += ky0[z] * (jnp.where(lane == 0, edge_low, pltpu.roll(u, 1, 1)) - u)
    total += ky1[z] * (
        jnp.where(lane == columns - 1, edge_high, pltpu.roll(u, columns - 1, 1)) - u
    )
    return total + kz[z] * (below - u) + kz[z + 1] * (above - u)


def advance(idx, source_of, gx_ref, gy_ref, phz, psz, t_ref, e_ref, x_sends, z_sends):
    planes, extent, columns = t_ref.shape
    rows = extent - EXTRA
    sums = jnp.zeros((extent, 128), F32)
    below, above = jnp.zeros((rows, columns), F32), jnp.zeros((rows, columns), F32)
    for z in range(planes):
        high, low = split(source_of(z))
        out = mm(gx_ref[z], jnp.concatenate([high, low], axis=1))
        t = out[:extent, :columns] + (out[:extent, columns:] + out[extent:, :columns])
        high, low = split(t)
        out = mm(jnp.concatenate([high, low], axis=0), gy_ref[z])
        out = out[:extent] + (out[extent:] + mm(high, gy_ref[planes + z]))
        t_ref[z] = out[:, :columns]
        sums += out[:, columns:]
        main = out[:rows, :columns]
        below += phz[z + 1][0:1, :] * main
        above += psz[z + 1][0:1, :] * main
    e_ref[...] = sums
    for b, send in enumerate(x_sends):
        take = jnp.where((idx[0] >> b) % 2 == 0, 0, 1)
        for z in range(planes):
            pair = t_ref[z, rows + 2 : rows + 4, :]
            send[z : z + 1, :] = jnp.where(take == 0, pair[0:1], pair[1:2])
        pair = sums[rows + 2 : rows + 4, :]
        send[planes:, :] = jnp.broadcast_to(
            jnp.where(take == 0, pair[0:1], pair[1:2]), (8, 128)
        )
    for b, send in enumerate(z_sends):
        send[...] = jnp.where((idx[2] >> b) % 2 == 0, below, above)


def start_kernel(sizes, n_sends, idx, got, d_ref, u_ref, gx_ref, gy_ref, co,
                 joule, t_ref, e_ref, *rest):
    phz, psz = groups_of(sizes, co, "phz", "psz")
    sends, (r_scr, k_scr) = rest[:-2], rest[-2:]
    joule_into(got, joule, r_scr, k_scr)

    def source_of(z):
        return d_ref[z] + OHMIC_POWER * ((1.0 + WARMING_SLOPE * u_ref[z]) * joule[z])

    advance(
        idx, source_of, gx_ref, gy_ref, phz, psz, t_ref, e_ref,
        sends[: n_sends], sends[n_sends:],
    )


def x_kernel(sizes, idx, e_ref, co, *rest):
    gots, (e_out, f_out, send) = rest[:-3], rest[-3:]
    planes, nx = sizes[0], sizes[3]
    dx, dxl, lx = groups_of(sizes, co, "dx", "dxl", "lx")
    me = idx[0]
    sums = [[jnp.zeros((planes, 128), F32), jnp.zeros((8, 128), F32)] for _ in range(2)]
    for k, got in zip(range(1, nx), gots):
        other = partner(me, k, nx)
        far = jnp.abs(me - other)
        pair = got[:planes, :] * dx[far], got[planes:, :] * dxl[far]
        for side, keep in ((0, other < me), (1, other > me)):
            for part in range(2):
                sums[side][part] += jnp.where(keep, pair[part], 0.0)
    f_out[:planes, :], f_out[planes:, :] = sums[0][0], sums[1][0]
    row, lane = iota((planes, 128), 0), iota((planes, 128), 1)
    own = lane % planes == row
    ext = jnp.concatenate(
        [jnp.where(own, sums[0][1][0:1, :], 0.0), jnp.where(own, sums[1][1][0:1, :], 0.0)],
        axis=0,
    )
    e = e_ref[...] + exact(lx[0][:, : 2 * planes], ext)
    e_out[...] = e
    send[...] = e.T[2 * planes : 4 * planes]


def four(rows):
    return jnp.concatenate([rows] * 4, axis=0)


def weights(ref, planes):
    row = iota((planes, 128), 0)
    values = jnp.zeros((planes, 128), F32)
    for z in range(planes):
        values = jnp.where(row == z, ref[z + 1][0:1, :], values)
    return values


def y_kernel(sizes, idx, t_ref, e_ref, f_ref, co, *rest):
    ny = sizes[4]
    dy, lx, by, cg, phz, psz, mz = groups_of(
        sizes, co, "dy", "lx", "by", "cg", "phz", "psz", "mz"
    )
    gots, rest = rest[: ny - 1], rest[ny - 1 :]
    q_ref, l_ref, b_ref = rest[:3]
    sends = rest[3:]
    planes, extent, columns = t_ref.shape
    rows = extent - EXTRA
    me = idx[1]
    row = iota((2 * planes, extent), 0)
    across = jnp.zeros((2 * planes, extent), F32)
    for k, got in zip(range(1, ny), gots):
        other = partner(me, k, ny)
        far = jnp.concatenate([dy[jnp.abs(me - other)][:, 0:1]] * 2, axis=0)
        keep = (row < planes) == (other < me)
        across += jnp.where(keep, got[...] * far, 0.0)
    others = jnp.concatenate(
        [
            jnp.zeros((2 * planes, extent), F32),
            across,
            jnp.zeros((128 - 4 * planes, extent), F32),
        ],
        axis=0,
    ).T
    lane = iota((extent, 128), 1)
    q = jnp.where(lane < 2 * planes, e_ref[...], 0.0) + exact(others, cg[0])
    q_ref[...] = q
    left = lx[0] + others
    l_ref[...] = left
    right = jnp.concatenate([f_ref[...], by[idx[2]]], axis=0)
    b_ref[...] = right
    edge = exact(q[:rows], mz[1]).T
    ghost = slice(rows, rows + 8)
    low, high = weights(phz, planes), weights(psz, planes)
    both = jnp.concatenate([right * four(low), right * four(high)], axis=1)
    ghosts = exact(left[ghost, : 4 * planes], both)
    g_low, g_high = ghosts[:, :128], ghosts[:, 128:]
    for z in range(planes):
        value = t_ref[z, ghost, :]
        g_low += phz[z + 1][0:1, :] * value
        g_high += psz[z + 1][0:1, :] * value
    for b, send in enumerate(sends):
        lower = (idx[2] >> b) % 2 == 0
        scale = jnp.where(lower, low, high)
        twice = jnp.concatenate([scale] * 2, axis=0)
        send[:8, :] = jnp.where(lower, g_low, g_high)
        send[8 : 8 + 2 * planes, :] = f_ref[...] * twice
        at = 8 + 2 * planes
        for part in range(rows // 128):
            cols = slice(part * 128, (part + 1) * 128)
            send[at : at + 8, :] = edge[0:8, cols]
            send[at + 8 : at + 8 + 2 * planes, :] = across[:, cols] * twice
            at += 8 + 2 * planes


def carried(nz, idx, bigs, smalls, ax, by, rows, ghosts):
    me = idx[2]
    planes = by.each // 2
    below = above = None
    g_below = g_above = edges = 0.0
    lefts, rights = [], []
    sub = iota((8, rows), 0)
    for k, big, small in zip(range(1, nz), bigs, smalls):
        other = partner(me, k, nz)
        lower = other < me

        def add(total, value, keep):
            value = jnp.where(keep, value, 0.0)
            return value if total is None else total + value

        below = add(below, big[...], lower)
        above = add(above, big[...], jnp.logical_not(lower))
        at, stride = 8 + 2 * planes, 8 + 2 * planes
        parts = [at + p * stride for p in range(rows // 128)]
        across = jnp.concatenate([small[p + 8 : p + stride, :] for p in parts], axis=1)
        halves = rows // 128
        near = [ax[other * halves + half] for half in range(halves)]
        lefts += [jnp.concatenate(near, axis=1), across]
        right = jnp.concatenate([small[8:at, :], by[other]], axis=0)
        rights.append(
            jnp.concatenate(
                [jnp.where(lower, right, 0.0), jnp.where(lower, 0.0, right)], axis=1
            )
        )
        if ghosts:
            g_below += jnp.where(lower, small[:8, :], 0.0)
            g_above += jnp.where(lower, 0.0, small[:8, :])
            value = jnp.concatenate([small[p : p + 8, :] for p in parts], axis=1)
            edges += jnp.where(sub // 2 == jnp.where(lower, 0, 1), value, 0.0)
    more = exact(
        jnp.concatenate(lefts, axis=0), jnp.concatenate(rights, axis=0), ((0,), (0,))
    )
    below, above = below + more[:, :128], above + more[:, 128:]
    return below, above, g_below, g_above, edges


def whole_planes(t_ref, l_ref, b_ref, second, extent):
    planes = t_ref.shape[0]
    high, low = split(l_ref[:extent, : 4 * planes])
    pair = jnp.concatenate([high, low], axis=0)
    right = b_ref[...]
    row = iota(right.shape, 0) % planes
    for z in range(planes):
        r_high, r_low = split(jnp.where(row == z, right, 0.0))
        out = mm(pair, r_high)
        second[z] = t_ref[z, :extent, :] + (out[:extent] + (out[extent:] + mm(high, r_low)))


def change(outside, second, phz, psz, below, above, emit):
    planes = second.shape[0]
    tails = [above]
    for z in range(planes - 1, -1, -1):
        tails.append(tails[-1] + psz[z + 1][0:1, :] * second[z])
    tails = tails[::-1]
    if outside:
        emit(-1, psz[0][0:1, :] * below + phz[0][0:1, :] * tails[0])
    head = below
    for z in range(planes):
        head = head + phz[z + 1][0:1, :] * second[z]
        emit(z, psz[z + 1][0:1, :] * head + phz[z + 1][0:1, :] * tails[z + 1])
    if outside:
        emit(planes, psz[planes + 1][0:1, :] * head + phz[planes + 1][0:1, :] * above)


def rise_kernel(sizes, n_sends, idx, t_in, l_ref, b_ref, q_ref, co,
                u_ref, ux, uy, uz, kx0, kx1, ky0, ky1, kz, joule, gx_ref, gy_ref, *rest):
    nz = sizes[5]
    phz, psz, mz, wz, ax, by = groups_of(sizes, co, "phz", "psz", "mz", "wz", "ax", "by")
    bigs, smalls, rest = rest[: nz - 1], rest[nz - 1 : 2 * nz - 2], rest[2 * nz - 2 :]
    u_out, ux_out, uy_out, uz_out, t_ref, e_ref = rest[:6]
    sends, second = rest[6:-1], rest[-1]
    planes, rows, columns = u_ref.shape
    whole_planes(t_in, l_ref, b_ref, second, rows + 8)
    below, above, g_below, g_above, edges = carried(nz, idx, bigs, smalls, ax, by, rows, True)

    def emit(z, value):
        if z == -1:
            uz_out[0] = uz[0] + value[:rows]
        elif z == planes:
            uz_out[1] = uz[1] + value[:rows]
        else:
            u_out[z] = u_ref[z] + value[:rows]
            ux_out[z] = ux[z] + value[rows:]

    change(
        True, second, phz, psz,
        jnp.concatenate([below, g_below], axis=0),
        jnp.concatenate([above, g_above], axis=0),
        emit,
    )
    grown = exact(q_ref[:rows, :], mz[0]) + exact(edges, wz[0], ((0,), (0,)))
    uy_out[...] = uy[...]
    uy_out[:rows, :] = uy[:rows, :] + grown

    def source_of(z):
        out = outflow(z, u_out, ux_out, uy_out, uz_out, kx0, kx1, ky0, ky1, kz)
        return out + OHMIC_POWER * ((1.0 + WARMING_SLOPE * u_out[z]) * joule[z])

    advance(
        idx, source_of, gx_ref, gy_ref, phz, psz, t_ref, e_ref,
        sends[:n_sends], sends[n_sends:],
    )


def finish_kernel(sizes, idx, t_in, l_ref, b_ref, co, u_ref, joule, *rest):
    nz = sizes[5]
    phz, psz, ax, by = groups_of(sizes, co, "phz", "psz", "ax", "by")
    bigs, smalls, rest = rest[: nz - 1], rest[nz - 1 : 2 * nz - 2], rest[2 * nz - 2 :]
    u_out, heat_out, second = rest
    rows = u_ref.shape[1]
    whole_planes(t_in, l_ref, b_ref, second, rows)
    below, above, _, _, _ = carried(nz, idx, bigs, smalls, ax, by, rows, False)

    def emit(z, value):
        u = u_ref[z] + value
        u_out[z] = u
        heat_out[z] = (1.0 + WARMING_SLOPE * u) * joule[z]

    change(False, second, phz, psz, below, above, emit)


def per_device(
    starting_warmth,
    sheet_stratum_number,
    stratum_heat_conduction,
    substance_kind,
    substance_kind_scaling,
    wire_piece_amperes,
    wire_piece_ohms_base,
    wire_piece_tile,
    wire_piece_voxel,
):
    planes, rows, columns = starting_warmth.shape
    counts = tuple(lax.axis_size(axis) for axis in ("gx", "gy", "gz"))
    nx, ny, nz = counts
    bits = [(n - 1).bit_length() for n in counts]
    devices = nx * ny * nz
    extent = rows + EXTRA
    idx = jnp.stack([lax.axis_index(axis) for axis in ("gx", "gy", "gz")]).astype(jnp.int32)
    block = shaped(planes, rows, columns)
    n_planes = sheet_stratum_number.shape[0]
    layers = jnp.arange(stratum_heat_conduction.shape[0], dtype=jnp.int32)
    matches = sheet_stratum_number[:, None] == layers[None, :]
    scalars = jnp.concatenate(
        [
            jnp.sum(jnp.where(matches, stratum_heat_conduction[None, :], 0.0), axis=1),
            substance_kind_scaling,
        ]
    )

    count = wire_piece_amperes.shape[0]
    capacity = 2 * count // devices
    lanes = 128
    chunks = count // lanes
    segments = jnp.stack(
        [
            wire_piece_amperes * wire_piece_amperes * wire_piece_ohms_base,
            wire_piece_tile[:, 0].astype(F32),
            wire_piece_voxel.astype(F32),
        ]
    ).reshape(3, chunks, lanes)
    (send,) = call(
        functools.partial(dispatch_kernel, devices, capacity),
        [shaped(devices, 2 * capacity)],
        (segments,),
        scratch=[
            pltpu.VMEM((6 * devices, count), BF16),
            pltpu.VMEM((capacity, count), BF16),
            pltpu.VMEM((chunks * devices, lanes), BF16),
        ],
    )
    warmth, kinds, send = lax.optimization_barrier((starting_warmth, substance_kind, send))
    got = lax.all_to_all(send, ("gx", "gy", "gz"), split_axis=0, concat_axis=0, tiled=True)

    xs0, xs1, ys0, ys1, zs0, zs1 = call(
        functools.partial(faces_kernel, n_planes),
        [shaped(2, planes, columns)] * 2
        + [shaped(rows, 128)] * 2
        + [shaped(2, rows, columns)] * 2,
        (idx, scalars, warmth, kinds),
        smem=2,
    )
    zr = next_pairs(zs0, zs1, "gz")
    xr = next_pairs(xs0, xs1, "gx")
    yr = next_pairs(ys0, ys1, "gy")
    sizes = (planes, rows, columns, nx, ny, nz)
    gx_m, gy_m, co = call(
        functools.partial(prep_kernel, sizes),
        [
            shaped(planes, 2 * extent, rows, dtype=BF16),
            shaped(2 * planes, columns, 256, dtype=BF16),
            shaped(table_rows(*sizes)[1], lanes),
        ],
        (idx, scalars),
        smem=2,
        scratch=[pltpu.VMEM((2 * planes * nz + 4, 8, lanes), F32)],
    )
    d0, ux, uy, uz, *conduct = call(
        functools.partial(slope_kernel, counts, n_planes),
        [block, shaped(planes, 8, columns), shaped(extent, 128), shaped(2, rows, columns)]
        + [block] * 4
        + [shaped(planes + 1, rows, columns)],
        (idx, scalars, warmth, kinds, *xr, *yr, *zr),
        smem=2,
    )
    step_out = [shaped(planes, extent, columns), shaped(extent, 128)]
    step_out += [shaped(planes + 8, columns)] * bits[0] + [shaped(rows, columns)] * bits[2]
    total = devices * capacity
    joule, t, e, *sends = call(
        functools.partial(start_kernel, sizes, bits[0]),
        [block] + step_out,
        (idx, got, d0, warmth, gx_m, gy_m, co),
        smem=1,
        scratch=[
            pltpu.VMEM((2 * columns, total), BF16),
            pltpu.VMEM((8, total), jnp.int32),
        ],
    )
    u = warmth
    small = shaped(8 + 2 * planes + (8 + 2 * planes) * (rows // 128), 128)
    for repeat in range(STEPS):
        gots = all_pairs(sends[: bits[0]], "gx")
        bigs = all_pairs(sends[bits[0] :], "gz")
        e, f, send = call(
            functools.partial(x_kernel, sizes),
            [shaped(extent, 128), shaped(2 * planes, columns), shaped(2 * planes, extent)],
            (idx, e, co, *gots),
            smem=1,
        )
        gots = all_pairs([send] * bits[1], "gy")
        q, left, right, *sends = call(
            functools.partial(y_kernel, sizes),
            [shaped(extent, 128)] * 2 + [shaped(4 * planes, columns)] + [small] * bits[2],
            (idx, t, e, f, co, *gots),
            smem=1,
        )
        smalls = all_pairs(sends, "gz")
        if repeat < STEPS - 1:
            u, ux, uy, uz, t, e, *sends = call(
                functools.partial(rise_kernel, sizes, bits[0]),
                [block, shaped(planes, 8, columns), shaped(extent, 128)]
                + [shaped(2, rows, columns)]
                + step_out,
                (idx, t, left, right, q, co, u, ux, uy, uz, *conduct)
                + (joule, gx_m, gy_m, *bigs, *smalls),
                smem=1,
                scratch=[pltpu.VMEM((planes, rows + 8, columns), F32)],
            )
    return tuple(
        call(
            functools.partial(finish_kernel, sizes),
            [block, block],
            (idx, t, left, right, co, u, joule, *bigs, *smalls),
            smem=1,
            scratch=[pltpu.VMEM((planes, rows, columns), F32)],
        )
    )


def solution(mesh):
    return jax.shard_map(
        per_device,
        mesh=mesh,
        in_specs=(
            P("gz", "gx", "gy"),
            P(),
            P(),
            P("gz", "gx", "gy"),
            P(),
            P(("gx", "gy", "gz")),
            P(("gx", "gy", "gz")),
            P(("gx", "gy", "gz"), None),
            P(("gx", "gy", "gz")),
        ),
        out_specs=(P("gz", "gx", "gy"), P("gz", "gx", "gy")),
        check_vma=False,
    )
```

time: 119 us -> 108 us (0.908)
  waiting for transfers between devices: 33.6 us -> 18.3 us
  starting transfers between devices: 27.1 us -> 39.9 us
  local copies, waits for them, and re-layouts: 13.5 us -> 5.88 us
  Pallas kernels: 43.7 us -> 38.5 us
  other arithmetic: 0.08 us -> 3.76 us
    pallas_call x3 -> x0, Pallas kernels: 20.4 us -> none  [the longest x1 14 us: per_device(): pl.pallas_call(start_kernel, out_shape=outs, in_specs=[pl.BlockSpec(memor...]
    ppermute x14 -> x20, waiting for transfers between devices: 33.6 us -> 15.6 us  [all_pairs(): lax.ppermute(arrays[b], axis, [(i, i ^ k) for i in range(n)])]
    pallas_call x8 -> x11, Pallas kernels: 23.3 us -> 38.5 us  [call(): pl.pallas_call(kernel, out_shape=out_shapes, in_specs=specs, out_specs=[p...]
    ppermute x14 -> x20, starting transfers between devices: 14.6 us -> 27.4 us  [all_pairs(): lax.ppermute(arrays[b], axis, [(i, i ^ k) for i in range(n)])]
    unnamed x55 -> x13, local copies, waits for them, and re-layouts: 12.8 us -> 5.2 us
    all_to_all x1, waiting for transfers between devices: 0.01 us -> 2.71 us  [per_device(): lax.all_to_all(send, ('gx', 'gy', 'gz'), split_axis=0, concat_axis=0, til...]
    another operation x0 -> x3, other arithmetic: none -> 1.47 us  [per_device(): jnp.stack([wire_piece_amperes * wire_piece_amperes * wire_piece_ohms_base...]
  transfers between devices with their start and end apart: 20 -> 26, of which waited for: 13 -> 13; matrix products, arithmetic and copies ran while one was open for 1% -> 1% of each run, Pallas kernels for 5% -> 8%
where the time goes in v2:
time: 108 us; the launch traced here: 107 us
  starting transfers between devices  39.9 us (37%)
  Pallas kernels  38.5 us (36%)
  waiting for transfers between devices  18.3 us (17%)
  local copies, waits for them, and re-layouts  5.88 us (5%)
  other arithmetic  3.76 us (3%)
    pallas_call x11, Pallas kernels, call(): pl.pallas_call(kernel, out_shape=out_shapes, in_specs=specs, out_specs=[p...  38.5 us
    ppermute x20, starting transfers between devices, all_pairs(): lax.ppermute(arrays[b], axis, [(i, i ^ k) for i in range(n)])  27.4 us
    ppermute x20, waiting for transfers between devices, all_pairs(): lax.ppermute(arrays[b], axis, [(i, i ^ k) for i in range(n)])  15.6 us
    unnamed x13, local copies, waits for them, and re-layouts  5.2 us
    ppermute x3, starting transfers between devices, next_pairs(): first = lax.ppermute(even, axis, [(i, i ^ 1) for i in range(n)])  4.86 us
    ppermute x2, starting transfers between devices, next_pairs(): return (first, lax.ppermute(odd, axis, list(other.items())))  3.94 us
    all_to_all x1, starting transfers between devices, per_device(): lax.all_to_all(send, ('gx', 'gy', 'gz'), split_axis=0, concat_axis=0, til...  3.71 us
    all_to_all x1, waiting for transfers between devices, per_device(): lax.all_to_all(send, ('gx', 'gy', 'gz'), split_axis=0, concat_axis=0, til...  2.71 us
  transfers between devices with their start and end apart: 26, of which 13 were waited for; matrix products, arithmetic and copies ran while one was open for 1% of the time, Pallas kernels for 8%

profile of v2, /device:TPU:0, one launch (start us, length us, event | category | flops | bytes accessed | tf_op | source)
XLA Modules:
  0.0 107.2 jit_solution(15340207641781160260)
XLA Ops:
  0.6 0.7 convert_element_type.17
  1.4 0.7 convert_bitcast_fusion
  2.1 0.7 multiply_bitcast_fusion
  2.8 1.8 %shard_map.104 = f32[32,512]{1,0:T(8,128)S(1)} custom-call(f32[3,32,128]{2,1,0:T(8,128)S(1)} %pad_maximum_fusion.segments), custom_call_target="tpu_custom_call" | custom-call | bytes 1 | tf_op jit(solution)/shard_map/pallas_call | solution.py:25
  4.6 0.8 select_reduce_fusion
  5.4 0.7 pad_maximum_fusion.1.scalars
  6.1 0.1 pad_add_fusion.idx
  6.2 1.2 %copy-done = f32[8,256,128]{2,1,0:T(8,128)S(1)} copy-done((f32[8,256,128]{2,1,0:T(8,128)S(1)}, f32[8,256,128]{2,1,0:T(8,128)}, u32[]{:S(2)}) %copy-start) | copy-done | bytes 1048600
  7.4 1.2 %copy-done.4 = s32[8,256,128]{2,1,0:T(8,128)S(1)} copy-done((s32[8,256,128]{2,1,0:T(8,128)S(1)}, s32[8,256,128]{2,1,0:T(8,128)}, u32[]{:S(2)}) %copy-start.4) | copy-done | bytes 1048600
  8.6 2.5 %shard_map.105 = (f32[2,8,128]{2,1,0:T(8,128)S(1)}, f32[2,8,128]{2,1,0:T(8,128)S(1)}, f32[256,128]{1,0:T(8,128)S(1)}, f32[256,128]{1,0:T(8,128)}, f32[2,256,128]{2,1,0:T(8,128)}, /*index=5*/f32[2,256,128]{2,1,0:T(8,128)}) custom-call(s32[3]{0:T(128)S(1)} %pad_add_fusion.idx, f32[36]{0:T(128)S(1)} %pad_maximum_fusion.1.scalars, f32[8,256,128]{2,1,0:T(8,128)S(1)} %copy-done, ...), custom_call_target="tpu_custom_call" | custom-call | bytes 1 | tf_op jit(solution)/shard_map/pallas_call | solution.py:25
  11.1 3.0 %collective-permute-start.3 = (f32[2,256,128]{2,1,0:T(8,128)}, f32[2,256,128]{2,1,0:T(8,128)S(1)}, u32[]{:S(2)}, u32[]{:S(2)}) collective-permute-start(f32[2,256,128]{2,1,0:T(8,128)} %get-tuple-element.57), channel_id=1, source_target_pairs={{0,1},{1,0},{2,3},{3,2},{4,5},{5,4},{6,7},{7,6},{8,9},{9,8},{10,11... | collective-permute-start | bytes 786440 | tf_op jit(solution)/shard_map/ppermute | solution.py:119
  14.1 2.5 %collective-permute-start.4 = (f32[2,256,128]{2,1,0:T(8,128)}, f32[2,256,128]{2,1,0:T(8,128)S(1)}, u32[]{:S(2)}, u32[]{:S(2)}) collective-permute-start(f32[2,256,128]{2,1,0:T(8,128)} %get-tuple-element.58), channel_id=1, source_target_pairs={{0,3},{1,2},{2,1},{3,0},{4,7},{5,6},{6,5},{7,4},{8,11},{9,10},{10,... | collective-permute-start | bytes 786440 | tf_op jit(solution)/shard_map/ppermute | solution.py:123
  16.6 0.7 copy.12
  17.3 3.7 %all-to-all-start = ((f32[32,1,512]{2,1,0:T(1,128)}), f32[32,1,512]{2,1,0:T(1,128)S(1)}, u32[]{:S(2)}, u32[]{:S(2)}) async-start(f32[32,1,512]{2,1,0:T(1,128)} %copy.12), calls=%async_computation | async-start | bytes 131072 | tf_op jit(solution)/shard_map/all_to_all | solution.py:805
  21.0 1.8 %collective-permute-start = (f32[2,8,128]{2,1,0:T(8,128)S(1)}, f32[2,8,128]{2,1,0:T(8,128)S(1)}, u32[]{:S(2)}, u32[]{:S(2)}) collective-permute-start(f32[2,8,128]{2,1,0:T(8,128)S(1)} %get-tuple-element.54), channel_id=1, source_target_pairs={{0,8},{8,0},{16,24},{24,16},{1,9},{9,1},{17,25},{25,17},{2,10},{10... | collective-permute-start | bytes 24584 | tf_op jit(solution)/shard_map/ppermute | solution.py:119
  22.9 1.5 %collective-permute-start.1 = (f32[2,8,128]{2,1,0:T(8,128)S(1)}, f32[2,8,128]{2,1,0:T(8,128)S(1)}, u32[]{:S(2)}, u32[]{:S(2)}) collective-permute-start(f32[2,8,128]{2,1,0:T(8,128)S(1)} %get-tuple-element.55), channel_id=1, source_target_pairs={{0,24},{8,16},{16,8},{24,0},{1,25},{9,17},{17,9},{25,1},{2,26},{10... | collective-permute-start | bytes 24584 | tf_op jit(solution)/shard_map/ppermute | solution.py:123
  24.3 3.2 %shard_map.107 = (bf16[8,544,256]{2,1,0:T(8,128)(2,1)S(1)}, bf16[16,128,256]{2,1,0:T(8,128)(2,1)S(1)}, f32[1096,128]{1,0:T(8,128)S(1)}) custom-call(s32[3]{0:T(128)S(1)} %pad_add_fusion.idx, f32[36]{0:T(128)S(1)} %pad_maximum_fusion.1.scalars), custom_call_target="tpu_custom_call" | custom-call | bytes 1 | tf_op jit(solution)/shard_map/pallas_call | solution.py:25
  27.5 1.4 %copy-done.2 = bf16[8,544,256]{2,1,0:T(8,128)(2,1)} copy-done((bf16[8,544,256]{2,1,0:T(8,128)(2,1)}, bf16[8,544,256]{2,1,0:T(8,128)(2,1)S(1)}, u32[]{:S(2)}) %copy-start.2) | copy-done | bytes 2228248
  28.9 2.7 %all-to-all-done = f32[32,1,512]{2,1,0:T(1,128)S(1)} async-done(((f32[32,1,512]{2,1,0:T(1,128)}), f32[32,1,512]{2,1,0:T(1,128)S(1)}, u32[]{:S(2)}, u32[]{:S(2)}) %all-to-all-start) | async-done | bytes 65568 | tf_op jit(solution)/shard_map/all_to_all | solution.py:805
  31.6 0.0 collective-permute-done.1.xr1
  31.6 0.0 collective-permute-done.2.yr0.yr1
  31.7 0.0 collective-permute-done.4.zr1
  31.7 0.0 copy-start.5
  31.7 1.4 %copy-done.5 = s32[8,256,128]{2,1,0:T(8,128)S(1)} copy-done((s32[8,256,128]{2,1,0:T(8,128)S(1)}, s32[8,256,128]{2,1,0:T(8,128)}, u32[]{:S(2)}) %copy-start.5) | copy-done | bytes 1048600
  33.1 3.3 %shard_map.106 = (f32[8,256,128]{2,1,0:T(8,128)S(1)}, f32[8,8,128]{2,1,0:T(8,128)S(1)}, f32[272,128]{1,0:T(8,128)S(1)}, f32[2,256,128]{2,1,0:T(8,128)S(1)}, f32[...) custom-call(s32[3]{0:T(128)S(1)} %pad_add_fusion.idx, ...), custom_call_target="tpu_custom_call" | custom-call | bytes 1 | tf_op jit(solution)/shard_map/pallas_call | solution.py:25
  36.4 14.1 %shard_map.108 = (f32[8,256,128]{2,1,0:T(8,128)S(1)}, f32[8,272,128]{2,1,0:T(8,128)S(1)}, f32[272,128]{1,0:T(8,128)S(1)}, f32[16,128]{1,0:T(8,128)S(1)}, f32[16,...) custom-call(s32[3]{0:T(128)S(1)} %pad_add_fusion.idx, f32[32,512]{1,0:T(8,128)S(1)} %bitcast.12, ...), custom_call_target="tpu_custom_call" | custom-call | bytes 1 | tf_op jit(solution)/shard_map/pallas_call | solution.py:25
  50.5 0.9 collective-permute-start.9
  51.4 2.4 %collective-permute-start.11 = (f32[256,128]{1,0:T(8,128)S(1)}, f32[256,128]{1,0:T(8,128)S(1)}, u32[]{:S(2)}, u32[]{:S(2)}) collective-permute-start(f32[256,128]{1,0:T(8,128)S(1)} %get-tuple-element.83), channel_id=1, source_target_pairs={{0,3},{1,2},{2,1},{3,0},{4,7},{5,6},{6,5},{7,4},{8,11},{9,10},{10,... | collective-permute-start | bytes 393224 | tf_op jit(solution)/shard_map/ppermute | solution.py:112
  53.8 0.3 collective-permute-start.10
  54.0 0.7 collective-permute-start.5
  54.8 1.5 %collective-permute-start.7 = (f32[16,128]{1,0:T(8,128)S(1)}, f32[16,128]{1,0:T(8,128)S(1)}, u32[]{:S(2)}, u32[]{:S(2)}) collective-permute-start(f32[16,128]{1,0:T(8,128)S(1)} %get-tuple-element.66), channel_id=1, source_target_pairs={{0,24},{8,16},{16,8},{24,0},{1,25},{9,17},{17,9},{25,1},{2,26},{10... | collective-permute-start | bytes 24584 | tf_op jit(solution)/shard_map/ppermute | solution.py:112
  56.2 1.5 %collective-permute-done.5.rest_0_ = f32[16,128]{1,0:T(8,128)S(1)} collective-permute-done((f32[16,128]{1,0:T(8,128)S(1)}, f32[16,128]{1,0:T(8,128)S(1)}, u32[]{:S(2)}, u32[]{:S(2)}) %collective-permute-start.5) | collective-permute-done | bytes 8224 | tf_op jit(solution)/shard_map/ppermute | solution.py:112
  57.7 0.7 collective-permute-start.6
  58.4 0.9 collective-permute-done.7.rest_2_
  59.3 2.0 %collective-permute-done.6.rest_1_ = f32[16,128]{1,0:T(8,128)S(1)} collective-permute-done((f32[16,128]{1,0:T(8,128)S(1)}, f32[16,128]{1,0:T(8,128)S(1)}, u32[]{:S(2)}, u32[]{:S(2)}) %collective-permute-start.6) | collective-permute-done | bytes 8224 | tf_op jit(solution)/shard_map/ppermute | solution.py:112
  61.4 0.8 shard_map.109
  62.2 0.1 collective-permute-start.8
  62.3 1.2 %collective-permute-done.8.rest_0_ = f32[16,272]{1,0:T(8,128)S(1)} collective-permute-done((f32[16,272]{1,0:T(8,128)S(1)}, f32[16,272]{1,0:T(8,128)S(1)}, u32[]{:S(2)}, u32[]{:S(2)}) %collective-permute-start.8) | collective-permute-done | bytes 17440 | tf_op jit(solution)/shard_map/ppermute | solution.py:112
  63.5 1.4 %shard_map.110 = (f32[272,128]{1,0:T(8,128)S(1)}, f32[272,128]{1,0:T(8,128)S(1)}, f32[32,128]{1,0:T(8,128)S(1)}, f32[72,128]{1,0:T(8,128)S(1)}, f32[72,128]{1,0:T(8,128)S(1)}) custom-call(s32[3]{0:T(128)S(1)} %pad_add_fusion.idx, f32[8,272,128]{2,1,0:T(8,128)S(1)} %get-tuple-element.63.t_ref.t_in, f32[272,128]{1,0:T(8,128)S(1)} %get-tuple-element.67.e_ref, ...), custom_call_target="tpu_custom_call" | custom-call | bytes 1 | tf_op jit(solution)/shard_map/pallas_call | solution.py:25
  64.8 1.8 %collective-permute-start.12 = (f32[72,128]{1,0:T(8,128)S(1)}, f32[72,128]{1,0:T(8,128)S(1)}, u32[]{:S(2)}, u32[]{:S(2)}) collective-permute-start(f32[72,128]{1,0:T(8,128)S(1)} %get-tuple-element.84), channel_id=1, source_target_pairs={{0,1},{1,0},{2,3},{3,2},{4,5},{5,4},{6,7},{7,6},{8,9},{9,8},{10,11... | collective-permute-start | bytes 110600 | tf_op jit(solution)/shard_map/ppermute | solution.py:112
  66.6 2.4 %collective-permute-start.14 = (f32[72,128]{1,0:T(8,128)S(1)}, f32[72,128]{1,0:T(8,128)S(1)}, u32[]{:S(2)}, u32[]{:S(2)}) collective-permute-start(f32[72,128]{1,0:T(8,128)S(1)} %get-tuple-element.85), channel_id=1, source_target_pairs={{0,3},{1,2},{2,1},{3,0},{4,7},{5,6},{6,5},{7,4},{8,11},{9,10},{10,... | collective-permute-start | bytes 110600 | tf_op jit(solution)/shard_map/ppermute | solution.py:112
  69.0 2.5 %collective-permute-start.13 = (f32[72,128]{1,0:T(8,128)S(1)}, f32[72,128]{1,0:T(8,128)S(1)}, u32[]{:S(2)}, u32[]{:S(2)}) collective-permute-start(f32[72,128]{1,0:T(8,128)S(1)} %get-tuple-element.85), channel_id=1, source_target_pairs={{0,2},{1,3},{2,0},{3,1},{4,6},{5,7},{6,4},{7,5},{8,10},{9,11},{10,... | collective-permute-start | bytes 110600 | tf_op jit(solution)/shard_map/ppermute | solution.py:112
  71.6 0.8 collective-permute-done.14.rest_5_
  72.4 1.5 %collective-permute-done.13.rest_4_ = f32[72,128]{1,0:T(8,128)S(1)} collective-permute-done((f32[72,128]{1,0:T(8,128)S(1)}, f32[72,128]{1,0:T(8,128)S(1)}, u32[]{:S(2)}, u32[]{:S(2)}) %collective-permute-start.13) | collective-permute-done | bytes 36896 | tf_op jit(solution)/shard_map/ppermute | solution.py:112
  73.9 0.0 collective-permute-done.10.rest_1_
  73.9 5.7 %shard_map.111 = (f32[8,256,128]{2,1,0:T(8,128)S(1)}, f32[8,8,128]{2,1,0:T(8,128)}, f32[272,128]{1,0:T(8,128)}, f32[2,256,128]{2,1,0:T(8,128)}, f32[8,272,128]{2...) custom-call(s32[3]{0:T(128)S(1)} %pad_add_fusion.idx, ...), custom_call_target="tpu_custom_call" | custom-call | bytes 1 | tf_op jit(solution)/shard_map/pallas_call | solution.py:25
  79.6 1.6 %collective-permute-start.19 = (f32[256,128]{1,0:T(8,128)S(1)}, f32[256,128]{1,0:T(8,128)S(1)}, u32[]{:S(2)}, u32[]{:S(2)}) collective-permute-start(f32[256,128]{1,0:T(8,128)S(1)} %get-tuple-element.96), channel_id=1, source_target_pairs={{0,1},{1,0},{2,3},{3,2},{4,5},{5,4},{6,7},{7,6},{8,9},{9,8},{10,11... | collective-permute-start | bytes 393224 | tf_op jit(solution)/shard_map/ppermute | solution.py:112
  81.1 2.5 %collective-permute-start.21 = (f32[256,128]{1,0:T(8,128)S(1)}, f32[256,128]{1,0:T(8,128)S(1)}, u32[]{:S(2)}, u32[]{:S(2)}) collective-permute-start(f32[256,128]{1,0:T(8,128)S(1)} %get-tuple-element.97), channel_id=1, source_target_pairs={{0,3},{1,2},{2,1},{3,0},{4,7},{5,6},{6,5},{7,4},{8,11},{9,10},{10,... | collective-permute-start | bytes 393224 | tf_op jit(solution)/shard_map/ppermute | solution.py:112
  83.6 1.0 collective-permute-start.15
  84.5 1.3 %collective-permute-start.17 = (f32[16,128]{1,0:T(8,128)S(1)}, f32[16,128]{1,0:T(8,128)S(1)}, u32[]{:S(2)}, u32[]{:S(2)}) collective-permute-start(f32[16,128]{1,0:T(8,128)S(1)} %get-tuple-element.89), channel_id=1, source_target_pairs={{0,24},{8,16},{16,8},{24,0},{1,25},{9,17},{17,9},{25,1},{2,26},{10... | collective-permute-start | bytes 24584 | tf_op jit(solution)/shard_map/ppermute | solution.py:112
  85.8 1.4 %collective-permute-done.15.rest_0_ = f32[16,128]{1,0:T(8,128)S(1)} collective-permute-done((f32[16,128]{1,0:T(8,128)S(1)}, f32[16,128]{1,0:T(8,128)S(1)}, u32[]{:S(2)}, u32[]{:S(2)}) %collective-permute-start.15) | collective-permute-done | bytes 8224 | tf_op jit(solution)/shard_map/ppermute | solution.py:112
  87.2 0.8 collective-permute-start.16
  88.0 1.1 collective-permute-done.17.rest_2_
  89.1 1.8 %collective-permute-done.16.rest_1_ = f32[16,128]{1,0:T(8,128)S(1)} collective-permute-done((f32[16,128]{1,0:T(8,128)S(1)}, f32[16,128]{1,0:T(8,128)S(1)}, u32[]{:S(2)}, u32[]{:S(2)}) %collective-permute-start.16) | collective-permute-done | bytes 8224 | tf_op jit(solution)/shard_map/ppermute | solution.py:112
  90.9 0.8 shard_map.112
  91.7 0.1 collective-permute-start.18
  91.8 1.2 %collective-permute-done.18.rest_0_ = f32[16,272]{1,0:T(8,128)S(1)} collective-permute-done((f32[16,272]{1,0:T(8,128)S(1)}, f32[16,272]{1,0:T(8,128)S(1)}, u32[]{:S(2)}, u32[]{:S(2)}) %collective-permute-start.18) | collective-permute-done | bytes 17440 | tf_op jit(solution)/shard_map/ppermute | solution.py:112
  93.0 1.8 %shard_map.113 = (f32[272,128]{1,0:T(8,128)}, f32[272,128]{1,0:T(8,128)S(1)}, f32[32,128]{1,0:T(8,128)S(1)}, f32[72,128]{1,0:T(8,128)S(1)}, f32[72,128]{1,0:T(8,128)S(1)}) custom-call(s32[3]{0:T(128)S(1)} %pad_add_fusion.idx, f32[8,272,128]{2,1,0:T(8,128)S(1)} %get-tuple-element.86.t_ref.t_in, f32[272,128]{1,0:T(8,128)S(1)} %get-tuple-element.90.e_ref, ...), custom_call_target="tpu_custom_call" | custom-call | bytes 1 | tf_op jit(solution)/shard_map/pallas_call | solution.py:25
  94.8 1.9 %collective-permute-start.22 = (f32[72,128]{1,0:T(8,128)S(1)}, f32[72,128]{1,0:T(8,128)S(1)}, u32[]{:S(2)}, u32[]{:S(2)}) collective-permute-start(f32[72,128]{1,0:T(8,128)S(1)} %get-tuple-element.98), channel_id=1, source_target_pairs={{0,1},{1,0},{2,3},{3,2},{4,5},{5,4},{6,7},{7,6},{8,9},{9,8},{10,11... | collective-permute-start | bytes 110600 | tf_op jit(solution)/shard_map/ppermute | solution.py:112
  96.8 2.5 %collective-permute-start.24 = (f32[72,128]{1,0:T(8,128)S(1)}, f32[72,128]{1,0:T(8,128)S(1)}, u32[]{:S(2)}, u32[]{:S(2)}) collective-permute-start(f32[72,128]{1,0:T(8,128)S(1)} %get-tuple-element.99), channel_id=1, source_target_pairs={{0,3},{1,2},{2,1},{3,0},{4,7},{5,6},{6,5},{7,4},{8,11},{9,10},{10,... | collective-permute-start | bytes 110600 | tf_op jit(solution)/shard_map/ppermute | solution.py:112
  99.2 2.6 %collective-permute-start.23 = (f32[72,128]{1,0:T(8,128)S(1)}, f32[72,128]{1,0:T(8,128)S(1)}, u32[]{:S(2)}, u32[]{:S(2)}) collective-permute-start(f32[72,128]{1,0:T(8,128)S(1)} %get-tuple-element.99), channel_id=1, source_target_pairs={{0,2},{1,3},{2,0},{3,1},{4,6},{5,7},{6,4},{7,5},{8,10},{9,11},{10,... | collective-permute-start | bytes 110600 | tf_op jit(solution)/shard_map/ppermute | solution.py:112
  101.8 0.7 collective-permute-done.24.rest_5_
  102.5 1.5 %collective-permute-done.23.rest_4_ = f32[72,128]{1,0:T(8,128)S(1)} collective-permute-done((f32[72,128]{1,0:T(8,128)S(1)}, f32[72,128]{1,0:T(8,128)S(1)}, u32[]{:S(2)}, u32[]{:S(2)}) %collective-permute-start.23) | collective-permute-done | bytes 36896 | tf_op jit(solution)/shard_map/ppermute | solution.py:112
  104.1 3.0 %shard_map.114 = (f32[8,256,128]{2,1,0:T(8,128)}, f32[8,256,128]{2,1,0:T(8,128)}) custom-call(s32[3]{0:T(128)S(1)} %pad_add_fusion.idx, f32[8,272,128]{2,1,0:T(8,128)S(1)} %get-tuple-element.86.t_ref.t_in, f32[272,128]{1,0:T(8,128)S(1)} %get-tuple-element.93.l_ref, f32[32,128]{1,0:T(8,128)S(1)} %get-tuple-element.94.b_ref, ...), custom_call_target="tpu_custom_call" | custom-call | bytes 1 | tf_op jit(solution)/shard_map/pallas_call | solution.py:25
  (20 shorter events, 0.1 us)
Async XLA Ops:
  6.2 1.2 %copy-start = (f32[8,256,128]{2,1,0:T(8,128)S(1)}, f32[8,256,128]{2,1,0:T(8,128)}, u32[]{:S(2)}) copy-start(f32[8,256,128]{2,1,0:T(8,128)} %u_ref.3) | copy-start | bytes 3145732
  7.4 1.2 %copy-start.4 = (s32[8,256,128]{2,1,0:T(8,128)S(1)}, s32[8,256,128]{2,1,0:T(8,128)}, u32[]{:S(2)}) copy-start(s32[8,256,128]{2,1,0:T(8,128)} %kind_ref.1) | copy-start | bytes 3145732
  8.6 23.1 %copy-start.1 = (f32[8,256,128]{2,1,0:T(8,128)S(1)}, f32[8,256,128]{2,1,0:T(8,128)}, u32[]{:S(2)}) copy-start(f32[8,256,128]{2,1,0:T(8,128)} %u_ref.3) | copy-start | bytes 3145732
  11.1 20.5 %collective-permute-start.3 = (f32[2,256,128]{2,1,0:T(8,128)}, f32[2,256,128]{2,1,0:T(8,128)S(1)}, u32[]{:S(2)}, u32[]{:S(2)}) collective-permute-start(f32[2,256,128]{2,1,0:T(8,128)} %get-tuple-element.57), channel_id=1, source_target_pairs={{0,1},{1,0},{2,3},{3,2},{4,5},{5,4},{6,7},{7,6},{8,9},{9,8},{10,11... | collective-permute-start | bytes 786440 | tf_op jit(solution)/shard_map/ppermute | solution.py:119
  14.1 17.5 %collective-permute-start.4 = (f32[2,256,128]{2,1,0:T(8,128)}, f32[2,256,128]{2,1,0:T(8,128)S(1)}, u32[]{:S(2)}, u32[]{:S(2)}) collective-permute-start(f32[2,256,128]{2,1,0:T(8,128)} %get-tuple-element.58), channel_id=1, source_target_pairs={{0,3},{1,2},{2,1},{3,0},{4,7},{5,6},{6,5},{7,4},{8,11},{9,10},{10,... | collective-permute-start | bytes 786440 | tf_op jit(solution)/shard_map/ppermute | solution.py:123
  16.6 15.0 %collective-permute-start.2 = (f32[256,128]{1,0:T(8,128)S(1)}, f32[256,128]{1,0:T(8,128)S(1)}, u32[]{:S(2)}, u32[]{:S(2)}) collective-permute-start(f32[256,128]{1,0:T(8,128)S(1)} %get-tuple-element.56), channel_id=1, source_target_pairs={{0,4},{4,0},{1,5},{5,1},{2,6},{6,2},{3,7},{7,3},{8,12},{12,8},{9,1... | collective-permute-start | bytes 393224 | tf_op jit(solution)/shard_map/ppermute | solution.py:119
  17.3 14.3 %all-to-all-start = ((f32[32,1,512]{2,1,0:T(1,128)}), f32[32,1,512]{2,1,0:T(1,128)S(1)}, u32[]{:S(2)}, u32[]{:S(2)}) async-start(f32[32,1,512]{2,1,0:T(1,128)} %copy.12), calls=%async_computation | async-start | bytes 131072 | tf_op jit(solution)/shard_map/all_to_all | solution.py:805
  21.0 10.6 %collective-permute-start = (f32[2,8,128]{2,1,0:T(8,128)S(1)}, f32[2,8,128]{2,1,0:T(8,128)S(1)}, u32[]{:S(2)}, u32[]{:S(2)}) collective-permute-start(f32[2,8,128]{2,1,0:T(8,128)S(1)} %get-tuple-element.54), channel_id=1, source_target_pairs={{0,8},{8,0},{16,24},{24,16},{1,9},{9,1},{17,25},{25,17},{2,10},{10... | collective-permute-start | bytes 24584 | tf_op jit(solution)/shard_map/ppermute | solution.py:119
  22.9 8.8 %collective-permute-start.1 = (f32[2,8,128]{2,1,0:T(8,128)S(1)}, f32[2,8,128]{2,1,0:T(8,128)S(1)}, u32[]{:S(2)}, u32[]{:S(2)}) collective-permute-start(f32[2,8,128]{2,1,0:T(8,128)S(1)} %get-tuple-element.55), channel_id=1, source_target_pairs={{0,24},{8,16},{16,8},{24,0},{1,25},{9,17},{17,9},{25,1},{2,26},{10... | collective-permute-start | bytes 24584 | tf_op jit(solution)/shard_map/ppermute | solution.py:123
  27.5 1.4 %copy-start.2 = (bf16[8,544,256]{2,1,0:T(8,128)(2,1)}, bf16[8,544,256]{2,1,0:T(8,128)(2,1)S(1)}, u32[]{:S(2)}) copy-start(bf16[8,544,256]{2,1,0:T(8,128)(2,1)S(1)} %get-tuple-element.60.gx_ref) | copy-start | bytes 6684676
  31.6 4.8 %copy-start.3 = (bf16[8,544,256]{2,1,0:T(8,128)(2,1)S(1)}, bf16[8,544,256]{2,1,0:T(8,128)(2,1)}, u32[]{:S(2)}) copy-start(bf16[8,544,256]{2,1,0:T(8,128)(2,1)} %copy-done.2) | copy-start | bytes 6684676
  31.7 1.4 %copy-start.5 = (s32[8,256,128]{2,1,0:T(8,128)S(1)}, s32[8,256,128]{2,1,0:T(8,128)}, u32[]{:S(2)}) copy-start(s32[8,256,128]{2,1,0:T(8,128)} %kind_ref.1) | copy-start | bytes 3145732
  50.5 23.4 %collective-permute-start.9 = (f32[256,128]{1,0:T(8,128)S(1)}, f32[256,128]{1,0:T(8,128)S(1)}, u32[]{:S(2)}, u32[]{:S(2)}) collective-permute-start(f32[256,128]{1,0:T(8,128)S(1)} %get-tuple-element.82), channel_id=1, source_target_pairs={{0,1},{1,0},{2,3},{3,2},{4,5},{5,4},{6,7},{7,6},{8,9},{9,8},{10,11... | collective-permute-start | bytes 393224 | tf_op jit(solution)/shard_map/ppermute | solution.py:112
  51.4 22.5 %collective-permute-start.11 = (f32[256,128]{1,0:T(8,128)S(1)}, f32[256,128]{1,0:T(8,128)S(1)}, u32[]{:S(2)}, u32[]{:S(2)}) collective-permute-start(f32[256,128]{1,0:T(8,128)S(1)} %get-tuple-element.83), channel_id=1, source_target_pairs={{0,3},{1,2},{2,1},{3,0},{4,7},{5,6},{6,5},{7,4},{8,11},{9,10},{10,... | collective-permute-start | bytes 393224 | tf_op jit(solution)/shard_map/ppermute | solution.py:112
  53.8 20.1 %collective-permute-start.10 = (f32[256,128]{1,0:T(8,128)S(1)}, f32[256,128]{1,0:T(8,128)S(1)}, u32[]{:S(2)}, u32[]{:S(2)}) collective-permute-start(f32[256,128]{1,0:T(8,128)S(1)} %get-tuple-element.83), channel_id=1, source_target_pairs={{0,2},{1,3},{2,0},{3,1},{4,6},{5,7},{6,4},{7,5},{8,10},{9,11},{10,... | collective-permute-start | bytes 393224 | tf_op jit(solution)/shard_map/ppermute | solution.py:112
  54.0 3.7 %collective-permute-start.5 = (f32[16,128]{1,0:T(8,128)S(1)}, f32[16,128]{1,0:T(8,128)S(1)}, u32[]{:S(2)}, u32[]{:S(2)}) collective-permute-start(f32[16,128]{1,0:T(8,128)S(1)} %get-tuple-element.65), channel_id=1, source_target_pairs={{0,8},{8,0},{16,24},{24,16},{1,9},{9,1},{17,25},{25,17},{2,10},{10... | collective-permute-start | bytes 24584 | tf_op jit(solution)/shard_map/ppermute | solution.py:112
  54.8 4.5 %collective-permute-start.7 = (f32[16,128]{1,0:T(8,128)S(1)}, f32[16,128]{1,0:T(8,128)S(1)}, u32[]{:S(2)}, u32[]{:S(2)}) collective-permute-start(f32[16,128]{1,0:T(8,128)S(1)} %get-tuple-element.66), channel_id=1, source_target_pairs={{0,24},{8,16},{16,8},{24,0},{1,25},{9,17},{17,9},{25,1},{2,26},{10... | collective-permute-start | bytes 24584 | tf_op jit(solution)/shard_map/ppermute | solution.py:112
  57.7 3.7 %collective-permute-start.6 = (f32[16,128]{1,0:T(8,128)S(1)}, f32[16,128]{1,0:T(8,128)S(1)}, u32[]{:S(2)}, u32[]{:S(2)}) collective-permute-start(f32[16,128]{1,0:T(8,128)S(1)} %get-tuple-element.66), channel_id=1, source_target_pairs={{0,16},{8,24},{16,0},{24,8},{1,17},{9,25},{17,1},{25,9},{2,18},{10... | collective-permute-start | bytes 24584 | tf_op jit(solution)/shard_map/ppermute | solution.py:112
  62.2 1.3 %collective-permute-start.8 = (f32[16,272]{1,0:T(8,128)S(1)}, f32[16,272]{1,0:T(8,128)S(1)}, u32[]{:S(2)}, u32[]{:S(2)}) collective-permute-start(f32[16,272]{1,0:T(8,128)S(1)} %get-tuple-element.69), channel_id=1, source_target_pairs={{0,4},{4,0},{1,5},{5,1},{2,6},{6,2},{3,7},{7,3},{8,12},{12,8},{9,1... | collective-permute-start | bytes 52232 | tf_op jit(solution)/shard_map/ppermute | solution.py:112
  64.8 4.2 %collective-permute-start.12 = (f32[72,128]{1,0:T(8,128)S(1)}, f32[72,128]{1,0:T(8,128)S(1)}, u32[]{:S(2)}, u32[]{:S(2)}) collective-permute-start(f32[72,128]{1,0:T(8,128)S(1)} %get-tuple-element.84), channel_id=1, source_target_pairs={{0,1},{1,0},{2,3},{3,2},{4,5},{5,4},{6,7},{7,6},{8,9},{9,8},{10,11... | collective-permute-start | bytes 110600 | tf_op jit(solution)/shard_map/ppermute | solution.py:112
  66.6 5.8 %collective-permute-start.14 = (f32[72,128]{1,0:T(8,128)S(1)}, f32[72,128]{1,0:T(8,128)S(1)}, u32[]{:S(2)}, u32[]{:S(2)}) collective-permute-start(f32[72,128]{1,0:T(8,128)S(1)} %get-tuple-element.85), channel_id=1, source_target_pairs={{0,3},{1,2},{2,1},{3,0},{4,7},{5,6},{6,5},{7,4},{8,11},{9,10},{10,... | collective-permute-start | bytes 110600 | tf_op jit(solution)/shard_map/ppermute | solution.py:112
  69.0 4.9 %collective-permute-start.13 = (f32[72,128]{1,0:T(8,128)S(1)}, f32[72,128]{1,0:T(8,128)S(1)}, u32[]{:S(2)}, u32[]{:S(2)}) collective-permute-start(f32[72,128]{1,0:T(8,128)S(1)} %get-tuple-element.85), channel_id=1, source_target_pairs={{0,2},{1,3},{2,0},{3,1},{4,6},{5,7},{6,4},{7,5},{8,10},{9,11},{10,... | collective-permute-start | bytes 110600 | tf_op jit(solution)/shard_map/ppermute | solution.py:112
  79.6 24.5 %collective-permute-start.19 = (f32[256,128]{1,0:T(8,128)S(1)}, f32[256,128]{1,0:T(8,128)S(1)}, u32[]{:S(2)}, u32[]{:S(2)}) collective-permute-start(f32[256,128]{1,0:T(8,128)S(1)} %get-tuple-element.96), channel_id=1, source_target_pairs={{0,1},{1,0},{2,3},{3,2},{4,5},{5,4},{6,7},{7,6},{8,9},{9,8},{10,11... | collective-permute-start | bytes 393224 | tf_op jit(solution)/shard_map/ppermute | solution.py:112
  81.1 23.0 %collective-permute-start.21 = (f32[256,128]{1,0:T(8,128)S(1)}, f32[256,128]{1,0:T(8,128)S(1)}, u32[]{:S(2)}, u32[]{:S(2)}) collective-permute-start(f32[256,128]{1,0:T(8,128)S(1)} %get-tuple-element.97), channel_id=1, source_target_pairs={{0,3},{1,2},{2,1},{3,0},{4,7},{5,6},{6,5},{7,4},{8,11},{9,10},{10,... | collective-permute-start | bytes 393224 | tf_op jit(solution)/shard_map/ppermute | solution.py:112
  83.6 20.5 %collective-permute-start.20 = (f32[256,128]{1,0:T(8,128)S(1)}, f32[256,128]{1,0:T(8,128)S(1)}, u32[]{:S(2)}, u32[]{:S(2)}) collective-permute-start(f32[256,128]{1,0:T(8,128)S(1)} %get-tuple-element.97), channel_id=1, source_target_pairs={{0,2},{1,3},{2,0},{3,1},{4,6},{5,7},{6,4},{7,5},{8,10},{9,11},{10,... | collective-permute-start | bytes 393224 | tf_op jit(solution)/shard_map/ppermute | solution.py:112
  83.6 3.7 %collective-permute-start.15 = (f32[16,128]{1,0:T(8,128)S(1)}, f32[16,128]{1,0:T(8,128)S(1)}, u32[]{:S(2)}, u32[]{:S(2)}) collective-permute-start(f32[16,128]{1,0:T(8,128)S(1)} %get-tuple-element.88), channel_id=1, source_target_pairs={{0,8},{8,0},{16,24},{24,16},{1,9},{9,1},{17,25},{25,17},{2,10},{10... | collective-permute-start | bytes 24584 | tf_op jit(solution)/shard_map/ppermute | solution.py:112
  84.5 4.5 %collective-permute-start.17 = (f32[16,128]{1,0:T(8,128)S(1)}, f32[16,128]{1,0:T(8,128)S(1)}, u32[]{:S(2)}, u32[]{:S(2)}) collective-permute-start(f32[16,128]{1,0:T(8,128)S(1)} %get-tuple-element.89), channel_id=1, source_target_pairs={{0,24},{8,16},{16,8},{24,0},{1,25},{9,17},{17,9},{25,1},{2,26},{10... | collective-permute-start | bytes 24584 | tf_op jit(solution)/shard_map/ppermute | solution.py:112
  87.2 3.7 %collective-permute-start.16 = (f32[16,128]{1,0:T(8,128)S(1)}, f32[16,128]{1,0:T(8,128)S(1)}, u32[]{:S(2)}, u32[]{:S(2)}) collective-permute-start(f32[16,128]{1,0:T(8,128)S(1)} %get-tuple-element.89), channel_id=1, source_target_pairs={{0,16},{8,24},{16,0},{24,8},{1,17},{9,25},{17,1},{25,9},{2,18},{10... | collective-permute-start | bytes 24584 | tf_op jit(solution)/shard_map/ppermute | solution.py:112
  91.7 1.3 %collective-permute-start.18 = (f32[16,272]{1,0:T(8,128)S(1)}, f32[16,272]{1,0:T(8,128)S(1)}, u32[]{:S(2)}, u32[]{:S(2)}) collective-permute-start(f32[16,272]{1,0:T(8,128)S(1)} %get-tuple-element.92), channel_id=1, source_target_pairs={{0,4},{4,0},{1,5},{5,1},{2,6},{6,2},{3,7},{7,3},{8,12},{12,8},{9,1... | collective-permute-start | bytes 52232 | tf_op jit(solution)/shard_map/ppermute | solution.py:112
  94.8 4.4 %collective-permute-start.22 = (f32[72,128]{1,0:T(8,128)S(1)}, f32[72,128]{1,0:T(8,128)S(1)}, u32[]{:S(2)}, u32[]{:S(2)}) collective-permute-start(f32[72,128]{1,0:T(8,128)S(1)} %get-tuple-element.98), channel_id=1, source_target_pairs={{0,1},{1,0},{2,3},{3,2},{4,5},{5,4},{6,7},{7,6},{8,9},{9,8},{10,11... | collective-permute-start | bytes 110600 | tf_op jit(solution)/shard_map/ppermute | solution.py:112
  96.8 5.8 %collective-permute-start.24 = (f32[72,128]{1,0:T(8,128)S(1)}, f32[72,128]{1,0:T(8,128)S(1)}, u32[]{:S(2)}, u32[]{:S(2)}) collective-permute-start(f32[72,128]{1,0:T(8,128)S(1)} %get-tuple-element.99), channel_id=1, source_target_pairs={{0,3},{1,2},{2,1},{3,0},{4,7},{5,6},{6,5},{7,4},{8,11},{9,10},{10,... | collective-permute-start | bytes 110600 | tf_op jit(solution)/shard_map/ppermute | solution.py:112
  99.2 4.9 %collective-permute-start.23 = (f32[72,128]{1,0:T(8,128)S(1)}, f32[72,128]{1,0:T(8,128)S(1)}, u32[]{:S(2)}, u32[]{:S(2)}) collective-permute-start(f32[72,128]{1,0:T(8,128)S(1)} %get-tuple-element.99), channel_id=1, source_target_pairs={{0,2},{1,3},{2,0},{3,1},{4,6},{5,7},{6,4},{7,5},{8,10},{9,11},{10,... | collective-permute-start | bytes 110600 | tf_op jit(solution)/shard_map/ppermute | solution.py:112

commit v3 on v2

--- a/solution.py
+++ b/solution.py
@@ -19,14 +19,16 @@
 EXACT = lax.Precision.HIGHEST
 
 
-def call(kernel, out_shapes, args, smem=0, scratch=(), vmem=24):
+def call(kernel, out_shapes, args, smem=0, scratch=(), vmem=24, far=0, far_out=False):
     specs = [pl.BlockSpec(memory_space=pltpu.SMEM)] * smem
-    specs += [pl.BlockSpec(memory_space=pltpu.VMEM)] * (len(args) - smem)
+    specs += [pl.BlockSpec(memory_space=pltpu.VMEM)] * (len(args) - smem - far)
+    specs += [pl.BlockSpec(memory_space=pl.ANY)] * far
     return pl.pallas_call(
         kernel,
         out_shape=out_shapes,
         in_specs=specs,
-        out_specs=[pl.BlockSpec(memory_space=pltpu.VMEM)] * len(out_shapes),
+        out_specs=[pl.BlockSpec(memory_space=pl.ANY if far_out else pltpu.VMEM)]
+        * len(out_shapes),
         scratch_shapes=list(scratch),
         compiler_params=pltpu.CompilerParams(vmem_limit_bytes=vmem * 2**20),
         cost_estimate=pl.CostEstimate(flops=0, bytes_accessed=1, transcendentals=0),
@@ -44,6 +46,26 @@
 
 def iota(shape, dim):
     return lax.broadcasted_iota(jnp.int32, shape, dim)
+
+
+def copies(pairs, sems):
+    return [
+        pltpu.make_async_copy(src, dst, sems.at[k]) for k, (src, dst) in enumerate(pairs)
+    ]
+
+
+def plane_copies(pairs, sems):
+    started = [
+        [
+            pltpu.make_async_copy(src.at[z], dst.at[z], sems.at[k, z])
+            for z in range(dst.shape[0])
+        ]
+        for k, (src, dst) in enumerate(pairs)
+    ]
+    for copies_of_plane in zip(*started):
+        for copy in copies_of_plane:
+            copy.start()
+    return started
 
 
 def mm(a, b):
@@ -114,32 +136,39 @@
     ]
 
 
+def crossed(array, k, axis):
+    return lax.ppermute(array, axis, [(i, i ^ k) for i in range(lax.axis_size(axis))])
+
+
 def next_pairs(even, odd, axis):
     n = lax.axis_size(axis)
     first = lax.ppermute(even, axis, [(i, i ^ 1) for i in range(n)])
     if n == 2:
         return first, first
-    other = {i: (i + 1) % n if i % 2 else (i - 1) % n for i in range(n)}
-    return first, lax.ppermute(odd, axis, list(other.items()))
-
-
-def conductance(z, idx, scalars, kind_ref, n_planes):
+    pairs = [(i, i + 1) for i in range(1, n - 1, 2)]
+    return first, lax.ppermute(odd, axis, pairs + [(b, a) for a, b in pairs])
+
+
+def conductance(z, idx, sheet, table, scaling, kind_ref):
     factor = jnp.zeros(kind_ref.shape[1:], F32)
-    for category in range(scalars.shape[0] - n_planes):
-        factor = jnp.where(kind_ref[z] == category, scalars[n_planes + category], factor)
-    return scalars[idx[2] * kind_ref.shape[0] + z] * factor
+    for category in range(scaling.shape[0]):
+        factor = jnp.where(kind_ref[z] == category, scaling[category], factor)
+    return table[sheet[idx[2] * kind_ref.shape[0] + z]] * factor
 
 
 def faces_kernel(
-    n_planes, idx, scalars, u_ref, kind_ref, xs0, xs1, ys0, ys1, zs0, zs1
+    idx, sheet, table, scaling, u_in, kind_in, xs0, xs1, ys0, ys1, zs0, zs1, u_ref, kind_ref, sems
 ):
     planes, rows, columns = u_ref.shape
+    started = plane_copies([(u_in, u_ref), (kind_in, kind_ref)], sems)
     even = [idx[d] % 2 == 0 for d in range(3)]
     lane = iota((rows, columns), 1)
     low = jnp.zeros((rows, columns), F32)
     high = jnp.zeros((rows, columns), F32)
     for z in range(planes):
-        u, c = u_ref[z], conductance(z, idx, scalars, kind_ref, n_planes)
+        started[0][z].wait()
+        started[1][z].wait()
+        u, c = u_ref[z], conductance(z, idx, sheet, table, scaling, kind_ref)
         if z == 0:
             zs0[1], zs1[1] = c, c
         elif z == planes - 1:
@@ -158,74 +187,160 @@
     zs1[0] = jnp.where(even[2], u_ref[0], u_ref[planes - 1])
 
 
-def dispatch_kernel(blocks, capacity, segments, send, a_scr, b_scr, o_scr):
-    _, chunks, lanes = segments.shape
-    power, tile, cell = segments[0], segments[1].astype(jnp.int32), segments[2].astype(jnp.int32)
-    block_row = iota((blocks, lanes), 0)
-    for c in range(chunks):
-        hit = block_row == tile[c : c + 1, :]
-        o_scr[c * blocks : (c + 1) * blocks, :] = jnp.where(hit, 1.0, 0.0).astype(BF16)
+def shares(capacity):
+    return capacity // 4, capacity - capacity // 4
+
+
+def dispatch_kernel(blocks, planes, area, capacity, amps_in, ohms_in, tile_in, cell_in,
+                    send, amps, ohms, tiles, cells, a_scr, b_scr, z_scr, k_scr, sems):
+    started = copies(
+        [(amps_in, amps), (ohms_in, ohms), (tile_in, tiles), (cell_in, cells)], sems
+    )
+    for copy in started:
+        copy.start()
+    for copy in started:
+        copy.wait()
+    chunks, lanes = amps.shape
+    share, spare = shares(capacity)
+    keys, main = blocks * planes, planes * share
+    power = amps[...] * amps[...] * ohms[...]
+    tile, cell = tiles[...], cells[...]
+    plane, within = cell // area, cell % area
+    key = tile * planes + plane
+    p_high, p_low = split(power)
+    pieces = [
+        p_high.astype(F32),
+        p_low.astype(F32),
+        (within >> 8).astype(F32),
+        (within & 255).astype(F32),
+        plane.astype(F32),
+    ]
+    key_row, block_row = iota((keys, lanes), 0), iota((blocks, lanes), 0)
+    place = iota((main, lanes), 0)
     ahead = jnp.where(iota((lanes, lanes), 0) < iota((lanes, lanes), 1), 1.0, 0.0)
     both = jnp.concatenate([ahead, jnp.ones((lanes, lanes), F32)], axis=1).astype(BF16)
-    counted = mm(o_scr[...], both)
-    base = jnp.zeros((blocks, lanes), F32)
-    ranks = iota((capacity, lanes), 0)
-    p_high, p_mid = split(power)
-    p_low = (power - p_high.astype(F32) - p_mid.astype(F32))
-    pieces = [
-        p_high.astype(F32),
-        p_mid.astype(F32),
-        p_low,
-        (cell >> 16).astype(F32),
-        ((cell >> 8) & 255).astype(F32),
-        (cell & 255).astype(F32),
-    ]
+    base = jnp.zeros((keys, lanes), F32)
     for c in range(chunks):
-        part = slice(c * blocks, (c + 1) * blocks)
-        cols = slice(c * lanes, (c + 1) * lanes)
-        hit = block_row == tile[c : c + 1, :]
-        order = jnp.where(hit, counted[part, :lanes] + base, 0.0)
-        base = base + counted[part, lanes:]
-        rank = jnp.sum(order, axis=0, keepdims=True).astype(jnp.int32)
-        b_scr[:, cols] = jnp.where(ranks == rank, 1.0, 0.0).astype(BF16)
+        row, cols = slice(c, c + 1), slice(c * lanes, (c + 1) * lanes)
+        hit = key_row == key[row, :]
+        counted = mm(jnp.where(hit, 1.0, 0.0).astype(BF16), both)
+        rank = jnp.sum(jnp.where(hit, counted[:, :lanes] + base, 0.0), axis=0, keepdims=True)
+        base = base + counted[:, lanes:]
+        rank = rank.astype(jnp.int32)
+        k_scr[row, :] = rank
+        slot = jnp.where(rank < share, plane[row, :] * share + rank, -1)
+        b_scr[:main, cols] = jnp.where(place == slot, 1.0, 0.0).astype(BF16)
+        hit = block_row == tile[row, :]
         for k, piece in enumerate(pieces):
             a_scr[k * blocks : (k + 1) * blocks, cols] = jnp.where(
-                hit, piece[c : c + 1, :], 0.0
+                hit, piece[row, :], 0.0
             ).astype(BF16)
-    out = mm_nt(a_scr[...], b_scr[...])
-    r = [out[k * blocks : (k + 1) * blocks] for k in range(6)]
-    send[...] = jnp.concatenate(
-        [r[0] + r[1] + r[2], r[3] * 65536.0 + r[4] * 256.0 + r[5]], axis=1
-    )
+    out = mm_nt(a_scr[: 4 * blocks, :], b_scr[:main, :])
+    r = [out[k * blocks : (k + 1) * blocks] for k in range(4)]
+    total = main + spare
+    send[:, 0, :main] = r[0] + r[1]
+    send[:, 0, total : total + main] = r[2] * 256.0 + r[3]
+    send[:, 0, main:total] = jnp.zeros((blocks, spare), F32)
+    send[:, 0, total + main :] = jnp.zeros((blocks, spare), F32)
+    z_scr[...] = jnp.maximum(base - float(share), 0.0)
+
+    @pl.when(jnp.max(z_scr[...]) > 0.0)
+    def _():
+        step = min(keys, 256)
+        r, n = iota((step, step), 0), iota((step, step), 1)
+        earlier = jnp.where((r // planes == n // planes) & (n < r), 1.0, 0.0).astype(BF16)
+        for at in range(0, keys, step):
+            part = slice(at, at + step)
+            z_scr[part, :] = mm(earlier, z_scr[part, :].astype(BF16))
+        place = iota((spare, lanes), 0)
+        for c in range(chunks):
+            row, cols = slice(c, c + 1), slice(c * lanes, (c + 1) * lanes)
+            hit = key_row == key[row, :]
+            first = jnp.sum(jnp.where(hit, z_scr[...], 0.0), axis=0, keepdims=True)
+            rank = k_scr[row, :]
+            slot = jnp.where(rank < share, -1, rank - share + first.astype(jnp.int32))
+            b_scr[:spare, cols] = jnp.where(place == slot, 1.0, 0.0).astype(BF16)
+        out = mm_nt(a_scr[...], b_scr[:spare, :])
+        r = [out[k * blocks : (k + 1) * blocks] for k in range(5)]
+        send[:, 0, main:total] = r[0] + r[1]
+        send[:, 0, total + main :] = r[2] * 256.0 + r[3] + r[4] * float(area)
 
 
 def joule_into(got, joule, r_scr, k_scr):
     planes, rows, columns = joule.shape
-    sources, capacity = got.shape[0], got.shape[1] // 2
-    column = iota((columns, capacity), 0)
-    for s in range(sources):
-        power = got[s : s + 1, :capacity]
-        cell = got[s : s + 1, capacity:].astype(jnp.int32)
-        part = slice(s * capacity, (s + 1) * capacity)
+    sources, total = got.shape[0], got.shape[1] // 2
+    spare = r_scr.shape[1] // sources
+    main = total - spare
+    share = main // planes
+    lanes = 128
+    per = lanes // share
+    each = sources // per
+    lane = iota((each, lanes), 1) // share
+    row = iota((rows, lanes), 0).astype(F32).astype(BF16)
+    column = iota((columns, lanes), 0).astype(F32).astype(BF16)
+    one, none = jnp.ones((rows, lanes), BF16), jnp.zeros((rows, lanes), BF16)
+    blank = jnp.zeros((columns, lanes), BF16)
+
+    def gathered(values, h):
+        out = values[:each]
+        for g in range(per):
+            part = values[g * each : (g + 1) * each]
+            by = (g - h) * share % lanes
+            part = pltpu.roll(part, by, 1) if by else part
+            out = part if g == 0 else jnp.where(lane == g, part, out)
+        return out
+
+    for z in range(planes):
+        at = z * share // lanes * lanes
+        power = gathered(got[:, at : at + lanes], z % per)
+        cell = gathered(got[:, total + at : total + at + lanes], z % per).astype(jnp.int32)
         high, low = split(power)
-        hit = column == cell % columns
-        r_scr[:columns, part] = jnp.where(hit, high.astype(F32), 0.0).astype(BF16)
-        r_scr[columns:, part] = jnp.where(hit, low.astype(F32), 0.0).astype(BF16)
-        k_scr[:, part] = jnp.broadcast_to(cell // columns, (8, capacity))
-    total = sources * capacity
-    step = min(total, 2048)
-    row = iota((rows, step), 0)
-
-    def plane(z, carry):
-        sums = jnp.zeros((rows, 2 * columns), F32)
-        for at in range(0, total, step):
-            hit = row == k_scr[0:1, at : at + step] - z * rows
-            onehot = jnp.where(hit, 1.0, 0.0).astype(BF16)
-            sums = sums + mm_nt(onehot, r_scr[:, at : at + step])
+        high, low = high.astype(F32), low.astype(F32)
+        x = (cell // columns).astype(F32)
+        y = (cell % columns).astype(F32)
+        lefts, rights = [], []
+        for s in range(each):
+            part = slice(s, s + 1)
+            lefts.append(jnp.where(row == x[part, :].astype(BF16), one, none))
+            hit = column == y[part, :].astype(BF16)
+            rights.append(
+                jnp.concatenate(
+                    [
+                        jnp.where(hit, high[part, :].astype(BF16), blank),
+                        jnp.where(hit, low[part, :].astype(BF16), blank),
+                    ],
+                    axis=0,
+                )
+            )
+        sums = mm_nt(jnp.concatenate(lefts, axis=1), jnp.concatenate(rights, axis=1))
         joule[z] = sums[:, :columns] + sums[:, columns:]
-        return carry
-
-    lax.fori_loop(0, planes, plane, 0)
+
+    @pl.when(jnp.max(got[:, main:total]) > 0.0)
+    def _():
+        column = iota((columns, spare), 0)
+        for s in range(sources):
+            power = got[s : s + 1, main:total]
+            cell = got[s : s + 1, total + main :].astype(jnp.int32)
+            part = slice(s * spare, (s + 1) * spare)
+            high, low = split(power)
+            hit = column == cell % columns
+            r_scr[:columns, part] = jnp.where(hit, high.astype(F32), 0.0).astype(BF16)
+            r_scr[columns:, part] = jnp.where(hit, low.astype(F32), 0.0).astype(BF16)
+            k_scr[:, part] = jnp.broadcast_to(cell // columns, (8, spare))
+        width = sources * spare
+        step = 2048 if width % 2048 == 0 else width
+        row = iota((rows, step), 0)
+
+        def plane(z, carry):
+            sums = jnp.zeros((rows, 2 * columns), F32)
+            for at in range(0, width, step):
+                hit = row == k_scr[0:1, at : at + step] - z * rows
+                onehot = jnp.where(hit, 1.0, 0.0).astype(BF16)
+                sums = sums + mm_nt(onehot, r_scr[:, at : at + step])
+            joule[z] += sums[:, :columns] + sums[:, columns:]
+            return carry
+
+        lax.fori_loop(0, planes, plane, 0)
 
 
 def line_parts(position, theta, start, cells):
@@ -244,7 +359,7 @@
 
 
 def prep_kernel(
-    sizes, idx, scalars, gx_ref, gy_ref, co, z_scr,
+    sizes, idx, sheet, table, gx_out, gy_out, co_out, gx_ref, gy_ref, co, z_scr, sems,
 ):
     planes, rows, columns, nx, ny, nz = sizes
     lanes = 128
@@ -262,7 +377,7 @@
     def rows_of(first):
         value = jnp.ones((planes, lanes), F32)
         for z in range(planes):
-            one = scalars[first + z]
+            one = table[sheet[first + z]]
             value = jnp.where(iota((planes, lanes), 0) == z, one, value)
         return value
 
@@ -271,7 +386,7 @@
     by_lane = jnp.ones((8, lanes), F32)
     own = []
     for z in range(planes):
-        value = scalars[gz * planes + z]
+        value = table[sheet[gz * planes + z]]
         own.append(value)
         by_lane = jnp.where(lane_z == z, value, by_lane)
     theta_lane, scale_lane = line(by_lane, yn)
@@ -320,6 +435,7 @@
     at_or_past = index_w >= iota((extent, rows), 1)
     lane = iota((extent, lanes), 1)
     packed = jnp.zeros((extent, lanes), F32)
+    started = []
     y_col = iota((columns, columns), 0).astype(F32)
     y_i, y_j = iota((columns, columns), 0), iota((columns, columns), 1)
     y_past = y_j >= y_i
@@ -351,10 +467,15 @@
             ext = jnp.where(y_j == e * planes + z, values, ext)
         gy_ref[z, :, :lanes], gy_ref[planes + z, :, :lanes] = split(g)
         gy_ref[z, :, lanes:], gy_ref[planes + z, :, lanes:] = split(ext)
+        for k, (src, dst, at) in enumerate(
+            ((gx_ref, gx_out, z), (gy_ref, gy_out, z), (gy_ref, gy_out, planes + z))
+        ):
+            started.append(pltpu.make_async_copy(src.at[at], dst.at[at], sems.at[3 * z + k]))
+            started[-1].start()
     lx[0] = packed
 
     total = planes * nz
-    cond = [jnp.full((8, lanes), scalars[z], F32) for z in range(total)]
+    cond = [jnp.full((8, lanes), table[sheet[z]], F32) for z in range(total)]
     lead = [HEAT_SPREADING * STIFF * 0.5 * (cond[z] + cond[z + 1]) for z in range(total - 1)]
     lower = [jnp.ones((8, lanes), F32)]
     flux = HEAT_SPREADING * STIFF * cond[0]
@@ -410,11 +531,15 @@
         high_lane,
         jnp.where((row8 >= 2) & (row8 < 4) & (lane_e == row8 - 2), low_lane, 0.0),
     )
-
-
-def slope_kernel(
-    counts, n_planes, idx, scalars, u_ref, kind_ref, xr0, xr1, yr0, yr1, zr0, zr1,
-    d_ref, ux, uy, uz, kx0, kx1, ky0, ky1, kz,
+    started.append(pltpu.make_async_copy(co, co_out, sems.at[3 * planes]))
+    started[-1].start()
+    for copy in started:
+        copy.wait()
+
+
+def slopes(
+    counts, idx, sheet, table, scaling, u_ref, kind_ref, xr0, xr1, yr0, yr1, zr0, zr1,
+    ux, uy, uz, kx0, kx1, ky0, ky1, kz,
 ):
     planes, rows, columns = u_ref.shape
     even = [idx[d] % 2 == 0 for d in range(3)]
@@ -445,7 +570,7 @@
     y_low, y_high = ends(yr0[...], yr1[...], 1)
     c_before = None
     for z in range(planes):
-        c = conductance(z, idx, scalars, kind_ref, n_planes)
+        c = conductance(z, idx, sheet, table, scaling, kind_ref)
         first = jnp.where(at_low[0], -c[0:1, :], x_low[z : z + 1, :])
         final = jnp.where(at_high[0], -c[rows - 1 :, :], x_high[z : z + 1, :])
         kx0[z] = half * (c + jnp.where(row == 0, first, pltpu.roll(c, 1, 0)))
@@ -461,8 +586,6 @@
         c_before = c
         if z == planes - 1:
             kz[planes] = half * jnp.where(at_high[2], 0.0, c + z_high)
-    for z in range(planes):
-        d_ref[z] = outflow(z, u_ref, ux, uy, uz, kx0, kx1, ky0, ky1, kz)
 
 
 def outflow(z, u_ref, ux, uy, uz, kx0, kx1, ky0, ky1, kz):
@@ -485,7 +608,7 @@
     return total + kz[z] * (below - u) + kz[z + 1] * (above - u)
 
 
-def advance(idx, source_of, gx_ref, gy_ref, phz, psz, t_ref, e_ref, x_sends, z_sends):
+def advance(idx, source_of, gx_ref, gy_ref, phz, psz, t_ref, e_ref, z_send, x_sends):
     planes, extent, columns = t_ref.shape
     rows = extent - EXTRA
     sums = jnp.zeros((extent, 128), F32)
@@ -512,28 +635,42 @@
         send[planes:, :] = jnp.broadcast_to(
             jnp.where(take == 0, pair[0:1], pair[1:2]), (8, 128)
         )
-    for b, send in enumerate(z_sends):
-        send[...] = jnp.where((idx[2] >> b) % 2 == 0, below, above)
-
-
-def start_kernel(sizes, n_sends, idx, got, d_ref, u_ref, gx_ref, gy_ref, co,
+    z_send[0], z_send[1] = below, above
+
+
+def start_kernel(sizes, idx, sheet, table, scaling, u_ref, kind_ref,
+                 xr0, xr1, yr0, yr1, zr0, zr1, got_in, gx_in, gy_in, co_in, ux, uy, uz, kx0, kx1, ky0, ky1, kz,
                  joule, t_ref, e_ref, *rest):
+    sends, (r_scr, k_scr, gx_ref, gy_ref, co, got, sems) = rest[:-7], rest[-7:]
+    started = copies(
+        [(got_in.at[:, 0, :], got), (gx_in, gx_ref), (gy_in, gy_ref), (co_in, co)], sems
+    )
+    for copy in started:
+        copy.start()
     phz, psz = groups_of(sizes, co, "phz", "psz")
-    sends, (r_scr, k_scr) = rest[:-2], rest[-2:]
+    slopes(
+        sizes[3:], idx, sheet, table, scaling, u_ref, kind_ref, xr0, xr1, yr0, yr1, zr0, zr1,
+        ux, uy, uz, kx0, kx1, ky0, ky1, kz,
+    )
+    started[0].wait()
     joule_into(got, joule, r_scr, k_scr)
+    for copy in started[1:]:
+        copy.wait()
 
     def source_of(z):
-        return d_ref[z] + OHMIC_POWER * ((1.0 + WARMING_SLOPE * u_ref[z]) * joule[z])
+        out = outflow(z, u_ref, ux, uy, uz, kx0, kx1, ky0, ky1, kz)
+        return out + OHMIC_POWER * ((1.0 + WARMING_SLOPE * u_ref[z]) * joule[z])
 
     advance(
-        idx, source_of, gx_ref, gy_ref, phz, psz, t_ref, e_ref,
-        sends[: n_sends], sends[n_sends:],
-    )
-
-
-def x_kernel(sizes, idx, e_ref, co, *rest):
-    gots, (e_out, f_out, send) = rest[:-3], rest[-3:]
+        idx, source_of, gx_ref, gy_ref, phz, psz, t_ref, e_ref, sends[0], sends[1:]
+    )
+
+
+def x_kernel(sizes, idx, e_ref, co, pair, near, *rest):
     planes, nx = sizes[0], sizes[3]
+    gots, (e_out, f_out, send), far = rest[: nx - 1], rest[nx - 1 : nx + 2], rest[nx + 2 :]
+    for out in far:
+        out[...] = jnp.where((idx[2] >> 1) % 2 == 0, pair[0] + near[0], pair[1] + near[1])
     dx, dxl, lx = groups_of(sizes, co, "dx", "dxl", "lx")
     me = idx[0]
     sums = [[jnp.zeros((planes, 128), F32), jnp.zeros((8, 128), F32)] for _ in range(2)]
@@ -628,20 +765,20 @@
 def carried(nz, idx, bigs, smalls, ax, by, rows, ghosts):
     me = idx[2]
     planes = by.each // 2
-    below = above = None
+    at_top = me % 2 == 1
+    below = jnp.where(at_top, bigs[0][0], 0.0)
+    above = jnp.where(at_top, 0.0, bigs[0][1])
+    for b, big in enumerate(bigs[1:], 1):
+        at_top = (me >> b) % 2 == 1
+        below += jnp.where(at_top, big[...], 0.0)
+        above += jnp.where(at_top, 0.0, big[...])
     g_below = g_above = edges = 0.0
     lefts, rights = [], []
     sub = iota((8, rows), 0)
-    for k, big, small in zip(range(1, nz), bigs, smalls):
+    for k, small in zip(range(1, nz), smalls):
         other = partner(me, k, nz)
         lower = other < me
 
-        def add(total, value, keep):
-            value = jnp.where(keep, value, 0.0)
-            return value if total is None else total + value
-
-        below = add(below, big[...], lower)
-        above = add(above, big[...], jnp.logical_not(lower))
         at, stride = 8 + 2 * planes, 8 + 2 * planes
         parts = [at + p * stride for p in range(rows // 128)]
         across = jnp.concatenate([small[p + 8 : p + stride, :] for p in parts], axis=1)
@@ -694,11 +831,12 @@
         emit(planes, psz[planes + 1][0:1, :] * head + phz[planes + 1][0:1, :] * above)
 
 
-def rise_kernel(sizes, n_sends, idx, t_in, l_ref, b_ref, q_ref, co,
+def rise_kernel(sizes, idx, t_in, l_ref, b_ref, q_ref, co,
                 u_ref, ux, uy, uz, kx0, kx1, ky0, ky1, kz, joule, gx_ref, gy_ref, *rest):
     nz = sizes[5]
     phz, psz, mz, wz, ax, by = groups_of(sizes, co, "phz", "psz", "mz", "wz", "ax", "by")
-    bigs, smalls, rest = rest[: nz - 1], rest[nz - 1 : 2 * nz - 2], rest[2 * nz - 2 :]
+    deep = (nz - 1).bit_length()
+    bigs, smalls, rest = rest[:deep], rest[deep : deep + nz - 1], rest[deep + nz - 1 :]
     u_out, ux_out, uy_out, uz_out, t_ref, e_ref = rest[:6]
     sends, second = rest[6:-1], rest[-1]
     planes, rows, columns = u_ref.shape
@@ -729,15 +867,15 @@
         return out + OHMIC_POWER * ((1.0 + WARMING_SLOPE * u_out[z]) * joule[z])
 
     advance(
-        idx, source_of, gx_ref, gy_ref, phz, psz, t_ref, e_ref,
-        sends[:n_sends], sends[n_sends:],
+        idx, source_of, gx_ref, gy_ref, phz, psz, t_ref, e_ref, sends[0], sends[1:]
     )
 
 
 def finish_kernel(sizes, idx, t_in, l_ref, b_ref, co, u_ref, joule, *rest):
     nz = sizes[5]
     phz, psz, ax, by = groups_of(sizes, co, "phz", "psz", "ax", "by")
-    bigs, smalls, rest = rest[: nz - 1], rest[nz - 1 : 2 * nz - 2], rest[2 * nz - 2 :]
+    deep = (nz - 1).bit_length()
+    bigs, smalls, rest = rest[:deep], rest[deep : deep + nz - 1], rest[deep + nz - 1 :]
     u_out, heat_out, second = rest
     rows = u_ref.shape[1]
     whole_planes(t_in, l_ref, b_ref, second, rows)
@@ -770,95 +908,108 @@
     extent = rows + EXTRA
     idx = jnp.stack([lax.axis_index(axis) for axis in ("gx", "gy", "gz")]).astype(jnp.int32)
     block = shaped(planes, rows, columns)
-    n_planes = sheet_stratum_number.shape[0]
-    layers = jnp.arange(stratum_heat_conduction.shape[0], dtype=jnp.int32)
-    matches = sheet_stratum_number[:, None] == layers[None, :]
-    scalars = jnp.concatenate(
-        [
-            jnp.sum(jnp.where(matches, stratum_heat_conduction[None, :], 0.0), axis=1),
-            substance_kind_scaling,
-        ]
-    )
+    tables = sheet_stratum_number, stratum_heat_conduction, substance_kind_scaling
 
     count = wire_piece_amperes.shape[0]
     capacity = 2 * count // devices
     lanes = 128
     chunks = count // lanes
-    segments = jnp.stack(
-        [
-            wire_piece_amperes * wire_piece_amperes * wire_piece_ohms_base,
-            wire_piece_tile[:, 0].astype(F32),
-            wire_piece_voxel.astype(F32),
-        ]
-    ).reshape(3, chunks, lanes)
+    segments = tuple(
+        part.reshape(chunks, lanes)
+        for part in (
+            wire_piece_amperes, wire_piece_ohms_base, wire_piece_tile, wire_piece_voxel
+        )
+    )
+    share, spare = shares(capacity)
+    slots = planes * share + spare
     (send,) = call(
-        functools.partial(dispatch_kernel, devices, capacity),
-        [shaped(devices, 2 * capacity)],
-        (segments,),
-        scratch=[
-            pltpu.VMEM((6 * devices, count), BF16),
-            pltpu.VMEM((capacity, count), BF16),
-            pltpu.VMEM((chunks * devices, lanes), BF16),
+        functools.partial(dispatch_kernel, devices, planes, rows * columns, capacity),
+        [shaped(devices, 1, 2 * slots)],
+        segments,
+        far=4,
+        vmem=60,
+        scratch=[pltpu.VMEM((chunks, lanes), part.dtype) for part in segments]
+        + [
+            pltpu.VMEM((5 * devices, count), BF16),
+            pltpu.VMEM((max(planes * share, spare), count), BF16),
+            pltpu.VMEM((devices * planes, lanes), F32),
+            pltpu.VMEM((chunks, lanes), jnp.int32),
+            pltpu.SemaphoreType.DMA((4,)),
         ],
     )
-    warmth, kinds, send = lax.optimization_barrier((starting_warmth, substance_kind, send))
     got = lax.all_to_all(send, ("gx", "gy", "gz"), split_axis=0, concat_axis=0, tiled=True)
 
     xs0, xs1, ys0, ys1, zs0, zs1 = call(
-        functools.partial(faces_kernel, n_planes),
+        faces_kernel,
         [shaped(2, planes, columns)] * 2
         + [shaped(rows, 128)] * 2
         + [shaped(2, rows, columns)] * 2,
-        (idx, scalars, warmth, kinds),
-        smem=2,
+        (idx, *tables, starting_warmth, substance_kind),
+        smem=4,
+        far=2,
+        vmem=60,
+        scratch=[
+            pltpu.VMEM(block.shape, F32),
+            pltpu.VMEM(block.shape, jnp.int32),
+            pltpu.SemaphoreType.DMA((2, planes)),
+        ],
     )
     zr = next_pairs(zs0, zs1, "gz")
     xr = next_pairs(xs0, xs1, "gx")
     yr = next_pairs(ys0, ys1, "gy")
     sizes = (planes, rows, columns, nx, ny, nz)
+    coefficients = [
+        shaped(planes, 2 * extent, rows, dtype=BF16),
+        shaped(2 * planes, columns, 256, dtype=BF16),
+        shaped(table_rows(*sizes)[1], lanes),
+    ]
+    room = [pltpu.VMEM(o.shape, o.dtype) for o in coefficients]
     gx_m, gy_m, co = call(
         functools.partial(prep_kernel, sizes),
-        [
-            shaped(planes, 2 * extent, rows, dtype=BF16),
-            shaped(2 * planes, columns, 256, dtype=BF16),
-            shaped(table_rows(*sizes)[1], lanes),
+        coefficients,
+        (idx, *tables[:2]),
+        smem=3,
+        vmem=60,
+        scratch=room
+        + [
+            pltpu.VMEM((2 * planes * nz + 4, 8, lanes), F32),
+            pltpu.SemaphoreType.DMA((3 * planes + 1,)),
         ],
-        (idx, scalars),
-        smem=2,
-        scratch=[pltpu.VMEM((2 * planes * nz + 4, 8, lanes), F32)],
-    )
-    d0, ux, uy, uz, *conduct = call(
-        functools.partial(slope_kernel, counts, n_planes),
-        [block, shaped(planes, 8, columns), shaped(extent, 128), shaped(2, rows, columns)]
-        + [block] * 4
-        + [shaped(planes + 1, rows, columns)],
-        (idx, scalars, warmth, kinds, *xr, *yr, *zr),
-        smem=2,
+        far_out=True,
     )
     step_out = [shaped(planes, extent, columns), shaped(extent, 128)]
-    step_out += [shaped(planes + 8, columns)] * bits[0] + [shaped(rows, columns)] * bits[2]
-    total = devices * capacity
-    joule, t, e, *sends = call(
-        functools.partial(start_kernel, sizes, bits[0]),
-        [block] + step_out,
-        (idx, got, d0, warmth, gx_m, gy_m, co),
-        smem=1,
+    step_out += [shaped(2, rows, columns)] + [shaped(planes + 8, columns)] * bits[0]
+    total = devices * spare
+    ghosts = [shaped(planes, 8, columns), shaped(extent, 128), shaped(2, rows, columns)]
+    ux, uy, uz, *rest = call(
+        functools.partial(start_kernel, sizes),
+        ghosts + [block] * 4 + [shaped(planes + 1, rows, columns), block] + step_out,
+        (idx, *tables, starting_warmth, substance_kind, *xr, *yr, *zr, got, gx_m, gy_m, co),
+        smem=4,
+        far=4,
         scratch=[
             pltpu.VMEM((2 * columns, total), BF16),
             pltpu.VMEM((8, total), jnp.int32),
+            *room,
+            pltpu.VMEM((devices, 2 * slots), F32),
+            pltpu.SemaphoreType.DMA((4,)),
         ],
     )
-    u = warmth
+    conduct, (joule, t, e, *sends) = rest[:5], rest[5:]
+    u = starting_warmth
     small = shaped(8 + 2 * planes + (8 + 2 * planes) * (rows // 128), 128)
     for repeat in range(STEPS):
-        gots = all_pairs(sends[: bits[0]], "gx")
-        bigs = all_pairs(sends[bits[0] :], "gz")
-        e, f, send = call(
+        pair, *sends = sends
+        gots = all_pairs(sends, "gx")
+        near = crossed(pair, 1, "gz")
+        e, f, send, *far = call(
             functools.partial(x_kernel, sizes),
-            [shaped(extent, 128), shaped(2 * planes, columns), shaped(2 * planes, extent)],
-            (idx, e, co, *gots),
+            [shaped(extent, 128), shaped(2 * planes, columns), shaped(2 * planes, extent)]
+            + [shaped(rows, columns)] * (bits[2] - 1),
+            (idx, e, co, pair, near, *gots),
             smem=1,
         )
+        bigs = [near] + [crossed(array, 2, "gz") for array in far]
         gots = all_pairs([send] * bits[1], "gy")
         q, left, right, *sends = call(
             functools.partial(y_kernel, sizes),
@@ -869,7 +1020,7 @@
         smalls = all_pairs(sends, "gz")
         if repeat < STEPS - 1:
             u, ux, uy, uz, t, e, *sends = call(
-                functools.partial(rise_kernel, sizes, bits[0]),
+                functools.partial(rise_kernel, sizes),
                 [block, shaped(planes, 8, columns), shaped(extent, 128)]
                 + [shaped(2, rows, columns)]
                 + step_out,

time: 108 us -> 95 us (0.88)
  starting transfers between devices: 39.9 us -> 36.3 us
  Pallas kernels: 38.5 us -> 35 us
  other arithmetic: 3.76 us -> 0.67 us
  local copies, waits for them, and re-layouts: 5.88 us -> 3.95 us
    ppermute x20 -> x14, starting transfers between devices: 27.4 us -> 17.8 us  [all_pairs(): lax.ppermute(arrays[b], axis, [(i, i ^ k) for i in range(n)])]
    ppermute x2 -> x6, starting transfers between devices: 3.94 us -> 7.8 us  [the longest x4 6.3 us: crossed(): lax.ppermute(array, axis, [(i, i ^ k) for i in range(lax.axis_size(axis))])]
    all_to_all x1, starting transfers between devices: 3.71 us -> 7.3 us  [per_device(): lax.all_to_all(send, ('gx', 'gy', 'gz'), split_axis=0, concat_axis=0, til...]
    pallas_call x11 -> x10, Pallas kernels: 38.5 us -> 35 us  [call(): pl.pallas_call(kernel, out_shape=out_shapes, in_specs=specs, out_specs=[p...]
    all_to_all x1, waiting for transfers between devices: 2.71 us -> 0.01 us  [per_device(): lax.all_to_all(send, ('gx', 'gy', 'gz'), split_axis=0, concat_axis=0, til...]
    ppermute x20 -> x14, waiting for transfers between devices: 15.6 us -> 17.7 us  [all_pairs(): lax.ppermute(arrays[b], axis, [(i, i ^ k) for i in range(n)])]
    another operation x3 -> x0, other arithmetic: 1.47 us -> none  [per_device(): jnp.stack([wire_piece_amperes * wire_piece_amperes * wire_piece_ohms_base...]
    ppermute x3, starting transfers between devices: 4.86 us -> 3.44 us  [next_pairs(): first = lax.ppermute(even, axis, [(i, i ^ 1) for i in range(n)])]
  transfers between devices with their start and end apart: 26 -> 24, of which waited for: 13 -> 12; matrix products, arithmetic and copies ran while one was open for 1% -> 1% of each run, Pallas kernels for 8% -> 13%
where the time goes in v3:
time: 95 us; the launch traced here: 94.6 us
  starting transfers between devices  36.3 us (38%)
  Pallas kernels  35 us (37%)
  waiting for transfers between devices  17.7 us (19%)
  local copies, waits for them, and re-layouts  3.95 us (4%)
    pallas_call x10, Pallas kernels, call(): pl.pallas_call(kernel, out_shape=out_shapes, in_specs=specs, out_specs=[p...  35 us
    ppermute x14, starting transfers between devices, all_pairs(): lax.ppermute(arrays[b], axis, [(i, i ^ k) for i in range(n)])  17.8 us
    ppermute x14, waiting for transfers between devices, all_pairs(): lax.ppermute(arrays[b], axis, [(i, i ^ k) for i in range(n)])  17.7 us
    all_to_all x1, starting transfers between devices, per_device(): lax.all_to_all(send, ('gx', 'gy', 'gz'), split_axis=0, concat_axis=0, til...  7.3 us
    ppermute x4, starting transfers between devices, crossed(): lax.ppermute(array, axis, [(i, i ^ k) for i in range(lax.axis_size(axis))])  6.3 us
    unnamed x24, local copies, waits for them, and re-layouts  3.95 us
    ppermute x3, starting transfers between devices, next_pairs(): first = lax.ppermute(even, axis, [(i, i ^ 1) for i in range(n)])  3.44 us
  transfers between devices with their start and end apart: 24, of which 12 were waited for; matrix products, arithmetic and copies ran while one was open for 1% of the time, Pallas kernels for 13%

profile of v3, /device:TPU:0, one launch (start us, length us, event | category | flops | bytes accessed | tf_op | source)
XLA Modules:
  0.0 94.6 jit_solution(14148496949173109377)
XLA Ops:
  0.6 5.1 %shard_map.105 = f32[32,1,1408]{2,1,0:T(1,128)} custom-call(f32[32,128]{1,0:T(8,128)} %bitcast.7, f32[32,128]{1,0:T(8,128)} %bitcast.8, s32[32,128]{1,0:T(8,128)} %bitcast.9, s32[32,128]{1,0:T(8,128)} %bitcast.10), custom_call_target="tpu_custom_call" | custom-call | bytes 1 | tf_op jit(solution)/shard_map/pallas_call | solution.py:26
  5.8 0.0 copy-start.2
  5.8 0.0 copy-start.7
  5.8 0.0 copy-start.9
  5.8 0.0 copy-start.10
  5.8 0.0 copy-start.11
  5.8 7.3 %all-to-all-start = ((f32[32,1,1408]{2,1,0:T(1,128)}), f32[32,1,1408]{2,1,0:T(1,128)S(1)}, u32[]{:S(2)}, u32[]{:S(2)}) async-start(f32[32,1,1408]{2,1,0:T(1,128)} %shard_map.105), calls=%async_computation | async-start | bytes 360448 | tf_op jit(solution)/shard_map/all_to_all | solution.py:940
  13.2 0.7 pad_add_fusion.idx
  13.8 4.3 %shard_map.104 = (f32[2,8,128]{2,1,0:T(8,128)}, f32[2,8,128]{2,1,0:T(8,128)}, f32[256,128]{1,0:T(8,128)}, f32[256,128]{1,0:T(8,128)}, f32[2,256,128]{2,1,0:T(8,128)}, /*index=5*/f32[2,256,128]{2,1,0:T(8,128)}) custom-call(s32[3]{0:T(128)} %pad_add_fusion.idx, s32[32]{0:T(128)} %sheet.5, f32[16]{0:T(128)} %table.5, f32[4]{0:T(128)} %scaling.3, ...), custom_call_target="tpu_custom_call" | custom-call | bytes 1 | tf_op jit(solution)/shard_map/pallas_call | solution.py:26
  18.1 1.8 %collective-permute-start.3 = (f32[2,256,128]{2,1,0:T(8,128)}, f32[2,256,128]{2,1,0:T(8,128)S(1)}, u32[]{:S(2)}, u32[]{:S(2)}) collective-permute-start(f32[2,256,128]{2,1,0:T(8,128)} %get-tuple-element.50), channel_id=1, source_target_pairs={{0,1},{1,0},{2,3},{3,2},{4,5},{5,4},{6,7},{7,6},{8,9},{9,8},{10,11... | collective-permute-start | bytes 786440 | tf_op jit(solution)/shard_map/ppermute | solution.py:145
  20.0 0.7 collective-permute-start.4
  20.6 0.1 collective-permute-start.2
  20.7 1.5 %collective-permute-start = (f32[2,8,128]{2,1,0:T(8,128)}, f32[2,8,128]{2,1,0:T(8,128)S(1)}, u32[]{:S(2)}, u32[]{:S(2)}) collective-permute-start(f32[2,8,128]{2,1,0:T(8,128)} %get-tuple-element.47), channel_id=1, source_target_pairs={{0,8},{8,0},{16,24},{24,16},{1,9},{9,1},{17,25},{25,17},{2,10},{10... | collective-permute-start | bytes 24584 | tf_op jit(solution)/shard_map/ppermute | solution.py:145
  22.2 0.8 collective-permute-start.1
  23.1 4.4 %shard_map.106 = (bf16[8,544,256]{2,1,0:T(8,128)(2,1)}, bf16[16,128,256]{2,1,0:T(8,128)(2,1)}, f32[1096,128]{1,0:T(8,128)}) custom-call(s32[3]{0:T(128)} %pad_add_fusion.idx, s32[32]{0:T(128)} %sheet.5, f32[16]{0:T(128)} %table.5), custom_call_target="tpu_custom_call" | custom-call | bytes 1 | tf_op jit(solution)/shard_map/pallas_call | solution.py:26
  27.5 0.0 collective-permute-done.1.xr1
  27.5 0.0 collective-permute-done.2.yr0.yr1
  27.5 0.0 collective-permute-done.4.zr1
  27.5 0.0 all-to-all-done.got_in
  27.6 0.0 copy-start
  27.6 1.0 %copy-done = f32[1096,128]{1,0:T(8,128)S(1)} copy-done((f32[1096,128]{1,0:T(8,128)S(1)}, f32[1096,128]{1,0:T(8,128)}, u32[]{:S(2)}) %copy-start) | copy-done | bytes 561176
  28.7 1.6 %copy-done.3 = bf16[8,544,256]{2,1,0:T(8,128)(2,1)S(1)} copy-done((bf16[8,544,256]{2,1,0:T(8,128)(2,1)S(1)}, bf16[8,544,256]{2,1,0:T(8,128)(2,1)}, u32[]{:S(2)}) %copy-start.3) | copy-done | bytes 2228248
  30.3 1.2 %copy-done.5 = bf16[16,128,256]{2,1,0:T(8,128)(2,1)S(1)} copy-done((bf16[16,128,256]{2,1,0:T(8,128)(2,1)S(1)}, bf16[16,128,256]{2,1,0:T(8,128)(2,1)}, u32[]{:S(2)}) %copy-start.5) | copy-done | bytes 1048600
  31.5 7.8 %shard_map.107 = (f32[8,8,128]{2,1,0:T(8,128)S(1)}, f32[272,128]{1,0:T(8,128)S(1)}, f32[2,256,128]{2,1,0:T(8,128)S(1)}, f32[8,256,128]{2,1,0:T(8,128)S(1)}, f32[...) custom-call(s32[3]{0:T(128)S(1)} %copy-done.8, ...), custom_call_target="tpu_custom_call" | custom-call | bytes 1 | tf_op jit(solution)/shard_map/pallas_call | solution.py:26
  39.3 4.3 %collective-permute-start.5 = (f32[2,256,128]{2,1,0:T(8,128)S(1)}, f32[2,256,128]{2,1,0:T(8,128)S(1)}, u32[]{:S(2)}, u32[]{:S(2)}) collective-permute-start(f32[2,256,128]{2,1,0:T(8,128)S(1)} %get-tuple-element.57.pair), channel_id=1, source_target_pairs={{0,1},{1,0},{2,3},{3,2},{4,5},{5,4},{6,7},{7,6},{8,9},{9,8},{10,11... | collective-permute-start | bytes 786440 | tf_op jit(solution)/shard_map/ppermute | solution.py:140
  43.6 4.2 %collective-permute-start.6 = (f32[16,128]{1,0:T(8,128)S(1)}, f32[16,128]{1,0:T(8,128)S(1)}, u32[]{:S(2)}, u32[]{:S(2)}) collective-permute-start(f32[16,128]{1,0:T(8,128)S(1)} %get-tuple-element.58), channel_id=1, source_target_pairs={{0,8},{8,0},{16,24},{24,16},{1,9},{9,1},{17,25},{25,17},{2,10},{10... | collective-permute-start | bytes 24584 | tf_op jit(solution)/shard_map/ppermute | solution.py:134
  47.8 0.5 collective-permute-start.8
  48.3 0.9 %collective-permute-start.7 = (f32[16,128]{1,0:T(8,128)S(1)}, f32[16,128]{1,0:T(8,128)S(1)}, u32[]{:S(2)}, u32[]{:S(2)}) collective-permute-start(f32[16,128]{1,0:T(8,128)S(1)} %get-tuple-element.59), channel_id=1, source_target_pairs={{0,16},{8,24},{16,0},{24,8},{1,17},{9,25},{17,1},{25,9},{2,18},{10... | collective-permute-start | bytes 24584 | tf_op jit(solution)/shard_map/ppermute | solution.py:134
  49.2 0.2 collective-permute-done.6.rest_0_
  49.4 2.9 %collective-permute-done.8.rest_2_ = f32[16,128]{1,0:T(8,128)S(1)} collective-permute-done((f32[16,128]{1,0:T(8,128)S(1)}, f32[16,128]{1,0:T(8,128)S(1)}, u32[]{:S(2)}, u32[]{:S(2)}) %collective-permute-start.8) | collective-permute-done | bytes 8224 | tf_op jit(solution)/shard_map/ppermute | solution.py:134
  52.3 0.0 collective-permute-done.7.rest_1_
  52.3 0.0 collective-permute-done.5.near.rest_0_
  52.3 0.9 shard_map.108
  53.2 0.0 copy-start.1
  53.2 0.1 collective-permute-start.10
  53.3 0.1 collective-permute-start.9
  53.4 1.2 %collective-permute-done.9.rest_0_ = f32[16,272]{1,0:T(8,128)S(1)} collective-permute-done((f32[16,272]{1,0:T(8,128)S(1)}, f32[16,272]{1,0:T(8,128)S(1)}, u32[]{:S(2)}, u32[]{:S(2)}) %collective-permute-start.9) | collective-permute-done | bytes 17440 | tf_op jit(solution)/shard_map/ppermute | solution.py:134
  54.6 1.4 %shard_map.109 = (f32[272,128]{1,0:T(8,128)S(1)}, f32[272,128]{1,0:T(8,128)S(1)}, f32[32,128]{1,0:T(8,128)S(1)}, f32[72,128]{1,0:T(8,128)S(1)}, f32[72,128]{1,0:T(8,128)S(1)}) custom-call(s32[3]{0:T(128)S(1)} %copy-done.8, f32[8,272,128]{2,1,0:T(8,128)S(1)} %get-tuple-element.55.t_ref.t_in, f32[272,128]{1,0:T(8,128)S(1)} %get-tuple-element.60.e_ref, ...), custom_call_target="tpu_custom_call" | custom-call | bytes 1 | tf_op jit(solution)/shard_map/pallas_call | solution.py:26
  55.9 1.5 %collective-permute-start.11 = (f32[72,128]{1,0:T(8,128)S(1)}, f32[72,128]{1,0:T(8,128)S(1)}, u32[]{:S(2)}, u32[]{:S(2)}) collective-permute-start(f32[72,128]{1,0:T(8,128)S(1)} %get-tuple-element.76), channel_id=1, source_target_pairs={{0,1},{1,0},{2,3},{3,2},{4,5},{5,4},{6,7},{7,6},{8,9},{9,8},{10,11... | collective-permute-start | bytes 110600 | tf_op jit(solution)/shard_map/ppermute | solution.py:134
  57.4 2.9 %collective-permute-start.13 = (f32[72,128]{1,0:T(8,128)S(1)}, f32[72,128]{1,0:T(8,128)S(1)}, u32[]{:S(2)}, u32[]{:S(2)}) collective-permute-start(f32[72,128]{1,0:T(8,128)S(1)} %get-tuple-element.77), channel_id=1, source_target_pairs={{0,3},{1,2},{2,1},{3,0},{4,7},{5,6},{6,5},{7,4},{8,11},{9,10},{10,... | collective-permute-start | bytes 110600 | tf_op jit(solution)/shard_map/ppermute | solution.py:134
  60.3 0.0 collective-permute-start.12
  60.3 1.0 %collective-permute-done.11.rest_2_ = f32[72,128]{1,0:T(8,128)S(1)} collective-permute-done((f32[72,128]{1,0:T(8,128)S(1)}, f32[72,128]{1,0:T(8,128)S(1)}, u32[]{:S(2)}, u32[]{:S(2)}) %collective-permute-start.11) | collective-permute-done | bytes 36896 | tf_op jit(solution)/shard_map/ppermute | solution.py:134
  61.3 1.9 %collective-permute-done.13.rest_4_ = f32[72,128]{1,0:T(8,128)S(1)} collective-permute-done((f32[72,128]{1,0:T(8,128)S(1)}, f32[72,128]{1,0:T(8,128)S(1)}, u32[]{:S(2)}, u32[]{:S(2)}) %collective-permute-start.13) | collective-permute-done | bytes 36896 | tf_op jit(solution)/shard_map/ppermute | solution.py:134
  63.2 1.9 %collective-permute-done.12.rest_3_ = f32[72,128]{1,0:T(8,128)S(1)} collective-permute-done((f32[72,128]{1,0:T(8,128)S(1)}, f32[72,128]{1,0:T(8,128)S(1)}, u32[]{:S(2)}, u32[]{:S(2)}) %collective-permute-start.12) | collective-permute-done | bytes 36896 | tf_op jit(solution)/shard_map/ppermute | solution.py:134
  65.2 0.0 collective-permute-done.10.rest_1_
  65.2 5.5 %shard_map.110 = (f32[8,256,128]{2,1,0:T(8,128)S(1)}, f32[8,8,128]{2,1,0:T(8,128)}, f32[272,128]{1,0:T(8,128)}, f32[2,256,128]{2,1,0:T(8,128)}, f32[8,272,128]{2...) custom-call(s32[3]{0:T(128)S(1)} %copy-done.8, ...), custom_call_target="tpu_custom_call" | custom-call | bytes 1 | tf_op jit(solution)/shard_map/pallas_call | solution.py:26
  70.6 0.0 collective-permute-start.14
  70.6 2.7 %collective-permute-start.15 = (f32[16,128]{1,0:T(8,128)S(1)}, f32[16,128]{1,0:T(8,128)S(1)}, u32[]{:S(2)}, u32[]{:S(2)}) collective-permute-start(f32[16,128]{1,0:T(8,128)S(1)} %get-tuple-element.81), channel_id=1, source_target_pairs={{0,8},{8,0},{16,24},{24,16},{1,9},{9,1},{17,25},{25,17},{2,10},{10... | collective-permute-start | bytes 24584 | tf_op jit(solution)/shard_map/ppermute | solution.py:134
  73.4 0.5 collective-permute-start.17
  73.9 0.9 collective-permute-start.16
  74.8 0.2 collective-permute-done.15.rest_0_
  75.0 2.9 %collective-permute-done.17.rest_2_ = f32[16,128]{1,0:T(8,128)S(1)} collective-permute-done((f32[16,128]{1,0:T(8,128)S(1)}, f32[16,128]{1,0:T(8,128)S(1)}, u32[]{:S(2)}, u32[]{:S(2)}) %collective-permute-start.17) | collective-permute-done | bytes 8224 | tf_op jit(solution)/shard_map/ppermute | solution.py:134
  77.9 0.0 collective-permute-done.16.rest_1_
  77.9 0.9 shard_map.111
  78.8 1.9 %collective-permute-start.19 = (f32[256,128]{1,0:T(8,128)S(1)}, f32[256,128]{1,0:T(8,128)S(1)}, u32[]{:S(2)}, u32[]{:S(2)}) collective-permute-start(f32[256,128]{1,0:T(8,128)S(1)} %get-tuple-element.89), channel_id=1, source_target_pairs={{0,2},{1,3},{2,0},{3,1},{4,6},{5,7},{6,4},{7,5},{8,10},{9,11},{10,... | collective-permute-start | bytes 393224 | tf_op jit(solution)/shard_map/ppermute | solution.py:140
  80.8 1.2 %collective-permute-done.18.rest_0_ = f32[16,272]{1,0:T(8,128)S(1)} collective-permute-done((f32[16,272]{1,0:T(8,128)S(1)}, f32[16,272]{1,0:T(8,128)S(1)}, u32[]{:S(2)}, u32[]{:S(2)}) %collective-permute-start.18) | collective-permute-done | bytes 17440 | tf_op jit(solution)/shard_map/ppermute | solution.py:134
  82.0 1.8 %shard_map.112 = (f32[272,128]{1,0:T(8,128)}, f32[272,128]{1,0:T(8,128)S(1)}, f32[32,128]{1,0:T(8,128)S(1)}, f32[72,128]{1,0:T(8,128)S(1)}, f32[72,128]{1,0:T(8,128)S(1)}) custom-call(s32[3]{0:T(128)S(1)} %copy-done.8, f32[8,272,128]{2,1,0:T(8,128)S(1)} %get-tuple-element.78.t_ref.t_in, f32[272,128]{1,0:T(8,128)S(1)} %get-tuple-element.83.e_ref, ...), custom_call_target="tpu_custom_call" | custom-call | bytes 1 | tf_op jit(solution)/shard_map/pallas_call | solution.py:26
  83.8 0.2 collective-permute-start.20
  84.0 2.3 %collective-permute-start.22 = (f32[72,128]{1,0:T(8,128)S(1)}, f32[72,128]{1,0:T(8,128)S(1)}, u32[]{:S(2)}, u32[]{:S(2)}) collective-permute-start(f32[72,128]{1,0:T(8,128)S(1)} %get-tuple-element.91), channel_id=1, source_target_pairs={{0,3},{1,2},{2,1},{3,0},{4,7},{5,6},{6,5},{7,4},{8,11},{9,10},{10,... | collective-permute-start | bytes 110600 | tf_op jit(solution)/shard_map/ppermute | solution.py:134
  86.3 1.0 %collective-permute-start.21 = (f32[72,128]{1,0:T(8,128)S(1)}, f32[72,128]{1,0:T(8,128)S(1)}, u32[]{:S(2)}, u32[]{:S(2)}) collective-permute-start(f32[72,128]{1,0:T(8,128)S(1)} %get-tuple-element.91), channel_id=1, source_target_pairs={{0,2},{1,3},{2,0},{3,1},{4,6},{5,7},{6,4},{7,5},{8,10},{9,11},{10,... | collective-permute-start | bytes 110600 | tf_op jit(solution)/shard_map/ppermute | solution.py:134
  87.3 0.5 collective-permute-done.20.rest_2_
  87.7 2.4 %collective-permute-done.22.rest_4_ = f32[72,128]{1,0:T(8,128)S(1)} collective-permute-done((f32[72,128]{1,0:T(8,128)S(1)}, f32[72,128]{1,0:T(8,128)S(1)}, u32[]{:S(2)}, u32[]{:S(2)}) %collective-permute-start.22) | collective-permute-done | bytes 36896 | tf_op jit(solution)/shard_map/ppermute | solution.py:134
  90.1 1.4 %collective-permute-done.21.rest_3_ = f32[72,128]{1,0:T(8,128)S(1)} collective-permute-done((f32[72,128]{1,0:T(8,128)S(1)}, f32[72,128]{1,0:T(8,128)S(1)}, u32[]{:S(2)}, u32[]{:S(2)}) %collective-permute-start.21) | collective-permute-done | bytes 36896 | tf_op jit(solution)/shard_map/ppermute | solution.py:134
  91.5 3.0 %shard_map.113 = (f32[8,256,128]{2,1,0:T(8,128)}, f32[8,256,128]{2,1,0:T(8,128)}) custom-call(s32[3]{0:T(128)S(1)} %copy-done.8, f32[8,272,128]{2,1,0:T(8,128)S(1)} %get-tuple-element.78.t_ref.t_in, f32[272,128]{1,0:T(8,128)S(1)} %get-tuple-element.86.l_ref, f32[32,128]{1,0:T(8,128)S(1)} %get-tuple-element.87.b_ref, f32[1096,128]{1,0:T(8,128)S(1)} %copy-done.1, ...), custom_call_target="tpu_custom_call" | custom-call | bytes 1 | tf_op jit(solution)/shard_map/pallas_call | solution.py:26
  (19 shorter events, 0.0 us)
Async XLA Ops:
  5.8 21.8 %copy-start.2 = (f32[8,256,128]{2,1,0:T(8,128)S(1)}, f32[8,256,128]{2,1,0:T(8,128)}, u32[]{:S(2)}) copy-start(f32[8,256,128]{2,1,0:T(8,128)} %u_ref.3) | copy-start | bytes 3145732
  5.8 21.8 %copy-start.7 = (s32[8,256,128]{2,1,0:T(8,128)S(1)}, s32[8,256,128]{2,1,0:T(8,128)}, u32[]{:S(2)}) copy-start(s32[8,256,128]{2,1,0:T(8,128)} %kind_ref.1) | copy-start | bytes 3145732
  5.8 21.8 %copy-start.9 = (s32[32]{0:T(128)S(1)}, s32[32]{0:T(128)}, u32[]{:S(2)}) copy-start(s32[32]{0:T(128)} %sheet.5) | copy-start | bytes 388
  5.8 21.8 %copy-start.10 = (f32[16]{0:T(128)S(1)}, f32[16]{0:T(128)}, u32[]{:S(2)}) copy-start(f32[16]{0:T(128)} %table.5) | copy-start | bytes 196
  5.8 21.8 %copy-start.11 = (f32[4]{0:T(128)S(1)}, f32[4]{0:T(128)}, u32[]{:S(2)}) copy-start(f32[4]{0:T(128)} %scaling.3) | copy-start | bytes 52
  5.8 21.7 %all-to-all-start = ((f32[32,1,1408]{2,1,0:T(1,128)}), f32[32,1,1408]{2,1,0:T(1,128)S(1)}, u32[]{:S(2)}, u32[]{:S(2)}) async-start(f32[32,1,1408]{2,1,0:T(1,128)} %shard_map.105), calls=%async_computation | async-start | bytes 360448 | tf_op jit(solution)/shard_map/all_to_all | solution.py:940
  13.8 13.8 %copy-start.8 = (s32[3]{0:T(128)S(1)}, s32[3]{0:T(128)}, u32[]{:S(2)}) copy-start(s32[3]{0:T(128)} %pad_add_fusion.idx) | copy-start | bytes 40
  18.1 9.4 %collective-permute-start.3 = (f32[2,256,128]{2,1,0:T(8,128)}, f32[2,256,128]{2,1,0:T(8,128)S(1)}, u32[]{:S(2)}, u32[]{:S(2)}) collective-permute-start(f32[2,256,128]{2,1,0:T(8,128)} %get-tuple-element.50), channel_id=1, source_target_pairs={{0,1},{1,0},{2,3},{3,2},{4,5},{5,4},{6,7},{7,6},{8,9},{9,8},{10,11... | collective-permute-start | bytes 786440 | tf_op jit(solution)/shard_map/ppermute | solution.py:145
  20.0 7.5 %collective-permute-start.4 = (f32[2,256,128]{2,1,0:T(8,128)}, f32[2,256,128]{2,1,0:T(8,128)S(1)}, u32[]{:S(2)}, u32[]{:S(2)}) collective-permute-start(f32[2,256,128]{2,1,0:T(8,128)} %get-tuple-element.51), channel_id=1, source_target_pairs={{1,2},{2,1},{5,6},{6,5},{9,10},{10,9},{13,14},{14,13},{17,18},{18,... | collective-permute-start | bytes 786440 | tf_op jit(solution)/shard_map/ppermute | solution.py:149
  20.6 6.9 %collective-permute-start.2 = (f32[256,128]{1,0:T(8,128)}, f32[256,128]{1,0:T(8,128)S(1)}, u32[]{:S(2)}, u32[]{:S(2)}) collective-permute-start(f32[256,128]{1,0:T(8,128)} %get-tuple-element.49), channel_id=1, source_target_pairs={{0,4},{4,0},{1,5},{5,1},{2,6},{6,2},{3,7},{7,3},{8,12},{12,8},{9,1... | collective-permute-start | bytes 393224 | tf_op jit(solution)/shard_map/ppermute | solution.py:145
  20.7 6.8 %collective-permute-start = (f32[2,8,128]{2,1,0:T(8,128)}, f32[2,8,128]{2,1,0:T(8,128)S(1)}, u32[]{:S(2)}, u32[]{:S(2)}) collective-permute-start(f32[2,8,128]{2,1,0:T(8,128)} %get-tuple-element.47), channel_id=1, source_target_pairs={{0,8},{8,0},{16,24},{24,16},{1,9},{9,1},{17,25},{25,17},{2,10},{10... | collective-permute-start | bytes 24584 | tf_op jit(solution)/shard_map/ppermute | solution.py:145
  22.2 5.2 %collective-permute-start.1 = (f32[2,8,128]{2,1,0:T(8,128)}, f32[2,8,128]{2,1,0:T(8,128)S(1)}, u32[]{:S(2)}, u32[]{:S(2)}) collective-permute-start(f32[2,8,128]{2,1,0:T(8,128)} %get-tuple-element.48), channel_id=1, source_target_pairs={{8,16},{16,8},{9,17},{17,9},{10,18},{18,10},{11,19},{19,11},{12,20... | collective-permute-start | bytes 24584 | tf_op jit(solution)/shard_map/ppermute | solution.py:149
  27.6 1.1 %copy-start = (f32[1096,128]{1,0:T(8,128)S(1)}, f32[1096,128]{1,0:T(8,128)}, u32[]{:S(2)}) copy-start(f32[1096,128]{1,0:T(8,128)} %get-tuple-element.54.co_in.co) | copy-start | bytes 1683460
  28.6 1.6 %copy-start.3 = (bf16[8,544,256]{2,1,0:T(8,128)(2,1)S(1)}, bf16[8,544,256]{2,1,0:T(8,128)(2,1)}, u32[]{:S(2)}) copy-start(bf16[8,544,256]{2,1,0:T(8,128)(2,1)} %get-tuple-element.52.gx_in.gx_ref) | copy-start | bytes 6684676
  30.3 1.2 %copy-start.5 = (bf16[16,128,256]{2,1,0:T(8,128)(2,1)S(1)}, bf16[16,128,256]{2,1,0:T(8,128)(2,1)}, u32[]{:S(2)}) copy-start(bf16[16,128,256]{2,1,0:T(8,128)(2,1)} %get-tuple-element.53.gy_in.gy_ref) | copy-start | bytes 3145732
  31.5 33.7 %copy-start.6 = (bf16[16,128,256]{2,1,0:T(8,128)(2,1)S(1)}, bf16[16,128,256]{2,1,0:T(8,128)(2,1)}, u32[]{:S(2)}) copy-start(bf16[16,128,256]{2,1,0:T(8,128)(2,1)} %get-tuple-element.53.gy_in.gy_ref) | copy-start | bytes 3145732
  39.3 13.0 %collective-permute-start.5 = (f32[2,256,128]{2,1,0:T(8,128)S(1)}, f32[2,256,128]{2,1,0:T(8,128)S(1)}, u32[]{:S(2)}, u32[]{:S(2)}) collective-permute-start(f32[2,256,128]{2,1,0:T(8,128)S(1)} %get-tuple-element.57.pair), channel_id=1, source_target_pairs={{0,1},{1,0},{2,3},{3,2},{4,5},{5,4},{6,7},{7,6},{8,9},{9,8},{10,11... | collective-permute-start | bytes 786440 | tf_op jit(solution)/shard_map/ppermute | solution.py:140
  43.6 5.8 %collective-permute-start.6 = (f32[16,128]{1,0:T(8,128)S(1)}, f32[16,128]{1,0:T(8,128)S(1)}, u32[]{:S(2)}, u32[]{:S(2)}) collective-permute-start(f32[16,128]{1,0:T(8,128)S(1)} %get-tuple-element.58), channel_id=1, source_target_pairs={{0,8},{8,0},{16,24},{24,16},{1,9},{9,1},{17,25},{25,17},{2,10},{10... | collective-permute-start | bytes 24584 | tf_op jit(solution)/shard_map/ppermute | solution.py:134
  47.8 4.5 %collective-permute-start.8 = (f32[16,128]{1,0:T(8,128)S(1)}, f32[16,128]{1,0:T(8,128)S(1)}, u32[]{:S(2)}, u32[]{:S(2)}) collective-permute-start(f32[16,128]{1,0:T(8,128)S(1)} %get-tuple-element.59), channel_id=1, source_target_pairs={{0,24},{8,16},{16,8},{24,0},{1,25},{9,17},{17,9},{25,1},{2,26},{10... | collective-permute-start | bytes 24584 | tf_op jit(solution)/shard_map/ppermute | solution.py:134
  48.3 4.0 %collective-permute-start.7 = (f32[16,128]{1,0:T(8,128)S(1)}, f32[16,128]{1,0:T(8,128)S(1)}, u32[]{:S(2)}, u32[]{:S(2)}) collective-permute-start(f32[16,128]{1,0:T(8,128)S(1)} %get-tuple-element.59), channel_id=1, source_target_pairs={{0,16},{8,24},{16,0},{24,8},{1,17},{9,25},{17,1},{25,9},{2,18},{10... | collective-permute-start | bytes 24584 | tf_op jit(solution)/shard_map/ppermute | solution.py:134
  52.3 12.8 %copy-start.4 = (bf16[8,544,256]{2,1,0:T(8,128)(2,1)S(1)}, bf16[8,544,256]{2,1,0:T(8,128)(2,1)}, u32[]{:S(2)}) copy-start(bf16[8,544,256]{2,1,0:T(8,128)(2,1)} %get-tuple-element.52.gx_in.gx_ref) | copy-start | bytes 6684676
  53.2 12.0 %copy-start.1 = (f32[1096,128]{1,0:T(8,128)S(1)}, f32[1096,128]{1,0:T(8,128)}, u32[]{:S(2)}) copy-start(f32[1096,128]{1,0:T(8,128)} %get-tuple-element.54.co_in.co) | copy-start | bytes 1683460
  53.2 11.9 %collective-permute-start.10 = (f32[256,128]{1,0:T(8,128)S(1)}, f32[256,128]{1,0:T(8,128)S(1)}, u32[]{:S(2)}, u32[]{:S(2)}) collective-permute-start(f32[256,128]{1,0:T(8,128)S(1)} %get-tuple-element.75), channel_id=1, source_target_pairs={{0,2},{1,3},{2,0},{3,1},{4,6},{5,7},{6,4},{7,5},{8,10},{9,11},{10,... | collective-permute-start | bytes 393224 | tf_op jit(solution)/shard_map/ppermute | solution.py:140
  53.3 1.3 %collective-permute-start.9 = (f32[16,272]{1,0:T(8,128)S(1)}, f32[16,272]{1,0:T(8,128)S(1)}, u32[]{:S(2)}, u32[]{:S(2)}) collective-permute-start(f32[16,272]{1,0:T(8,128)S(1)} %get-tuple-element.62), channel_id=1, source_target_pairs={{0,4},{4,0},{1,5},{5,1},{2,6},{6,2},{3,7},{7,3},{8,12},{12,8},{9,1... | collective-permute-start | bytes 52232 | tf_op jit(solution)/shard_map/ppermute | solution.py:134
  55.9 5.4 %collective-permute-start.11 = (f32[72,128]{1,0:T(8,128)S(1)}, f32[72,128]{1,0:T(8,128)S(1)}, u32[]{:S(2)}, u32[]{:S(2)}) collective-permute-start(f32[72,128]{1,0:T(8,128)S(1)} %get-tuple-element.76), channel_id=1, source_target_pairs={{0,1},{1,0},{2,3},{3,2},{4,5},{5,4},{6,7},{7,6},{8,9},{9,8},{10,11... | collective-permute-start | bytes 110600 | tf_op jit(solution)/shard_map/ppermute | solution.py:134
  57.4 5.9 %collective-permute-start.13 = (f32[72,128]{1,0:T(8,128)S(1)}, f32[72,128]{1,0:T(8,128)S(1)}, u32[]{:S(2)}, u32[]{:S(2)}) collective-permute-start(f32[72,128]{1,0:T(8,128)S(1)} %get-tuple-element.77), channel_id=1, source_target_pairs={{0,3},{1,2},{2,1},{3,0},{4,7},{5,6},{6,5},{7,4},{8,11},{9,10},{10,... | collective-permute-start | bytes 110600 | tf_op jit(solution)/shard_map/ppermute | solution.py:134
  60.3 4.9 %collective-permute-start.12 = (f32[72,128]{1,0:T(8,128)S(1)}, f32[72,128]{1,0:T(8,128)S(1)}, u32[]{:S(2)}, u32[]{:S(2)}) collective-permute-start(f32[72,128]{1,0:T(8,128)S(1)} %get-tuple-element.77), channel_id=1, source_target_pairs={{0,2},{1,3},{2,0},{3,1},{4,6},{5,7},{6,4},{7,5},{8,10},{9,11},{10,... | collective-permute-start | bytes 110600 | tf_op jit(solution)/shard_map/ppermute | solution.py:134
  70.6 7.3 %collective-permute-start.14 = (f32[2,256,128]{2,1,0:T(8,128)S(1)}, f32[2,256,128]{2,1,0:T(8,128)S(1)}, u32[]{:S(2)}, u32[]{:S(2)}) collective-permute-start(f32[2,256,128]{2,1,0:T(8,128)S(1)} %get-tuple-element.80.pair), channel_id=1, source_target_pairs={{0,1},{1,0},{2,3},{3,2},{4,5},{5,4},{6,7},{7,6},{8,9},{9,8},{10,11... | collective-permute-start | bytes 786440 | tf_op jit(solution)/shard_map/ppermute | solution.py:140
  70.6 4.3 %collective-permute-start.15 = (f32[16,128]{1,0:T(8,128)S(1)}, f32[16,128]{1,0:T(8,128)S(1)}, u32[]{:S(2)}, u32[]{:S(2)}) collective-permute-start(f32[16,128]{1,0:T(8,128)S(1)} %get-tuple-element.81), channel_id=1, source_target_pairs={{0,8},{8,0},{16,24},{24,16},{1,9},{9,1},{17,25},{25,17},{2,10},{10... | collective-permute-start | bytes 24584 | tf_op jit(solution)/shard_map/ppermute | solution.py:134
  73.4 4.5 %collective-permute-start.17 = (f32[16,128]{1,0:T(8,128)S(1)}, f32[16,128]{1,0:T(8,128)S(1)}, u32[]{:S(2)}, u32[]{:S(2)}) collective-permute-start(f32[16,128]{1,0:T(8,128)S(1)} %get-tuple-element.82), channel_id=1, source_target_pairs={{0,24},{8,16},{16,8},{24,0},{1,25},{9,17},{17,9},{25,1},{2,26},{10... | collective-permute-start | bytes 24584 | tf_op jit(solution)/shard_map/ppermute | solution.py:134
  73.9 4.0 %collective-permute-start.16 = (f32[16,128]{1,0:T(8,128)S(1)}, f32[16,128]{1,0:T(8,128)S(1)}, u32[]{:S(2)}, u32[]{:S(2)}) collective-permute-start(f32[16,128]{1,0:T(8,128)S(1)} %get-tuple-element.82), channel_id=1, source_target_pairs={{0,16},{8,24},{16,0},{24,8},{1,17},{9,25},{17,1},{25,9},{2,18},{10... | collective-permute-start | bytes 24584 | tf_op jit(solution)/shard_map/ppermute | solution.py:134
  78.8 12.7 %collective-permute-start.19 = (f32[256,128]{1,0:T(8,128)S(1)}, f32[256,128]{1,0:T(8,128)S(1)}, u32[]{:S(2)}, u32[]{:S(2)}) collective-permute-start(f32[256,128]{1,0:T(8,128)S(1)} %get-tuple-element.89), channel_id=1, source_target_pairs={{0,2},{1,3},{2,0},{3,1},{4,6},{5,7},{6,4},{7,5},{8,10},{9,11},{10,... | collective-permute-start | bytes 393224 | tf_op jit(solution)/shard_map/ppermute | solution.py:140
  80.8 1.2 %collective-permute-start.18 = (f32[16,272]{1,0:T(8,128)S(1)}, f32[16,272]{1,0:T(8,128)S(1)}, u32[]{:S(2)}, u32[]{:S(2)}) collective-permute-start(f32[16,272]{1,0:T(8,128)S(1)} %get-tuple-element.85), channel_id=1, source_target_pairs={{0,4},{4,0},{1,5},{5,1},{2,6},{6,2},{3,7},{7,3},{8,12},{12,8},{9,1... | collective-permute-start | bytes 52232 | tf_op jit(solution)/shard_map/ppermute | solution.py:134
  83.8 4.0 %collective-permute-start.20 = (f32[72,128]{1,0:T(8,128)S(1)}, f32[72,128]{1,0:T(8,128)S(1)}, u32[]{:S(2)}, u32[]{:S(2)}) collective-permute-start(f32[72,128]{1,0:T(8,128)S(1)} %get-tuple-element.90), channel_id=1, source_target_pairs={{0,1},{1,0},{2,3},{3,2},{4,5},{5,4},{6,7},{7,6},{8,9},{9,8},{10,11... | collective-permute-start | bytes 110600 | tf_op jit(solution)/shard_map/ppermute | solution.py:134
  84.0 6.1 %collective-permute-start.22 = (f32[72,128]{1,0:T(8,128)S(1)}, f32[72,128]{1,0:T(8,128)S(1)}, u32[]{:S(2)}, u32[]{:S(2)}) collective-permute-start(f32[72,128]{1,0:T(8,128)S(1)} %get-tuple-element.91), channel_id=1, source_target_pairs={{0,3},{1,2},{2,1},{3,0},{4,7},{5,6},{6,5},{7,4},{8,11},{9,10},{10,... | collective-permute-start | bytes 110600 | tf_op jit(solution)/shard_map/ppermute | solution.py:134
  86.3 5.3 %collective-permute-start.21 = (f32[72,128]{1,0:T(8,128)S(1)}, f32[72,128]{1,0:T(8,128)S(1)}, u32[]{:S(2)}, u32[]{:S(2)}) collective-permute-start(f32[72,128]{1,0:T(8,128)S(1)} %get-tuple-element.91), channel_id=1, source_target_pairs={{0,2},{1,3},{2,0},{3,1},{4,6},{5,7},{6,4},{7,5},{8,10},{9,11},{10,... | collective-permute-start | bytes 110600 | tf_op jit(solution)/shard_map/ppermute | solution.py:134

commit v4 on v3

--- a/solution.py
+++ b/solution.py
@@ -74,6 +74,14 @@
 
 def exact(a, b, dims=((1,), (0,))):
     return lax.dot_general(a, b, (dims, ((), ())), precision=EXACT, preferred_element_type=F32)
+
+
+def stacked(a, b):
+    (a_high, a_low), (b_high, b_low) = split(a), split(b)
+    return mm(
+        jnp.concatenate([a_high, a_low, a_high], axis=1),
+        jnp.concatenate([b_high, b_high, b_low], axis=0),
+    )
 
 
 def mm_nt(a, b):
@@ -156,11 +164,10 @@
     return table[sheet[idx[2] * kind_ref.shape[0] + z]] * factor
 
 
-def faces_kernel(
-    idx, sheet, table, scaling, u_in, kind_in, xs0, xs1, ys0, ys1, zs0, zs1, u_ref, kind_ref, sems
+def faces(
+    idx, sheet, table, scaling, u_ref, kind_ref, started, xs0, xs1, ys0, ys1, zs0, zs1
 ):
     planes, rows, columns = u_ref.shape
-    started = plane_copies([(u_in, u_ref), (kind_in, kind_ref)], sems)
     even = [idx[d] % 2 == 0 for d in range(3)]
     lane = iota((rows, columns), 1)
     low = jnp.zeros((rows, columns), F32)
@@ -191,15 +198,30 @@
     return capacity // 4, capacity - capacity // 4
 
 
-def dispatch_kernel(blocks, planes, area, capacity, amps_in, ohms_in, tile_in, cell_in,
-                    send, amps, ohms, tiles, cells, a_scr, b_scr, z_scr, k_scr, sems):
+def first_kernel(blocks, planes, area, capacity, idx, sheet, table, scaling,
+                 amps_in, ohms_in, tile_in, cell_in, u_in, kind_in,
+                 send, xs0, xs1, ys0, ys1, zs0, zs1,
+                 amps, ohms, tiles, cells, a_scr, b_scr, z_scr, k_scr, u_ref, kind_ref,
+                 sems, plane_sems):
     started = copies(
         [(amps_in, amps), (ohms_in, ohms), (tile_in, tiles), (cell_in, cells)], sems
     )
     for copy in started:
         copy.start()
+    loads = plane_copies([(u_in, u_ref), (kind_in, kind_ref)], plane_sems)
     for copy in started:
         copy.wait()
+    dispatch(
+        blocks, planes, area, capacity, amps, ohms, tiles, cells, send,
+        a_scr, b_scr, z_scr, k_scr,
+    )
+    faces(
+        idx, sheet, table, scaling, u_ref, kind_ref, loads, xs0, xs1, ys0, ys1, zs0, zs1
+    )
+
+
+def dispatch(blocks, planes, area, capacity, amps, ohms, tiles, cells, send,
+             a_scr, b_scr, z_scr, k_scr):
     chunks, lanes = amps.shape
     share, spare = shares(capacity)
     keys, main = blocks * planes, planes * share
@@ -217,24 +239,27 @@
     ]
     key_row, block_row = iota((keys, lanes), 0), iota((blocks, lanes), 0)
     place = iota((main, lanes), 0)
-    ahead = jnp.where(iota((lanes, lanes), 0) < iota((lanes, lanes), 1), 1.0, 0.0)
-    both = jnp.concatenate([ahead, jnp.ones((lanes, lanes), F32)], axis=1).astype(BF16)
+    pair = 2 * lanes
+    ahead = jnp.where(iota((pair, pair), 0) < iota((pair, pair), 1), 1.0, 0.0).astype(BF16)
     base = jnp.zeros((keys, lanes), F32)
-    for c in range(chunks):
-        row, cols = slice(c, c + 1), slice(c * lanes, (c + 1) * lanes)
-        hit = key_row == key[row, :]
-        counted = mm(jnp.where(hit, 1.0, 0.0).astype(BF16), both)
-        rank = jnp.sum(jnp.where(hit, counted[:, :lanes] + base, 0.0), axis=0, keepdims=True)
-        base = base + counted[:, lanes:]
-        rank = rank.astype(jnp.int32)
-        k_scr[row, :] = rank
-        slot = jnp.where(rank < share, plane[row, :] * share + rank, -1)
-        b_scr[:main, cols] = jnp.where(place == slot, 1.0, 0.0).astype(BF16)
-        hit = block_row == tile[row, :]
-        for k, piece in enumerate(pieces):
-            a_scr[k * blocks : (k + 1) * blocks, cols] = jnp.where(
-                hit, piece[row, :], 0.0
-            ).astype(BF16)
+    for c in range(0, chunks, 2):
+        hits = [key_row == key[c + k : c + k + 1, :] for k in range(2)]
+        ones = [jnp.where(hit, 1.0, 0.0) for hit in hits]
+        counted = mm(jnp.concatenate(ones, axis=1).astype(BF16), ahead)
+        for k in range(2):
+            row, cols = slice(c + k, c + k + 1), slice((c + k) * lanes, (c + k + 1) * lanes)
+            order = counted[:, k * lanes : (k + 1) * lanes] + base
+            rank = jnp.sum(jnp.where(hits[k], order, 0.0), axis=0, keepdims=True)
+            rank = rank.astype(jnp.int32)
+            k_scr[row, :] = rank
+            slot = jnp.where(rank < share, plane[row, :] * share + rank, -1)
+            b_scr[:main, cols] = jnp.where(place == slot, 1.0, 0.0).astype(BF16)
+            hit = block_row == tile[row, :]
+            for n, piece in enumerate(pieces):
+                a_scr[n * blocks : (n + 1) * blocks, cols] = jnp.where(
+                    hit, piece[row, :], 0.0
+                ).astype(BF16)
+        base = base + (counted[:, pair - 1 :] + ones[1][:, lanes - 1 :])
     out = mm_nt(a_scr[: 4 * blocks, :], b_scr[:main, :])
     r = [out[k * blocks : (k + 1) * blocks] for k in range(4)]
     total = main + spare
@@ -358,9 +383,7 @@
     return theta, scale
 
 
-def prep_kernel(
-    sizes, idx, sheet, table, gx_out, gy_out, co_out, gx_ref, gy_ref, co, z_scr, sems,
-):
+def coefficients(sizes, idx, sheet, table, gx_ref, gy_ref, co, z_scr):
     planes, rows, columns, nx, ny, nz = sizes
     lanes = 128
     extent = rows + EXTRA
@@ -435,7 +458,6 @@
     at_or_past = index_w >= iota((extent, rows), 1)
     lane = iota((extent, lanes), 1)
     packed = jnp.zeros((extent, lanes), F32)
-    started = []
     y_col = iota((columns, columns), 0).astype(F32)
     y_i, y_j = iota((columns, columns), 0), iota((columns, columns), 1)
     y_past = y_j >= y_i
@@ -467,11 +489,6 @@
             ext = jnp.where(y_j == e * planes + z, values, ext)
         gy_ref[z, :, :lanes], gy_ref[planes + z, :, :lanes] = split(g)
         gy_ref[z, :, lanes:], gy_ref[planes + z, :, lanes:] = split(ext)
-        for k, (src, dst, at) in enumerate(
-            ((gx_ref, gx_out, z), (gy_ref, gy_out, z), (gy_ref, gy_out, planes + z))
-        ):
-            started.append(pltpu.make_async_copy(src.at[at], dst.at[at], sems.at[3 * z + k]))
-            started[-1].start()
     lx[0] = packed
 
     total = planes * nz
@@ -531,10 +548,6 @@
         high_lane,
         jnp.where((row8 >= 2) & (row8 < 4) & (lane_e == row8 - 2), low_lane, 0.0),
     )
-    started.append(pltpu.make_async_copy(co, co_out, sems.at[3 * planes]))
-    started[-1].start()
-    for copy in started:
-        copy.wait()
 
 
 def slopes(
@@ -618,8 +631,8 @@
         out = mm(gx_ref[z], jnp.concatenate([high, low], axis=1))
         t = out[:extent, :columns] + (out[:extent, columns:] + out[extent:, :columns])
         high, low = split(t)
-        out = mm(jnp.concatenate([high, low], axis=0), gy_ref[z])
-        out = out[:extent] + (out[extent:] + mm(high, gy_ref[planes + z]))
+        twice = jnp.concatenate([gy_ref[z], gy_ref[z]], axis=0)
+        out = mm(jnp.concatenate([high, low], axis=1), twice) + mm(high, gy_ref[planes + z])
         t_ref[z] = out[:, :columns]
         sums += out[:, columns:]
         main = out[:rows, :columns]
@@ -638,24 +651,30 @@
     z_send[0], z_send[1] = below, above
 
 
-def start_kernel(sizes, idx, sheet, table, scaling, u_ref, kind_ref,
-                 xr0, xr1, yr0, yr1, zr0, zr1, got_in, gx_in, gy_in, co_in, ux, uy, uz, kx0, kx1, ky0, ky1, kz,
+def start_kernel(sizes, idx, sheet, table, scaling, xr0, xr1, yr0, yr1,
+                 got_in, u_in, kind_in, zr0_in, zr1_in, gx_ref, gy_ref, co, ux, uy, uz, kx0, kx1, ky0, ky1, kz,
                  joule, t_ref, e_ref, *rest):
-    sends, (r_scr, k_scr, gx_ref, gy_ref, co, got, sems) = rest[:-7], rest[-7:]
+    sends, scratch = rest[:-9], rest[-9:]
+    r_scr, k_scr, z_scr, got, u_ref, kind_ref, zr0, zr1, sems = scratch
     started = copies(
-        [(got_in.at[:, 0, :], got), (gx_in, gx_ref), (gy_in, gy_ref), (co_in, co)], sems
+        [
+            (got_in.at[:, 0, :], got), (u_in, u_ref), (kind_in, kind_ref),
+            (zr0_in, zr0), (zr1_in, zr1),
+        ],
+        sems,
     )
     for copy in started:
         copy.start()
     phz, psz = groups_of(sizes, co, "phz", "psz")
-    slopes(
-        sizes[3:], idx, sheet, table, scaling, u_ref, kind_ref, xr0, xr1, yr0, yr1, zr0, zr1,
-        ux, uy, uz, kx0, kx1, ky0, ky1, kz,
-    )
+    coefficients(sizes, idx, sheet, table, gx_ref, gy_ref, co, z_scr)
     started[0].wait()
     joule_into(got, joule, r_scr, k_scr)
     for copy in started[1:]:
         copy.wait()
+    slopes(
+        sizes[3:], idx, sheet, table, scaling, u_ref, kind_ref, xr0, xr1, yr0, yr1, zr0, zr1,
+        ux, uy, uz, kx0, kx1, ky0, ky1, kz,
+    )
 
     def source_of(z):
         out = outflow(z, u_ref, ux, uy, uz, kx0, kx1, ky0, ky1, kz)
@@ -688,7 +707,7 @@
         [jnp.where(own, sums[0][1][0:1, :], 0.0), jnp.where(own, sums[1][1][0:1, :], 0.0)],
         axis=0,
     )
-    e = e_ref[...] + exact(lx[0][:, : 2 * planes], ext)
+    e = e_ref[...] + stacked(lx[0][:, : 2 * planes], ext)
     e_out[...] = e
     send[...] = e.T[2 * planes : 4 * planes]
 
@@ -705,14 +724,14 @@
     return values
 
 
-def y_kernel(sizes, idx, t_ref, e_ref, f_ref, co, *rest):
+def y_kernel(sizes, final, idx, t_ref, e_ref, f_ref, co, *rest):
     ny = sizes[4]
     dy, lx, by, cg, phz, psz, mz = groups_of(
         sizes, co, "dy", "lx", "by", "cg", "phz", "psz", "mz"
     )
     gots, rest = rest[: ny - 1], rest[ny - 1 :]
-    q_ref, l_ref, b_ref = rest[:3]
-    sends = rest[3:]
+    l_ref, b_ref = rest[:2]
+    sends, q_ref = (rest[2:], None) if final else (rest[3:], rest[2])
     planes, extent, columns = t_ref.shape
     rows = extent - EXTRA
     me = idx[1]
@@ -731,28 +750,31 @@
         ],
         axis=0,
     ).T
-    lane = iota((extent, 128), 1)
-    q = jnp.where(lane < 2 * planes, e_ref[...], 0.0) + exact(others, cg[0])
-    q_ref[...] = q
     left = lx[0] + others
     l_ref[...] = left
     right = jnp.concatenate([f_ref[...], by[idx[2]]], axis=0)
     b_ref[...] = right
-    edge = exact(q[:rows], mz[1]).T
-    ghost = slice(rows, rows + 8)
     low, high = weights(phz, planes), weights(psz, planes)
-    both = jnp.concatenate([right * four(low), right * four(high)], axis=1)
-    ghosts = exact(left[ghost, : 4 * planes], both)
-    g_low, g_high = ghosts[:, :128], ghosts[:, 128:]
-    for z in range(planes):
-        value = t_ref[z, ghost, :]
-        g_low += phz[z + 1][0:1, :] * value
-        g_high += psz[z + 1][0:1, :] * value
+    if final:
+        edge, g_low, g_high = jnp.zeros((8, rows), F32), 0.0, 0.0
+    else:
+        lane = iota((extent, 128), 1)
+        q = jnp.where(lane < 2 * planes, e_ref[...], 0.0) + stacked(others, cg[0])
+        q_ref[...] = q
+        edge = stacked(q[:rows], mz[1]).T
+        ghost = slice(rows, rows + 8)
+        both = jnp.concatenate([right * four(low), right * four(high)], axis=1)
+        ghosts = stacked(left[ghost, : 4 * planes], both)
+        g_low, g_high = ghosts[:, :128], ghosts[:, 128:]
+        for z in range(planes):
+            value = t_ref[z, ghost, :]
+            g_low += phz[z + 1][0:1, :] * value
+            g_high += psz[z + 1][0:1, :] * value
     for b, send in enumerate(sends):
         lower = (idx[2] >> b) % 2 == 0
         scale = jnp.where(lower, low, high)
         twice = jnp.concatenate([scale] * 2, axis=0)
-        send[:8, :] = jnp.where(lower, g_low, g_high)
+        send[:8, :] = jnp.broadcast_to(jnp.where(lower, g_low, g_high), (8, 128))
         send[8 : 8 + 2 * planes, :] = f_ref[...] * twice
         at = 8 + 2 * planes
         for part in range(rows // 128):
@@ -804,15 +826,17 @@
 
 
 def whole_planes(t_ref, l_ref, b_ref, second, extent):
-    planes = t_ref.shape[0]
+    planes, _, columns = t_ref.shape
     high, low = split(l_ref[:extent, : 4 * planes])
-    pair = jnp.concatenate([high, low], axis=0)
+    left = jnp.concatenate([high, low, high], axis=1)
     right = b_ref[...]
     row = iota(right.shape, 0) % planes
-    for z in range(planes):
-        r_high, r_low = split(jnp.where(row == z, right, 0.0))
-        out = mm(pair, r_high)
-        second[z] = t_ref[z, :extent, :] + (out[:extent] + (out[extent:] + mm(high, r_low)))
+    for z in range(0, planes, 2):
+        own = [jnp.where(row == z + k, right, 0.0) for k in range(2)]
+        r_high, r_low = split(jnp.concatenate(own, axis=1))
+        out = mm(left, jnp.concatenate([r_high, r_high, r_low], axis=0))
+        for k in range(2):
+            second[z + k] = t_ref[z + k, :extent, :] + out[:, k * columns : (k + 1) * columns]
 
 
 def change(outside, second, phz, psz, below, above, emit):
@@ -858,7 +882,7 @@
         jnp.concatenate([above, g_above], axis=0),
         emit,
     )
-    grown = exact(q_ref[:rows, :], mz[0]) + exact(edges, wz[0], ((0,), (0,)))
+    grown = stacked(q_ref[:rows, :], mz[0]) + exact(edges, wz[0], ((0,), (0,)))
     uy_out[...] = uy[...]
     uy_out[:rows, :] = uy[:rows, :] + grown
 
@@ -876,17 +900,23 @@
     phz, psz, ax, by = groups_of(sizes, co, "phz", "psz", "ax", "by")
     deep = (nz - 1).bit_length()
     bigs, smalls, rest = rest[:deep], rest[deep : deep + nz - 1], rest[deep + nz - 1 :]
-    u_out, heat_out, second = rest
+    u_out, heat_out, u_scr, heat_scr, second, sems = rest
     rows = u_ref.shape[1]
+    started = []
     whole_planes(t_in, l_ref, b_ref, second, rows)
     below, above, _, _, _ = carried(nz, idx, bigs, smalls, ax, by, rows, False)
 
     def emit(z, value):
         u = u_ref[z] + value
-        u_out[z] = u
-        heat_out[z] = (1.0 + WARMING_SLOPE * u) * joule[z]
+        u_scr[z] = u
+        heat_scr[z] = (1.0 + WARMING_SLOPE * u) * joule[z]
+        for k, (src, dst) in enumerate(((u_scr, u_out), (heat_scr, heat_out))):
+            started.append(pltpu.make_async_copy(src.at[z], dst.at[z], sems.at[k, z]))
+            started[-1].start()
 
     change(False, second, phz, psz, below, above, emit)
+    for copy in started:
+        copy.wait()
 
 
 def per_device(
@@ -922,11 +952,15 @@
     )
     share, spare = shares(capacity)
     slots = planes * share + spare
-    (send,) = call(
-        functools.partial(dispatch_kernel, devices, planes, rows * columns, capacity),
-        [shaped(devices, 1, 2 * slots)],
-        segments,
-        far=4,
+    send, xs0, xs1, ys0, ys1, zs0, zs1 = call(
+        functools.partial(first_kernel, devices, planes, rows * columns, capacity),
+        [shaped(devices, 1, 2 * slots)]
+        + [shaped(2, planes, columns)] * 2
+        + [shaped(rows, 128)] * 2
+        + [shaped(2, rows, columns)] * 2,
+        (idx, *tables, *segments, starting_warmth, substance_kind),
+        smem=4,
+        far=6,
         vmem=60,
         scratch=[pltpu.VMEM((chunks, lanes), part.dtype) for part in segments]
         + [
@@ -934,65 +968,44 @@
             pltpu.VMEM((max(planes * share, spare), count), BF16),
             pltpu.VMEM((devices * planes, lanes), F32),
             pltpu.VMEM((chunks, lanes), jnp.int32),
-            pltpu.SemaphoreType.DMA((4,)),
-        ],
-    )
-    got = lax.all_to_all(send, ("gx", "gy", "gz"), split_axis=0, concat_axis=0, tiled=True)
-
-    xs0, xs1, ys0, ys1, zs0, zs1 = call(
-        faces_kernel,
-        [shaped(2, planes, columns)] * 2
-        + [shaped(rows, 128)] * 2
-        + [shaped(2, rows, columns)] * 2,
-        (idx, *tables, starting_warmth, substance_kind),
-        smem=4,
-        far=2,
-        vmem=60,
-        scratch=[
             pltpu.VMEM(block.shape, F32),
             pltpu.VMEM(block.shape, jnp.int32),
+            pltpu.SemaphoreType.DMA((4,)),
             pltpu.SemaphoreType.DMA((2, planes)),
         ],
     )
+    got = lax.all_to_all(send, ("gx", "gy", "gz"), split_axis=0, concat_axis=0, tiled=True)
+
     zr = next_pairs(zs0, zs1, "gz")
     xr = next_pairs(xs0, xs1, "gx")
     yr = next_pairs(ys0, ys1, "gy")
     sizes = (planes, rows, columns, nx, ny, nz)
-    coefficients = [
+    parts = [
         shaped(planes, 2 * extent, rows, dtype=BF16),
         shaped(2 * planes, columns, 256, dtype=BF16),
         shaped(table_rows(*sizes)[1], lanes),
     ]
-    room = [pltpu.VMEM(o.shape, o.dtype) for o in coefficients]
-    gx_m, gy_m, co = call(
-        functools.partial(prep_kernel, sizes),
-        coefficients,
-        (idx, *tables[:2]),
-        smem=3,
-        vmem=60,
-        scratch=room
-        + [
-            pltpu.VMEM((2 * planes * nz + 4, 8, lanes), F32),
-            pltpu.SemaphoreType.DMA((3 * planes + 1,)),
-        ],
-        far_out=True,
-    )
     step_out = [shaped(planes, extent, columns), shaped(extent, 128)]
     step_out += [shaped(2, rows, columns)] + [shaped(planes + 8, columns)] * bits[0]
     total = devices * spare
     ghosts = [shaped(planes, 8, columns), shaped(extent, 128), shaped(2, rows, columns)]
-    ux, uy, uz, *rest = call(
+    gx_m, gy_m, co, ux, uy, uz, *rest = call(
         functools.partial(start_kernel, sizes),
-        ghosts + [block] * 4 + [shaped(planes + 1, rows, columns), block] + step_out,
-        (idx, *tables, starting_warmth, substance_kind, *xr, *yr, *zr, got, gx_m, gy_m, co),
+        parts + ghosts + [block] * 4 + [shaped(planes + 1, rows, columns), block] + step_out,
+        (idx, *tables, *xr, *yr, got, starting_warmth, substance_kind, *zr),
         smem=4,
-        far=4,
+        far=5,
+        vmem=36,
         scratch=[
             pltpu.VMEM((2 * columns, total), BF16),
             pltpu.VMEM((8, total), jnp.int32),
-            *room,
+            pltpu.VMEM((2 * planes * nz + 4, 8, lanes), F32),
             pltpu.VMEM((devices, 2 * slots), F32),
-            pltpu.SemaphoreType.DMA((4,)),
+            pltpu.VMEM(block.shape, F32),
+            pltpu.VMEM(block.shape, jnp.int32),
+            pltpu.VMEM((2, rows, columns), F32),
+            pltpu.VMEM((2, rows, columns), F32),
+            pltpu.SemaphoreType.DMA((5,)),
         ],
     )
     conduct, (joule, t, e, *sends) = rest[:5], rest[5:]
@@ -1011,14 +1024,19 @@
         )
         bigs = [near] + [crossed(array, 2, "gz") for array in far]
         gots = all_pairs([send] * bits[1], "gy")
-        q, left, right, *sends = call(
-            functools.partial(y_kernel, sizes),
-            [shaped(extent, 128)] * 2 + [shaped(4 * planes, columns)] + [small] * bits[2],
+        final = repeat == STEPS - 1
+        q = [] if final else [shaped(extent, 128)]
+        left, right, *sends = call(
+            functools.partial(y_kernel, sizes, final),
+            [shaped(extent, 128), shaped(4 * planes, columns)] + q + [small] * bits[2],
             (idx, t, e, f, co, *gots),
             smem=1,
         )
-        smalls = all_pairs(sends, "gz")
-        if repeat < STEPS - 1:
+        if final:
+            smalls = all_pairs(sends, "gz")
+        else:
+            q, *sends = sends
+            smalls = all_pairs(sends, "gz")
             u, ux, uy, uz, t, e, *sends = call(
                 functools.partial(rise_kernel, sizes),
                 [block, shaped(planes, 8, columns), shaped(extent, 128)]
@@ -1035,7 +1053,9 @@
             [block, block],
             (idx, t, left, right, co, u, joule, *bigs, *smalls),
             smem=1,
-            scratch=[pltpu.VMEM((planes, rows, columns), F32)],
+            scratch=[pltpu.VMEM((planes, rows, columns), F32)] * 3
+            + [pltpu.SemaphoreType.DMA((2, planes))],
+            far_out=True,
         )
     )
 

time: 95 us -> 88.7 us (0.934)
  waiting for transfers between devices: 17.7 us -> 25.6 us
  Pallas kernels: 35 us -> 29.8 us
  starting transfers between devices: 36.3 us -> 31.6 us
  local copies, waits for them, and re-layouts: 3.95 us -> 0.03 us
    ppermute x3, waiting for transfers between devices: 0.01 us -> 6.6 us  [next_pairs(): first = lax.ppermute(even, axis, [(i, i ^ 1) for i in range(n)])]
    pallas_call x10 -> x8, Pallas kernels: 35 us -> 29.8 us  [call(): pl.pallas_call(kernel, out_shape=out_shapes, in_specs=specs, out_specs=[p...]
    unnamed x24 -> x12, local copies, waits for them, and re-layouts: 3.95 us -> 0.03 us
    ppermute x4, starting transfers between devices: 6.3 us -> 3.89 us  [crossed(): lax.ppermute(array, axis, [(i, i ^ k) for i in range(lax.axis_size(axis))])]
    ppermute x14, starting transfers between devices: 17.8 us -> 15.6 us  [all_pairs(): lax.ppermute(arrays[b], axis, [(i, i ^ k) for i in range(n)])]
  transfers between devices with their start and end apart: 24 -> 24, of which waited for: 12 -> 16; matrix products, arithmetic and copies ran while one was open for 1% -> 0% of each run, Pallas kernels for 13% -> 2%
where the time goes in v4:
time: 88.7 us; the launch traced here: 88.5 us
  starting transfers between devices  31.6 us (36%)
  Pallas kernels  29.8 us (34%)
  waiting for transfers between devices  25.6 us (29%)
  between operations  0.96 us (1%)
    pallas_call x8, Pallas kernels, call(): pl.pallas_call(kernel, out_shape=out_shapes, in_specs=specs, out_specs=[p...  29.8 us
    ppermute x14, waiting for transfers between devices, all_pairs(): lax.ppermute(arrays[b], axis, [(i, i ^ k) for i in range(n)])  18.3 us
    ppermute x14, starting transfers between devices, all_pairs(): lax.ppermute(arrays[b], axis, [(i, i ^ k) for i in range(n)])  15.6 us
    all_to_all x1, starting transfers between devices, per_device(): lax.all_to_all(send, ('gx', 'gy', 'gz'), split_axis=0, concat_axis=0, til...  7.3 us
    ppermute x3, waiting for transfers between devices, next_pairs(): first = lax.ppermute(even, axis, [(i, i ^ 1) for i in range(n)])  6.6 us
    ppermute x4, starting transfers between devices, crossed(): lax.ppermute(array, axis, [(i, i ^ k) for i in range(lax.axis_size(axis))])  3.89 us
    ppermute x3, starting transfers between devices, next_pairs(): first = lax.ppermute(even, axis, [(i, i ^ 1) for i in range(n)])  3.44 us
  transfers between devices with their start and end apart: 24, of which 16 were waited for; matrix products, arithmetic and copies ran while one was open for 0% of the time, Pallas kernels for 2%

profile of v4, /device:TPU:0, one launch (start us, length us, event | category | flops | bytes accessed | tf_op | source)
XLA Modules:
  0.0 88.5 jit_solution(7302458854731208524)
XLA Ops:
  0.6 0.7 pad_add_fusion.idx
  1.3 0.0 copy-start.4
  1.3 0.0 copy-start.5
  1.3 8.8 %shard_map.104 = (f32[32,1,1408]{2,1,0:T(1,128)}, f32[2,8,128]{2,1,0:T(8,128)}, f32[2,8,128]{2,1,0:T(8,128)}, f32[256,128]{1,0:T(8,128)}, f32[256,128]{1,0:T(8,1...) custom-call(s32[3]{0:T(128)} %pad_add_fusion.idx, s32[32]{0:T(128)} %sheet.3, f32[16]{0:T(128)} %table.3, f32[4]{0:T(128)} %scaling.3, ...), custom_call_target="tpu_custom_call" | custom-call | bytes 1 | tf_op jit(solution)/shard_map/pallas_call | solution.py:26
  10.2 7.3 %all-to-all-start = ((f32[32,1,1408]{2,1,0:T(1,128)}), f32[32,1,1408]{2,1,0:T(1,128)S(1)}, u32[]{:S(2)}, u32[]{:S(2)}) async-start(f32[32,1,1408]{2,1,0:T(1,128)} %get-tuple-element.51), calls=%async_computation | async-start | bytes 360448 | tf_op jit(solution)/shard_map/all_to_all | solution.py:977
  17.5 1.8 %collective-permute-start.3 = (f32[2,256,128]{2,1,0:T(8,128)}, f32[2,256,128]{2,1,0:T(8,128)S(1)}, u32[]{:S(2)}, u32[]{:S(2)}) collective-permute-start(f32[2,256,128]{2,1,0:T(8,128)} %get-tuple-element.52), channel_id=1, source_target_pairs={{0,1},{1,0},{2,3},{3,2},{4,5},{5,4},{6,7},{7,6},{8,9},{9,8},{10,11... | collective-permute-start | bytes 786440 | tf_op jit(solution)/shard_map/ppermute | solution.py:153
  19.3 0.7 collective-permute-start.4
  20.0 0.1 collective-permute-start.2
  20.1 1.5 %collective-permute-start = (f32[2,8,128]{2,1,0:T(8,128)}, f32[2,8,128]{2,1,0:T(8,128)S(1)}, u32[]{:S(2)}, u32[]{:S(2)}) collective-permute-start(f32[2,8,128]{2,1,0:T(8,128)} %get-tuple-element.48), channel_id=1, source_target_pairs={{0,8},{8,0},{16,24},{24,16},{1,9},{9,1},{17,25},{25,17},{2,10},{10... | collective-permute-start | bytes 24584 | tf_op jit(solution)/shard_map/ppermute | solution.py:153
  21.6 0.6 collective-permute-start.1
  22.2 1.7 %collective-permute-done.xr0 = f32[2,8,128]{2,1,0:T(8,128)S(1)} collective-permute-done((f32[2,8,128]{2,1,0:T(8,128)}, f32[2,8,128]{2,1,0:T(8,128)S(1)}, u32[]{:S(2)}, u32[]{:S(2)}) %collective-permute-start) | collective-permute-done | bytes 8224 | tf_op jit(solution)/shard_map/ppermute | solution.py:153
  24.0 0.0 collective-permute-done.1.xr1
  24.0 0.0 collective-permute-done.2.yr0.yr1
  24.0 4.9 %collective-permute-done.3.zr0_in = f32[2,256,128]{2,1,0:T(8,128)S(1)} collective-permute-done((f32[2,256,128]{2,1,0:T(8,128)}, f32[2,256,128]{2,1,0:T(8,128)S(1)}, u32[]{:S(2)}, u32[]{:S(2)}) %collective-permute-start.3) | collective-permute-done | bytes 262176 | tf_op jit(solution)/shard_map/ppermute | solution.py:153
  28.9 0.0 collective-permute-done.4.zr1_in
  28.9 0.0 all-to-all-done.got_in
  28.9 0.0 copy-done
  28.9 0.0 copy-done.1
  28.9 0.0 copy-done.2
  28.9 0.0 copy-done.3
  28.9 0.0 copy-done.4
  28.9 10.0 %shard_map.105 = (bf16[8,544,256]{2,1,0:T(8,128)(2,1)S(1)}, bf16[16,128,256]{2,1,0:T(8,128)(2,1)S(1)}, f32[1096,128]{1,0:T(8,128)S(1)}, f32[8,8,128]{2,1,0:T(8,1...) custom-call(s32[3]{0:T(128)S(1)} %copy-done.2, ...), custom_call_target="tpu_custom_call" | custom-call | bytes 1 | tf_op jit(solution)/shard_map/pallas_call | solution.py:26
  38.9 2.5 %collective-permute-start.5 = (f32[2,256,128]{2,1,0:T(8,128)S(1)}, f32[2,256,128]{2,1,0:T(8,128)S(1)}, u32[]{:S(2)}, u32[]{:S(2)}) collective-permute-start(f32[2,256,128]{2,1,0:T(8,128)S(1)} %get-tuple-element.57.pair), channel_id=1, source_target_pairs={{0,1},{1,0},{2,3},{3,2},{4,5},{5,4},{6,7},{7,6},{8,9},{9,8},{10,11... | collective-permute-start | bytes 786440 | tf_op jit(solution)/shard_map/ppermute | solution.py:148
  41.4 1.8 %collective-permute-start.6 = (f32[16,128]{1,0:T(8,128)S(1)}, f32[16,128]{1,0:T(8,128)S(1)}, u32[]{:S(2)}, u32[]{:S(2)}) collective-permute-start(f32[16,128]{1,0:T(8,128)S(1)} %get-tuple-element.58), channel_id=1, source_target_pairs={{0,8},{8,0},{16,24},{24,16},{1,9},{9,1},{17,25},{25,17},{2,10},{10... | collective-permute-start | bytes 24584 | tf_op jit(solution)/shard_map/ppermute | solution.py:142
  43.2 2.4 %collective-permute-start.8 = (f32[16,128]{1,0:T(8,128)S(1)}, f32[16,128]{1,0:T(8,128)S(1)}, u32[]{:S(2)}, u32[]{:S(2)}) collective-permute-start(f32[16,128]{1,0:T(8,128)S(1)} %get-tuple-element.59), channel_id=1, source_target_pairs={{0,24},{8,16},{16,8},{24,0},{1,25},{9,17},{17,9},{25,1},{2,26},{10... | collective-permute-start | bytes 24584 | tf_op jit(solution)/shard_map/ppermute | solution.py:142
  45.6 0.0 collective-permute-start.7
  45.6 0.0 collective-permute-done.6.rest_0_
  45.6 2.1 %collective-permute-done.8.rest_2_ = f32[16,128]{1,0:T(8,128)S(1)} collective-permute-done((f32[16,128]{1,0:T(8,128)S(1)}, f32[16,128]{1,0:T(8,128)S(1)}, u32[]{:S(2)}, u32[]{:S(2)}) %collective-permute-start.8) | collective-permute-done | bytes 8224 | tf_op jit(solution)/shard_map/ppermute | solution.py:142
  47.7 1.5 %collective-permute-done.7.rest_1_ = f32[16,128]{1,0:T(8,128)S(1)} collective-permute-done((f32[16,128]{1,0:T(8,128)S(1)}, f32[16,128]{1,0:T(8,128)S(1)}, u32[]{:S(2)}, u32[]{:S(2)}) %collective-permute-start.7) | collective-permute-done | bytes 8224 | tf_op jit(solution)/shard_map/ppermute | solution.py:142
  49.2 0.0 collective-permute-done.5.near.rest_0_
  49.2 0.8 shard_map.106
  50.1 0.1 collective-permute-start.10
  50.2 0.1 collective-permute-start.9
  50.2 1.2 %collective-permute-done.9.rest_0_ = f32[16,272]{1,0:T(8,128)S(1)} collective-permute-done((f32[16,272]{1,0:T(8,128)S(1)}, f32[16,272]{1,0:T(8,128)S(1)}, u32[]{:S(2)}, u32[]{:S(2)}) %collective-permute-start.9) | collective-permute-done | bytes 17440 | tf_op jit(solution)/shard_map/ppermute | solution.py:142
  51.4 1.0 %shard_map.107 = (f32[272,128]{1,0:T(8,128)S(1)}, f32[32,128]{1,0:T(8,128)S(1)}, f32[272,128]{1,0:T(8,128)S(1)}, f32[72,128]{1,0:T(8,128)S(1)}, f32[72,128]{1,0:T(8,128)S(1)}) custom-call(s32[3]{0:T(128)S(1)} %copy-done.2, f32[8,272,128]{2,1,0:T(8,128)S(1)} %get-tuple-element.54.t_ref.t_in, f32[272,128]{1,0:T(8,128)S(1)} %get-tuple-element.60.e_ref, ...), custom_call_target="tpu_custom_call" | custom-call | bytes 1 | tf_op jit(solution)/shard_map/pallas_call | solution.py:26
  52.5 1.4 %collective-permute-start.11 = (f32[72,128]{1,0:T(8,128)S(1)}, f32[72,128]{1,0:T(8,128)S(1)}, u32[]{:S(2)}, u32[]{:S(2)}) collective-permute-start(f32[72,128]{1,0:T(8,128)S(1)} %get-tuple-element.78), channel_id=1, source_target_pairs={{0,1},{1,0},{2,3},{3,2},{4,5},{5,4},{6,7},{7,6},{8,9},{9,8},{10,11... | collective-permute-start | bytes 110600 | tf_op jit(solution)/shard_map/ppermute | solution.py:142
  53.9 2.9 %collective-permute-start.13 = (f32[72,128]{1,0:T(8,128)S(1)}, f32[72,128]{1,0:T(8,128)S(1)}, u32[]{:S(2)}, u32[]{:S(2)}) collective-permute-start(f32[72,128]{1,0:T(8,128)S(1)} %get-tuple-element.79), channel_id=1, source_target_pairs={{0,3},{1,2},{2,1},{3,0},{4,7},{5,6},{6,5},{7,4},{8,11},{9,10},{10,... | collective-permute-start | bytes 110600 | tf_op jit(solution)/shard_map/ppermute | solution.py:142
  56.8 0.0 collective-permute-start.12
  56.8 0.5 collective-permute-done.11.rest_2_
  57.3 2.5 %collective-permute-done.13.rest_4_ = f32[72,128]{1,0:T(8,128)S(1)} collective-permute-done((f32[72,128]{1,0:T(8,128)S(1)}, f32[72,128]{1,0:T(8,128)S(1)}, u32[]{:S(2)}, u32[]{:S(2)}) %collective-permute-start.13) | collective-permute-done | bytes 36896 | tf_op jit(solution)/shard_map/ppermute | solution.py:142
  59.8 1.9 %collective-permute-done.12.rest_3_ = f32[72,128]{1,0:T(8,128)S(1)} collective-permute-done((f32[72,128]{1,0:T(8,128)S(1)}, f32[72,128]{1,0:T(8,128)S(1)}, u32[]{:S(2)}, u32[]{:S(2)}) %collective-permute-start.12) | collective-permute-done | bytes 36896 | tf_op jit(solution)/shard_map/ppermute | solution.py:142
  61.7 0.0 collective-permute-done.10.rest_1_
  61.7 4.6 %shard_map.108 = (f32[8,256,128]{2,1,0:T(8,128)S(1)}, f32[8,8,128]{2,1,0:T(8,128)}, f32[272,128]{1,0:T(8,128)}, f32[2,256,128]{2,1,0:T(8,128)}, f32[8,272,128]{2...) custom-call(s32[3]{0:T(128)S(1)} %copy-done.2, ...), custom_call_target="tpu_custom_call" | custom-call | bytes 1 | tf_op jit(solution)/shard_map/pallas_call | solution.py:26
  66.2 0.0 collective-permute-start.14
  66.2 0.7 collective-permute-start.15
  67.0 2.0 %collective-permute-start.17 = (f32[16,128]{1,0:T(8,128)S(1)}, f32[16,128]{1,0:T(8,128)S(1)}, u32[]{:S(2)}, u32[]{:S(2)}) collective-permute-start(f32[16,128]{1,0:T(8,128)S(1)} %get-tuple-element.84), channel_id=1, source_target_pairs={{0,24},{8,16},{16,8},{24,0},{1,25},{9,17},{17,9},{25,1},{2,26},{10... | collective-permute-start | bytes 24584 | tf_op jit(solution)/shard_map/ppermute | solution.py:142
  69.0 0.7 collective-permute-start.16
  69.7 0.2 collective-permute-done.15.rest_0_
  69.9 1.6 %collective-permute-done.17.rest_2_ = f32[16,128]{1,0:T(8,128)S(1)} collective-permute-done((f32[16,128]{1,0:T(8,128)S(1)}, f32[16,128]{1,0:T(8,128)S(1)}, u32[]{:S(2)}, u32[]{:S(2)}) %collective-permute-start.17) | collective-permute-done | bytes 8224 | tf_op jit(solution)/shard_map/ppermute | solution.py:142
  71.5 1.1 %collective-permute-done.16.rest_1_ = f32[16,128]{1,0:T(8,128)S(1)} collective-permute-done((f32[16,128]{1,0:T(8,128)S(1)}, f32[16,128]{1,0:T(8,128)S(1)}, u32[]{:S(2)}, u32[]{:S(2)}) %collective-permute-start.16) | collective-permute-done | bytes 8224 | tf_op jit(solution)/shard_map/ppermute | solution.py:142
  72.6 0.6 collective-permute-done.14.near.rest_0_
  73.3 0.8 shard_map.109
  74.1 1.3 %collective-permute-start.19 = (f32[256,128]{1,0:T(8,128)S(1)}, f32[256,128]{1,0:T(8,128)S(1)}, u32[]{:S(2)}, u32[]{:S(2)}) collective-permute-start(f32[256,128]{1,0:T(8,128)S(1)} %get-tuple-element.91), channel_id=1, source_target_pairs={{0,2},{1,3},{2,0},{3,1},{4,6},{5,7},{6,4},{7,5},{8,10},{9,11},{10,... | collective-permute-start | bytes 393224 | tf_op jit(solution)/shard_map/ppermute | solution.py:148
  75.4 0.0 collective-permute-start.18
  75.4 1.2 %collective-permute-done.18.rest_0_ = f32[16,272]{1,0:T(8,128)S(1)} collective-permute-done((f32[16,272]{1,0:T(8,128)S(1)}, f32[16,272]{1,0:T(8,128)S(1)}, u32[]{:S(2)}, u32[]{:S(2)}) %collective-permute-start.18) | collective-permute-done | bytes 17440 | tf_op jit(solution)/shard_map/ppermute | solution.py:142
  76.6 0.7 shard_map.110
  77.3 0.7 collective-permute-start.20
  78.0 2.5 %collective-permute-start.22 = (f32[72,128]{1,0:T(8,128)S(1)}, f32[72,128]{1,0:T(8,128)S(1)}, u32[]{:S(2)}, u32[]{:S(2)}) collective-permute-start(f32[72,128]{1,0:T(8,128)S(1)} %get-tuple-element.93), channel_id=1, source_target_pairs={{0,3},{1,2},{2,1},{3,0},{4,7},{5,6},{6,5},{7,4},{8,11},{9,10},{10,... | collective-permute-start | bytes 110600 | tf_op jit(solution)/shard_map/ppermute | solution.py:142
  80.5 0.3 collective-permute-start.21
  80.9 1.1 %collective-permute-done.20.rest_2_ = f32[72,128]{1,0:T(8,128)S(1)} collective-permute-done((f32[72,128]{1,0:T(8,128)S(1)}, f32[72,128]{1,0:T(8,128)S(1)}, u32[]{:S(2)}, u32[]{:S(2)}) %collective-permute-start.20) | collective-permute-done | bytes 36896 | tf_op jit(solution)/shard_map/ppermute | solution.py:142
  82.0 1.9 %collective-permute-done.22.rest_4_ = f32[72,128]{1,0:T(8,128)S(1)} collective-permute-done((f32[72,128]{1,0:T(8,128)S(1)}, f32[72,128]{1,0:T(8,128)S(1)}, u32[]{:S(2)}, u32[]{:S(2)}) %collective-permute-start.22) | collective-permute-done | bytes 36896 | tf_op jit(solution)/shard_map/ppermute | solution.py:142
  83.9 1.5 %collective-permute-done.21.rest_3_ = f32[72,128]{1,0:T(8,128)S(1)} collective-permute-done((f32[72,128]{1,0:T(8,128)S(1)}, f32[72,128]{1,0:T(8,128)S(1)}, u32[]{:S(2)}, u32[]{:S(2)}) %collective-permute-start.21) | collective-permute-done | bytes 36896 | tf_op jit(solution)/shard_map/ppermute | solution.py:142
  85.4 0.0 collective-permute-done.19.rest_1_
  85.4 3.0 %shard_map.111 = (f32[8,256,128]{2,1,0:T(8,128)}, f32[8,256,128]{2,1,0:T(8,128)}) custom-call(s32[3]{0:T(128)S(1)} %copy-done.2, f32[8,272,128]{2,1,0:T(8,128)S(1)} %get-tuple-element.80.t_ref.t_in, f32[272,128]{1,0:T(8,128)S(1)} %get-tuple-element.88.l_ref, f32[32,128]{1,0:T(8,128)S(1)} %get-tuple-element.89.b_ref, f32[1096,128]{1,0:T(8,128)S(1)} %get-tuple-element.56.co, ...), custom_call_target="tpu_custom_call" | custom-call | bytes 1 | tf_op jit(solution)/shard_map/pallas_call | solution.py:26
  (5 shorter events, 0.0 us)
Async XLA Ops:
  1.3 27.6 %copy-start = (f32[8,256,128]{2,1,0:T(8,128)S(1)}, f32[8,256,128]{2,1,0:T(8,128)}, u32[]{:S(2)}) copy-start(f32[8,256,128]{2,1,0:T(8,128)} %u_ref.1) | copy-start | bytes 3145732
  1.3 27.6 %copy-start.1 = (s32[8,256,128]{2,1,0:T(8,128)S(1)}, s32[8,256,128]{2,1,0:T(8,128)}, u32[]{:S(2)}) copy-start(s32[8,256,128]{2,1,0:T(8,128)} %kind_in.3) | copy-start | bytes 3145732
  1.3 27.6 %copy-start.2 = (s32[3]{0:T(128)S(1)}, s32[3]{0:T(128)}, u32[]{:S(2)}) copy-start(s32[3]{0:T(128)} %pad_add_fusion.idx) | copy-start | bytes 40
  1.3 27.6 %copy-start.3 = (s32[32]{0:T(128)S(1)}, s32[32]{0:T(128)}, u32[]{:S(2)}) copy-start(s32[32]{0:T(128)} %sheet.3) | copy-start | bytes 388
  1.3 27.6 %copy-start.4 = (f32[16]{0:T(128)S(1)}, f32[16]{0:T(128)}, u32[]{:S(2)}) copy-start(f32[16]{0:T(128)} %table.3) | copy-start | bytes 196
  1.3 27.6 %copy-start.5 = (f32[4]{0:T(128)S(1)}, f32[4]{0:T(128)}, u32[]{:S(2)}) copy-start(f32[4]{0:T(128)} %scaling.3) | copy-start | bytes 52
  10.2 18.7 %all-to-all-start = ((f32[32,1,1408]{2,1,0:T(1,128)}), f32[32,1,1408]{2,1,0:T(1,128)S(1)}, u32[]{:S(2)}, u32[]{:S(2)}) async-start(f32[32,1,1408]{2,1,0:T(1,128)} %get-tuple-element.51), calls=%async_computation | async-start | bytes 360448 | tf_op jit(solution)/shard_map/all_to_all | solution.py:977
  17.5 11.4 %collective-permute-start.3 = (f32[2,256,128]{2,1,0:T(8,128)}, f32[2,256,128]{2,1,0:T(8,128)S(1)}, u32[]{:S(2)}, u32[]{:S(2)}) collective-permute-start(f32[2,256,128]{2,1,0:T(8,128)} %get-tuple-element.52), channel_id=1, source_target_pairs={{0,1},{1,0},{2,3},{3,2},{4,5},{5,4},{6,7},{7,6},{8,9},{9,8},{10,11... | collective-permute-start | bytes 786440 | tf_op jit(solution)/shard_map/ppermute | solution.py:153
  19.3 9.5 %collective-permute-start.4 = (f32[2,256,128]{2,1,0:T(8,128)}, f32[2,256,128]{2,1,0:T(8,128)S(1)}, u32[]{:S(2)}, u32[]{:S(2)}) collective-permute-start(f32[2,256,128]{2,1,0:T(8,128)} %get-tuple-element.53), channel_id=1, source_target_pairs={{1,2},{2,1},{5,6},{6,5},{9,10},{10,9},{13,14},{14,13},{17,18},{18,... | collective-permute-start | bytes 786440 | tf_op jit(solution)/shard_map/ppermute | solution.py:157
  20.0 4.0 %collective-permute-start.2 = (f32[256,128]{1,0:T(8,128)}, f32[256,128]{1,0:T(8,128)S(1)}, u32[]{:S(2)}, u32[]{:S(2)}) collective-permute-start(f32[256,128]{1,0:T(8,128)} %get-tuple-element.50), channel_id=1, source_target_pairs={{0,4},{4,0},{1,5},{5,1},{2,6},{6,2},{3,7},{7,3},{8,12},{12,8},{9,1... | collective-permute-start | bytes 393224 | tf_op jit(solution)/shard_map/ppermute | solution.py:153
  20.1 3.9 %collective-permute-start = (f32[2,8,128]{2,1,0:T(8,128)}, f32[2,8,128]{2,1,0:T(8,128)S(1)}, u32[]{:S(2)}, u32[]{:S(2)}) collective-permute-start(f32[2,8,128]{2,1,0:T(8,128)} %get-tuple-element.48), channel_id=1, source_target_pairs={{0,8},{8,0},{16,24},{24,16},{1,9},{9,1},{17,25},{25,17},{2,10},{10... | collective-permute-start | bytes 24584 | tf_op jit(solution)/shard_map/ppermute | solution.py:153
  21.6 2.4 %collective-permute-start.1 = (f32[2,8,128]{2,1,0:T(8,128)}, f32[2,8,128]{2,1,0:T(8,128)S(1)}, u32[]{:S(2)}, u32[]{:S(2)}) collective-permute-start(f32[2,8,128]{2,1,0:T(8,128)} %get-tuple-element.49), channel_id=1, source_target_pairs={{8,16},{16,8},{9,17},{17,9},{10,18},{18,10},{11,19},{19,11},{12,20... | collective-permute-start | bytes 24584 | tf_op jit(solution)/shard_map/ppermute | solution.py:157
  38.9 10.3 %collective-permute-start.5 = (f32[2,256,128]{2,1,0:T(8,128)S(1)}, f32[2,256,128]{2,1,0:T(8,128)S(1)}, u32[]{:S(2)}, u32[]{:S(2)}) collective-permute-start(f32[2,256,128]{2,1,0:T(8,128)S(1)} %get-tuple-element.57.pair), channel_id=1, source_target_pairs={{0,1},{1,0},{2,3},{3,2},{4,5},{5,4},{6,7},{7,6},{8,9},{9,8},{10,11... | collective-permute-start | bytes 786440 | tf_op jit(solution)/shard_map/ppermute | solution.py:148
  41.4 4.2 %collective-permute-start.6 = (f32[16,128]{1,0:T(8,128)S(1)}, f32[16,128]{1,0:T(8,128)S(1)}, u32[]{:S(2)}, u32[]{:S(2)}) collective-permute-start(f32[16,128]{1,0:T(8,128)S(1)} %get-tuple-element.58), channel_id=1, source_target_pairs={{0,8},{8,0},{16,24},{24,16},{1,9},{9,1},{17,25},{25,17},{2,10},{10... | collective-permute-start | bytes 24584 | tf_op jit(solution)/shard_map/ppermute | solution.py:142
  43.2 4.5 %collective-permute-start.8 = (f32[16,128]{1,0:T(8,128)S(1)}, f32[16,128]{1,0:T(8,128)S(1)}, u32[]{:S(2)}, u32[]{:S(2)}) collective-permute-start(f32[16,128]{1,0:T(8,128)S(1)} %get-tuple-element.59), channel_id=1, source_target_pairs={{0,24},{8,16},{16,8},{24,0},{1,25},{9,17},{17,9},{25,1},{2,26},{10... | collective-permute-start | bytes 24584 | tf_op jit(solution)/shard_map/ppermute | solution.py:142
  45.6 3.7 %collective-permute-start.7 = (f32[16,128]{1,0:T(8,128)S(1)}, f32[16,128]{1,0:T(8,128)S(1)}, u32[]{:S(2)}, u32[]{:S(2)}) collective-permute-start(f32[16,128]{1,0:T(8,128)S(1)} %get-tuple-element.59), channel_id=1, source_target_pairs={{0,16},{8,24},{16,0},{24,8},{1,17},{9,25},{17,1},{25,9},{2,18},{10... | collective-permute-start | bytes 24584 | tf_op jit(solution)/shard_map/ppermute | solution.py:142
  50.1 11.6 %collective-permute-start.10 = (f32[256,128]{1,0:T(8,128)S(1)}, f32[256,128]{1,0:T(8,128)S(1)}, u32[]{:S(2)}, u32[]{:S(2)}) collective-permute-start(f32[256,128]{1,0:T(8,128)S(1)} %get-tuple-element.77), channel_id=1, source_target_pairs={{0,2},{1,3},{2,0},{3,1},{4,6},{5,7},{6,4},{7,5},{8,10},{9,11},{10,... | collective-permute-start | bytes 393224 | tf_op jit(solution)/shard_map/ppermute | solution.py:148
  50.2 1.3 %collective-permute-start.9 = (f32[16,272]{1,0:T(8,128)S(1)}, f32[16,272]{1,0:T(8,128)S(1)}, u32[]{:S(2)}, u32[]{:S(2)}) collective-permute-start(f32[16,272]{1,0:T(8,128)S(1)} %get-tuple-element.62), channel_id=1, source_target_pairs={{0,4},{4,0},{1,5},{5,1},{2,6},{6,2},{3,7},{7,3},{8,12},{12,8},{9,1... | collective-permute-start | bytes 52232 | tf_op jit(solution)/shard_map/ppermute | solution.py:142
  52.5 4.8 %collective-permute-start.11 = (f32[72,128]{1,0:T(8,128)S(1)}, f32[72,128]{1,0:T(8,128)S(1)}, u32[]{:S(2)}, u32[]{:S(2)}) collective-permute-start(f32[72,128]{1,0:T(8,128)S(1)} %get-tuple-element.78), channel_id=1, source_target_pairs={{0,1},{1,0},{2,3},{3,2},{4,5},{5,4},{6,7},{7,6},{8,9},{9,8},{10,11... | collective-permute-start | bytes 110600 | tf_op jit(solution)/shard_map/ppermute | solution.py:142
  53.9 5.9 %collective-permute-start.13 = (f32[72,128]{1,0:T(8,128)S(1)}, f32[72,128]{1,0:T(8,128)S(1)}, u32[]{:S(2)}, u32[]{:S(2)}) collective-permute-start(f32[72,128]{1,0:T(8,128)S(1)} %get-tuple-element.79), channel_id=1, source_target_pairs={{0,3},{1,2},{2,1},{3,0},{4,7},{5,6},{6,5},{7,4},{8,11},{9,10},{10,... | collective-permute-start | bytes 110600 | tf_op jit(solution)/shard_map/ppermute | solution.py:142
  56.8 4.9 %collective-permute-start.12 = (f32[72,128]{1,0:T(8,128)S(1)}, f32[72,128]{1,0:T(8,128)S(1)}, u32[]{:S(2)}, u32[]{:S(2)}) collective-permute-start(f32[72,128]{1,0:T(8,128)S(1)} %get-tuple-element.79), channel_id=1, source_target_pairs={{0,2},{1,3},{2,0},{3,1},{4,6},{5,7},{6,4},{7,5},{8,10},{9,11},{10,... | collective-permute-start | bytes 110600 | tf_op jit(solution)/shard_map/ppermute | solution.py:142
  66.2 7.1 %collective-permute-start.14 = (f32[2,256,128]{2,1,0:T(8,128)S(1)}, f32[2,256,128]{2,1,0:T(8,128)S(1)}, u32[]{:S(2)}, u32[]{:S(2)}) collective-permute-start(f32[2,256,128]{2,1,0:T(8,128)S(1)} %get-tuple-element.82.pair), channel_id=1, source_target_pairs={{0,1},{1,0},{2,3},{3,2},{4,5},{5,4},{6,7},{7,6},{8,9},{9,8},{10,11... | collective-permute-start | bytes 786440 | tf_op jit(solution)/shard_map/ppermute | solution.py:148
  66.2 3.7 %collective-permute-start.15 = (f32[16,128]{1,0:T(8,128)S(1)}, f32[16,128]{1,0:T(8,128)S(1)}, u32[]{:S(2)}, u32[]{:S(2)}) collective-permute-start(f32[16,128]{1,0:T(8,128)S(1)} %get-tuple-element.83), channel_id=1, source_target_pairs={{0,8},{8,0},{16,24},{24,16},{1,9},{9,1},{17,25},{25,17},{2,10},{10... | collective-permute-start | bytes 24584 | tf_op jit(solution)/shard_map/ppermute | solution.py:142
  67.0 4.5 %collective-permute-start.17 = (f32[16,128]{1,0:T(8,128)S(1)}, f32[16,128]{1,0:T(8,128)S(1)}, u32[]{:S(2)}, u32[]{:S(2)}) collective-permute-start(f32[16,128]{1,0:T(8,128)S(1)} %get-tuple-element.84), channel_id=1, source_target_pairs={{0,24},{8,16},{16,8},{24,0},{1,25},{9,17},{17,9},{25,1},{2,26},{10... | collective-permute-start | bytes 24584 | tf_op jit(solution)/shard_map/ppermute | solution.py:142
  69.0 3.7 %collective-permute-start.16 = (f32[16,128]{1,0:T(8,128)S(1)}, f32[16,128]{1,0:T(8,128)S(1)}, u32[]{:S(2)}, u32[]{:S(2)}) collective-permute-start(f32[16,128]{1,0:T(8,128)S(1)} %get-tuple-element.84), channel_id=1, source_target_pairs={{0,16},{8,24},{16,0},{24,8},{1,17},{9,25},{17,1},{25,9},{2,18},{10... | collective-permute-start | bytes 24584 | tf_op jit(solution)/shard_map/ppermute | solution.py:142
  74.1 11.3 %collective-permute-start.19 = (f32[256,128]{1,0:T(8,128)S(1)}, f32[256,128]{1,0:T(8,128)S(1)}, u32[]{:S(2)}, u32[]{:S(2)}) collective-permute-start(f32[256,128]{1,0:T(8,128)S(1)} %get-tuple-element.91), channel_id=1, source_target_pairs={{0,2},{1,3},{2,0},{3,1},{4,6},{5,7},{6,4},{7,5},{8,10},{9,11},{10,... | collective-permute-start | bytes 393224 | tf_op jit(solution)/shard_map/ppermute | solution.py:148
  75.4 1.2 %collective-permute-start.18 = (f32[16,272]{1,0:T(8,128)S(1)}, f32[16,272]{1,0:T(8,128)S(1)}, u32[]{:S(2)}, u32[]{:S(2)}) collective-permute-start(f32[16,272]{1,0:T(8,128)S(1)} %get-tuple-element.87), channel_id=1, source_target_pairs={{0,4},{4,0},{1,5},{5,1},{2,6},{6,2},{3,7},{7,3},{8,12},{12,8},{9,1... | collective-permute-start | bytes 52232 | tf_op jit(solution)/shard_map/ppermute | solution.py:142
  77.3 4.6 %collective-permute-start.20 = (f32[72,128]{1,0:T(8,128)S(1)}, f32[72,128]{1,0:T(8,128)S(1)}, u32[]{:S(2)}, u32[]{:S(2)}) collective-permute-start(f32[72,128]{1,0:T(8,128)S(1)} %get-tuple-element.92), channel_id=1, source_target_pairs={{0,1},{1,0},{2,3},{3,2},{4,5},{5,4},{6,7},{7,6},{8,9},{9,8},{10,11... | collective-permute-start | bytes 110600 | tf_op jit(solution)/shard_map/ppermute | solution.py:142
  78.0 5.8 %collective-permute-start.22 = (f32[72,128]{1,0:T(8,128)S(1)}, f32[72,128]{1,0:T(8,128)S(1)}, u32[]{:S(2)}, u32[]{:S(2)}) collective-permute-start(f32[72,128]{1,0:T(8,128)S(1)} %get-tuple-element.93), channel_id=1, source_target_pairs={{0,3},{1,2},{2,1},{3,0},{4,7},{5,6},{6,5},{7,4},{8,11},{9,10},{10,... | collective-permute-start | bytes 110600 | tf_op jit(solution)/shard_map/ppermute | solution.py:142
  80.5 4.9 %collective-permute-start.21 = (f32[72,128]{1,0:T(8,128)S(1)}, f32[72,128]{1,0:T(8,128)S(1)}, u32[]{:S(2)}, u32[]{:S(2)}) collective-permute-start(f32[72,128]{1,0:T(8,128)S(1)} %get-tuple-element.93), channel_id=1, source_target_pairs={{0,2},{1,3},{2,0},{3,1},{4,6},{5,7},{6,4},{7,5},{8,10},{9,11},{10,... | collective-permute-start | bytes 110600 | tf_op jit(solution)/shard_map/ppermute | solution.py:142

commit v5 on v4

--- a/solution.py
+++ b/solution.py
@@ -19,9 +19,8 @@
 EXACT = lax.Precision.HIGHEST
 
 
-def call(kernel, out_shapes, args, smem=0, scratch=(), vmem=24, far=0, far_out=False):
-    specs = [pl.BlockSpec(memory_space=pltpu.SMEM)] * smem
-    specs += [pl.BlockSpec(memory_space=pltpu.VMEM)] * (len(args) - smem - far)
+def call(kernel, out_shapes, args, scratch=(), vmem=24, far=0, far_out=False):
+    specs = [pl.BlockSpec(memory_space=pltpu.VMEM)] * (len(args) - far)
     specs += [pl.BlockSpec(memory_space=pl.ANY)] * far
     return pl.pallas_call(
         kernel,
@@ -46,6 +45,10 @@
 
 def iota(shape, dim):
     return lax.broadcasted_iota(jnp.int32, shape, dim)
+
+
+def place():
+    return [lax.axis_index(axis) for axis in ("gx", "gy", "gz")]
 
 
 def copies(pairs, sems):
@@ -88,7 +91,7 @@
     return lax.dot_general(a, b, (((1,), (1,)), ((), ())), preferred_element_type=F32)
 
 
-def table_rows(planes, rows, columns, nx, ny, nz):
+def table_rows(planes, rows, columns, nx, ny, nz, classes):
     at, places = 0, {}
     for name, items, each in (
         ("lx", 1, rows + EXTRA),
@@ -102,6 +105,8 @@
         ("psz", planes + 2, 8),
         ("mz", 2, 128),
         ("wz", 1, 8),
+        ("cond", planes, 8),
+        ("kinds", classes, 8),
     ):
         places[name] = (at, each)
         at += items * each
@@ -157,17 +162,19 @@
     return first, lax.ppermute(odd, axis, pairs + [(b, a) for a, b in pairs])
 
 
-def conductance(z, idx, sheet, table, scaling, kind_ref):
-    factor = jnp.zeros(kind_ref.shape[1:], F32)
-    for category in range(scaling.shape[0]):
-        factor = jnp.where(kind_ref[z] == category, scaling[category], factor)
-    return table[sheet[idx[2] * kind_ref.shape[0] + z]] * factor
+def conductance(kind, own, scales):
+    factor = jnp.zeros(kind.shape, F32)
+    for category, scale in enumerate(scales):
+        factor = jnp.where(kind == category, scale, factor)
+    return own * factor
 
 
 def faces(
     idx, sheet, table, scaling, u_ref, kind_ref, started, xs0, xs1, ys0, ys1, zs0, zs1
 ):
     planes, rows, columns = u_ref.shape
+    own = [table[sheet[idx[2] * planes + z]] for z in range(planes)]
+    scales = [scaling[category] for category in range(scaling.shape[0])]
     even = [idx[d] % 2 == 0 for d in range(3)]
     lane = iota((rows, columns), 1)
     low = jnp.zeros((rows, columns), F32)
@@ -175,7 +182,7 @@
     for z in range(planes):
         started[0][z].wait()
         started[1][z].wait()
-        u, c = u_ref[z], conductance(z, idx, sheet, table, scaling, kind_ref)
+        u, c = u_ref[z], conductance(kind_ref[z], own[z], scales)
         if z == 0:
             zs0[1], zs1[1] = c, c
         elif z == planes - 1:
@@ -198,13 +205,18 @@
     return capacity // 4, capacity - capacity // 4
 
 
-def first_kernel(blocks, planes, area, capacity, idx, sheet, table, scaling,
-                 amps_in, ohms_in, tile_in, cell_in, u_in, kind_in,
+def first_kernel(blocks, planes, area, capacity,
+                 sheet_in, table_in, scaling_in, amps_in, ohms_in, tile_in, cell_in,
+                 u_in, kind_in,
                  send, xs0, xs1, ys0, ys1, zs0, zs1,
                  amps, ohms, tiles, cells, a_scr, b_scr, z_scr, k_scr, u_ref, kind_ref,
-                 sems, plane_sems):
+                 sheet, table, scaling, sems, plane_sems):
     started = copies(
-        [(amps_in, amps), (ohms_in, ohms), (tile_in, tiles), (cell_in, cells)], sems
+        [
+            (amps_in, amps), (ohms_in, ohms), (tile_in, tiles), (cell_in, cells),
+            (sheet_in, sheet), (table_in, table), (scaling_in, scaling),
+        ],
+        sems,
     )
     for copy in started:
         copy.start()
@@ -216,7 +228,7 @@
         a_scr, b_scr, z_scr, k_scr,
     )
     faces(
-        idx, sheet, table, scaling, u_ref, kind_ref, loads, xs0, xs1, ys0, ys1, zs0, zs1
+        place(), sheet, table, scaling, u_ref, kind_ref, loads, xs0, xs1, ys0, ys1, zs0, zs1
     )
 
 
@@ -383,13 +395,16 @@
     return theta, scale
 
 
-def coefficients(sizes, idx, sheet, table, gx_ref, gy_ref, co, z_scr):
-    planes, rows, columns, nx, ny, nz = sizes
+def coefficients(sizes, idx, sheet, table, scaling, gx_ref, gy_ref, co, z_scr):
+    planes, rows, columns, nx, ny, nz, classes = sizes
     lanes = 128
     extent = rows + EXTRA
-    lx, ax, by, dx, dxl, dy, cg, phz, psz, mz, wz = groups_of(
-        sizes, co, "lx", "ax", "by", "dx", "dxl", "dy", "cg", "phz", "psz", "mz", "wz"
-    )
+    lx, ax, by, dx, dxl, dy, cg, phz, psz, mz, wz, cond_rows, kind_rows = groups_of(
+        sizes, co, "lx", "ax", "by", "dx", "dxl", "dy", "cg", "phz", "psz", "mz", "wz",
+        "cond", "kinds",
+    )
+    for category in range(classes):
+        kind_rows[category] = jnp.full((8, lanes), scaling[category], F32)
     gx, gy, gz = idx[0], idx[1], idx[2]
     x0, xn = (gx * rows).astype(F32), float(nx * rows)
     y0, yn = (gy * columns).astype(F32), float(ny * columns)
@@ -411,6 +426,7 @@
     for z in range(planes):
         value = table[sheet[gz * planes + z]]
         own.append(value)
+        cond_rows[z] = jnp.full((8, lanes), value, F32)
         by_lane = jnp.where(lane_z == z, value, by_lane)
     theta_lane, scale_lane = line(by_lane, yn)
     theta_rows, _ = line(rows_of(gz * planes), 1.0)
@@ -551,7 +567,7 @@
 
 
 def slopes(
-    counts, idx, sheet, table, scaling, u_ref, kind_ref, xr0, xr1, yr0, yr1, zr0, zr1,
+    counts, idx, cond, scales, u_ref, kind_ref, xr0, xr1, yr0, yr1, zr0, zr1,
     ux, uy, uz, kx0, kx1, ky0, ky1, kz,
 ):
     planes, rows, columns = u_ref.shape
@@ -583,7 +599,7 @@
     y_low, y_high = ends(yr0[...], yr1[...], 1)
     c_before = None
     for z in range(planes):
-        c = conductance(z, idx, sheet, table, scaling, kind_ref)
+        c = conductance(kind_ref[z], cond[z][0:1, :], scales)
         first = jnp.where(at_low[0], -c[0:1, :], x_low[z : z + 1, :])
         final = jnp.where(at_high[0], -c[rows - 1 :, :], x_high[z : z + 1, :])
         kx0[z] = half * (c + jnp.where(row == 0, first, pltpu.roll(c, 1, 0)))
@@ -651,28 +667,32 @@
     z_send[0], z_send[1] = below, above
 
 
-def start_kernel(sizes, idx, sheet, table, scaling, xr0, xr1, yr0, yr1,
-                 got_in, u_in, kind_in, zr0_in, zr1_in, gx_ref, gy_ref, co, ux, uy, uz, kx0, kx1, ky0, ky1, kz,
-                 joule, t_ref, e_ref, *rest):
-    sends, scratch = rest[:-9], rest[-9:]
-    r_scr, k_scr, z_scr, got, u_ref, kind_ref, zr0, zr1, sems = scratch
+def joule_kernel(sizes, sheet_in, table_in, scaling_in, got_in, gx_ref, gy_ref, co, joule,
+                 r_scr, k_scr, z_scr, got, sheet, table, scaling, sems):
     started = copies(
         [
-            (got_in.at[:, 0, :], got), (u_in, u_ref), (kind_in, kind_ref),
-            (zr0_in, zr0), (zr1_in, zr1),
+            (sheet_in, sheet), (table_in, table), (scaling_in, scaling),
+            (got_in.at[:, 0, :], got),
         ],
         sems,
     )
     for copy in started:
         copy.start()
-    phz, psz = groups_of(sizes, co, "phz", "psz")
-    coefficients(sizes, idx, sheet, table, gx_ref, gy_ref, co, z_scr)
-    started[0].wait()
+    for copy in started[:3]:
+        copy.wait()
+    coefficients(sizes, place(), sheet, table, scaling, gx_ref, gy_ref, co, z_scr)
+    started[3].wait()
     joule_into(got, joule, r_scr, k_scr)
-    for copy in started[1:]:
-        copy.wait()
+
+
+def start_kernel(sizes, xr0, xr1, yr0, yr1, zr0, zr1,
+                 u_ref, kind_ref, gx_ref, gy_ref, co, joule,
+                 ux, uy, uz, kx0, kx1, ky0, ky1, kz, t_ref, e_ref, *sends):
+    idx = place()
+    phz, psz, cond, kinds = groups_of(sizes, co, "phz", "psz", "cond", "kinds")
+    scales = [kinds[category][0:1, :] for category in range(sizes[6])]
     slopes(
-        sizes[3:], idx, sheet, table, scaling, u_ref, kind_ref, xr0, xr1, yr0, yr1, zr0, zr1,
+        sizes[3:], idx, cond, scales, u_ref, kind_ref, xr0, xr1, yr0, yr1, zr0, zr1,
         ux, uy, uz, kx0, kx1, ky0, ky1, kz,
     )
 
@@ -685,7 +705,8 @@
     )
 
 
-def x_kernel(sizes, idx, e_ref, co, pair, near, *rest):
+def x_kernel(sizes, e_ref, co, pair, near, *rest):
+    idx = place()
     planes, nx = sizes[0], sizes[3]
     gots, (e_out, f_out, send), far = rest[: nx - 1], rest[nx - 1 : nx + 2], rest[nx + 2 :]
     for out in far:
@@ -724,7 +745,8 @@
     return values
 
 
-def y_kernel(sizes, final, idx, t_ref, e_ref, f_ref, co, *rest):
+def y_kernel(sizes, final, t_ref, e_ref, f_ref, co, *rest):
+    idx = place()
     ny = sizes[4]
     dy, lx, by, cg, phz, psz, mz = groups_of(
         sizes, co, "dy", "lx", "by", "cg", "phz", "psz", "mz"
@@ -755,9 +777,7 @@
     right = jnp.concatenate([f_ref[...], by[idx[2]]], axis=0)
     b_ref[...] = right
     low, high = weights(phz, planes), weights(psz, planes)
-    if final:
-        edge, g_low, g_high = jnp.zeros((8, rows), F32), 0.0, 0.0
-    else:
+    if not final:
         lane = iota((extent, 128), 1)
         q = jnp.where(lane < 2 * planes, e_ref[...], 0.0) + stacked(others, cg[0])
         q_ref[...] = q
@@ -770,18 +790,25 @@
             value = t_ref[z, ghost, :]
             g_low += phz[z + 1][0:1, :] * value
             g_high += psz[z + 1][0:1, :] * value
+    if ny == 2:
+        across = jnp.where(me == 1, across[:planes], across[planes:])
     for b, send in enumerate(sends):
         lower = (idx[2] >> b) % 2 == 0
         scale = jnp.where(lower, low, high)
-        twice = jnp.concatenate([scale] * 2, axis=0)
-        send[:8, :] = jnp.broadcast_to(jnp.where(lower, g_low, g_high), (8, 128))
-        send[8 : 8 + 2 * planes, :] = f_ref[...] * twice
-        at = 8 + 2 * planes
+        at = 0
+        if not final:
+            send[:2, :] = jnp.where(lower, g_low[:2], g_high[:2])
+            ends = jnp.where(lower, edge[:2], edge[2:4])
+            for part in range(rows // 128):
+                send[2 + 2 * part : 4 + 2 * part, :] = ends[:, part * 128 : (part + 1) * 128]
+            at = 8
+        send[at : at + 2 * planes, :] = f_ref[...] * jnp.concatenate([scale] * 2, axis=0)
+        at += 2 * planes
+        many = across.shape[0]
+        scale = jnp.concatenate([scale] * (many // planes), axis=0)
         for part in range(rows // 128):
-            cols = slice(part * 128, (part + 1) * 128)
-            send[at : at + 8, :] = edge[0:8, cols]
-            send[at + 8 : at + 8 + 2 * planes, :] = across[:, cols] * twice
-            at += 8 + 2 * planes
+            send[at : at + many, :] = across[:, part * 128 : (part + 1) * 128] * scale
+            at += many
 
 
 def carried(nz, idx, bigs, smalls, ax, by, rows, ghosts):
@@ -794,30 +821,43 @@
         at_top = (me >> b) % 2 == 1
         below += jnp.where(at_top, big[...], 0.0)
         above += jnp.where(at_top, 0.0, big[...])
-    g_below = g_above = edges = 0.0
+    g_below = g_above = 0.0
+    ends = [0.0, 0.0]
     lefts, rights = [], []
-    sub = iota((8, rows), 0)
     for k, small in zip(range(1, nz), smalls):
         other = partner(me, k, nz)
         lower = other < me
-
-        at, stride = 8 + 2 * planes, 8 + 2 * planes
-        parts = [at + p * stride for p in range(rows // 128)]
-        across = jnp.concatenate([small[p + 8 : p + stride, :] for p in parts], axis=1)
+        at = 0
         halves = rows // 128
+        if ghosts:
+            g_below += jnp.where(lower, small[:2, :], 0.0)
+            g_above += jnp.where(lower, 0.0, small[:2, :])
+            value = jnp.concatenate(
+                [small[2 + 2 * p : 4 + 2 * p, :] for p in range(halves)], axis=1
+            )
+            ends[0] += jnp.where(lower, value, 0.0)
+            ends[1] += jnp.where(lower, 0.0, value)
+            at = 8
+        both = at + 2 * planes
+        many = (small.shape[0] - both) // halves
+        across = [small[both + p * many : both + (p + 1) * many, :] for p in range(halves)]
         near = [ax[other * halves + half] for half in range(halves)]
-        lefts += [jnp.concatenate(near, axis=1), across]
-        right = jnp.concatenate([small[8:at, :], by[other]], axis=0)
+        lefts += [jnp.concatenate(near, axis=1), jnp.concatenate(across, axis=1)]
+        lines = by[other]
+        if many == planes:
+            lines = jnp.where(idx[1] == 1, lines[:planes], lines[planes:])
+        right = jnp.concatenate([small[at:both, :], lines], axis=0)
         rights.append(
             jnp.concatenate(
                 [jnp.where(lower, right, 0.0), jnp.where(lower, 0.0, right)], axis=1
             )
         )
-        if ghosts:
-            g_below += jnp.where(lower, small[:8, :], 0.0)
-            g_above += jnp.where(lower, 0.0, small[:8, :])
-            value = jnp.concatenate([small[p : p + 8, :] for p in parts], axis=1)
-            edges += jnp.where(sub // 2 == jnp.where(lower, 0, 1), value, 0.0)
+    edges = None
+    if ghosts:
+        edges = jnp.concatenate(ends + [jnp.zeros((4, rows), F32)], axis=0)
+        none = jnp.zeros((6, 128), F32)
+        g_below = jnp.concatenate([g_below, none], axis=0)
+        g_above = jnp.concatenate([g_above, none], axis=0)
     more = exact(
         jnp.concatenate(lefts, axis=0), jnp.concatenate(rights, axis=0), ((0,), (0,))
     )
@@ -855,8 +895,9 @@
         emit(planes, psz[planes + 1][0:1, :] * head + phz[planes + 1][0:1, :] * above)
 
 
-def rise_kernel(sizes, idx, t_in, l_ref, b_ref, q_ref, co,
+def rise_kernel(sizes, t_in, l_ref, b_ref, q_ref, co,
                 u_ref, ux, uy, uz, kx0, kx1, ky0, ky1, kz, joule, gx_ref, gy_ref, *rest):
+    idx = place()
     nz = sizes[5]
     phz, psz, mz, wz, ax, by = groups_of(sizes, co, "phz", "psz", "mz", "wz", "ax", "by")
     deep = (nz - 1).bit_length()
@@ -895,7 +936,8 @@
     )
 
 
-def finish_kernel(sizes, idx, t_in, l_ref, b_ref, co, u_ref, joule, *rest):
+def finish_kernel(sizes, t_in, l_ref, b_ref, co, u_ref, joule, *rest):
+    idx = place()
     nz = sizes[5]
     phz, psz, ax, by = groups_of(sizes, co, "phz", "psz", "ax", "by")
     deep = (nz - 1).bit_length()
@@ -936,9 +978,9 @@
     bits = [(n - 1).bit_length() for n in counts]
     devices = nx * ny * nz
     extent = rows + EXTRA
-    idx = jnp.stack([lax.axis_index(axis) for axis in ("gx", "gy", "gz")]).astype(jnp.int32)
     block = shaped(planes, rows, columns)
     tables = sheet_stratum_number, stratum_heat_conduction, substance_kind_scaling
+    scalars = [pltpu.SMEM(part.shape, part.dtype) for part in tables]
 
     count = wire_piece_amperes.shape[0]
     capacity = 2 * count // devices
@@ -958,9 +1000,8 @@
         + [shaped(2, planes, columns)] * 2
         + [shaped(rows, 128)] * 2
         + [shaped(2, rows, columns)] * 2,
-        (idx, *tables, *segments, starting_warmth, substance_kind),
-        smem=4,
-        far=6,
+        (*tables, *segments, starting_warmth, substance_kind),
+        far=9,
         vmem=60,
         scratch=[pltpu.VMEM((chunks, lanes), part.dtype) for part in segments]
         + [
@@ -970,7 +1011,8 @@
             pltpu.VMEM((chunks, lanes), jnp.int32),
             pltpu.VMEM(block.shape, F32),
             pltpu.VMEM(block.shape, jnp.int32),
-            pltpu.SemaphoreType.DMA((4,)),
+            *scalars,
+            pltpu.SemaphoreType.DMA((7,)),
             pltpu.SemaphoreType.DMA((2, planes)),
         ],
     )
@@ -979,7 +1021,7 @@
     zr = next_pairs(zs0, zs1, "gz")
     xr = next_pairs(xs0, xs1, "gx")
     yr = next_pairs(ys0, ys1, "gy")
-    sizes = (planes, rows, columns, nx, ny, nz)
+    sizes = (planes, rows, columns, nx, ny, nz, substance_kind_scaling.shape[0])
     parts = [
         shaped(planes, 2 * extent, rows, dtype=BF16),
         shaped(2 * planes, columns, 256, dtype=BF16),
@@ -989,28 +1031,30 @@
     step_out += [shaped(2, rows, columns)] + [shaped(planes + 8, columns)] * bits[0]
     total = devices * spare
     ghosts = [shaped(planes, 8, columns), shaped(extent, 128), shaped(2, rows, columns)]
-    gx_m, gy_m, co, ux, uy, uz, *rest = call(
-        functools.partial(start_kernel, sizes),
-        parts + ghosts + [block] * 4 + [shaped(planes + 1, rows, columns), block] + step_out,
-        (idx, *tables, *xr, *yr, got, starting_warmth, substance_kind, *zr),
-        smem=4,
-        far=5,
-        vmem=36,
+    gx_m, gy_m, co, joule = call(
+        functools.partial(joule_kernel, sizes),
+        parts + [block],
+        (*tables, got),
+        far=4,
+        vmem=24,
         scratch=[
             pltpu.VMEM((2 * columns, total), BF16),
             pltpu.VMEM((8, total), jnp.int32),
             pltpu.VMEM((2 * planes * nz + 4, 8, lanes), F32),
             pltpu.VMEM((devices, 2 * slots), F32),
-            pltpu.VMEM(block.shape, F32),
-            pltpu.VMEM(block.shape, jnp.int32),
-            pltpu.VMEM((2, rows, columns), F32),
-            pltpu.VMEM((2, rows, columns), F32),
-            pltpu.SemaphoreType.DMA((5,)),
+            *scalars,
+            pltpu.SemaphoreType.DMA((4,)),
         ],
     )
-    conduct, (joule, t, e, *sends) = rest[:5], rest[5:]
+    ux, uy, uz, *rest = call(
+        functools.partial(start_kernel, sizes),
+        ghosts + [block] * 4 + [shaped(planes + 1, rows, columns)] + step_out,
+        (*xr, *yr, *zr, starting_warmth, substance_kind, gx_m, gy_m, co, joule),
+    )
+    conduct, (t, e, *sends) = rest[:5], rest[5:]
     u = starting_warmth
-    small = shaped(8 + 2 * planes + (8 + 2 * planes) * (rows // 128), 128)
+    lines = planes if ny == 2 else 2 * planes
+    small_rows = 2 * planes + lines * (rows // 128)
     for repeat in range(STEPS):
         pair, *sends = sends
         gots = all_pairs(sends, "gx")
@@ -1019,18 +1063,17 @@
             functools.partial(x_kernel, sizes),
             [shaped(extent, 128), shaped(2 * planes, columns), shaped(2 * planes, extent)]
             + [shaped(rows, columns)] * (bits[2] - 1),
-            (idx, e, co, pair, near, *gots),
-            smem=1,
+            (e, co, pair, near, *gots),
         )
         bigs = [near] + [crossed(array, 2, "gz") for array in far]
         gots = all_pairs([send] * bits[1], "gy")
         final = repeat == STEPS - 1
         q = [] if final else [shaped(extent, 128)]
+        small = shaped(small_rows + (0 if final else 8), 128)
         left, right, *sends = call(
             functools.partial(y_kernel, sizes, final),
             [shaped(extent, 128), shaped(4 * planes, columns)] + q + [small] * bits[2],
-            (idx, t, e, f, co, *gots),
-            smem=1,
+            (t, e, f, co, *gots),
         )
         if final:
             smalls = all_pairs(sends, "gz")
@@ -1042,17 +1085,15 @@
                 [block, shaped(planes, 8, columns), shaped(extent, 128)]
                 + [shaped(2, rows, columns)]
                 + step_out,
-                (idx, t, left, right, q, co, u, ux, uy, uz, *conduct)
+                (t, left, right, q, co, u, ux, uy, uz, *conduct)
                 + (joule, gx_m, gy_m, *bigs, *smalls),
-                smem=1,
                 scratch=[pltpu.VMEM((planes, rows + 8, columns), F32)],
             )
     return tuple(
         call(
             functools.partial(finish_kernel, sizes),
             [block, block],
-            (idx, t, left, right, co, u, joule, *bigs, *smalls),
-            smem=1,
+            (t, left, right, co, u, joule, *bigs, *smalls),
             scratch=[pltpu.VMEM((planes, rows, columns), F32)] * 3
             + [pltpu.SemaphoreType.DMA((2, planes))],
             far_out=True,

time: 88.7 us -> 79.7 us (0.90)
  Pallas kernels: 29.8 us -> 25.5 us
  waiting for transfers between devices: 25.6 us -> 22.1 us
    ppermute x3, waiting for transfers between devices: 6.6 us -> 0.01 us  [next_pairs(): first = lax.ppermute(even, axis, [(i, i ^ 1) for i in range(n)])]
    all_to_all x1, waiting for transfers between devices: 0.01 us -> 4.44 us  [per_device(): lax.all_to_all(send, ('gx', 'gy', 'gz'), split_axis=0, concat_axis=0, til...]
    pallas_call x8 -> x9, Pallas kernels: 29.8 us -> 25.5 us  [call(): pl.pallas_call(kernel, out_shape=out_shapes, in_specs=specs, out_specs=[p...]
    ppermute x4, starting transfers between devices: 3.89 us -> 1.44 us  [crossed(): lax.ppermute(array, axis, [(i, i ^ k) for i in range(lax.axis_size(axis))])]
    ppermute x14, starting transfers between devices: 15.6 us -> 17.4 us  [all_pairs(): lax.ppermute(arrays[b], axis, [(i, i ^ k) for i in range(n)])]
  transfers between devices with their start and end apart: 24 -> 24, of which waited for: 16 -> 13; matrix products, arithmetic and copies ran while one was open for 0% -> 0% of each run, Pallas kernels for 2% -> 8%
where the time goes in v5:
time: 79.7 us; the launch traced here: 79.5 us
  starting transfers between devices  30.9 us (39%)
  Pallas kernels  25.5 us (32%)
  waiting for transfers between devices  22.1 us (28%)
  between operations  0.99 us (1%)
    pallas_call x9, Pallas kernels, call(): pl.pallas_call(kernel, out_shape=out_shapes, in_specs=specs, out_specs=[p...  25.5 us
    ppermute x14, waiting for transfers between devices, all_pairs(): lax.ppermute(arrays[b], axis, [(i, i ^ k) for i in range(n)])  17.6 us
    ppermute x14, starting transfers between devices, all_pairs(): lax.ppermute(arrays[b], axis, [(i, i ^ k) for i in range(n)])  17.4 us
    all_to_all x1, starting transfers between devices, per_device(): lax.all_to_all(send, ('gx', 'gy', 'gz'), split_axis=0, concat_axis=0, til...  7.3 us
    all_to_all x1, waiting for transfers between devices, per_device(): lax.all_to_all(send, ('gx', 'gy', 'gz'), split_axis=0, concat_axis=0, til...  4.44 us
    ppermute x3, starting transfers between devices, next_pairs(): first = lax.ppermute(even, axis, [(i, i ^ 1) for i in range(n)])  3.44 us
  transfers between devices with their start and end apart: 24, of which 13 were waited for; matrix products, arithmetic and copies ran while one was open for 0% of the time, Pallas kernels for 8%

profile of v5, /device:TPU:0, one launch (start us, length us, event | category | flops | bytes accessed | tf_op | source)
XLA Modules:
  0.0 79.5 jit_solution(10442260709055249072)
XLA Ops:
  0.6 0.0 copy-start.2
  0.6 0.0 copy-start.3
  0.7 0.0 copy-start.4
  0.7 0.0 copy-start
  0.7 0.0 copy-start.1
  0.7 8.1 %shard_map.104 = (f32[32,1,1408]{2,1,0:T(1,128)}, f32[2,8,128]{2,1,0:T(8,128)}, f32[2,8,128]{2,1,0:T(8,128)}, f32[256,128]{1,0:T(8,128)}, f32[256,128]{1,0:T(8,1...) custom-call(s32[32]{0:T(128)} %sheet_in.3, f32[16]{0:T(128)} %table_in.3, f32[4]{0:T(128)} %scaling_in.3, ...), custom_call_target="tpu_custom_call" | custom-call | bytes 1 | tf_op jit(solution)/shard_map/pallas_call | solution.py:25
  8.8 7.3 %all-to-all-start = ((f32[32,1,1408]{2,1,0:T(1,128)}), f32[32,1,1408]{2,1,0:T(1,128)S(1)}, u32[]{:S(2)}, u32[]{:S(2)}) async-start(f32[32,1,1408]{2,1,0:T(1,128)} %get-tuple-element.53), calls=%async_computation | async-start | bytes 360448 | tf_op jit(solution)/shard_map/all_to_all | solution.py:1019
  16.1 1.8 %collective-permute-start.3 = (f32[2,256,128]{2,1,0:T(8,128)}, f32[2,256,128]{2,1,0:T(8,128)S(1)}, u32[]{:S(2)}, u32[]{:S(2)}) collective-permute-start(f32[2,256,128]{2,1,0:T(8,128)} %get-tuple-element.51), channel_id=1, source_target_pairs={{0,1},{1,0},{2,3},{3,2},{4,5},{5,4},{6,7},{7,6},{8,9},{9,8},{10,11... | collective-permute-start | bytes 786440 | tf_op jit(solution)/shard_map/ppermute | solution.py:158
  17.9 0.7 collective-permute-start.4
  18.6 0.1 collective-permute-start.2
  18.7 1.5 %collective-permute-start = (f32[2,8,128]{2,1,0:T(8,128)}, f32[2,8,128]{2,1,0:T(8,128)S(1)}, u32[]{:S(2)}, u32[]{:S(2)}) collective-permute-start(f32[2,8,128]{2,1,0:T(8,128)} %get-tuple-element.48), channel_id=1, source_target_pairs={{0,8},{8,0},{16,24},{24,16},{1,9},{9,1},{17,25},{25,17},{2,10},{10... | collective-permute-start | bytes 24584 | tf_op jit(solution)/shard_map/ppermute | solution.py:158
  20.2 0.6 collective-permute-start.1
  20.9 4.4 %all-to-all-done.got_in = f32[32,1,1408]{2,1,0:T(1,128)S(1)} async-done(((f32[32,1,1408]{2,1,0:T(1,128)}), f32[32,1,1408]{2,1,0:T(1,128)S(1)}, u32[]{:S(2)}, u32[]{:S(2)}) %all-to-all-start) | async-done | bytes 180256 | tf_op jit(solution)/shard_map/all_to_all | solution.py:1019
  25.3 0.0 copy-done.2
  25.3 0.0 copy-done.3
  25.3 6.0 %shard_map.105 = (bf16[8,544,256]{2,1,0:T(8,128)(2,1)S(1)}, bf16[16,128,256]{2,1,0:T(8,128)(2,1)S(1)}, f32[1192,128]{1,0:T(8,128)S(1)}, f32[8,256,128]{2,1,0:T(8,128)S(1)}) custom-call(s32[32]{0:T(128)S(1)} %copy-done.2, f32[16]{0:T(128)S(1)} %copy-done.3, f32[4]{0:T(128)S(1)} %copy-done.4, f32[32,1,1408]{2,1,0:T(1,128)S(1)} %all-to-all-done.got_in), custom_call_target="tpu_custom_call" | custom-call | bytes 1 | tf_op jit(solution)/shard_map/pallas_call | solution.py:25
  31.4 0.0 collective-permute-done.xr0
  31.4 0.0 collective-permute-done.1.xr1
  31.4 0.0 collective-permute-done.2.yr0.yr1
  31.4 0.0 collective-permute-done.3.zr0
  31.4 0.0 collective-permute-done.4.zr1
  31.4 3.6 %shard_map.106 = (f32[8,8,128]{2,1,0:T(8,128)S(1)}, f32[272,128]{1,0:T(8,128)S(1)}, f32[2,256,128]{2,1,0:T(8,128)S(1)}, f32[8,256,128]{2,1,0:T(8,128)S(1)}, f32[...) custom-call(f32[2,8,128]{2,1,0:T(8,128)S(1)} %collective-permute-don, ...), custom_call_target="tpu_custom_call" | custom-call | bytes 1 | tf_op jit(solution)/shard_map/pallas_call | solution.py:25
  35.1 0.1 collective-permute-start.5
  35.2 4.0 %collective-permute-start.6 = (f32[16,128]{1,0:T(8,128)S(1)}, f32[16,128]{1,0:T(8,128)S(1)}, u32[]{:S(2)}, u32[]{:S(2)}) collective-permute-start(f32[16,128]{1,0:T(8,128)S(1)} %get-tuple-element.61), channel_id=1, source_target_pairs={{0,8},{8,0},{16,24},{24,16},{1,9},{9,1},{17,25},{25,17},{2,10},{10... | collective-permute-start | bytes 24584 | tf_op jit(solution)/shard_map/ppermute | solution.py:147
  39.2 0.5 collective-permute-start.8
  39.7 1.0 %collective-permute-start.7 = (f32[16,128]{1,0:T(8,128)S(1)}, f32[16,128]{1,0:T(8,128)S(1)}, u32[]{:S(2)}, u32[]{:S(2)}) collective-permute-start(f32[16,128]{1,0:T(8,128)S(1)} %get-tuple-element.62), channel_id=1, source_target_pairs={{0,16},{8,24},{16,0},{24,8},{1,17},{9,25},{17,1},{25,9},{2,18},{10... | collective-permute-start | bytes 24584 | tf_op jit(solution)/shard_map/ppermute | solution.py:147
  40.6 0.2 collective-permute-done.6.rest_0_
  40.8 2.9 %collective-permute-done.8.rest_2_ = f32[16,128]{1,0:T(8,128)S(1)} collective-permute-done((f32[16,128]{1,0:T(8,128)S(1)}, f32[16,128]{1,0:T(8,128)S(1)}, u32[]{:S(2)}, u32[]{:S(2)}) %collective-permute-start.8) | collective-permute-done | bytes 8224 | tf_op jit(solution)/shard_map/ppermute | solution.py:147
  43.7 0.0 collective-permute-done.7.rest_1_
  43.7 0.0 collective-permute-done.5.near.rest_0_
  43.7 0.3 shard_map.107
  44.0 0.2 collective-permute-start.10
  44.2 0.0 collective-permute-start.9
  44.2 1.2 %collective-permute-done.9.rest_0_ = f32[16,272]{1,0:T(8,128)S(1)} collective-permute-done((f32[16,272]{1,0:T(8,128)S(1)}, f32[16,272]{1,0:T(8,128)S(1)}, u32[]{:S(2)}, u32[]{:S(2)}) %collective-permute-start.9) | collective-permute-done | bytes 17440 | tf_op jit(solution)/shard_map/ppermute | solution.py:147
  45.4 0.5 shard_map.108
  45.9 1.4 %collective-permute-start.11 = (f32[40,128]{1,0:T(8,128)S(1)}, f32[40,128]{1,0:T(8,128)S(1)}, u32[]{:S(2)}, u32[]{:S(2)}) collective-permute-start(f32[40,128]{1,0:T(8,128)S(1)} %get-tuple-element.78), channel_id=1, source_target_pairs={{0,1},{1,0},{2,3},{3,2},{4,5},{5,4},{6,7},{7,6},{8,9},{9,8},{10,11... | collective-permute-start | bytes 61448 | tf_op jit(solution)/shard_map/ppermute | solution.py:147
  47.3 2.9 %collective-permute-start.13 = (f32[40,128]{1,0:T(8,128)S(1)}, f32[40,128]{1,0:T(8,128)S(1)}, u32[]{:S(2)}, u32[]{:S(2)}) collective-permute-start(f32[40,128]{1,0:T(8,128)S(1)} %get-tuple-element.79), channel_id=1, source_target_pairs={{0,3},{1,2},{2,1},{3,0},{4,7},{5,6},{6,5},{7,4},{8,11},{9,10},{10,... | collective-permute-start | bytes 61448 | tf_op jit(solution)/shard_map/ppermute | solution.py:147
  50.2 0.0 collective-permute-start.12
  50.2 0.4 collective-permute-done.11.rest_2_
  50.6 2.3 %collective-permute-done.13.rest_4_ = f32[40,128]{1,0:T(8,128)S(1)} collective-permute-done((f32[40,128]{1,0:T(8,128)S(1)}, f32[40,128]{1,0:T(8,128)S(1)}, u32[]{:S(2)}, u32[]{:S(2)}) %collective-permute-start.13) | collective-permute-done | bytes 20512 | tf_op jit(solution)/shard_map/ppermute | solution.py:147
  52.9 2.0 %collective-permute-done.12.rest_3_ = f32[40,128]{1,0:T(8,128)S(1)} collective-permute-done((f32[40,128]{1,0:T(8,128)S(1)}, f32[40,128]{1,0:T(8,128)S(1)}, u32[]{:S(2)}, u32[]{:S(2)}) %collective-permute-start.12) | collective-permute-done | bytes 20512 | tf_op jit(solution)/shard_map/ppermute | solution.py:147
  54.9 0.0 collective-permute-done.10.rest_1_
  54.9 4.0 %shard_map.109 = (f32[8,256,128]{2,1,0:T(8,128)S(1)}, f32[8,8,128]{2,1,0:T(8,128)}, f32[272,128]{1,0:T(8,128)}, f32[2,256,128]{2,1,0:T(8,128)}, f32[8,272,128]{2...) custom-call(f32[8,272,128]{2,1,0:T(8,128)S(1)} %get-tuple-element.58, ...), custom_call_target="tpu_custom_call" | custom-call | bytes 1 | tf_op jit(solution)/shard_map/pallas_call | solution.py:25
  58.9 0.0 collective-permute-start.14
  58.9 2.6 %collective-permute-start.15 = (f32[16,128]{1,0:T(8,128)S(1)}, f32[16,128]{1,0:T(8,128)S(1)}, u32[]{:S(2)}, u32[]{:S(2)}) collective-permute-start(f32[16,128]{1,0:T(8,128)S(1)} %get-tuple-element.83), channel_id=1, source_target_pairs={{0,8},{8,0},{16,24},{24,16},{1,9},{9,1},{17,25},{25,17},{2,10},{10... | collective-permute-start | bytes 24584 | tf_op jit(solution)/shard_map/ppermute | solution.py:147
  61.6 0.5 collective-permute-start.17
  62.1 1.0 %collective-permute-start.16 = (f32[16,128]{1,0:T(8,128)S(1)}, f32[16,128]{1,0:T(8,128)S(1)}, u32[]{:S(2)}, u32[]{:S(2)}) collective-permute-start(f32[16,128]{1,0:T(8,128)S(1)} %get-tuple-element.84), channel_id=1, source_target_pairs={{0,16},{8,24},{16,0},{24,8},{1,17},{9,25},{17,1},{25,9},{2,18},{10... | collective-permute-start | bytes 24584 | tf_op jit(solution)/shard_map/ppermute | solution.py:147
  63.0 0.2 collective-permute-done.15.rest_0_
  63.2 2.9 %collective-permute-done.17.rest_2_ = f32[16,128]{1,0:T(8,128)S(1)} collective-permute-done((f32[16,128]{1,0:T(8,128)S(1)}, f32[16,128]{1,0:T(8,128)S(1)}, u32[]{:S(2)}, u32[]{:S(2)}) %collective-permute-start.17) | collective-permute-done | bytes 8224 | tf_op jit(solution)/shard_map/ppermute | solution.py:147
  66.1 0.0 collective-permute-done.16.rest_1_
  66.1 0.0 collective-permute-done.14.near.rest_0_
  66.1 0.3 shard_map.110
  66.4 1.2 %collective-permute-start.19 = (f32[256,128]{1,0:T(8,128)S(1)}, f32[256,128]{1,0:T(8,128)S(1)}, u32[]{:S(2)}, u32[]{:S(2)}) collective-permute-start(f32[256,128]{1,0:T(8,128)S(1)} %get-tuple-element.91), channel_id=1, source_target_pairs={{0,2},{1,3},{2,0},{3,1},{4,6},{5,7},{6,4},{7,5},{8,10},{9,11},{10,... | collective-permute-start | bytes 393224 | tf_op jit(solution)/shard_map/ppermute | solution.py:153
  67.6 0.0 collective-permute-start.18
  67.6 1.2 %collective-permute-done.18.rest_0_ = f32[16,272]{1,0:T(8,128)S(1)} collective-permute-done((f32[16,272]{1,0:T(8,128)S(1)}, f32[16,272]{1,0:T(8,128)S(1)}, u32[]{:S(2)}, u32[]{:S(2)}) %collective-permute-start.18) | collective-permute-done | bytes 17440 | tf_op jit(solution)/shard_map/ppermute | solution.py:147
  68.8 0.2 shard_map.111
  69.0 0.4 collective-permute-start.20
  69.4 2.9 %collective-permute-start.22 = (f32[32,128]{1,0:T(8,128)S(1)}, f32[32,128]{1,0:T(8,128)S(1)}, u32[]{:S(2)}, u32[]{:S(2)}) collective-permute-start(f32[32,128]{1,0:T(8,128)S(1)} %get-tuple-element.93), channel_id=1, source_target_pairs={{0,3},{1,2},{2,1},{3,0},{4,7},{5,6},{6,5},{7,4},{8,11},{9,10},{10,... | collective-permute-start | bytes 49160 | tf_op jit(solution)/shard_map/ppermute | solution.py:147
  72.3 0.2 collective-permute-start.21
  72.5 0.2 collective-permute-done.20.rest_2_
  72.8 2.2 %collective-permute-done.22.rest_4_ = f32[32,128]{1,0:T(8,128)S(1)} collective-permute-done((f32[32,128]{1,0:T(8,128)S(1)}, f32[32,128]{1,0:T(8,128)S(1)}, u32[]{:S(2)}, u32[]{:S(2)}) %collective-permute-start.22) | collective-permute-done | bytes 16416 | tf_op jit(solution)/shard_map/ppermute | solution.py:147
  74.9 2.0 %collective-permute-done.21.rest_3_ = f32[32,128]{1,0:T(8,128)S(1)} collective-permute-done((f32[32,128]{1,0:T(8,128)S(1)}, f32[32,128]{1,0:T(8,128)S(1)}, u32[]{:S(2)}, u32[]{:S(2)}) %collective-permute-start.21) | collective-permute-done | bytes 16416 | tf_op jit(solution)/shard_map/ppermute | solution.py:147
  76.9 0.0 collective-permute-done.19.rest_1_
  76.9 2.4 %shard_map.112 = (f32[8,256,128]{2,1,0:T(8,128)}, f32[8,256,128]{2,1,0:T(8,128)}) custom-call(f32[8,272,128]{2,1,0:T(8,128)S(1)} %get-tuple-element.80.t_ref.t_in, f32[272,128]{1,0:T(8,128)S(1)} %get-tuple-element.88.l_ref, f32[32,128]{1,0:T(8,128)S(1)} %get-tuple-element.89.b_ref, f32[1192,128]{1,0:T(8,128)S(1)} %get-tuple-element.56.co, ...), custom_call_target="tpu_custom_call" | custom-call | bytes 1 | tf_op jit(solution)/shard_map/pallas_call | solution.py:25
  (3 shorter events, 0.0 us)
Async XLA Ops:
  0.6 24.7 %copy-start.2 = (s32[32]{0:T(128)S(1)}, s32[32]{0:T(128)}, u32[]{:S(2)}) copy-start(s32[32]{0:T(128)} %sheet_in.3) | copy-start | bytes 388
  0.6 24.7 %copy-start.3 = (f32[16]{0:T(128)S(1)}, f32[16]{0:T(128)}, u32[]{:S(2)}) copy-start(f32[16]{0:T(128)} %table_in.3) | copy-start | bytes 196
  0.7 24.7 %copy-start.4 = (f32[4]{0:T(128)S(1)}, f32[4]{0:T(128)}, u32[]{:S(2)}) copy-start(f32[4]{0:T(128)} %scaling_in.3) | copy-start | bytes 52
  0.7 30.8 %copy-start = (f32[8,256,128]{2,1,0:T(8,128)S(1)}, f32[8,256,128]{2,1,0:T(8,128)}, u32[]{:S(2)}) copy-start(f32[8,256,128]{2,1,0:T(8,128)} %u_ref.3) | copy-start | bytes 3145732
  0.7 30.8 %copy-start.1 = (s32[8,256,128]{2,1,0:T(8,128)S(1)}, s32[8,256,128]{2,1,0:T(8,128)}, u32[]{:S(2)}) copy-start(s32[8,256,128]{2,1,0:T(8,128)} %kind_ref.1) | copy-start | bytes 3145732
  8.8 16.5 %all-to-all-start = ((f32[32,1,1408]{2,1,0:T(1,128)}), f32[32,1,1408]{2,1,0:T(1,128)S(1)}, u32[]{:S(2)}, u32[]{:S(2)}) async-start(f32[32,1,1408]{2,1,0:T(1,128)} %get-tuple-element.53), calls=%async_computation | async-start | bytes 360448 | tf_op jit(solution)/shard_map/all_to_all | solution.py:1019
  16.1 15.3 %collective-permute-start.3 = (f32[2,256,128]{2,1,0:T(8,128)}, f32[2,256,128]{2,1,0:T(8,128)S(1)}, u32[]{:S(2)}, u32[]{:S(2)}) collective-permute-start(f32[2,256,128]{2,1,0:T(8,128)} %get-tuple-element.51), channel_id=1, source_target_pairs={{0,1},{1,0},{2,3},{3,2},{4,5},{5,4},{6,7},{7,6},{8,9},{9,8},{10,11... | collective-permute-start | bytes 786440 | tf_op jit(solution)/shard_map/ppermute | solution.py:158
  17.9 13.5 %collective-permute-start.4 = (f32[2,256,128]{2,1,0:T(8,128)}, f32[2,256,128]{2,1,0:T(8,128)S(1)}, u32[]{:S(2)}, u32[]{:S(2)}) collective-permute-start(f32[2,256,128]{2,1,0:T(8,128)} %get-tuple-element.52), channel_id=1, source_target_pairs={{1,2},{2,1},{5,6},{6,5},{9,10},{10,9},{13,14},{14,13},{17,18},{18,... | collective-permute-start | bytes 786440 | tf_op jit(solution)/shard_map/ppermute | solution.py:162
  18.6 12.8 %collective-permute-start.2 = (f32[256,128]{1,0:T(8,128)}, f32[256,128]{1,0:T(8,128)S(1)}, u32[]{:S(2)}, u32[]{:S(2)}) collective-permute-start(f32[256,128]{1,0:T(8,128)} %get-tuple-element.50), channel_id=1, source_target_pairs={{0,4},{4,0},{1,5},{5,1},{2,6},{6,2},{3,7},{7,3},{8,12},{12,8},{9,1... | collective-permute-start | bytes 393224 | tf_op jit(solution)/shard_map/ppermute | solution.py:158
  18.7 12.7 %collective-permute-start = (f32[2,8,128]{2,1,0:T(8,128)}, f32[2,8,128]{2,1,0:T(8,128)S(1)}, u32[]{:S(2)}, u32[]{:S(2)}) collective-permute-start(f32[2,8,128]{2,1,0:T(8,128)} %get-tuple-element.48), channel_id=1, source_target_pairs={{0,8},{8,0},{16,24},{24,16},{1,9},{9,1},{17,25},{25,17},{2,10},{10... | collective-permute-start | bytes 24584 | tf_op jit(solution)/shard_map/ppermute | solution.py:158
  20.2 11.1 %collective-permute-start.1 = (f32[2,8,128]{2,1,0:T(8,128)}, f32[2,8,128]{2,1,0:T(8,128)S(1)}, u32[]{:S(2)}, u32[]{:S(2)}) collective-permute-start(f32[2,8,128]{2,1,0:T(8,128)} %get-tuple-element.49), channel_id=1, source_target_pairs={{8,16},{16,8},{9,17},{17,9},{10,18},{18,10},{11,19},{19,11},{12,20... | collective-permute-start | bytes 24584 | tf_op jit(solution)/shard_map/ppermute | solution.py:162
  35.1 8.6 %collective-permute-start.5 = (f32[2,256,128]{2,1,0:T(8,128)S(1)}, f32[2,256,128]{2,1,0:T(8,128)S(1)}, u32[]{:S(2)}, u32[]{:S(2)}) collective-permute-start(f32[2,256,128]{2,1,0:T(8,128)S(1)} %get-tuple-element.60.pair), channel_id=1, source_target_pairs={{0,1},{1,0},{2,3},{3,2},{4,5},{5,4},{6,7},{7,6},{8,9},{9,8},{10,11... | collective-permute-start | bytes 786440 | tf_op jit(solution)/shard_map/ppermute | solution.py:153
  35.2 5.6 %collective-permute-start.6 = (f32[16,128]{1,0:T(8,128)S(1)}, f32[16,128]{1,0:T(8,128)S(1)}, u32[]{:S(2)}, u32[]{:S(2)}) collective-permute-start(f32[16,128]{1,0:T(8,128)S(1)} %get-tuple-element.61), channel_id=1, source_target_pairs={{0,8},{8,0},{16,24},{24,16},{1,9},{9,1},{17,25},{25,17},{2,10},{10... | collective-permute-start | bytes 24584 | tf_op jit(solution)/shard_map/ppermute | solution.py:147
  39.2 4.5 %collective-permute-start.8 = (f32[16,128]{1,0:T(8,128)S(1)}, f32[16,128]{1,0:T(8,128)S(1)}, u32[]{:S(2)}, u32[]{:S(2)}) collective-permute-start(f32[16,128]{1,0:T(8,128)S(1)} %get-tuple-element.62), channel_id=1, source_target_pairs={{0,24},{8,16},{16,8},{24,0},{1,25},{9,17},{17,9},{25,1},{2,26},{10... | collective-permute-start | bytes 24584 | tf_op jit(solution)/shard_map/ppermute | solution.py:147
  39.7 4.0 %collective-permute-start.7 = (f32[16,128]{1,0:T(8,128)S(1)}, f32[16,128]{1,0:T(8,128)S(1)}, u32[]{:S(2)}, u32[]{:S(2)}) collective-permute-start(f32[16,128]{1,0:T(8,128)S(1)} %get-tuple-element.62), channel_id=1, source_target_pairs={{0,16},{8,24},{16,0},{24,8},{1,17},{9,25},{17,1},{25,9},{2,18},{10... | collective-permute-start | bytes 24584 | tf_op jit(solution)/shard_map/ppermute | solution.py:147
  44.0 10.9 %collective-permute-start.10 = (f32[256,128]{1,0:T(8,128)S(1)}, f32[256,128]{1,0:T(8,128)S(1)}, u32[]{:S(2)}, u32[]{:S(2)}) collective-permute-start(f32[256,128]{1,0:T(8,128)S(1)} %get-tuple-element.77), channel_id=1, source_target_pairs={{0,2},{1,3},{2,0},{3,1},{4,6},{5,7},{6,4},{7,5},{8,10},{9,11},{10,... | collective-permute-start | bytes 393224 | tf_op jit(solution)/shard_map/ppermute | solution.py:153
  44.2 1.2 %collective-permute-start.9 = (f32[16,272]{1,0:T(8,128)S(1)}, f32[16,272]{1,0:T(8,128)S(1)}, u32[]{:S(2)}, u32[]{:S(2)}) collective-permute-start(f32[16,272]{1,0:T(8,128)S(1)} %get-tuple-element.65), channel_id=1, source_target_pairs={{0,4},{4,0},{1,5},{5,1},{2,6},{6,2},{3,7},{7,3},{8,12},{12,8},{9,1... | collective-permute-start | bytes 52232 | tf_op jit(solution)/shard_map/ppermute | solution.py:147
  45.9 4.7 %collective-permute-start.11 = (f32[40,128]{1,0:T(8,128)S(1)}, f32[40,128]{1,0:T(8,128)S(1)}, u32[]{:S(2)}, u32[]{:S(2)}) collective-permute-start(f32[40,128]{1,0:T(8,128)S(1)} %get-tuple-element.78), channel_id=1, source_target_pairs={{0,1},{1,0},{2,3},{3,2},{4,5},{5,4},{6,7},{7,6},{8,9},{9,8},{10,11... | collective-permute-start | bytes 61448 | tf_op jit(solution)/shard_map/ppermute | solution.py:147
  47.3 5.6 %collective-permute-start.13 = (f32[40,128]{1,0:T(8,128)S(1)}, f32[40,128]{1,0:T(8,128)S(1)}, u32[]{:S(2)}, u32[]{:S(2)}) collective-permute-start(f32[40,128]{1,0:T(8,128)S(1)} %get-tuple-element.79), channel_id=1, source_target_pairs={{0,3},{1,2},{2,1},{3,0},{4,7},{5,6},{6,5},{7,4},{8,11},{9,10},{10,... | collective-permute-start | bytes 61448 | tf_op jit(solution)/shard_map/ppermute | solution.py:147
  50.2 4.7 %collective-permute-start.12 = (f32[40,128]{1,0:T(8,128)S(1)}, f32[40,128]{1,0:T(8,128)S(1)}, u32[]{:S(2)}, u32[]{:S(2)}) collective-permute-start(f32[40,128]{1,0:T(8,128)S(1)} %get-tuple-element.79), channel_id=1, source_target_pairs={{0,2},{1,3},{2,0},{3,1},{4,6},{5,7},{6,4},{7,5},{8,10},{9,11},{10,... | collective-permute-start | bytes 61448 | tf_op jit(solution)/shard_map/ppermute | solution.py:147
  58.9 7.2 %collective-permute-start.14 = (f32[2,256,128]{2,1,0:T(8,128)S(1)}, f32[2,256,128]{2,1,0:T(8,128)S(1)}, u32[]{:S(2)}, u32[]{:S(2)}) collective-permute-start(f32[2,256,128]{2,1,0:T(8,128)S(1)} %get-tuple-element.82.pair), channel_id=1, source_target_pairs={{0,1},{1,0},{2,3},{3,2},{4,5},{5,4},{6,7},{7,6},{8,9},{9,8},{10,11... | collective-permute-start | bytes 786440 | tf_op jit(solution)/shard_map/ppermute | solution.py:153
  58.9 4.3 %collective-permute-start.15 = (f32[16,128]{1,0:T(8,128)S(1)}, f32[16,128]{1,0:T(8,128)S(1)}, u32[]{:S(2)}, u32[]{:S(2)}) collective-permute-start(f32[16,128]{1,0:T(8,128)S(1)} %get-tuple-element.83), channel_id=1, source_target_pairs={{0,8},{8,0},{16,24},{24,16},{1,9},{9,1},{17,25},{25,17},{2,10},{10... | collective-permute-start | bytes 24584 | tf_op jit(solution)/shard_map/ppermute | solution.py:147
  61.6 4.5 %collective-permute-start.17 = (f32[16,128]{1,0:T(8,128)S(1)}, f32[16,128]{1,0:T(8,128)S(1)}, u32[]{:S(2)}, u32[]{:S(2)}) collective-permute-start(f32[16,128]{1,0:T(8,128)S(1)} %get-tuple-element.84), channel_id=1, source_target_pairs={{0,24},{8,16},{16,8},{24,0},{1,25},{9,17},{17,9},{25,1},{2,26},{10... | collective-permute-start | bytes 24584 | tf_op jit(solution)/shard_map/ppermute | solution.py:147
  62.1 4.0 %collective-permute-start.16 = (f32[16,128]{1,0:T(8,128)S(1)}, f32[16,128]{1,0:T(8,128)S(1)}, u32[]{:S(2)}, u32[]{:S(2)}) collective-permute-start(f32[16,128]{1,0:T(8,128)S(1)} %get-tuple-element.84), channel_id=1, source_target_pairs={{0,16},{8,24},{16,0},{24,8},{1,17},{9,25},{17,1},{25,9},{2,18},{10... | collective-permute-start | bytes 24584 | tf_op jit(solution)/shard_map/ppermute | solution.py:147
  66.4 10.5 %collective-permute-start.19 = (f32[256,128]{1,0:T(8,128)S(1)}, f32[256,128]{1,0:T(8,128)S(1)}, u32[]{:S(2)}, u32[]{:S(2)}) collective-permute-start(f32[256,128]{1,0:T(8,128)S(1)} %get-tuple-element.91), channel_id=1, source_target_pairs={{0,2},{1,3},{2,0},{3,1},{4,6},{5,7},{6,4},{7,5},{8,10},{9,11},{10,... | collective-permute-start | bytes 393224 | tf_op jit(solution)/shard_map/ppermute | solution.py:153
  67.6 1.2 %collective-permute-start.18 = (f32[16,272]{1,0:T(8,128)S(1)}, f32[16,272]{1,0:T(8,128)S(1)}, u32[]{:S(2)}, u32[]{:S(2)}) collective-permute-start(f32[16,272]{1,0:T(8,128)S(1)} %get-tuple-element.87), channel_id=1, source_target_pairs={{0,4},{4,0},{1,5},{5,1},{2,6},{6,2},{3,7},{7,3},{8,12},{12,8},{9,1... | collective-permute-start | bytes 52232 | tf_op jit(solution)/shard_map/ppermute | solution.py:147
  69.0 3.8 %collective-permute-start.20 = (f32[32,128]{1,0:T(8,128)S(1)}, f32[32,128]{1,0:T(8,128)S(1)}, u32[]{:S(2)}, u32[]{:S(2)}) collective-permute-start(f32[32,128]{1,0:T(8,128)S(1)} %get-tuple-element.92), channel_id=1, source_target_pairs={{0,1},{1,0},{2,3},{3,2},{4,5},{5,4},{6,7},{7,6},{8,9},{9,8},{10,11... | collective-permute-start | bytes 49160 | tf_op jit(solution)/shard_map/ppermute | solution.py:147
  69.4 5.5 %collective-permute-start.22 = (f32[32,128]{1,0:T(8,128)S(1)}, f32[32,128]{1,0:T(8,128)S(1)}, u32[]{:S(2)}, u32[]{:S(2)}) collective-permute-start(f32[32,128]{1,0:T(8,128)S(1)} %get-tuple-element.93), channel_id=1, source_target_pairs={{0,3},{1,2},{2,1},{3,0},{4,7},{5,6},{6,5},{7,4},{8,11},{9,10},{10,... | collective-permute-start | bytes 49160 | tf_op jit(solution)/shard_map/ppermute | solution.py:147
  72.3 4.6 %collective-permute-start.21 = (f32[32,128]{1,0:T(8,128)S(1)}, f32[32,128]{1,0:T(8,128)S(1)}, u32[]{:S(2)}, u32[]{:S(2)}) collective-permute-start(f32[32,128]{1,0:T(8,128)S(1)} %get-tuple-element.93), channel_id=1, source_target_pairs={{0,2},{1,3},{2,0},{3,1},{4,6},{5,7},{6,4},{7,5},{8,10},{9,11},{10,... | collective-permute-start | bytes 49160 | tf_op jit(solution)/shard_map/ppermute | solution.py:147

commit v6 on v5

--- a/solution.py
+++ b/solution.py
@@ -16,7 +16,6 @@
 F32 = jnp.float32
 BF16 = jnp.bfloat16
 EXTRA = 16
-EXACT = lax.Precision.HIGHEST
 
 
 def call(kernel, out_shapes, args, scratch=(), vmem=24, far=0, far_out=False):
@@ -75,15 +74,25 @@
     return jnp.dot(a, b, preferred_element_type=F32)
 
 
-def exact(a, b, dims=((1,), (0,))):
-    return lax.dot_general(a, b, (dims, ((), ())), precision=EXACT, preferred_element_type=F32)
-
-
 def stacked(a, b):
     (a_high, a_low), (b_high, b_low) = split(a), split(b)
     return mm(
         jnp.concatenate([a_high, a_low, a_high], axis=1),
         jnp.concatenate([b_high, b_high, b_low], axis=0),
+    )
+
+
+def stacked_rows(a, b):
+    more = -a.shape[0] % 16
+    if more:
+        a = jnp.concatenate([a, jnp.zeros((more, a.shape[1]), F32)], axis=0)
+        b = jnp.concatenate([b, jnp.zeros((more, b.shape[1]), F32)], axis=0)
+    (a_high, a_low), (b_high, b_low) = split(a), split(b)
+    return lax.dot_general(
+        jnp.concatenate([a_high, a_low, a_high], axis=0),
+        jnp.concatenate([b_high, b_high, b_low], axis=0),
+        (((0,), (0,)), ((), ())),
+        preferred_element_type=F32,
     )
 
 
@@ -169,36 +178,28 @@
     return own * factor
 
 
-def faces(
-    idx, sheet, table, scaling, u_ref, kind_ref, started, xs0, xs1, ys0, ys1, zs0, zs1
-):
+def faces(idx, own, scales, u_ref, kind_ref, zc, xs, ys):
     planes, rows, columns = u_ref.shape
-    own = [table[sheet[idx[2] * planes + z]] for z in range(planes)]
-    scales = [scaling[category] for category in range(scaling.shape[0])]
-    even = [idx[d] % 2 == 0 for d in range(3)]
+    even = [idx[d] % 2 == 0 for d in range(2)]
     lane = iota((rows, columns), 1)
-    low = jnp.zeros((rows, columns), F32)
-    high = jnp.zeros((rows, columns), F32)
+    kept = [jnp.zeros((rows, columns), F32) for _ in range(ys.shape[0])]
     for z in range(planes):
-        started[0][z].wait()
-        started[1][z].wait()
-        u, c = u_ref[z], conductance(kind_ref[z], own[z], scales)
-        if z == 0:
-            zs0[1], zs1[1] = c, c
-        elif z == planes - 1:
-            zs0[1] = jnp.where(even[2], c, zs0[1])
-            zs1[1] = jnp.where(even[2], zs1[1], c)
+        u = u_ref[z]
+        if z in (0, planes - 1):
+            c = zc[min(z, 1)]
+        else:
+            c = conductance(kind_ref[z], own[z], scales)
         for slot, values in ((0, u), (1, c)):
             at = slot * planes + z
-            low = jnp.where(lane == at, pltpu.roll(values, at, 1) if at else values, low)
-            high = jnp.where(lane == at, pltpu.roll(values, at + 1, 1), high)
+            for k in range(len(kept)):
+                upper = even[1] if k == 0 else jnp.logical_not(even[1])
+                turned = pltpu.roll(values, at + jnp.where(upper, 1, 0), 1)
+                kept[k] = jnp.where(lane == at, turned, kept[k])
             first, last = values[0:1, :], values[rows - 1 : rows, :]
-            xs0[slot, z : z + 1, :] = jnp.where(even[0], last, first)
-            xs1[slot, z : z + 1, :] = jnp.where(even[0], first, last)
-    ys0[...] = jnp.where(even[1], high, low)
-    ys1[...] = jnp.where(even[1], low, high)
-    zs0[0] = jnp.where(even[2], u_ref[planes - 1], u_ref[0])
-    zs1[0] = jnp.where(even[2], u_ref[0], u_ref[planes - 1])
+            xs[0, slot, z : z + 1, :] = jnp.where(even[0], last, first)
+            xs[1, slot, z : z + 1, :] = jnp.where(even[0], first, last)
+    for k, value in enumerate(kept):
+        ys[k] = value
 
 
 def shares(capacity):
@@ -208,9 +209,10 @@
 def first_kernel(blocks, planes, area, capacity,
                  sheet_in, table_in, scaling_in, amps_in, ohms_in, tile_in, cell_in,
                  u_in, kind_in,
-                 send, xs0, xs1, ys0, ys1, zs0, zs1,
+                 send_out, xs0_out, xs1_out, ys_out, zs0_out, zs1_out,
+                 send, xs, ys, zc,
                  amps, ohms, tiles, cells, a_scr, b_scr, z_scr, k_scr, u_ref, kind_ref,
-                 sheet, table, scaling, sems, plane_sems):
+                 sheet, table, scaling, sems, plane_sems, out_sems):
     started = copies(
         [
             (amps_in, amps), (ohms_in, ohms), (tile_in, tiles), (cell_in, cells),
@@ -227,9 +229,34 @@
         blocks, planes, area, capacity, amps, ohms, tiles, cells, send,
         a_scr, b_scr, z_scr, k_scr,
     )
-    faces(
-        place(), sheet, table, scaling, u_ref, kind_ref, loads, xs0, xs1, ys0, ys1, zs0, zs1
-    )
+    idx = place()
+    even = idx[2] % 2 == 0
+    top = u_ref.shape[0] - 1
+    own = [table[sheet[idx[2] * planes + z]] for z in range(planes)]
+    scales = [scaling[category] for category in range(scaling.shape[0])]
+    stores = [(send, send_out)]
+    for copies_of_plane in zip(*loads):
+        for copy in copies_of_plane:
+            copy.wait()
+    zc[0] = conductance(kind_ref[0], own[0], scales)
+    zc[1] = conductance(kind_ref[top], own[top], scales)
+    for out, upper in ((zs0_out, even), (zs1_out, jnp.logical_not(even))):
+        stores.append((u_ref.at[jnp.where(upper, top, 0)], out.at[0]))
+        stores.append((zc.at[jnp.where(upper, 1, 0)], out.at[1]))
+    stored = copies(stores, out_sems)
+    for copy in stored:
+        copy.start()
+    faces(idx, own, scales, u_ref, kind_ref, zc, xs, ys)
+    last = [
+        pltpu.make_async_copy(src, dst, out_sems.at[len(stores) + k])
+        for k, (src, dst) in enumerate(
+            ((xs.at[0], xs0_out), (xs.at[1], xs1_out), (ys, ys_out))
+        )
+    ]
+    for copy in last:
+        copy.start()
+    for copy in stored + last:
+        copy.wait()
 
 
 def dispatch(blocks, planes, area, capacity, amps, ohms, tiles, cells, send,
@@ -858,9 +885,7 @@
         none = jnp.zeros((6, 128), F32)
         g_below = jnp.concatenate([g_below, none], axis=0)
         g_above = jnp.concatenate([g_above, none], axis=0)
-    more = exact(
-        jnp.concatenate(lefts, axis=0), jnp.concatenate(rights, axis=0), ((0,), (0,))
-    )
+    more = stacked_rows(jnp.concatenate(lefts, axis=0), jnp.concatenate(rights, axis=0))
     below, above = below + more[:, :128], above + more[:, 128:]
     return below, above, g_below, g_above, edges
 
@@ -923,7 +948,7 @@
         jnp.concatenate([above, g_above], axis=0),
         emit,
     )
-    grown = stacked(q_ref[:rows, :], mz[0]) + exact(edges, wz[0], ((0,), (0,)))
+    grown = stacked(q_ref[:rows, :], mz[0]) + stacked_rows(edges, wz[0])
     uy_out[...] = uy[...]
     uy_out[:rows, :] = uy[:rows, :] + grown
 
@@ -994,16 +1019,28 @@
     )
     share, spare = shares(capacity)
     slots = planes * share + spare
-    send, xs0, xs1, ys0, ys1, zs0, zs1 = call(
+    y_faces = 1 if ny == 2 else 2
+    send, xs0, xs1, ys, zs0, zs1 = call(
         functools.partial(first_kernel, devices, planes, rows * columns, capacity),
-        [shaped(devices, 1, 2 * slots)]
-        + [shaped(2, planes, columns)] * 2
-        + [shaped(rows, 128)] * 2
-        + [shaped(2, rows, columns)] * 2,
+        [
+            shaped(devices, 1, 2 * slots),
+            shaped(2, planes, columns),
+            shaped(2, planes, columns),
+            shaped(y_faces, rows, 128),
+            shaped(2, rows, columns),
+            shaped(2, rows, columns),
+        ],
         (*tables, *segments, starting_warmth, substance_kind),
         far=9,
+        far_out=True,
         vmem=60,
-        scratch=[pltpu.VMEM((chunks, lanes), part.dtype) for part in segments]
+        scratch=[
+            pltpu.VMEM((devices, 1, 2 * slots), F32),
+            pltpu.VMEM((2, 2, planes, columns), F32),
+            pltpu.VMEM((y_faces, rows, 128), F32),
+            pltpu.VMEM((2, rows, columns), F32),
+        ]
+        + [pltpu.VMEM((chunks, lanes), part.dtype) for part in segments]
         + [
             pltpu.VMEM((5 * devices, count), BF16),
             pltpu.VMEM((max(planes * share, spare), count), BF16),
@@ -1014,13 +1051,14 @@
             *scalars,
             pltpu.SemaphoreType.DMA((7,)),
             pltpu.SemaphoreType.DMA((2, planes)),
+            pltpu.SemaphoreType.DMA((8,)),
         ],
     )
     got = lax.all_to_all(send, ("gx", "gy", "gz"), split_axis=0, concat_axis=0, tiled=True)
 
     zr = next_pairs(zs0, zs1, "gz")
     xr = next_pairs(xs0, xs1, "gx")
-    yr = next_pairs(ys0, ys1, "gy")
+    yr = next_pairs(ys[0], ys[-1], "gy")
     sizes = (planes, rows, columns, nx, ny, nz, substance_kind_scaling.shape[0])
     parts = [
         shaped(planes, 2 * extent, rows, dtype=BF16),

time: 79.7 us -> 78.2 us (0.981)
  Pallas kernels: 25.5 us -> 23.9 us
    pallas_call x9, Pallas kernels: 25.5 us -> 23.9 us  [call(): pl.pallas_call(kernel, out_shape=out_shapes, in_specs=specs, out_specs=[p...]
  transfers between devices with their start and end apart: 24 -> 24, of which waited for: 13 -> 13; matrix products, arithmetic and copies ran while one was open for 0% -> 0% of each run, Pallas kernels for 8% -> 9%
where the time goes in v6:
time: 78.2 us; the launch traced here: 78 us
  starting transfers between devices  31 us (40%)
  Pallas kernels  23.9 us (31%)
  waiting for transfers between devices  22.1 us (28%)
  between operations  0.99 us (1%)
    pallas_call x9, Pallas kernels, call(): pl.pallas_call(kernel, out_shape=out_shapes, in_specs=specs, out_specs=[p...  23.9 us
    ppermute x14, waiting for transfers between devices, all_pairs(): lax.ppermute(arrays[b], axis, [(i, i ^ k) for i in range(n)])  17.6 us
    ppermute x14, starting transfers between devices, all_pairs(): lax.ppermute(arrays[b], axis, [(i, i ^ k) for i in range(n)])  17.4 us
    all_to_all x1, starting transfers between devices, per_device(): lax.all_to_all(send, ('gx', 'gy', 'gz'), split_axis=0, concat_axis=0, til...  7.31 us
    all_to_all x1, waiting for transfers between devices, per_device(): lax.all_to_all(send, ('gx', 'gy', 'gz'), split_axis=0, concat_axis=0, til...  4.44 us
    ppermute x3, starting transfers between devices, next_pairs(): first = lax.ppermute(even, axis, [(i, i ^ 1) for i in range(n)])  3.44 us
  transfers between devices with their start and end apart: 24, of which 13 were waited for; matrix products, arithmetic and copies ran while one was open for 0% of the time, Pallas kernels for 9%

profile of v6, /device:TPU:0, one launch (start us, length us, event | category | flops | bytes accessed | tf_op | source)
XLA Modules:
  0.0 78.0 jit_solution(11811035159512095719)
XLA Ops:
  0.6 0.0 copy-start.2
  0.6 0.0 copy-start.3
  0.7 0.0 copy-start.4
  0.7 0.0 copy-start
  0.7 0.0 copy-start.1
  0.7 7.0 %shard_map.104 = (f32[32,1,1408]{2,1,0:T(1,128)}, f32[2,8,128]{2,1,0:T(8,128)}, f32[2,8,128]{2,1,0:T(8,128)}, f32[1,256,128]{2,1,0:T(8,128)}, f32[2,256,128]{2,1,0:T(8,128)}, /*index=5*/f32[2,256,128]{2,1,0:T(8,128)}) custom-call(s32[32]{0:T(128)} %sheet_in.3, f32[16]{0:T(128)} %table_in.3, f32[4]{0:T(128)} %scaling_in.3, f32[32,128]{1,0:T(8,128)} %bitcast.5, ...), custom_call_target="tpu_custom_call" | custom-call | bytes 1 | tf_op jit(solution)/shard_map/pallas_call | solution.py:24
  7.7 7.3 %all-to-all-start = ((f32[32,1,1408]{2,1,0:T(1,128)}), f32[32,1,1408]{2,1,0:T(1,128)S(1)}, u32[]{:S(2)}, u32[]{:S(2)}) async-start(f32[32,1,1408]{2,1,0:T(1,128)} %get-tuple-element.53), calls=%async_computation | async-start | bytes 360448 | tf_op jit(solution)/shard_map/all_to_all | solution.py:1057
  15.0 1.8 %collective-permute-start.3 = (f32[2,256,128]{2,1,0:T(8,128)}, f32[2,256,128]{2,1,0:T(8,128)S(1)}, u32[]{:S(2)}, u32[]{:S(2)}) collective-permute-start(f32[2,256,128]{2,1,0:T(8,128)} %get-tuple-element.51), channel_id=1, source_target_pairs={{0,1},{1,0},{2,3},{3,2},{4,5},{5,4},{6,7},{7,6},{8,9},{9,8},{10,11... | collective-permute-start | bytes 786440 | tf_op jit(solution)/shard_map/ppermute | solution.py:167
  16.9 0.7 collective-permute-start.4
  17.5 0.1 collective-permute-start.2
  17.6 1.5 %collective-permute-start = (f32[2,8,128]{2,1,0:T(8,128)}, f32[2,8,128]{2,1,0:T(8,128)S(1)}, u32[]{:S(2)}, u32[]{:S(2)}) collective-permute-start(f32[2,8,128]{2,1,0:T(8,128)} %get-tuple-element.48), channel_id=1, source_target_pairs={{0,8},{8,0},{16,24},{24,16},{1,9},{9,1},{17,25},{25,17},{2,10},{10... | collective-permute-start | bytes 24584 | tf_op jit(solution)/shard_map/ppermute | solution.py:167
  19.1 0.6 collective-permute-start.1
  19.8 4.4 %all-to-all-done.got_in = f32[32,1,1408]{2,1,0:T(1,128)S(1)} async-done(((f32[32,1,1408]{2,1,0:T(1,128)}), f32[32,1,1408]{2,1,0:T(1,128)S(1)}, u32[]{:S(2)}, u32[]{:S(2)}) %all-to-all-start) | async-done | bytes 180256 | tf_op jit(solution)/shard_map/all_to_all | solution.py:1057
  24.2 0.0 copy-done.2
  24.2 0.0 copy-done.3
  24.2 6.0 %shard_map.105 = (bf16[8,544,256]{2,1,0:T(8,128)(2,1)S(1)}, bf16[16,128,256]{2,1,0:T(8,128)(2,1)S(1)}, f32[1192,128]{1,0:T(8,128)S(1)}, f32[8,256,128]{2,1,0:T(8,128)S(1)}) custom-call(s32[32]{0:T(128)S(1)} %copy-done.2, f32[16]{0:T(128)S(1)} %copy-done.3, f32[4]{0:T(128)S(1)} %copy-done.4, f32[32,1,1408]{2,1,0:T(1,128)S(1)} %all-to-all-done.got_in), custom_call_target="tpu_custom_call" | custom-call | bytes 1 | tf_op jit(solution)/shard_map/pallas_call | solution.py:24
  30.3 0.0 collective-permute-done.xr0
  30.3 0.0 collective-permute-done.1.xr1
  30.3 0.0 collective-permute-done.2.yr0.yr1
  30.3 0.0 collective-permute-done.3.zr0
  30.3 0.0 collective-permute-done.4.zr1
  30.3 3.6 %shard_map.106 = (f32[8,8,128]{2,1,0:T(8,128)S(1)}, f32[272,128]{1,0:T(8,128)S(1)}, f32[2,256,128]{2,1,0:T(8,128)S(1)}, f32[8,256,128]{2,1,0:T(8,128)S(1)}, f32[...) custom-call(f32[2,8,128]{2,1,0:T(8,128)S(1)} %collective-permute-don, ...), custom_call_target="tpu_custom_call" | custom-call | bytes 1 | tf_op jit(solution)/shard_map/pallas_call | solution.py:24
  34.0 0.1 collective-permute-start.5
  34.1 4.0 %collective-permute-start.6 = (f32[16,128]{1,0:T(8,128)S(1)}, f32[16,128]{1,0:T(8,128)S(1)}, u32[]{:S(2)}, u32[]{:S(2)}) collective-permute-start(f32[16,128]{1,0:T(8,128)S(1)} %get-tuple-element.61), channel_id=1, source_target_pairs={{0,8},{8,0},{16,24},{24,16},{1,9},{9,1},{17,25},{25,17},{2,10},{10... | collective-permute-start | bytes 24584 | tf_op jit(solution)/shard_map/ppermute | solution.py:156
  38.1 0.5 collective-permute-start.8
  38.6 1.0 %collective-permute-start.7 = (f32[16,128]{1,0:T(8,128)S(1)}, f32[16,128]{1,0:T(8,128)S(1)}, u32[]{:S(2)}, u32[]{:S(2)}) collective-permute-start(f32[16,128]{1,0:T(8,128)S(1)} %get-tuple-element.62), channel_id=1, source_target_pairs={{0,16},{8,24},{16,0},{24,8},{1,17},{9,25},{17,1},{25,9},{2,18},{10... | collective-permute-start | bytes 24584 | tf_op jit(solution)/shard_map/ppermute | solution.py:156
  39.5 0.2 collective-permute-done.6.rest_0_
  39.7 2.9 %collective-permute-done.8.rest_2_ = f32[16,128]{1,0:T(8,128)S(1)} collective-permute-done((f32[16,128]{1,0:T(8,128)S(1)}, f32[16,128]{1,0:T(8,128)S(1)}, u32[]{:S(2)}, u32[]{:S(2)}) %collective-permute-start.8) | collective-permute-done | bytes 8224 | tf_op jit(solution)/shard_map/ppermute | solution.py:156
  42.6 0.0 collective-permute-done.7.rest_1_
  42.6 0.0 collective-permute-done.5.near.rest_0_
  42.6 0.3 shard_map.107
  42.9 0.2 collective-permute-start.10
  43.1 0.0 collective-permute-start.9
  43.1 1.2 %collective-permute-done.9.rest_0_ = f32[16,272]{1,0:T(8,128)S(1)} collective-permute-done((f32[16,272]{1,0:T(8,128)S(1)}, f32[16,272]{1,0:T(8,128)S(1)}, u32[]{:S(2)}, u32[]{:S(2)}) %collective-permute-start.9) | collective-permute-done | bytes 17440 | tf_op jit(solution)/shard_map/ppermute | solution.py:156
  44.3 0.5 shard_map.108
  44.8 1.4 %collective-permute-start.11 = (f32[40,128]{1,0:T(8,128)S(1)}, f32[40,128]{1,0:T(8,128)S(1)}, u32[]{:S(2)}, u32[]{:S(2)}) collective-permute-start(f32[40,128]{1,0:T(8,128)S(1)} %get-tuple-element.78), channel_id=1, source_target_pairs={{0,1},{1,0},{2,3},{3,2},{4,5},{5,4},{6,7},{7,6},{8,9},{9,8},{10,11... | collective-permute-start | bytes 61448 | tf_op jit(solution)/shard_map/ppermute | solution.py:156
  46.2 2.9 %collective-permute-start.13 = (f32[40,128]{1,0:T(8,128)S(1)}, f32[40,128]{1,0:T(8,128)S(1)}, u32[]{:S(2)}, u32[]{:S(2)}) collective-permute-start(f32[40,128]{1,0:T(8,128)S(1)} %get-tuple-element.79), channel_id=1, source_target_pairs={{0,3},{1,2},{2,1},{3,0},{4,7},{5,6},{6,5},{7,4},{8,11},{9,10},{10,... | collective-permute-start | bytes 61448 | tf_op jit(solution)/shard_map/ppermute | solution.py:156
  49.1 0.0 collective-permute-start.12
  49.1 0.4 collective-permute-done.11.rest_2_
  49.5 2.3 %collective-permute-done.13.rest_4_ = f32[40,128]{1,0:T(8,128)S(1)} collective-permute-done((f32[40,128]{1,0:T(8,128)S(1)}, f32[40,128]{1,0:T(8,128)S(1)}, u32[]{:S(2)}, u32[]{:S(2)}) %collective-permute-start.13) | collective-permute-done | bytes 20512 | tf_op jit(solution)/shard_map/ppermute | solution.py:156
  51.8 2.0 %collective-permute-done.12.rest_3_ = f32[40,128]{1,0:T(8,128)S(1)} collective-permute-done((f32[40,128]{1,0:T(8,128)S(1)}, f32[40,128]{1,0:T(8,128)S(1)}, u32[]{:S(2)}, u32[]{:S(2)}) %collective-permute-start.12) | collective-permute-done | bytes 20512 | tf_op jit(solution)/shard_map/ppermute | solution.py:156
  53.8 0.0 collective-permute-done.10.rest_1_
  53.8 3.8 %shard_map.109 = (f32[8,256,128]{2,1,0:T(8,128)S(1)}, f32[8,8,128]{2,1,0:T(8,128)}, f32[272,128]{1,0:T(8,128)}, f32[2,256,128]{2,1,0:T(8,128)}, f32[8,272,128]{2...) custom-call(f32[8,272,128]{2,1,0:T(8,128)S(1)} %get-tuple-element.58, ...), custom_call_target="tpu_custom_call" | custom-call | bytes 1 | tf_op jit(solution)/shard_map/pallas_call | solution.py:24
  57.6 0.0 collective-permute-start.14
  57.6 2.6 %collective-permute-start.15 = (f32[16,128]{1,0:T(8,128)S(1)}, f32[16,128]{1,0:T(8,128)S(1)}, u32[]{:S(2)}, u32[]{:S(2)}) collective-permute-start(f32[16,128]{1,0:T(8,128)S(1)} %get-tuple-element.83), channel_id=1, source_target_pairs={{0,8},{8,0},{16,24},{24,16},{1,9},{9,1},{17,25},{25,17},{2,10},{10... | collective-permute-start | bytes 24584 | tf_op jit(solution)/shard_map/ppermute | solution.py:156
  60.2 0.5 collective-permute-start.17
  60.7 1.0 %collective-permute-start.16 = (f32[16,128]{1,0:T(8,128)S(1)}, f32[16,128]{1,0:T(8,128)S(1)}, u32[]{:S(2)}, u32[]{:S(2)}) collective-permute-start(f32[16,128]{1,0:T(8,128)S(1)} %get-tuple-element.84), channel_id=1, source_target_pairs={{0,16},{8,24},{16,0},{24,8},{1,17},{9,25},{17,1},{25,9},{2,18},{10... | collective-permute-start | bytes 24584 | tf_op jit(solution)/shard_map/ppermute | solution.py:156
  61.7 0.2 collective-permute-done.15.rest_0_
  61.8 2.9 %collective-permute-done.17.rest_2_ = f32[16,128]{1,0:T(8,128)S(1)} collective-permute-done((f32[16,128]{1,0:T(8,128)S(1)}, f32[16,128]{1,0:T(8,128)S(1)}, u32[]{:S(2)}, u32[]{:S(2)}) %collective-permute-start.17) | collective-permute-done | bytes 8224 | tf_op jit(solution)/shard_map/ppermute | solution.py:156
  64.8 0.0 collective-permute-done.16.rest_1_
  64.8 0.0 collective-permute-done.14.near.rest_0_
  64.8 0.3 shard_map.110
  65.0 1.2 %collective-permute-start.19 = (f32[256,128]{1,0:T(8,128)S(1)}, f32[256,128]{1,0:T(8,128)S(1)}, u32[]{:S(2)}, u32[]{:S(2)}) collective-permute-start(f32[256,128]{1,0:T(8,128)S(1)} %get-tuple-element.91), channel_id=1, source_target_pairs={{0,2},{1,3},{2,0},{3,1},{4,6},{5,7},{6,4},{7,5},{8,10},{9,11},{10,... | collective-permute-start | bytes 393224 | tf_op jit(solution)/shard_map/ppermute | solution.py:162
  66.2 0.0 collective-permute-start.18
  66.3 1.2 %collective-permute-done.18.rest_0_ = f32[16,272]{1,0:T(8,128)S(1)} collective-permute-done((f32[16,272]{1,0:T(8,128)S(1)}, f32[16,272]{1,0:T(8,128)S(1)}, u32[]{:S(2)}, u32[]{:S(2)}) %collective-permute-start.18) | collective-permute-done | bytes 17440 | tf_op jit(solution)/shard_map/ppermute | solution.py:156
  67.4 0.2 shard_map.111
  67.6 0.4 collective-permute-start.20
  68.0 2.9 %collective-permute-start.22 = (f32[32,128]{1,0:T(8,128)S(1)}, f32[32,128]{1,0:T(8,128)S(1)}, u32[]{:S(2)}, u32[]{:S(2)}) collective-permute-start(f32[32,128]{1,0:T(8,128)S(1)} %get-tuple-element.93), channel_id=1, source_target_pairs={{0,3},{1,2},{2,1},{3,0},{4,7},{5,6},{6,5},{7,4},{8,11},{9,10},{10,... | collective-permute-start | bytes 49160 | tf_op jit(solution)/shard_map/ppermute | solution.py:156
  70.9 0.2 collective-permute-start.21
  71.2 0.2 collective-permute-done.20.rest_2_
  71.4 2.2 %collective-permute-done.22.rest_4_ = f32[32,128]{1,0:T(8,128)S(1)} collective-permute-done((f32[32,128]{1,0:T(8,128)S(1)}, f32[32,128]{1,0:T(8,128)S(1)}, u32[]{:S(2)}, u32[]{:S(2)}) %collective-permute-start.22) | collective-permute-done | bytes 16416 | tf_op jit(solution)/shard_map/ppermute | solution.py:156
  73.6 2.0 %collective-permute-done.21.rest_3_ = f32[32,128]{1,0:T(8,128)S(1)} collective-permute-done((f32[32,128]{1,0:T(8,128)S(1)}, f32[32,128]{1,0:T(8,128)S(1)}, u32[]{:S(2)}, u32[]{:S(2)}) %collective-permute-start.21) | collective-permute-done | bytes 16416 | tf_op jit(solution)/shard_map/ppermute | solution.py:156
  75.6 0.0 collective-permute-done.19.rest_1_
  75.6 2.3 %shard_map.112 = (f32[8,256,128]{2,1,0:T(8,128)}, f32[8,256,128]{2,1,0:T(8,128)}) custom-call(f32[8,272,128]{2,1,0:T(8,128)S(1)} %get-tuple-element.80.t_ref.t_in, f32[272,128]{1,0:T(8,128)S(1)} %get-tuple-element.88.l_ref, f32[32,128]{1,0:T(8,128)S(1)} %get-tuple-element.89.b_ref, f32[1192,128]{1,0:T(8,128)S(1)} %get-tuple-element.56.co, ...), custom_call_target="tpu_custom_call" | custom-call | bytes 1 | tf_op jit(solution)/shard_map/pallas_call | solution.py:24
  (3 shorter events, 0.0 us)
Async XLA Ops:
  0.6 23.6 %copy-start.2 = (s32[32]{0:T(128)S(1)}, s32[32]{0:T(128)}, u32[]{:S(2)}) copy-start(s32[32]{0:T(128)} %sheet_in.3) | copy-start | bytes 388
  0.6 23.6 %copy-start.3 = (f32[16]{0:T(128)S(1)}, f32[16]{0:T(128)}, u32[]{:S(2)}) copy-start(f32[16]{0:T(128)} %table_in.3) | copy-start | bytes 196
  0.7 23.6 %copy-start.4 = (f32[4]{0:T(128)S(1)}, f32[4]{0:T(128)}, u32[]{:S(2)}) copy-start(f32[4]{0:T(128)} %scaling_in.3) | copy-start | bytes 52
  0.7 29.7 %copy-start = (f32[8,256,128]{2,1,0:T(8,128)S(1)}, f32[8,256,128]{2,1,0:T(8,128)}, u32[]{:S(2)}) copy-start(f32[8,256,128]{2,1,0:T(8,128)} %u_ref.3) | copy-start | bytes 3145732
  0.7 29.7 %copy-start.1 = (s32[8,256,128]{2,1,0:T(8,128)S(1)}, s32[8,256,128]{2,1,0:T(8,128)}, u32[]{:S(2)}) copy-start(s32[8,256,128]{2,1,0:T(8,128)} %kind_ref.1) | copy-start | bytes 3145732
  7.7 16.5 %all-to-all-start = ((f32[32,1,1408]{2,1,0:T(1,128)}), f32[32,1,1408]{2,1,0:T(1,128)S(1)}, u32[]{:S(2)}, u32[]{:S(2)}) async-start(f32[32,1,1408]{2,1,0:T(1,128)} %get-tuple-element.53), calls=%async_computation | async-start | bytes 360448 | tf_op jit(solution)/shard_map/all_to_all | solution.py:1057
  15.0 15.3 %collective-permute-start.3 = (f32[2,256,128]{2,1,0:T(8,128)}, f32[2,256,128]{2,1,0:T(8,128)S(1)}, u32[]{:S(2)}, u32[]{:S(2)}) collective-permute-start(f32[2,256,128]{2,1,0:T(8,128)} %get-tuple-element.51), channel_id=1, source_target_pairs={{0,1},{1,0},{2,3},{3,2},{4,5},{5,4},{6,7},{7,6},{8,9},{9,8},{10,11... | collective-permute-start | bytes 786440 | tf_op jit(solution)/shard_map/ppermute | solution.py:167
  16.9 13.5 %collective-permute-start.4 = (f32[2,256,128]{2,1,0:T(8,128)}, f32[2,256,128]{2,1,0:T(8,128)S(1)}, u32[]{:S(2)}, u32[]{:S(2)}) collective-permute-start(f32[2,256,128]{2,1,0:T(8,128)} %get-tuple-element.52), channel_id=1, source_target_pairs={{1,2},{2,1},{5,6},{6,5},{9,10},{10,9},{13,14},{14,13},{17,18},{18,... | collective-permute-start | bytes 786440 | tf_op jit(solution)/shard_map/ppermute | solution.py:171
  17.5 12.8 %collective-permute-start.2 = (f32[256,128]{1,0:T(8,128)}, f32[256,128]{1,0:T(8,128)S(1)}, u32[]{:S(2)}, u32[]{:S(2)}) collective-permute-start(f32[256,128]{1,0:T(8,128)} %bitcast.9), channel_id=1, source_target_pairs={{0,4},{4,0},{1,5},{5,1},{2,6},{6,2},{3,7},{7,3},{8,12},{12,8},{9,1... | collective-permute-start | bytes 393224 | tf_op jit(solution)/shard_map/ppermute | solution.py:167
  17.6 12.7 %collective-permute-start = (f32[2,8,128]{2,1,0:T(8,128)}, f32[2,8,128]{2,1,0:T(8,128)S(1)}, u32[]{:S(2)}, u32[]{:S(2)}) collective-permute-start(f32[2,8,128]{2,1,0:T(8,128)} %get-tuple-element.48), channel_id=1, source_target_pairs={{0,8},{8,0},{16,24},{24,16},{1,9},{9,1},{17,25},{25,17},{2,10},{10... | collective-permute-start | bytes 24584 | tf_op jit(solution)/shard_map/ppermute | solution.py:167
  19.1 11.1 %collective-permute-start.1 = (f32[2,8,128]{2,1,0:T(8,128)}, f32[2,8,128]{2,1,0:T(8,128)S(1)}, u32[]{:S(2)}, u32[]{:S(2)}) collective-permute-start(f32[2,8,128]{2,1,0:T(8,128)} %get-tuple-element.49), channel_id=1, source_target_pairs={{8,16},{16,8},{9,17},{17,9},{10,18},{18,10},{11,19},{19,11},{12,20... | collective-permute-start | bytes 24584 | tf_op jit(solution)/shard_map/ppermute | solution.py:171
  34.0 8.6 %collective-permute-start.5 = (f32[2,256,128]{2,1,0:T(8,128)S(1)}, f32[2,256,128]{2,1,0:T(8,128)S(1)}, u32[]{:S(2)}, u32[]{:S(2)}) collective-permute-start(f32[2,256,128]{2,1,0:T(8,128)S(1)} %get-tuple-element.60.pair), channel_id=1, source_target_pairs={{0,1},{1,0},{2,3},{3,2},{4,5},{5,4},{6,7},{7,6},{8,9},{9,8},{10,11... | collective-permute-start | bytes 786440 | tf_op jit(solution)/shard_map/ppermute | solution.py:162
  34.1 5.6 %collective-permute-start.6 = (f32[16,128]{1,0:T(8,128)S(1)}, f32[16,128]{1,0:T(8,128)S(1)}, u32[]{:S(2)}, u32[]{:S(2)}) collective-permute-start(f32[16,128]{1,0:T(8,128)S(1)} %get-tuple-element.61), channel_id=1, source_target_pairs={{0,8},{8,0},{16,24},{24,16},{1,9},{9,1},{17,25},{25,17},{2,10},{10... | collective-permute-start | bytes 24584 | tf_op jit(solution)/shard_map/ppermute | solution.py:156
  38.1 4.5 %collective-permute-start.8 = (f32[16,128]{1,0:T(8,128)S(1)}, f32[16,128]{1,0:T(8,128)S(1)}, u32[]{:S(2)}, u32[]{:S(2)}) collective-permute-start(f32[16,128]{1,0:T(8,128)S(1)} %get-tuple-element.62), channel_id=1, source_target_pairs={{0,24},{8,16},{16,8},{24,0},{1,25},{9,17},{17,9},{25,1},{2,26},{10... | collective-permute-start | bytes 24584 | tf_op jit(solution)/shard_map/ppermute | solution.py:156
  38.6 4.0 %collective-permute-start.7 = (f32[16,128]{1,0:T(8,128)S(1)}, f32[16,128]{1,0:T(8,128)S(1)}, u32[]{:S(2)}, u32[]{:S(2)}) collective-permute-start(f32[16,128]{1,0:T(8,128)S(1)} %get-tuple-element.62), channel_id=1, source_target_pairs={{0,16},{8,24},{16,0},{24,8},{1,17},{9,25},{17,1},{25,9},{2,18},{10... | collective-permute-start | bytes 24584 | tf_op jit(solution)/shard_map/ppermute | solution.py:156
  42.9 10.9 %collective-permute-start.10 = (f32[256,128]{1,0:T(8,128)S(1)}, f32[256,128]{1,0:T(8,128)S(1)}, u32[]{:S(2)}, u32[]{:S(2)}) collective-permute-start(f32[256,128]{1,0:T(8,128)S(1)} %get-tuple-element.77), channel_id=1, source_target_pairs={{0,2},{1,3},{2,0},{3,1},{4,6},{5,7},{6,4},{7,5},{8,10},{9,11},{10,... | collective-permute-start | bytes 393224 | tf_op jit(solution)/shard_map/ppermute | solution.py:162
  43.1 1.2 %collective-permute-start.9 = (f32[16,272]{1,0:T(8,128)S(1)}, f32[16,272]{1,0:T(8,128)S(1)}, u32[]{:S(2)}, u32[]{:S(2)}) collective-permute-start(f32[16,272]{1,0:T(8,128)S(1)} %get-tuple-element.65), channel_id=1, source_target_pairs={{0,4},{4,0},{1,5},{5,1},{2,6},{6,2},{3,7},{7,3},{8,12},{12,8},{9,1... | collective-permute-start | bytes 52232 | tf_op jit(solution)/shard_map/ppermute | solution.py:156
  44.8 4.7 %collective-permute-start.11 = (f32[40,128]{1,0:T(8,128)S(1)}, f32[40,128]{1,0:T(8,128)S(1)}, u32[]{:S(2)}, u32[]{:S(2)}) collective-permute-start(f32[40,128]{1,0:T(8,128)S(1)} %get-tuple-element.78), channel_id=1, source_target_pairs={{0,1},{1,0},{2,3},{3,2},{4,5},{5,4},{6,7},{7,6},{8,9},{9,8},{10,11... | collective-permute-start | bytes 61448 | tf_op jit(solution)/shard_map/ppermute | solution.py:156
  46.2 5.6 %collective-permute-start.13 = (f32[40,128]{1,0:T(8,128)S(1)}, f32[40,128]{1,0:T(8,128)S(1)}, u32[]{:S(2)}, u32[]{:S(2)}) collective-permute-start(f32[40,128]{1,0:T(8,128)S(1)} %get-tuple-element.79), channel_id=1, source_target_pairs={{0,3},{1,2},{2,1},{3,0},{4,7},{5,6},{6,5},{7,4},{8,11},{9,10},{10,... | collective-permute-start | bytes 61448 | tf_op jit(solution)/shard_map/ppermute | solution.py:156
  49.1 4.7 %collective-permute-start.12 = (f32[40,128]{1,0:T(8,128)S(1)}, f32[40,128]{1,0:T(8,128)S(1)}, u32[]{:S(2)}, u32[]{:S(2)}) collective-permute-start(f32[40,128]{1,0:T(8,128)S(1)} %get-tuple-element.79), channel_id=1, source_target_pairs={{0,2},{1,3},{2,0},{3,1},{4,6},{5,7},{6,4},{7,5},{8,10},{9,11},{10,... | collective-permute-start | bytes 61448 | tf_op jit(solution)/shard_map/ppermute | solution.py:156
  57.6 7.2 %collective-permute-start.14 = (f32[2,256,128]{2,1,0:T(8,128)S(1)}, f32[2,256,128]{2,1,0:T(8,128)S(1)}, u32[]{:S(2)}, u32[]{:S(2)}) collective-permute-start(f32[2,256,128]{2,1,0:T(8,128)S(1)} %get-tuple-element.82.pair), channel_id=1, source_target_pairs={{0,1},{1,0},{2,3},{3,2},{4,5},{5,4},{6,7},{7,6},{8,9},{9,8},{10,11... | collective-permute-start | bytes 786440 | tf_op jit(solution)/shard_map/ppermute | solution.py:162
  57.6 4.3 %collective-permute-start.15 = (f32[16,128]{1,0:T(8,128)S(1)}, f32[16,128]{1,0:T(8,128)S(1)}, u32[]{:S(2)}, u32[]{:S(2)}) collective-permute-start(f32[16,128]{1,0:T(8,128)S(1)} %get-tuple-element.83), channel_id=1, source_target_pairs={{0,8},{8,0},{16,24},{24,16},{1,9},{9,1},{17,25},{25,17},{2,10},{10... | collective-permute-start | bytes 24584 | tf_op jit(solution)/shard_map/ppermute | solution.py:156
  60.2 4.5 %collective-permute-start.17 = (f32[16,128]{1,0:T(8,128)S(1)}, f32[16,128]{1,0:T(8,128)S(1)}, u32[]{:S(2)}, u32[]{:S(2)}) collective-permute-start(f32[16,128]{1,0:T(8,128)S(1)} %get-tuple-element.84), channel_id=1, source_target_pairs={{0,24},{8,16},{16,8},{24,0},{1,25},{9,17},{17,9},{25,1},{2,26},{10... | collective-permute-start | bytes 24584 | tf_op jit(solution)/shard_map/ppermute | solution.py:156
  60.7 4.0 %collective-permute-start.16 = (f32[16,128]{1,0:T(8,128)S(1)}, f32[16,128]{1,0:T(8,128)S(1)}, u32[]{:S(2)}, u32[]{:S(2)}) collective-permute-start(f32[16,128]{1,0:T(8,128)S(1)} %get-tuple-element.84), channel_id=1, source_target_pairs={{0,16},{8,24},{16,0},{24,8},{1,17},{9,25},{17,1},{25,9},{2,18},{10... | collective-permute-start | bytes 24584 | tf_op jit(solution)/shard_map/ppermute | solution.py:156
  65.0 10.5 %collective-permute-start.19 = (f32[256,128]{1,0:T(8,128)S(1)}, f32[256,128]{1,0:T(8,128)S(1)}, u32[]{:S(2)}, u32[]{:S(2)}) collective-permute-start(f32[256,128]{1,0:T(8,128)S(1)} %get-tuple-element.91), channel_id=1, source_target_pairs={{0,2},{1,3},{2,0},{3,1},{4,6},{5,7},{6,4},{7,5},{8,10},{9,11},{10,... | collective-permute-start | bytes 393224 | tf_op jit(solution)/shard_map/ppermute | solution.py:162
  66.2 1.2 %collective-permute-start.18 = (f32[16,272]{1,0:T(8,128)S(1)}, f32[16,272]{1,0:T(8,128)S(1)}, u32[]{:S(2)}, u32[]{:S(2)}) collective-permute-start(f32[16,272]{1,0:T(8,128)S(1)} %get-tuple-element.87), channel_id=1, source_target_pairs={{0,4},{4,0},{1,5},{5,1},{2,6},{6,2},{3,7},{7,3},{8,12},{12,8},{9,1... | collective-permute-start | bytes 52232 | tf_op jit(solution)/shard_map/ppermute | solution.py:156
  67.6 3.8 %collective-permute-start.20 = (f32[32,128]{1,0:T(8,128)S(1)}, f32[32,128]{1,0:T(8,128)S(1)}, u32[]{:S(2)}, u32[]{:S(2)}) collective-permute-start(f32[32,128]{1,0:T(8,128)S(1)} %get-tuple-element.92), channel_id=1, source_target_pairs={{0,1},{1,0},{2,3},{3,2},{4,5},{5,4},{6,7},{7,6},{8,9},{9,8},{10,11... | collective-permute-start | bytes 49160 | tf_op jit(solution)/shard_map/ppermute | solution.py:156
  68.0 5.5 %collective-permute-start.22 = (f32[32,128]{1,0:T(8,128)S(1)}, f32[32,128]{1,0:T(8,128)S(1)}, u32[]{:S(2)}, u32[]{:S(2)}) collective-permute-start(f32[32,128]{1,0:T(8,128)S(1)} %get-tuple-element.93), channel_id=1, source_target_pairs={{0,3},{1,2},{2,1},{3,0},{4,7},{5,6},{6,5},{7,4},{8,11},{9,10},{10,... | collective-permute-start | bytes 49160 | tf_op jit(solution)/shard_map/ppermute | solution.py:156
  70.9 4.6 %collective-permute-start.21 = (f32[32,128]{1,0:T(8,128)S(1)}, f32[32,128]{1,0:T(8,128)S(1)}, u32[]{:S(2)}, u32[]{:S(2)}) collective-permute-start(f32[32,128]{1,0:T(8,128)S(1)} %get-tuple-element.93), channel_id=1, source_target_pairs={{0,2},{1,3},{2,0},{3,1},{4,6},{5,7},{6,4},{7,5},{8,10},{9,11},{10,... | collective-permute-start | bytes 49160 | tf_op jit(solution)/shard_map/ppermute | solution.py:156

commit v7 on v6

--- a/solution.py
+++ b/solution.py
@@ -190,7 +190,7 @@
         else:
             c = conductance(kind_ref[z], own[z], scales)
         for slot, values in ((0, u), (1, c)):
-            at = slot * planes + z
+            at = 2 * (slot * planes + z)
             for k in range(len(kept)):
                 upper = even[1] if k == 0 else jnp.logical_not(even[1])
                 turned = pltpu.roll(values, at + jnp.where(upper, 1, 0), 1)
@@ -277,7 +277,8 @@
         plane.astype(F32),
     ]
     key_row, block_row = iota((keys, lanes), 0), iota((blocks, lanes), 0)
-    place = iota((main, lanes), 0)
+    place = iota((main, lanes), 0).astype(jnp.int16)
+    one, none = jnp.ones((main, lanes), BF16), jnp.zeros((main, lanes), BF16)
     pair = 2 * lanes
     ahead = jnp.where(iota((pair, pair), 0) < iota((pair, pair), 1), 1.0, 0.0).astype(BF16)
     base = jnp.zeros((keys, lanes), F32)
@@ -292,7 +293,7 @@
             rank = rank.astype(jnp.int32)
             k_scr[row, :] = rank
             slot = jnp.where(rank < share, plane[row, :] * share + rank, -1)
-            b_scr[:main, cols] = jnp.where(place == slot, 1.0, 0.0).astype(BF16)
+            b_scr[:main, cols] = jnp.where(place == slot.astype(jnp.int16), one, none)
             hit = block_row == tile[row, :]
             for n, piece in enumerate(pieces):
                 a_scr[n * blocks : (n + 1) * blocks, cols] = jnp.where(
@@ -447,7 +448,6 @@
         return value
 
     lane_z = iota((8, lanes), 1) % planes
-    lane_e = iota((8, lanes), 1) // planes
     by_lane = jnp.ones((8, lanes), F32)
     own = []
     for z in range(planes):
@@ -563,9 +563,11 @@
         psz[z] = jnp.where(mine + z == 0, zero, z_scr[total + 2 + mine + z])
 
     low_lane, high_lane = zero, zero
+    pair_z = iota((8, lanes), 1) // 2
+    side = jnp.where(pair_z < planes, 1 - iota((8, lanes), 1) % 2, -1)
     for z in range(planes):
-        low_lane = jnp.where(lane_z == z, phz[z + 1], low_lane)
-        high_lane = jnp.where(lane_z == z, psz[z + 1], high_lane)
+        low_lane = jnp.where(pair_z == z, phz[z + 1], low_lane)
+        high_lane = jnp.where(pair_z == z, psz[z + 1], high_lane)
     row_p, lane_p = iota((planes, lanes), 0), iota((planes, lanes), 1)
     low_rows, high_rows = jnp.zeros((planes, lanes), F32), jnp.zeros((planes, lanes), F32)
     for z in range(planes):
@@ -574,11 +576,11 @@
     blocks, ends = [], []
     for e in range(2):
         g = jnp.where(
-            lane_p % planes >= row_p,
+            lane_p // 2 >= row_p,
             low_rows * high_lane[0:1, :],
             high_rows * low_lane[0:1, :],
         )
-        blocks.append(jnp.where(lane_p // planes == e, g, 0.0))
+        blocks.append(jnp.where(side[0:1, :] == e, g, 0.0))
         ends.append(
             jnp.where(lane_p == e, low_rows, jnp.where(lane_p == 2 + e, high_rows, 0.0))
         )
@@ -587,9 +589,9 @@
     mz[1] = jnp.concatenate(ends + [rest], axis=0)
     row8 = iota((8, lanes), 0)
     wz[0] = jnp.where(
-        (row8 < 2) & (lane_e == row8),
+        (row8 < 2) & (side == row8),
         high_lane,
-        jnp.where((row8 >= 2) & (row8 < 4) & (lane_e == row8 - 2), low_lane, 0.0),
+        jnp.where((row8 >= 2) & (row8 < 4) & (side == row8 - 2), low_lane, 0.0),
     )
 
 
@@ -613,17 +615,14 @@
         ux[z, 1:2, :] = high[z : z + 1, :]
     x_low, x_high = ends(xr0[1], xr1[1], 0)
     low, high = ends(yr0[...], yr1[...], 1)
-    kind = iota((rows, 128), 1) // planes
+    both = jnp.where(lane % 2 == 0, high, pltpu.roll(low, 1, 1))
     uy[...] = jnp.zeros(uy.shape, F32)
-    uy[:rows, :] = jnp.where(
-        kind == 0, low, jnp.where(kind == 1, pltpu.roll(high, planes, 1), 0.0)
-    )
+    uy[:rows, :] = jnp.where(lane < 2 * planes, both, 0.0)
     low, high = ends(zr0[0], zr1[0], 2)
     uz[0] = jnp.where(at_low[2], 0.0, low)
     uz[1] = high
     z_low, z_high = ends(zr0[1], zr1[1], 2)
     half = 0.5 * HEAT_SPREADING
-    y_low, y_high = ends(yr0[...], yr1[...], 1)
     c_before = None
     for z in range(planes):
         c = conductance(kind_ref[z], cond[z][0:1, :], scales)
@@ -631,8 +630,9 @@
         final = jnp.where(at_high[0], -c[rows - 1 :, :], x_high[z : z + 1, :])
         kx0[z] = half * (c + jnp.where(row == 0, first, pltpu.roll(c, 1, 0)))
         kx1[z] = half * (c + jnp.where(row == rows - 1, final, pltpu.roll(c, rows - 1, 0)))
-        first = jnp.where(at_low[1], -c, pltpu.roll(y_low, columns - planes - z, 1))
-        final = jnp.where(at_high[1], -c, pltpu.roll(y_high, columns - 1 - planes - z, 1))
+        edge = pltpu.roll(both, columns - 1 - 2 * (planes + z), 1)
+        first = jnp.where(at_low[1], -c, edge)
+        final = jnp.where(at_high[1], -c, edge)
         ky0[z] = half * (c + jnp.where(lane == 0, first, pltpu.roll(c, 1, 1)))
         ky1[z] = half * (c + jnp.where(lane == columns - 1, final, pltpu.roll(c, columns - 1, 1)))
         if z == 0:
@@ -648,18 +648,16 @@
     planes, rows, columns = u_ref.shape
     u = u_ref[z]
     row, lane = iota((rows, columns), 0), iota((rows, columns), 1)
-    edge = uy[:rows, :]
-    edge_low = pltpu.roll(edge, columns - z, 1) if z else edge
-    edge_high = pltpu.roll(edge, columns - 1 - planes - z, 1)
+    edge = pltpu.roll(uy[:rows, :], columns - 1 - 2 * z, 1)
     below = uz[0] if z == 0 else u_ref[z - 1]
     above = uz[1] if z == planes - 1 else u_ref[z + 1]
     total = kx0[z] * (jnp.where(row == 0, ux[z, 0:1, :], pltpu.roll(u, 1, 0)) - u)
     total += kx1[z] * (
         jnp.where(row == rows - 1, ux[z, 1:2, :], pltpu.roll(u, rows - 1, 0)) - u
     )
-    total += ky0[z] * (jnp.where(lane == 0, edge_low, pltpu.roll(u, 1, 1)) - u)
+    total += ky0[z] * (jnp.where(lane == 0, edge, pltpu.roll(u, 1, 1)) - u)
     total += ky1[z] * (
-        jnp.where(lane == columns - 1, edge_high, pltpu.roll(u, columns - 1, 1)) - u
+        jnp.where(lane == columns - 1, edge, pltpu.roll(u, columns - 1, 1)) - u
     )
     return total + kz[z] * (below - u) + kz[z + 1] * (above - u)
 

time: 78.2 us -> 77.5 us (level)
  no operation moved by 1% of the time
where the time goes in v7:
time: 77.5 us; the launch traced here: 77.3 us
  starting transfers between devices  30.9 us (40%)
  Pallas kernels  23.2 us (30%)
  waiting for transfers between devices  22.1 us (29%)
  between operations  0.99 us (1%)
    pallas_call x9, Pallas kernels, call(): pl.pallas_call(kernel, out_shape=out_shapes, in_specs=specs, out_specs=[p...  23.2 us
    ppermute x14, waiting for transfers between devices, all_pairs(): lax.ppermute(arrays[b], axis, [(i, i ^ k) for i in range(n)])  17.6 us
    ppermute x14, starting transfers between devices, all_pairs(): lax.ppermute(arrays[b], axis, [(i, i ^ k) for i in range(n)])  17.4 us
    all_to_all x1, starting transfers between devices, per_device(): lax.all_to_all(send, ('gx', 'gy', 'gz'), split_axis=0, concat_axis=0, til...  7.3 us
    all_to_all x1, waiting for transfers between devices, per_device(): lax.all_to_all(send, ('gx', 'gy', 'gz'), split_axis=0, concat_axis=0, til...  4.44 us
    ppermute x3, starting transfers between devices, next_pairs(): first = lax.ppermute(even, axis, [(i, i ^ 1) for i in range(n)])  3.44 us
  transfers between devices with their start and end apart: 24, of which 13 were waited for; matrix products, arithmetic and copies ran while one was open for 0% of the time, Pallas kernels for 9%

profile of v7, /device:TPU:0, one launch (start us, length us, event | category | flops | bytes accessed | tf_op | source)
XLA Modules:
  0.0 77.3 jit_solution(1493108807339640674)
XLA Ops:
  0.6 0.0 copy-start.2
  0.6 0.0 copy-start.3
  0.7 0.0 copy-start.4
  0.7 0.0 copy-start
  0.7 6.5 %shard_map.104 = (f32[32,1,1408]{2,1,0:T(1,128)}, f32[2,8,128]{2,1,0:T(8,128)}, f32[2,8,128]{2,1,0:T(8,128)}, f32[1,256,128]{2,1,0:T(8,128)}, f32[2,256,128]{2,1,0:T(8,128)}, /*index=5*/f32[2,256,128]{2,1,0:T(8,128)}) custom-call(s32[32]{0:T(128)} %sheet_in.3, f32[16]{0:T(128)} %table_in.3, f32[4]{0:T(128)} %scaling_in.3, f32[32,128]{1,0:T(8,128)} %bitcast.5, ...), custom_call_target="tpu_custom_call" | custom-call | bytes 1 | tf_op jit(solution)/shard_map/pallas_call | solution.py:24
  7.1 7.3 %all-to-all-start = ((f32[32,1,1408]{2,1,0:T(1,128)}), f32[32,1,1408]{2,1,0:T(1,128)S(1)}, u32[]{:S(2)}, u32[]{:S(2)}) async-start(f32[32,1,1408]{2,1,0:T(1,128)} %get-tuple-element.53), calls=%async_computation | async-start | bytes 360448 | tf_op jit(solution)/shard_map/all_to_all | solution.py:1055
  14.5 1.8 %collective-permute-start.3 = (f32[2,256,128]{2,1,0:T(8,128)}, f32[2,256,128]{2,1,0:T(8,128)S(1)}, u32[]{:S(2)}, u32[]{:S(2)}) collective-permute-start(f32[2,256,128]{2,1,0:T(8,128)} %get-tuple-element.51), channel_id=1, source_target_pairs={{0,1},{1,0},{2,3},{3,2},{4,5},{5,4},{6,7},{7,6},{8,9},{9,8},{10,11... | collective-permute-start | bytes 786440 | tf_op jit(solution)/shard_map/ppermute | solution.py:167
  16.3 0.7 collective-permute-start.4
  17.0 0.1 collective-permute-start.2
  17.0 1.5 %collective-permute-start = (f32[2,8,128]{2,1,0:T(8,128)}, f32[2,8,128]{2,1,0:T(8,128)S(1)}, u32[]{:S(2)}, u32[]{:S(2)}) collective-permute-start(f32[2,8,128]{2,1,0:T(8,128)} %get-tuple-element.48), channel_id=1, source_target_pairs={{0,8},{8,0},{16,24},{24,16},{1,9},{9,1},{17,25},{25,17},{2,10},{10... | collective-permute-start | bytes 24584 | tf_op jit(solution)/shard_map/ppermute | solution.py:167
  18.6 0.6 collective-permute-start.1
  19.2 4.4 %all-to-all-done.got_in = f32[32,1,1408]{2,1,0:T(1,128)S(1)} async-done(((f32[32,1,1408]{2,1,0:T(1,128)}), f32[32,1,1408]{2,1,0:T(1,128)S(1)}, u32[]{:S(2)}, u32[]{:S(2)}) %all-to-all-start) | async-done | bytes 180256 | tf_op jit(solution)/shard_map/all_to_all | solution.py:1055
  23.7 0.0 copy-done.3
  23.7 6.0 %shard_map.105 = (bf16[8,544,256]{2,1,0:T(8,128)(2,1)S(1)}, bf16[16,128,256]{2,1,0:T(8,128)(2,1)S(1)}, f32[1192,128]{1,0:T(8,128)S(1)}, f32[8,256,128]{2,1,0:T(8,128)S(1)}) custom-call(s32[32]{0:T(128)S(1)} %copy-done.2, f32[16]{0:T(128)S(1)} %copy-done.3, f32[4]{0:T(128)S(1)} %copy-done.4, f32[32,1,1408]{2,1,0:T(1,128)S(1)} %all-to-all-done.got_in), custom_call_target="tpu_custom_call" | custom-call | bytes 1 | tf_op jit(solution)/shard_map/pallas_call | solution.py:24
  29.7 0.0 collective-permute-done.xr0
  29.7 0.0 collective-permute-done.1.xr1
  29.8 0.0 collective-permute-done.2.yr0.yr1
  29.8 0.0 collective-permute-done.3.zr0
  29.8 0.0 collective-permute-done.4.zr1
  29.8 0.0 copy-done
  29.8 0.0 copy-done.1
  29.8 3.3 %shard_map.106 = (f32[8,8,128]{2,1,0:T(8,128)S(1)}, f32[272,128]{1,0:T(8,128)S(1)}, f32[2,256,128]{2,1,0:T(8,128)S(1)}, f32[8,256,128]{2,1,0:T(8,128)S(1)}, f32[...) custom-call(f32[2,8,128]{2,1,0:T(8,128)S(1)} %collective-permute-don, ...), custom_call_target="tpu_custom_call" | custom-call | bytes 1 | tf_op jit(solution)/shard_map/pallas_call | solution.py:24
  33.1 0.1 collective-permute-start.5
  33.2 4.0 %collective-permute-start.6 = (f32[16,128]{1,0:T(8,128)S(1)}, f32[16,128]{1,0:T(8,128)S(1)}, u32[]{:S(2)}, u32[]{:S(2)}) collective-permute-start(f32[16,128]{1,0:T(8,128)S(1)} %get-tuple-element.61), channel_id=1, source_target_pairs={{0,8},{8,0},{16,24},{24,16},{1,9},{9,1},{17,25},{25,17},{2,10},{10... | collective-permute-start | bytes 24584 | tf_op jit(solution)/shard_map/ppermute | solution.py:156
  37.2 0.5 collective-permute-start.8
  37.7 1.0 %collective-permute-start.7 = (f32[16,128]{1,0:T(8,128)S(1)}, f32[16,128]{1,0:T(8,128)S(1)}, u32[]{:S(2)}, u32[]{:S(2)}) collective-permute-start(f32[16,128]{1,0:T(8,128)S(1)} %get-tuple-element.62), channel_id=1, source_target_pairs={{0,16},{8,24},{16,0},{24,8},{1,17},{9,25},{17,1},{25,9},{2,18},{10... | collective-permute-start | bytes 24584 | tf_op jit(solution)/shard_map/ppermute | solution.py:156
  38.7 0.2 collective-permute-done.6.rest_0_
  38.8 2.9 %collective-permute-done.8.rest_2_ = f32[16,128]{1,0:T(8,128)S(1)} collective-permute-done((f32[16,128]{1,0:T(8,128)S(1)}, f32[16,128]{1,0:T(8,128)S(1)}, u32[]{:S(2)}, u32[]{:S(2)}) %collective-permute-start.8) | collective-permute-done | bytes 8224 | tf_op jit(solution)/shard_map/ppermute | solution.py:156
  41.8 0.0 collective-permute-done.7.rest_1_
  41.8 0.0 collective-permute-done.5.near.rest_0_
  41.8 0.3 shard_map.107
  42.0 0.2 collective-permute-start.10
  42.2 0.0 collective-permute-start.9
  42.2 1.2 %collective-permute-done.9.rest_0_ = f32[16,272]{1,0:T(8,128)S(1)} collective-permute-done((f32[16,272]{1,0:T(8,128)S(1)}, f32[16,272]{1,0:T(8,128)S(1)}, u32[]{:S(2)}, u32[]{:S(2)}) %collective-permute-start.9) | collective-permute-done | bytes 17440 | tf_op jit(solution)/shard_map/ppermute | solution.py:156
  43.4 0.5 shard_map.108
  43.9 1.4 %collective-permute-start.11 = (f32[40,128]{1,0:T(8,128)S(1)}, f32[40,128]{1,0:T(8,128)S(1)}, u32[]{:S(2)}, u32[]{:S(2)}) collective-permute-start(f32[40,128]{1,0:T(8,128)S(1)} %get-tuple-element.78), channel_id=1, source_target_pairs={{0,1},{1,0},{2,3},{3,2},{4,5},{5,4},{6,7},{7,6},{8,9},{9,8},{10,11... | collective-permute-start | bytes 61448 | tf_op jit(solution)/shard_map/ppermute | solution.py:156
  45.3 2.9 %collective-permute-start.13 = (f32[40,128]{1,0:T(8,128)S(1)}, f32[40,128]{1,0:T(8,128)S(1)}, u32[]{:S(2)}, u32[]{:S(2)}) collective-permute-start(f32[40,128]{1,0:T(8,128)S(1)} %get-tuple-element.79), channel_id=1, source_target_pairs={{0,3},{1,2},{2,1},{3,0},{4,7},{5,6},{6,5},{7,4},{8,11},{9,10},{10,... | collective-permute-start | bytes 61448 | tf_op jit(solution)/shard_map/ppermute | solution.py:156
  48.3 0.0 collective-permute-start.12
  48.3 0.4 collective-permute-done.11.rest_2_
  48.7 2.3 %collective-permute-done.13.rest_4_ = f32[40,128]{1,0:T(8,128)S(1)} collective-permute-done((f32[40,128]{1,0:T(8,128)S(1)}, f32[40,128]{1,0:T(8,128)S(1)}, u32[]{:S(2)}, u32[]{:S(2)}) %collective-permute-start.13) | collective-permute-done | bytes 20512 | tf_op jit(solution)/shard_map/ppermute | solution.py:156
  50.9 2.0 %collective-permute-done.12.rest_3_ = f32[40,128]{1,0:T(8,128)S(1)} collective-permute-done((f32[40,128]{1,0:T(8,128)S(1)}, f32[40,128]{1,0:T(8,128)S(1)}, u32[]{:S(2)}, u32[]{:S(2)}) %collective-permute-start.12) | collective-permute-done | bytes 20512 | tf_op jit(solution)/shard_map/ppermute | solution.py:156
  52.9 0.0 collective-permute-done.10.rest_1_
  52.9 3.9 %shard_map.109 = (f32[8,256,128]{2,1,0:T(8,128)S(1)}, f32[8,8,128]{2,1,0:T(8,128)}, f32[272,128]{1,0:T(8,128)}, f32[2,256,128]{2,1,0:T(8,128)}, f32[8,272,128]{2...) custom-call(f32[8,272,128]{2,1,0:T(8,128)S(1)} %get-tuple-element.58, ...), custom_call_target="tpu_custom_call" | custom-call | bytes 1 | tf_op jit(solution)/shard_map/pallas_call | solution.py:24
  56.8 0.0 collective-permute-start.14
  56.8 2.6 %collective-permute-start.15 = (f32[16,128]{1,0:T(8,128)S(1)}, f32[16,128]{1,0:T(8,128)S(1)}, u32[]{:S(2)}, u32[]{:S(2)}) collective-permute-start(f32[16,128]{1,0:T(8,128)S(1)} %get-tuple-element.83), channel_id=1, source_target_pairs={{0,8},{8,0},{16,24},{24,16},{1,9},{9,1},{17,25},{25,17},{2,10},{10... | collective-permute-start | bytes 24584 | tf_op jit(solution)/shard_map/ppermute | solution.py:156
  59.5 0.5 collective-permute-start.17
  60.0 0.9 %collective-permute-start.16 = (f32[16,128]{1,0:T(8,128)S(1)}, f32[16,128]{1,0:T(8,128)S(1)}, u32[]{:S(2)}, u32[]{:S(2)}) collective-permute-start(f32[16,128]{1,0:T(8,128)S(1)} %get-tuple-element.84), channel_id=1, source_target_pairs={{0,16},{8,24},{16,0},{24,8},{1,17},{9,25},{17,1},{25,9},{2,18},{10... | collective-permute-start | bytes 24584 | tf_op jit(solution)/shard_map/ppermute | solution.py:156
  60.9 0.2 collective-permute-done.15.rest_0_
  61.1 2.9 %collective-permute-done.17.rest_2_ = f32[16,128]{1,0:T(8,128)S(1)} collective-permute-done((f32[16,128]{1,0:T(8,128)S(1)}, f32[16,128]{1,0:T(8,128)S(1)}, u32[]{:S(2)}, u32[]{:S(2)}) %collective-permute-start.17) | collective-permute-done | bytes 8224 | tf_op jit(solution)/shard_map/ppermute | solution.py:156
  64.0 0.0 collective-permute-done.16.rest_1_
  64.0 0.0 collective-permute-done.14.near.rest_0_
  64.0 0.3 shard_map.110
  64.3 1.2 %collective-permute-start.19 = (f32[256,128]{1,0:T(8,128)S(1)}, f32[256,128]{1,0:T(8,128)S(1)}, u32[]{:S(2)}, u32[]{:S(2)}) collective-permute-start(f32[256,128]{1,0:T(8,128)S(1)} %get-tuple-element.91), channel_id=1, source_target_pairs={{0,2},{1,3},{2,0},{3,1},{4,6},{5,7},{6,4},{7,5},{8,10},{9,11},{10,... | collective-permute-start | bytes 393224 | tf_op jit(solution)/shard_map/ppermute | solution.py:162
  65.5 0.0 collective-permute-start.18
  65.5 1.2 %collective-permute-done.18.rest_0_ = f32[16,272]{1,0:T(8,128)S(1)} collective-permute-done((f32[16,272]{1,0:T(8,128)S(1)}, f32[16,272]{1,0:T(8,128)S(1)}, u32[]{:S(2)}, u32[]{:S(2)}) %collective-permute-start.18) | collective-permute-done | bytes 17440 | tf_op jit(solution)/shard_map/ppermute | solution.py:156
  66.7 0.2 shard_map.111
  66.9 0.4 collective-permute-start.20
  67.3 2.9 %collective-permute-start.22 = (f32[32,128]{1,0:T(8,128)S(1)}, f32[32,128]{1,0:T(8,128)S(1)}, u32[]{:S(2)}, u32[]{:S(2)}) collective-permute-start(f32[32,128]{1,0:T(8,128)S(1)} %get-tuple-element.93), channel_id=1, source_target_pairs={{0,3},{1,2},{2,1},{3,0},{4,7},{5,6},{6,5},{7,4},{8,11},{9,10},{10,... | collective-permute-start | bytes 49160 | tf_op jit(solution)/shard_map/ppermute | solution.py:156
  70.2 0.2 collective-permute-start.21
  70.4 0.2 collective-permute-done.20.rest_2_
  70.7 2.2 %collective-permute-done.22.rest_4_ = f32[32,128]{1,0:T(8,128)S(1)} collective-permute-done((f32[32,128]{1,0:T(8,128)S(1)}, f32[32,128]{1,0:T(8,128)S(1)}, u32[]{:S(2)}, u32[]{:S(2)}) %collective-permute-start.22) | collective-permute-done | bytes 16416 | tf_op jit(solution)/shard_map/ppermute | solution.py:156
  72.8 2.0 %collective-permute-done.21.rest_3_ = f32[32,128]{1,0:T(8,128)S(1)} collective-permute-done((f32[32,128]{1,0:T(8,128)S(1)}, f32[32,128]{1,0:T(8,128)S(1)}, u32[]{:S(2)}, u32[]{:S(2)}) %collective-permute-start.21) | collective-permute-done | bytes 16416 | tf_op jit(solution)/shard_map/ppermute | solution.py:156
  74.8 0.0 collective-permute-done.19.rest_1_
  74.8 2.3 %shard_map.112 = (f32[8,256,128]{2,1,0:T(8,128)}, f32[8,256,128]{2,1,0:T(8,128)}) custom-call(f32[8,272,128]{2,1,0:T(8,128)S(1)} %get-tuple-element.80.t_ref.t_in, f32[272,128]{1,0:T(8,128)S(1)} %get-tuple-element.88.l_ref, f32[32,128]{1,0:T(8,128)S(1)} %get-tuple-element.89.b_ref, f32[1192,128]{1,0:T(8,128)S(1)} %get-tuple-element.56.co, ...), custom_call_target="tpu_custom_call" | custom-call | bytes 1 | tf_op jit(solution)/shard_map/pallas_call | solution.py:24
  (3 shorter events, 0.0 us)
Async XLA Ops:
  0.6 23.0 %copy-start.2 = (s32[32]{0:T(128)S(1)}, s32[32]{0:T(128)}, u32[]{:S(2)}) copy-start(s32[32]{0:T(128)} %sheet_in.3) | copy-start | bytes 388
  0.6 23.0 %copy-start.3 = (f32[16]{0:T(128)S(1)}, f32[16]{0:T(128)}, u32[]{:S(2)}) copy-start(f32[16]{0:T(128)} %table_in.3) | copy-start | bytes 196
  0.7 23.0 %copy-start.4 = (f32[4]{0:T(128)S(1)}, f32[4]{0:T(128)}, u32[]{:S(2)}) copy-start(f32[4]{0:T(128)} %scaling_in.3) | copy-start | bytes 52
  0.7 29.1 %copy-start = (f32[8,256,128]{2,1,0:T(8,128)S(1)}, f32[8,256,128]{2,1,0:T(8,128)}, u32[]{:S(2)}) copy-start(f32[8,256,128]{2,1,0:T(8,128)} %u_ref.3) | copy-start | bytes 3145732
  0.7 29.1 %copy-start.1 = (s32[8,256,128]{2,1,0:T(8,128)S(1)}, s32[8,256,128]{2,1,0:T(8,128)}, u32[]{:S(2)}) copy-start(s32[8,256,128]{2,1,0:T(8,128)} %kind_ref.1) | copy-start | bytes 3145732
  7.1 16.5 %all-to-all-start = ((f32[32,1,1408]{2,1,0:T(1,128)}), f32[32,1,1408]{2,1,0:T(1,128)S(1)}, u32[]{:S(2)}, u32[]{:S(2)}) async-start(f32[32,1,1408]{2,1,0:T(1,128)} %get-tuple-element.53), calls=%async_computation | async-start | bytes 360448 | tf_op jit(solution)/shard_map/all_to_all | solution.py:1055
  14.5 15.3 %collective-permute-start.3 = (f32[2,256,128]{2,1,0:T(8,128)}, f32[2,256,128]{2,1,0:T(8,128)S(1)}, u32[]{:S(2)}, u32[]{:S(2)}) collective-permute-start(f32[2,256,128]{2,1,0:T(8,128)} %get-tuple-element.51), channel_id=1, source_target_pairs={{0,1},{1,0},{2,3},{3,2},{4,5},{5,4},{6,7},{7,6},{8,9},{9,8},{10,11... | collective-permute-start | bytes 786440 | tf_op jit(solution)/shard_map/ppermute | solution.py:167
  16.3 13.5 %collective-permute-start.4 = (f32[2,256,128]{2,1,0:T(8,128)}, f32[2,256,128]{2,1,0:T(8,128)S(1)}, u32[]{:S(2)}, u32[]{:S(2)}) collective-permute-start(f32[2,256,128]{2,1,0:T(8,128)} %get-tuple-element.52), channel_id=1, source_target_pairs={{1,2},{2,1},{5,6},{6,5},{9,10},{10,9},{13,14},{14,13},{17,18},{18,... | collective-permute-start | bytes 786440 | tf_op jit(solution)/shard_map/ppermute | solution.py:171
  17.0 12.8 %collective-permute-start.2 = (f32[256,128]{1,0:T(8,128)}, f32[256,128]{1,0:T(8,128)S(1)}, u32[]{:S(2)}, u32[]{:S(2)}) collective-permute-start(f32[256,128]{1,0:T(8,128)} %bitcast.9), channel_id=1, source_target_pairs={{0,4},{4,0},{1,5},{5,1},{2,6},{6,2},{3,7},{7,3},{8,12},{12,8},{9,1... | collective-permute-start | bytes 393224 | tf_op jit(solution)/shard_map/ppermute | solution.py:167
  17.0 12.7 %collective-permute-start = (f32[2,8,128]{2,1,0:T(8,128)}, f32[2,8,128]{2,1,0:T(8,128)S(1)}, u32[]{:S(2)}, u32[]{:S(2)}) collective-permute-start(f32[2,8,128]{2,1,0:T(8,128)} %get-tuple-element.48), channel_id=1, source_target_pairs={{0,8},{8,0},{16,24},{24,16},{1,9},{9,1},{17,25},{25,17},{2,10},{10... | collective-permute-start | bytes 24584 | tf_op jit(solution)/shard_map/ppermute | solution.py:167
  18.6 11.2 %collective-permute-start.1 = (f32[2,8,128]{2,1,0:T(8,128)}, f32[2,8,128]{2,1,0:T(8,128)S(1)}, u32[]{:S(2)}, u32[]{:S(2)}) collective-permute-start(f32[2,8,128]{2,1,0:T(8,128)} %get-tuple-element.49), channel_id=1, source_target_pairs={{8,16},{16,8},{9,17},{17,9},{10,18},{18,10},{11,19},{19,11},{12,20... | collective-permute-start | bytes 24584 | tf_op jit(solution)/shard_map/ppermute | solution.py:171
  33.1 8.6 %collective-permute-start.5 = (f32[2,256,128]{2,1,0:T(8,128)S(1)}, f32[2,256,128]{2,1,0:T(8,128)S(1)}, u32[]{:S(2)}, u32[]{:S(2)}) collective-permute-start(f32[2,256,128]{2,1,0:T(8,128)S(1)} %get-tuple-element.60.pair), channel_id=1, source_target_pairs={{0,1},{1,0},{2,3},{3,2},{4,5},{5,4},{6,7},{7,6},{8,9},{9,8},{10,11... | collective-permute-start | bytes 786440 | tf_op jit(solution)/shard_map/ppermute | solution.py:162
  33.2 5.6 %collective-permute-start.6 = (f32[16,128]{1,0:T(8,128)S(1)}, f32[16,128]{1,0:T(8,128)S(1)}, u32[]{:S(2)}, u32[]{:S(2)}) collective-permute-start(f32[16,128]{1,0:T(8,128)S(1)} %get-tuple-element.61), channel_id=1, source_target_pairs={{0,8},{8,0},{16,24},{24,16},{1,9},{9,1},{17,25},{25,17},{2,10},{10... | collective-permute-start | bytes 24584 | tf_op jit(solution)/shard_map/ppermute | solution.py:156
  37.2 4.5 %collective-permute-start.8 = (f32[16,128]{1,0:T(8,128)S(1)}, f32[16,128]{1,0:T(8,128)S(1)}, u32[]{:S(2)}, u32[]{:S(2)}) collective-permute-start(f32[16,128]{1,0:T(8,128)S(1)} %get-tuple-element.62), channel_id=1, source_target_pairs={{0,24},{8,16},{16,8},{24,0},{1,25},{9,17},{17,9},{25,1},{2,26},{10... | collective-permute-start | bytes 24584 | tf_op jit(solution)/shard_map/ppermute | solution.py:156
  37.7 4.0 %collective-permute-start.7 = (f32[16,128]{1,0:T(8,128)S(1)}, f32[16,128]{1,0:T(8,128)S(1)}, u32[]{:S(2)}, u32[]{:S(2)}) collective-permute-start(f32[16,128]{1,0:T(8,128)S(1)} %get-tuple-element.62), channel_id=1, source_target_pairs={{0,16},{8,24},{16,0},{24,8},{1,17},{9,25},{17,1},{25,9},{2,18},{10... | collective-permute-start | bytes 24584 | tf_op jit(solution)/shard_map/ppermute | solution.py:156
  42.0 10.9 %collective-permute-start.10 = (f32[256,128]{1,0:T(8,128)S(1)}, f32[256,128]{1,0:T(8,128)S(1)}, u32[]{:S(2)}, u32[]{:S(2)}) collective-permute-start(f32[256,128]{1,0:T(8,128)S(1)} %get-tuple-element.77), channel_id=1, source_target_pairs={{0,2},{1,3},{2,0},{3,1},{4,6},{5,7},{6,4},{7,5},{8,10},{9,11},{10,... | collective-permute-start | bytes 393224 | tf_op jit(solution)/shard_map/ppermute | solution.py:162
  42.2 1.2 %collective-permute-start.9 = (f32[16,272]{1,0:T(8,128)S(1)}, f32[16,272]{1,0:T(8,128)S(1)}, u32[]{:S(2)}, u32[]{:S(2)}) collective-permute-start(f32[16,272]{1,0:T(8,128)S(1)} %get-tuple-element.65), channel_id=1, source_target_pairs={{0,4},{4,0},{1,5},{5,1},{2,6},{6,2},{3,7},{7,3},{8,12},{12,8},{9,1... | collective-permute-start | bytes 52232 | tf_op jit(solution)/shard_map/ppermute | solution.py:156
  43.9 4.7 %collective-permute-start.11 = (f32[40,128]{1,0:T(8,128)S(1)}, f32[40,128]{1,0:T(8,128)S(1)}, u32[]{:S(2)}, u32[]{:S(2)}) collective-permute-start(f32[40,128]{1,0:T(8,128)S(1)} %get-tuple-element.78), channel_id=1, source_target_pairs={{0,1},{1,0},{2,3},{3,2},{4,5},{5,4},{6,7},{7,6},{8,9},{9,8},{10,11... | collective-permute-start | bytes 61448 | tf_op jit(solution)/shard_map/ppermute | solution.py:156
  45.3 5.6 %collective-permute-start.13 = (f32[40,128]{1,0:T(8,128)S(1)}, f32[40,128]{1,0:T(8,128)S(1)}, u32[]{:S(2)}, u32[]{:S(2)}) collective-permute-start(f32[40,128]{1,0:T(8,128)S(1)} %get-tuple-element.79), channel_id=1, source_target_pairs={{0,3},{1,2},{2,1},{3,0},{4,7},{5,6},{6,5},{7,4},{8,11},{9,10},{10,... | collective-permute-start | bytes 61448 | tf_op jit(solution)/shard_map/ppermute | solution.py:156
  48.3 4.7 %collective-permute-start.12 = (f32[40,128]{1,0:T(8,128)S(1)}, f32[40,128]{1,0:T(8,128)S(1)}, u32[]{:S(2)}, u32[]{:S(2)}) collective-permute-start(f32[40,128]{1,0:T(8,128)S(1)} %get-tuple-element.79), channel_id=1, source_target_pairs={{0,2},{1,3},{2,0},{3,1},{4,6},{5,7},{6,4},{7,5},{8,10},{9,11},{10,... | collective-permute-start | bytes 61448 | tf_op jit(solution)/shard_map/ppermute | solution.py:156
  56.8 7.2 %collective-permute-start.14 = (f32[2,256,128]{2,1,0:T(8,128)S(1)}, f32[2,256,128]{2,1,0:T(8,128)S(1)}, u32[]{:S(2)}, u32[]{:S(2)}) collective-permute-start(f32[2,256,128]{2,1,0:T(8,128)S(1)} %get-tuple-element.82.pair), channel_id=1, source_target_pairs={{0,1},{1,0},{2,3},{3,2},{4,5},{5,4},{6,7},{7,6},{8,9},{9,8},{10,11... | collective-permute-start | bytes 786440 | tf_op jit(solution)/shard_map/ppermute | solution.py:162
  56.8 4.3 %collective-permute-start.15 = (f32[16,128]{1,0:T(8,128)S(1)}, f32[16,128]{1,0:T(8,128)S(1)}, u32[]{:S(2)}, u32[]{:S(2)}) collective-permute-start(f32[16,128]{1,0:T(8,128)S(1)} %get-tuple-element.83), channel_id=1, source_target_pairs={{0,8},{8,0},{16,24},{24,16},{1,9},{9,1},{17,25},{25,17},{2,10},{10... | collective-permute-start | bytes 24584 | tf_op jit(solution)/shard_map/ppermute | solution.py:156
  59.5 4.5 %collective-permute-start.17 = (f32[16,128]{1,0:T(8,128)S(1)}, f32[16,128]{1,0:T(8,128)S(1)}, u32[]{:S(2)}, u32[]{:S(2)}) collective-permute-start(f32[16,128]{1,0:T(8,128)S(1)} %get-tuple-element.84), channel_id=1, source_target_pairs={{0,24},{8,16},{16,8},{24,0},{1,25},{9,17},{17,9},{25,1},{2,26},{10... | collective-permute-start | bytes 24584 | tf_op jit(solution)/shard_map/ppermute | solution.py:156
  60.0 4.0 %collective-permute-start.16 = (f32[16,128]{1,0:T(8,128)S(1)}, f32[16,128]{1,0:T(8,128)S(1)}, u32[]{:S(2)}, u32[]{:S(2)}) collective-permute-start(f32[16,128]{1,0:T(8,128)S(1)} %get-tuple-element.84), channel_id=1, source_target_pairs={{0,16},{8,24},{16,0},{24,8},{1,17},{9,25},{17,1},{25,9},{2,18},{10... | collective-permute-start | bytes 24584 | tf_op jit(solution)/shard_map/ppermute | solution.py:156
  64.3 10.5 %collective-permute-start.19 = (f32[256,128]{1,0:T(8,128)S(1)}, f32[256,128]{1,0:T(8,128)S(1)}, u32[]{:S(2)}, u32[]{:S(2)}) collective-permute-start(f32[256,128]{1,0:T(8,128)S(1)} %get-tuple-element.91), channel_id=1, source_target_pairs={{0,2},{1,3},{2,0},{3,1},{4,6},{5,7},{6,4},{7,5},{8,10},{9,11},{10,... | collective-permute-start | bytes 393224 | tf_op jit(solution)/shard_map/ppermute | solution.py:162
  65.5 1.2 %collective-permute-start.18 = (f32[16,272]{1,0:T(8,128)S(1)}, f32[16,272]{1,0:T(8,128)S(1)}, u32[]{:S(2)}, u32[]{:S(2)}) collective-permute-start(f32[16,272]{1,0:T(8,128)S(1)} %get-tuple-element.87), channel_id=1, source_target_pairs={{0,4},{4,0},{1,5},{5,1},{2,6},{6,2},{3,7},{7,3},{8,12},{12,8},{9,1... | collective-permute-start | bytes 52232 | tf_op jit(solution)/shard_map/ppermute | solution.py:156
  66.9 3.8 %collective-permute-start.20 = (f32[32,128]{1,0:T(8,128)S(1)}, f32[32,128]{1,0:T(8,128)S(1)}, u32[]{:S(2)}, u32[]{:S(2)}) collective-permute-start(f32[32,128]{1,0:T(8,128)S(1)} %get-tuple-element.92), channel_id=1, source_target_pairs={{0,1},{1,0},{2,3},{3,2},{4,5},{5,4},{6,7},{7,6},{8,9},{9,8},{10,11... | collective-permute-start | bytes 49160 | tf_op jit(solution)/shard_map/ppermute | solution.py:156
  67.3 5.5 %collective-permute-start.22 = (f32[32,128]{1,0:T(8,128)S(1)}, f32[32,128]{1,0:T(8,128)S(1)}, u32[]{:S(2)}, u32[]{:S(2)}) collective-permute-start(f32[32,128]{1,0:T(8,128)S(1)} %get-tuple-element.93), channel_id=1, source_target_pairs={{0,3},{1,2},{2,1},{3,0},{4,7},{5,6},{6,5},{7,4},{8,11},{9,10},{10,... | collective-permute-start | bytes 49160 | tf_op jit(solution)/shard_map/ppermute | solution.py:156
  70.2 4.6 %collective-permute-start.21 = (f32[32,128]{1,0:T(8,128)S(1)}, f32[32,128]{1,0:T(8,128)S(1)}, u32[]{:S(2)}, u32[]{:S(2)}) collective-permute-start(f32[32,128]{1,0:T(8,128)S(1)} %get-tuple-element.93), channel_id=1, source_target_pairs={{0,2},{1,3},{2,0},{3,1},{4,6},{5,7},{6,4},{7,5},{8,10},{9,11},{10,... | collective-permute-start | bytes 49160 | tf_op jit(solution)/shard_map/ppermute | solution.py:156

commit v8 on v7

--- a/solution.py
+++ b/solution.py
@@ -662,7 +662,7 @@
     return total + kz[z] * (below - u) + kz[z + 1] * (above - u)
 
 
-def advance(idx, source_of, gx_ref, gy_ref, phz, psz, t_ref, e_ref, z_send, x_sends):
+def advance(idx, source_of, gx_ref, gy_ref, phz, psz, t_ref, e_ref, z_sends, x_sends):
     planes, extent, columns = t_ref.shape
     rows = extent - EXTRA
     sums = jnp.zeros((extent, 128), F32)
@@ -689,7 +689,11 @@
         send[planes:, :] = jnp.broadcast_to(
             jnp.where(take == 0, pair[0:1], pair[1:2]), (8, 128)
         )
-    z_send[0], z_send[1] = below, above
+    deep = len(z_sends) > 1
+    rising = (idx[2] >> (1 if deep else 0)) % 2 == 0
+    z_sends[0][...] = jnp.where(rising, below, above)
+    if deep:
+        z_sends[1][...] = jnp.where(rising, above, below)
 
 
 def joule_kernel(sizes, sheet_in, table_in, scaling_in, got_in, gx_ref, gy_ref, co, joule,
@@ -721,12 +725,15 @@
         ux, uy, uz, kx0, kx1, ky0, ky1, kz,
     )
 
+    deep = 2 if sizes[5] > 2 else 1
+
     def source_of(z):
         out = outflow(z, u_ref, ux, uy, uz, kx0, kx1, ky0, ky1, kz)
         return out + OHMIC_POWER * ((1.0 + WARMING_SLOPE * u_ref[z]) * joule[z])
 
     advance(
-        idx, source_of, gx_ref, gy_ref, phz, psz, t_ref, e_ref, sends[0], sends[1:]
+        idx, source_of, gx_ref, gy_ref, phz, psz, t_ref, e_ref,
+        sends[:deep], sends[deep:],
     )
 
 
@@ -735,7 +742,7 @@
     planes, nx = sizes[0], sizes[3]
     gots, (e_out, f_out, send), far = rest[: nx - 1], rest[nx - 1 : nx + 2], rest[nx + 2 :]
     for out in far:
-        out[...] = jnp.where((idx[2] >> 1) % 2 == 0, pair[0] + near[0], pair[1] + near[1])
+        out[...] = pair[...] + near[...]
     dx, dxl, lx = groups_of(sizes, co, "dx", "dxl", "lx")
     me = idx[0]
     sums = [[jnp.zeros((planes, 128), F32), jnp.zeros((8, 128), F32)] for _ in range(2)]
@@ -839,13 +846,15 @@
 def carried(nz, idx, bigs, smalls, ax, by, rows, ghosts):
     me = idx[2]
     planes = by.each // 2
-    at_top = me % 2 == 1
-    below = jnp.where(at_top, bigs[0][0], 0.0)
-    above = jnp.where(at_top, 0.0, bigs[0][1])
-    for b, big in enumerate(bigs[1:], 1):
-        at_top = (me >> b) % 2 == 1
-        below += jnp.where(at_top, big[...], 0.0)
-        above += jnp.where(at_top, 0.0, big[...])
+    if nz == 2:
+        below = jnp.where(me == 1, bigs[0][...], 0.0)
+        above = jnp.where(me == 1, 0.0, bigs[0][...])
+    else:
+        near, aside, far = (big[...] for big in bigs)
+        below = jnp.where(me == 1, near, 0.0) + jnp.where(me == 3, aside, 0.0)
+        above = jnp.where(me == 2, near, 0.0) + jnp.where(me == 0, aside, 0.0)
+        below += jnp.where(me > 1, far, 0.0)
+        above += jnp.where(me > 1, 0.0, far)
     g_below = g_above = 0.0
     ends = [0.0, 0.0]
     lefts, rights = [], []
@@ -918,15 +927,20 @@
         emit(planes, psz[planes + 1][0:1, :] * head + phz[planes + 1][0:1, :] * above)
 
 
-def rise_kernel(sizes, t_in, l_ref, b_ref, q_ref, co,
+def rise_kernel(sizes, final, t_in, l_ref, b_ref, q_ref, co,
                 u_ref, ux, uy, uz, kx0, kx1, ky0, ky1, kz, joule, gx_ref, gy_ref, *rest):
     idx = place()
     nz = sizes[5]
     phz, psz, mz, wz, ax, by = groups_of(sizes, co, "phz", "psz", "mz", "wz", "ax", "by")
-    deep = (nz - 1).bit_length()
-    bigs, smalls, rest = rest[:deep], rest[deep : deep + nz - 1], rest[deep + nz - 1 :]
-    u_out, ux_out, uy_out, uz_out, t_ref, e_ref = rest[:6]
-    sends, second = rest[6:-1], rest[-1]
+    deep = 2 if nz > 2 else 1
+    many = 3 if nz > 2 else 1
+    bigs, smalls, rest = rest[:many], rest[many : many + nz - 1], rest[many + nz - 1 :]
+    if final:
+        u_out, t_ref, e_ref = rest[:3]
+        sends, (second, ux_out, uy_out, uz_out) = rest[3:-4], rest[-4:]
+    else:
+        u_out, t_ref, e_ref, ux_out, uy_out, uz_out = rest[:6]
+        sends, second = rest[6:-1], rest[-1]
     planes, rows, columns = u_ref.shape
     whole_planes(t_in, l_ref, b_ref, second, rows + 8)
     below, above, g_below, g_above, edges = carried(nz, idx, bigs, smalls, ax, by, rows, True)
@@ -955,7 +969,8 @@
         return out + OHMIC_POWER * ((1.0 + WARMING_SLOPE * u_out[z]) * joule[z])
 
     advance(
-        idx, source_of, gx_ref, gy_ref, phz, psz, t_ref, e_ref, sends[0], sends[1:]
+        idx, source_of, gx_ref, gy_ref, phz, psz, t_ref, e_ref,
+        sends[:deep], sends[deep:],
     )
 
 
@@ -963,8 +978,9 @@
     idx = place()
     nz = sizes[5]
     phz, psz, ax, by = groups_of(sizes, co, "phz", "psz", "ax", "by")
-    deep = (nz - 1).bit_length()
-    bigs, smalls, rest = rest[:deep], rest[deep : deep + nz - 1], rest[deep + nz - 1 :]
+    deep = 2 if nz > 2 else 1
+    many = 3 if nz > 2 else 1
+    bigs, smalls, rest = rest[:many], rest[many : many + nz - 1], rest[many + nz - 1 :]
     u_out, heat_out, u_scr, heat_scr, second, sems = rest
     rows = u_ref.shape[1]
     started = []
@@ -998,6 +1014,7 @@
     planes, rows, columns = starting_warmth.shape
     counts = tuple(lax.axis_size(axis) for axis in ("gx", "gy", "gz"))
     nx, ny, nz = counts
+    assert nz in (2, 4)
     bits = [(n - 1).bit_length() for n in counts]
     devices = nx * ny * nz
     extent = rows + EXTRA
@@ -1064,7 +1081,7 @@
         shaped(table_rows(*sizes)[1], lanes),
     ]
     step_out = [shaped(planes, extent, columns), shaped(extent, 128)]
-    step_out += [shaped(2, rows, columns)] + [shaped(planes + 8, columns)] * bits[0]
+    step_out += [shaped(rows, columns)] * bits[2] + [shaped(planes + 8, columns)] * bits[0]
     total = devices * spare
     ghosts = [shaped(planes, 8, columns), shaped(extent, 128), shaped(2, rows, columns)]
     gx_m, gy_m, co, joule = call(
@@ -1092,8 +1109,8 @@
     lines = planes if ny == 2 else 2 * planes
     small_rows = 2 * planes + lines * (rows // 128)
     for repeat in range(STEPS):
-        pair, *sends = sends
-        gots = all_pairs(sends, "gx")
+        pair, *beside = sends[: bits[2]]
+        gots = all_pairs(sends[bits[2] :], "gx")
         near = crossed(pair, 1, "gz")
         e, f, send, *far = call(
             functools.partial(x_kernel, sizes),
@@ -1101,7 +1118,10 @@
             + [shaped(rows, columns)] * (bits[2] - 1),
             (e, co, pair, near, *gots),
         )
-        bigs = [near] + [crossed(array, 2, "gz") for array in far]
+        bigs = [near]
+        if nz > 2:
+            bigs.append(lax.ppermute(beside[0], "gz", [(1, 0), (2, 3)]))
+            bigs.append(crossed(far[0], 2, "gz"))
         gots = all_pairs([send] * bits[1], "gy")
         final = repeat == STEPS - 1
         q = [] if final else [shaped(extent, 128)]
@@ -1116,15 +1136,17 @@
         else:
             q, *sends = sends
             smalls = all_pairs(sends, "gz")
-            u, ux, uy, uz, t, e, *sends = call(
-                functools.partial(rise_kernel, sizes),
-                [block, shaped(planes, 8, columns), shaped(extent, 128)]
-                + [shaped(2, rows, columns)]
-                + step_out,
+            last = repeat == STEPS - 2
+            u, t, e, *sends = call(
+                functools.partial(rise_kernel, sizes, last),
+                [block] + step_out[:2] + ([] if last else ghosts) + step_out[2:],
                 (t, left, right, q, co, u, ux, uy, uz, *conduct)
                 + (joule, gx_m, gy_m, *bigs, *smalls),
-                scratch=[pltpu.VMEM((planes, rows + 8, columns), F32)],
+                scratch=[pltpu.VMEM((planes, rows + 8, columns), F32)]
+                + [pltpu.VMEM(o.shape, F32) for o in (ghosts if last else [])],
             )
+            if not last:
+                ux, uy, uz, *sends = sends
     return tuple(
         call(
             functools.partial(finish_kernel, sizes),

time: 77.5 us -> 76.3 us (0.985)
  waiting for transfers between devices: 22.1 us -> 19.4 us
  starting transfers between devices: 30.9 us -> 33.1 us
    ppermute x14, waiting for transfers between devices: 17.6 us -> 14.9 us  [all_pairs(): lax.ppermute(arrays[b], axis, [(i, i ^ k) for i in range(n)])]
    ppermute x0 -> x2, starting transfers between devices: none -> 2.56 us  [per_device(): bigs.append(lax.ppermute(beside[0], 'gz', [(1, 0), (2, 3)]))]
    ppermute x14, starting transfers between devices: 17.4 us -> 16.7 us  [all_pairs(): lax.ppermute(arrays[b], axis, [(i, i ^ k) for i in range(n)])]
  transfers between devices with their start and end apart: 24 -> 26, of which waited for: 13 -> 10; matrix products, arithmetic and copies ran while one was open for 0% -> 0% of each run, Pallas kernels for 9% -> 10%
where the time goes in v8:
time: 76.3 us; the launch traced here: 76.1 us
  starting transfers between devices  33.1 us (43%)
  Pallas kernels  22.5 us (29%)
  waiting for transfers between devices  19.4 us (25%)
  between operations  1.04 us (1%)
    pallas_call x9, Pallas kernels, call(): pl.pallas_call(kernel, out_shape=out_shapes, in_specs=specs, out_specs=[p...  22.5 us
    ppermute x14, starting transfers between devices, all_pairs(): lax.ppermute(arrays[b], axis, [(i, i ^ k) for i in range(n)])  16.7 us
    ppermute x14, waiting for transfers between devices, all_pairs(): lax.ppermute(arrays[b], axis, [(i, i ^ k) for i in range(n)])  14.9 us
    all_to_all x1, starting transfers between devices, per_device(): lax.all_to_all(send, ('gx', 'gy', 'gz'), split_axis=0, concat_axis=0, til...  7.3 us
    all_to_all x1, waiting for transfers between devices, per_device(): lax.all_to_all(send, ('gx', 'gy', 'gz'), split_axis=0, concat_axis=0, til...  4.44 us
    ppermute x3, starting transfers between devices, next_pairs(): first = lax.ppermute(even, axis, [(i, i ^ 1) for i in range(n)])  3.44 us
    ppermute x2, starting transfers between devices, per_device(): bigs.append(lax.ppermute(beside[0], 'gz', [(1, 0), (2, 3)]))  2.56 us
    ppermute x4, starting transfers between devices, crossed(): lax.ppermute(array, axis, [(i, i ^ k) for i in range(lax.axis_size(axis))])  1.77 us
  transfers between devices with their start and end apart: 26, of which 10 were waited for; matrix products, arithmetic and copies ran while one was open for 0% of the time, Pallas kernels for 10%

profile of v8, /device:TPU:0, one launch (start us, length us, event | category | flops | bytes accessed | tf_op | source)
XLA Modules:
  0.0 76.1 jit_solution(2600103542541581496)
XLA Ops:
  0.6 0.0 copy-start.2
  0.6 0.0 copy-start.3
  0.7 0.0 copy-start.4
  0.7 6.4 %shard_map.104 = (f32[32,1,1408]{2,1,0:T(1,128)}, f32[2,8,128]{2,1,0:T(8,128)}, f32[2,8,128]{2,1,0:T(8,128)}, f32[1,256,128]{2,1,0:T(8,128)}, f32[2,256,128]{2,1,0:T(8,128)}, /*index=5*/f32[2,256,128]{2,1,0:T(8,128)}) custom-call(s32[32]{0:T(128)} %sheet_in.3, f32[16]{0:T(128)} %table_in.3, f32[4]{0:T(128)} %scaling_in.3, f32[32,128]{1,0:T(8,128)} %bitcast.5, ...), custom_call_target="tpu_custom_call" | custom-call | bytes 1 | tf_op jit(solution)/shard_map/pallas_call | solution.py:24
  7.1 7.3 %all-to-all-start = ((f32[32,1,1408]{2,1,0:T(1,128)}), f32[32,1,1408]{2,1,0:T(1,128)S(1)}, u32[]{:S(2)}, u32[]{:S(2)}) async-start(f32[32,1,1408]{2,1,0:T(1,128)} %get-tuple-element.55), calls=%async_computation | async-start | bytes 360448 | tf_op jit(solution)/shard_map/all_to_all | solution.py:1072
  14.4 1.8 %collective-permute-start.3 = (f32[2,256,128]{2,1,0:T(8,128)}, f32[2,256,128]{2,1,0:T(8,128)S(1)}, u32[]{:S(2)}, u32[]{:S(2)}) collective-permute-start(f32[2,256,128]{2,1,0:T(8,128)} %get-tuple-element.53), channel_id=1, source_target_pairs={{0,1},{1,0},{2,3},{3,2},{4,5},{5,4},{6,7},{7,6},{8,9},{9,8},{10,11... | collective-permute-start | bytes 786440 | tf_op jit(solution)/shard_map/ppermute | solution.py:167
  16.3 0.7 collective-permute-start.4
  16.9 0.1 collective-permute-start.2
  17.0 1.5 %collective-permute-start = (f32[2,8,128]{2,1,0:T(8,128)}, f32[2,8,128]{2,1,0:T(8,128)S(1)}, u32[]{:S(2)}, u32[]{:S(2)}) collective-permute-start(f32[2,8,128]{2,1,0:T(8,128)} %get-tuple-element.50), channel_id=1, source_target_pairs={{0,8},{8,0},{16,24},{24,16},{1,9},{9,1},{17,25},{25,17},{2,10},{10... | collective-permute-start | bytes 24584 | tf_op jit(solution)/shard_map/ppermute | solution.py:167
  18.6 0.6 collective-permute-start.1
  19.2 4.4 %all-to-all-done.got_in = f32[32,1,1408]{2,1,0:T(1,128)S(1)} async-done(((f32[32,1,1408]{2,1,0:T(1,128)}), f32[32,1,1408]{2,1,0:T(1,128)S(1)}, u32[]{:S(2)}, u32[]{:S(2)}) %all-to-all-start) | async-done | bytes 180256 | tf_op jit(solution)/shard_map/all_to_all | solution.py:1072
  23.7 6.0 %shard_map.105 = (bf16[8,544,256]{2,1,0:T(8,128)(2,1)S(1)}, bf16[16,128,256]{2,1,0:T(8,128)(2,1)S(1)}, f32[1192,128]{1,0:T(8,128)S(1)}, f32[8,256,128]{2,1,0:T(8,128)S(1)}) custom-call(s32[32]{0:T(128)S(1)} %copy-done.2, f32[16]{0:T(128)S(1)} %copy-done.3, f32[4]{0:T(128)S(1)} %copy-done.4, f32[32,1,1408]{2,1,0:T(1,128)S(1)} %all-to-all-done.got_in), custom_call_target="tpu_custom_call" | custom-call | bytes 1 | tf_op jit(solution)/shard_map/pallas_call | solution.py:24
  29.7 0.0 collective-permute-done.xr0
  29.7 0.0 collective-permute-done.1.xr1
  29.7 0.0 collective-permute-done.2.yr0.yr1
  29.7 0.0 collective-permute-done.3.zr0
  29.8 0.0 collective-permute-done.4.zr1
  29.8 3.3 %shard_map.106 = (f32[8,8,128]{2,1,0:T(8,128)S(1)}, f32[272,128]{1,0:T(8,128)S(1)}, f32[2,256,128]{2,1,0:T(8,128)S(1)}, f32[8,256,128]{2,1,0:T(8,128)S(1)}, f32[...) custom-call(f32[2,8,128]{2,1,0:T(8,128)S(1)} %collective-permute-don, ...), custom_call_target="tpu_custom_call" | custom-call | bytes 1 | tf_op jit(solution)/shard_map/pallas_call | solution.py:24
  33.1 0.1 collective-permute-start.5
  33.2 4.0 %collective-permute-start.6 = (f32[16,128]{1,0:T(8,128)S(1)}, f32[16,128]{1,0:T(8,128)S(1)}, u32[]{:S(2)}, u32[]{:S(2)}) collective-permute-start(f32[16,128]{1,0:T(8,128)S(1)} %get-tuple-element.63), channel_id=1, source_target_pairs={{0,8},{8,0},{16,24},{24,16},{1,9},{9,1},{17,25},{25,17},{2,10},{10... | collective-permute-start | bytes 24584 | tf_op jit(solution)/shard_map/ppermute | solution.py:156
  37.2 0.5 collective-permute-start.8
  37.7 1.0 %collective-permute-start.7 = (f32[16,128]{1,0:T(8,128)S(1)}, f32[16,128]{1,0:T(8,128)S(1)}, u32[]{:S(2)}, u32[]{:S(2)}) collective-permute-start(f32[16,128]{1,0:T(8,128)S(1)} %get-tuple-element.64), channel_id=1, source_target_pairs={{0,16},{8,24},{16,0},{24,8},{1,17},{9,25},{17,1},{25,9},{2,18},{10... | collective-permute-start | bytes 24584 | tf_op jit(solution)/shard_map/ppermute | solution.py:156
  38.7 1.3 %collective-permute-start.10 = (f32[256,128]{1,0:T(8,128)S(1)}, f32[256,128]{1,0:T(8,128)S(1)}, u32[]{:S(2)}, u32[]{:S(2)}) collective-permute-start(f32[256,128]{1,0:T(8,128)S(1)} %get-tuple-element.79), channel_id=1, source_target_pairs={{1,0},{2,3},{5,4},{6,7},{9,8},{10,11},{13,12},{14,15},{17,16},{18,... | collective-permute-start | bytes 393224 | tf_op jit(solution)/shard_map/ppermute | solution.py:1123
  40.0 0.0 collective-permute-done.6.rest_0_
  40.0 1.8 %collective-permute-done.8.rest_2_ = f32[16,128]{1,0:T(8,128)S(1)} collective-permute-done((f32[16,128]{1,0:T(8,128)S(1)}, f32[16,128]{1,0:T(8,128)S(1)}, u32[]{:S(2)}, u32[]{:S(2)}) %collective-permute-start.8) | collective-permute-done | bytes 8224 | tf_op jit(solution)/shard_map/ppermute | solution.py:156
  41.8 0.0 collective-permute-done.7.rest_1_
  41.8 0.0 collective-permute-done.5.near.rest_0_
  41.8 0.3 shard_map.107
  42.1 0.4 collective-permute-start.11
  42.5 0.0 collective-permute-start.9
  42.5 1.2 %collective-permute-done.9.rest_0_ = f32[16,272]{1,0:T(8,128)S(1)} collective-permute-done((f32[16,272]{1,0:T(8,128)S(1)}, f32[16,272]{1,0:T(8,128)S(1)}, u32[]{:S(2)}, u32[]{:S(2)}) %collective-permute-start.9) | collective-permute-done | bytes 17440 | tf_op jit(solution)/shard_map/ppermute | solution.py:156
  43.7 0.5 shard_map.108
  44.2 1.2 %collective-permute-start.12 = (f32[40,128]{1,0:T(8,128)S(1)}, f32[40,128]{1,0:T(8,128)S(1)}, u32[]{:S(2)}, u32[]{:S(2)}) collective-permute-start(f32[40,128]{1,0:T(8,128)S(1)} %get-tuple-element.81), channel_id=1, source_target_pairs={{0,1},{1,0},{2,3},{3,2},{4,5},{5,4},{6,7},{7,6},{8,9},{9,8},{10,11... | collective-permute-start | bytes 61448 | tf_op jit(solution)/shard_map/ppermute | solution.py:156
  45.3 2.9 %collective-permute-start.14 = (f32[40,128]{1,0:T(8,128)S(1)}, f32[40,128]{1,0:T(8,128)S(1)}, u32[]{:S(2)}, u32[]{:S(2)}) collective-permute-start(f32[40,128]{1,0:T(8,128)S(1)} %get-tuple-element.82), channel_id=1, source_target_pairs={{0,3},{1,2},{2,1},{3,0},{4,7},{5,6},{6,5},{7,4},{8,11},{9,10},{10,... | collective-permute-start | bytes 61448 | tf_op jit(solution)/shard_map/ppermute | solution.py:156
  48.3 0.0 collective-permute-start.13
  48.3 0.0 collective-permute-done.10.rest_1_
  48.3 0.0 collective-permute-done.12.rest_3_
  48.3 2.8 %collective-permute-done.14.rest_5_ = f32[40,128]{1,0:T(8,128)S(1)} collective-permute-done((f32[40,128]{1,0:T(8,128)S(1)}, f32[40,128]{1,0:T(8,128)S(1)}, u32[]{:S(2)}, u32[]{:S(2)}) %collective-permute-start.14) | collective-permute-done | bytes 20512 | tf_op jit(solution)/shard_map/ppermute | solution.py:156
  51.1 1.9 %collective-permute-done.13.rest_4_ = f32[40,128]{1,0:T(8,128)S(1)} collective-permute-done((f32[40,128]{1,0:T(8,128)S(1)}, f32[40,128]{1,0:T(8,128)S(1)}, u32[]{:S(2)}, u32[]{:S(2)}) %collective-permute-start.13) | collective-permute-done | bytes 20512 | tf_op jit(solution)/shard_map/ppermute | solution.py:156
  52.9 0.0 collective-permute-done.11.rest_2_
  52.9 3.2 %shard_map.109 = (f32[8,256,128]{2,1,0:T(8,128)S(1)}, f32[8,272,128]{2,1,0:T(8,128)S(1)}, f32[272,128]{1,0:T(8,128)S(1)}, f32[256,128]{1,0:T(8,128)S(1)}, f32[25...) custom-call(f32[8,272,128]{2,1,0:T(8,128)S(1)} %get-tuple-element.60.t_ref.t_in, ...), custom_call_target="tpu_custom_call" | custom-call | bytes 1 | tf_op jit(solution)/shard_map/pallas_call | solution.py:24
  56.2 0.1 collective-permute-start.15
  56.3 2.0 %collective-permute-start.16 = (f32[16,128]{1,0:T(8,128)S(1)}, f32[16,128]{1,0:T(8,128)S(1)}, u32[]{:S(2)}, u32[]{:S(2)}) collective-permute-start(f32[16,128]{1,0:T(8,128)S(1)} %get-tuple-element.86), channel_id=1, source_target_pairs={{0,8},{8,0},{16,24},{24,16},{1,9},{9,1},{17,25},{25,17},{2,10},{10... | collective-permute-start | bytes 24584 | tf_op jit(solution)/shard_map/ppermute | solution.py:156
  58.3 0.5 collective-permute-start.18
  58.8 1.0 %collective-permute-start.17 = (f32[16,128]{1,0:T(8,128)S(1)}, f32[16,128]{1,0:T(8,128)S(1)}, u32[]{:S(2)}, u32[]{:S(2)}) collective-permute-start(f32[16,128]{1,0:T(8,128)S(1)} %get-tuple-element.87), channel_id=1, source_target_pairs={{0,16},{8,24},{16,0},{24,8},{1,17},{9,25},{17,1},{25,9},{2,18},{10... | collective-permute-start | bytes 24584 | tf_op jit(solution)/shard_map/ppermute | solution.py:156
  59.8 1.3 %collective-permute-start.20 = (f32[256,128]{1,0:T(8,128)S(1)}, f32[256,128]{1,0:T(8,128)S(1)}, u32[]{:S(2)}, u32[]{:S(2)}) collective-permute-start(f32[256,128]{1,0:T(8,128)S(1)} %get-tuple-element.94), channel_id=1, source_target_pairs={{1,0},{2,3},{5,4},{6,7},{9,8},{10,11},{13,12},{14,15},{17,16},{18,... | collective-permute-start | bytes 393224 | tf_op jit(solution)/shard_map/ppermute | solution.py:1123
  61.1 0.0 collective-permute-done.16.rest_0_
  61.1 1.7 %collective-permute-done.18.rest_2_ = f32[16,128]{1,0:T(8,128)S(1)} collective-permute-done((f32[16,128]{1,0:T(8,128)S(1)}, f32[16,128]{1,0:T(8,128)S(1)}, u32[]{:S(2)}, u32[]{:S(2)}) %collective-permute-start.18) | collective-permute-done | bytes 8224 | tf_op jit(solution)/shard_map/ppermute | solution.py:156
  62.8 0.0 collective-permute-done.17.rest_1_
  62.8 0.0 collective-permute-done.15.near.rest_0_
  62.8 0.3 shard_map.110
  63.1 1.2 %collective-permute-start.21 = (f32[256,128]{1,0:T(8,128)S(1)}, f32[256,128]{1,0:T(8,128)S(1)}, u32[]{:S(2)}, u32[]{:S(2)}) collective-permute-start(f32[256,128]{1,0:T(8,128)S(1)} %get-tuple-element.95), channel_id=1, source_target_pairs={{0,2},{1,3},{2,0},{3,1},{4,6},{5,7},{6,4},{7,5},{8,10},{9,11},{10,... | collective-permute-start | bytes 393224 | tf_op jit(solution)/shard_map/ppermute | solution.py:162
  64.3 0.0 collective-permute-start.19
  64.3 1.2 %collective-permute-done.19.rest_0_ = f32[16,272]{1,0:T(8,128)S(1)} collective-permute-done((f32[16,272]{1,0:T(8,128)S(1)}, f32[16,272]{1,0:T(8,128)S(1)}, u32[]{:S(2)}, u32[]{:S(2)}) %collective-permute-start.19) | collective-permute-done | bytes 17440 | tf_op jit(solution)/shard_map/ppermute | solution.py:156
  65.5 0.2 shard_map.111
  65.7 0.4 collective-permute-start.22
  66.1 2.9 %collective-permute-start.24 = (f32[32,128]{1,0:T(8,128)S(1)}, f32[32,128]{1,0:T(8,128)S(1)}, u32[]{:S(2)}, u32[]{:S(2)}) collective-permute-start(f32[32,128]{1,0:T(8,128)S(1)} %get-tuple-element.97), channel_id=1, source_target_pairs={{0,3},{1,2},{2,1},{3,0},{4,7},{5,6},{6,5},{7,4},{8,11},{9,10},{10,... | collective-permute-start | bytes 49160 | tf_op jit(solution)/shard_map/ppermute | solution.py:156
  69.0 0.3 collective-permute-start.23
  69.3 0.0 collective-permute-done.20.rest_1_
  69.3 0.2 collective-permute-done.22.rest_3_
  69.5 2.1 %collective-permute-done.24.rest_5_ = f32[32,128]{1,0:T(8,128)S(1)} collective-permute-done((f32[32,128]{1,0:T(8,128)S(1)}, f32[32,128]{1,0:T(8,128)S(1)}, u32[]{:S(2)}, u32[]{:S(2)}) %collective-permute-start.24) | collective-permute-done | bytes 16416 | tf_op jit(solution)/shard_map/ppermute | solution.py:156
  71.6 2.0 %collective-permute-done.23.rest_4_ = f32[32,128]{1,0:T(8,128)S(1)} collective-permute-done((f32[32,128]{1,0:T(8,128)S(1)}, f32[32,128]{1,0:T(8,128)S(1)}, u32[]{:S(2)}, u32[]{:S(2)}) %collective-permute-start.23) | collective-permute-done | bytes 16416 | tf_op jit(solution)/shard_map/ppermute | solution.py:156
  73.6 0.0 collective-permute-done.21.rest_2_
  73.7 2.3 %shard_map.112 = (f32[8,256,128]{2,1,0:T(8,128)}, f32[8,256,128]{2,1,0:T(8,128)}) custom-call(f32[8,272,128]{2,1,0:T(8,128)S(1)} %get-tuple-element.83.t_ref.t_in, f32[272,128]{1,0:T(8,128)S(1)} %get-tuple-element.91.l_ref, f32[32,128]{1,0:T(8,128)S(1)} %get-tuple-element.92.b_ref, f32[1192,128]{1,0:T(8,128)S(1)} %get-tuple-element.58.co, ...), custom_call_target="tpu_custom_call" | custom-call | bytes 1 | tf_op jit(solution)/shard_map/pallas_call | solution.py:24
  (7 shorter events, 0.0 us)
Async XLA Ops:
  0.6 23.0 %copy-start.2 = (s32[32]{0:T(128)S(1)}, s32[32]{0:T(128)}, u32[]{:S(2)}) copy-start(s32[32]{0:T(128)} %sheet_in.3) | copy-start | bytes 388
  0.6 23.0 %copy-start.3 = (f32[16]{0:T(128)S(1)}, f32[16]{0:T(128)}, u32[]{:S(2)}) copy-start(f32[16]{0:T(128)} %table_in.3) | copy-start | bytes 196
  0.7 23.0 %copy-start.4 = (f32[4]{0:T(128)S(1)}, f32[4]{0:T(128)}, u32[]{:S(2)}) copy-start(f32[4]{0:T(128)} %scaling_in.3) | copy-start | bytes 52
  0.7 29.1 %copy-start = (f32[8,256,128]{2,1,0:T(8,128)S(1)}, f32[8,256,128]{2,1,0:T(8,128)}, u32[]{:S(2)}) copy-start(f32[8,256,128]{2,1,0:T(8,128)} %u_ref.3) | copy-start | bytes 3145732
  0.7 29.1 %copy-start.1 = (s32[8,256,128]{2,1,0:T(8,128)S(1)}, s32[8,256,128]{2,1,0:T(8,128)}, u32[]{:S(2)}) copy-start(s32[8,256,128]{2,1,0:T(8,128)} %kind_ref.1) | copy-start | bytes 3145732
  7.1 16.5 %all-to-all-start = ((f32[32,1,1408]{2,1,0:T(1,128)}), f32[32,1,1408]{2,1,0:T(1,128)S(1)}, u32[]{:S(2)}, u32[]{:S(2)}) async-start(f32[32,1,1408]{2,1,0:T(1,128)} %get-tuple-element.55), calls=%async_computation | async-start | bytes 360448 | tf_op jit(solution)/shard_map/all_to_all | solution.py:1072
  14.4 15.3 %collective-permute-start.3 = (f32[2,256,128]{2,1,0:T(8,128)}, f32[2,256,128]{2,1,0:T(8,128)S(1)}, u32[]{:S(2)}, u32[]{:S(2)}) collective-permute-start(f32[2,256,128]{2,1,0:T(8,128)} %get-tuple-element.53), channel_id=1, source_target_pairs={{0,1},{1,0},{2,3},{3,2},{4,5},{5,4},{6,7},{7,6},{8,9},{9,8},{10,11... | collective-permute-start | bytes 786440 | tf_op jit(solution)/shard_map/ppermute | solution.py:167
  16.3 13.5 %collective-permute-start.4 = (f32[2,256,128]{2,1,0:T(8,128)}, f32[2,256,128]{2,1,0:T(8,128)S(1)}, u32[]{:S(2)}, u32[]{:S(2)}) collective-permute-start(f32[2,256,128]{2,1,0:T(8,128)} %get-tuple-element.54), channel_id=1, source_target_pairs={{1,2},{2,1},{5,6},{6,5},{9,10},{10,9},{13,14},{14,13},{17,18},{18,... | collective-permute-start | bytes 786440 | tf_op jit(solution)/shard_map/ppermute | solution.py:171
  16.9 12.8 %collective-permute-start.2 = (f32[256,128]{1,0:T(8,128)}, f32[256,128]{1,0:T(8,128)S(1)}, u32[]{:S(2)}, u32[]{:S(2)}) collective-permute-start(f32[256,128]{1,0:T(8,128)} %bitcast.9), channel_id=1, source_target_pairs={{0,4},{4,0},{1,5},{5,1},{2,6},{6,2},{3,7},{7,3},{8,12},{12,8},{9,1... | collective-permute-start | bytes 393224 | tf_op jit(solution)/shard_map/ppermute | solution.py:167
  17.0 12.7 %collective-permute-start = (f32[2,8,128]{2,1,0:T(8,128)}, f32[2,8,128]{2,1,0:T(8,128)S(1)}, u32[]{:S(2)}, u32[]{:S(2)}) collective-permute-start(f32[2,8,128]{2,1,0:T(8,128)} %get-tuple-element.50), channel_id=1, source_target_pairs={{0,8},{8,0},{16,24},{24,16},{1,9},{9,1},{17,25},{25,17},{2,10},{10... | collective-permute-start | bytes 24584 | tf_op jit(solution)/shard_map/ppermute | solution.py:167
  18.6 11.2 %collective-permute-start.1 = (f32[2,8,128]{2,1,0:T(8,128)}, f32[2,8,128]{2,1,0:T(8,128)S(1)}, u32[]{:S(2)}, u32[]{:S(2)}) collective-permute-start(f32[2,8,128]{2,1,0:T(8,128)} %get-tuple-element.51), channel_id=1, source_target_pairs={{8,16},{16,8},{9,17},{17,9},{10,18},{18,10},{11,19},{19,11},{12,20... | collective-permute-start | bytes 24584 | tf_op jit(solution)/shard_map/ppermute | solution.py:171
  33.1 8.6 %collective-permute-start.5 = (f32[256,128]{1,0:T(8,128)S(1)}, f32[256,128]{1,0:T(8,128)S(1)}, u32[]{:S(2)}, u32[]{:S(2)}) collective-permute-start(f32[256,128]{1,0:T(8,128)S(1)} %get-tuple-element.62.pair), channel_id=1, source_target_pairs={{0,1},{1,0},{2,3},{3,2},{4,5},{5,4},{6,7},{7,6},{8,9},{9,8},{10,11... | collective-permute-start | bytes 393224 | tf_op jit(solution)/shard_map/ppermute | solution.py:162
  33.2 6.8 %collective-permute-start.6 = (f32[16,128]{1,0:T(8,128)S(1)}, f32[16,128]{1,0:T(8,128)S(1)}, u32[]{:S(2)}, u32[]{:S(2)}) collective-permute-start(f32[16,128]{1,0:T(8,128)S(1)} %get-tuple-element.63), channel_id=1, source_target_pairs={{0,8},{8,0},{16,24},{24,16},{1,9},{9,1},{17,25},{25,17},{2,10},{10... | collective-permute-start | bytes 24584 | tf_op jit(solution)/shard_map/ppermute | solution.py:156
  37.2 4.5 %collective-permute-start.8 = (f32[16,128]{1,0:T(8,128)S(1)}, f32[16,128]{1,0:T(8,128)S(1)}, u32[]{:S(2)}, u32[]{:S(2)}) collective-permute-start(f32[16,128]{1,0:T(8,128)S(1)} %get-tuple-element.64), channel_id=1, source_target_pairs={{0,24},{8,16},{16,8},{24,0},{1,25},{9,17},{17,9},{25,1},{2,26},{10... | collective-permute-start | bytes 24584 | tf_op jit(solution)/shard_map/ppermute | solution.py:156
  37.7 4.0 %collective-permute-start.7 = (f32[16,128]{1,0:T(8,128)S(1)}, f32[16,128]{1,0:T(8,128)S(1)}, u32[]{:S(2)}, u32[]{:S(2)}) collective-permute-start(f32[16,128]{1,0:T(8,128)S(1)} %get-tuple-element.64), channel_id=1, source_target_pairs={{0,16},{8,24},{16,0},{24,8},{1,17},{9,25},{17,1},{25,9},{2,18},{10... | collective-permute-start | bytes 24584 | tf_op jit(solution)/shard_map/ppermute | solution.py:156
  38.7 9.6 %collective-permute-start.10 = (f32[256,128]{1,0:T(8,128)S(1)}, f32[256,128]{1,0:T(8,128)S(1)}, u32[]{:S(2)}, u32[]{:S(2)}) collective-permute-start(f32[256,128]{1,0:T(8,128)S(1)} %get-tuple-element.79), channel_id=1, source_target_pairs={{1,0},{2,3},{5,4},{6,7},{9,8},{10,11},{13,12},{14,15},{17,16},{18,... | collective-permute-start | bytes 393224 | tf_op jit(solution)/shard_map/ppermute | solution.py:1123
  42.1 10.9 %collective-permute-start.11 = (f32[256,128]{1,0:T(8,128)S(1)}, f32[256,128]{1,0:T(8,128)S(1)}, u32[]{:S(2)}, u32[]{:S(2)}) collective-permute-start(f32[256,128]{1,0:T(8,128)S(1)} %get-tuple-element.80), channel_id=1, source_target_pairs={{0,2},{1,3},{2,0},{3,1},{4,6},{5,7},{6,4},{7,5},{8,10},{9,11},{10,... | collective-permute-start | bytes 393224 | tf_op jit(solution)/shard_map/ppermute | solution.py:162
  42.5 1.2 %collective-permute-start.9 = (f32[16,272]{1,0:T(8,128)S(1)}, f32[16,272]{1,0:T(8,128)S(1)}, u32[]{:S(2)}, u32[]{:S(2)}) collective-permute-start(f32[16,272]{1,0:T(8,128)S(1)} %get-tuple-element.67), channel_id=1, source_target_pairs={{0,4},{4,0},{1,5},{5,1},{2,6},{6,2},{3,7},{7,3},{8,12},{12,8},{9,1... | collective-permute-start | bytes 52232 | tf_op jit(solution)/shard_map/ppermute | solution.py:156
  44.2 4.1 %collective-permute-start.12 = (f32[40,128]{1,0:T(8,128)S(1)}, f32[40,128]{1,0:T(8,128)S(1)}, u32[]{:S(2)}, u32[]{:S(2)}) collective-permute-start(f32[40,128]{1,0:T(8,128)S(1)} %get-tuple-element.81), channel_id=1, source_target_pairs={{0,1},{1,0},{2,3},{3,2},{4,5},{5,4},{6,7},{7,6},{8,9},{9,8},{10,11... | collective-permute-start | bytes 61448 | tf_op jit(solution)/shard_map/ppermute | solution.py:156
  45.3 5.7 %collective-permute-start.14 = (f32[40,128]{1,0:T(8,128)S(1)}, f32[40,128]{1,0:T(8,128)S(1)}, u32[]{:S(2)}, u32[]{:S(2)}) collective-permute-start(f32[40,128]{1,0:T(8,128)S(1)} %get-tuple-element.82), channel_id=1, source_target_pairs={{0,3},{1,2},{2,1},{3,0},{4,7},{5,6},{6,5},{7,4},{8,11},{9,10},{10,... | collective-permute-start | bytes 61448 | tf_op jit(solution)/shard_map/ppermute | solution.py:156
  48.3 4.7 %collective-permute-start.13 = (f32[40,128]{1,0:T(8,128)S(1)}, f32[40,128]{1,0:T(8,128)S(1)}, u32[]{:S(2)}, u32[]{:S(2)}) collective-permute-start(f32[40,128]{1,0:T(8,128)S(1)} %get-tuple-element.82), channel_id=1, source_target_pairs={{0,2},{1,3},{2,0},{3,1},{4,6},{5,7},{6,4},{7,5},{8,10},{9,11},{10,... | collective-permute-start | bytes 61448 | tf_op jit(solution)/shard_map/ppermute | solution.py:156
  56.2 6.6 %collective-permute-start.15 = (f32[256,128]{1,0:T(8,128)S(1)}, f32[256,128]{1,0:T(8,128)S(1)}, u32[]{:S(2)}, u32[]{:S(2)}) collective-permute-start(f32[256,128]{1,0:T(8,128)S(1)} %get-tuple-element.85.pair), channel_id=1, source_target_pairs={{0,1},{1,0},{2,3},{3,2},{4,5},{5,4},{6,7},{7,6},{8,9},{9,8},{10,11... | collective-permute-start | bytes 393224 | tf_op jit(solution)/shard_map/ppermute | solution.py:162
  56.3 4.8 %collective-permute-start.16 = (f32[16,128]{1,0:T(8,128)S(1)}, f32[16,128]{1,0:T(8,128)S(1)}, u32[]{:S(2)}, u32[]{:S(2)}) collective-permute-start(f32[16,128]{1,0:T(8,128)S(1)} %get-tuple-element.86), channel_id=1, source_target_pairs={{0,8},{8,0},{16,24},{24,16},{1,9},{9,1},{17,25},{25,17},{2,10},{10... | collective-permute-start | bytes 24584 | tf_op jit(solution)/shard_map/ppermute | solution.py:156
  58.3 4.5 %collective-permute-start.18 = (f32[16,128]{1,0:T(8,128)S(1)}, f32[16,128]{1,0:T(8,128)S(1)}, u32[]{:S(2)}, u32[]{:S(2)}) collective-permute-start(f32[16,128]{1,0:T(8,128)S(1)} %get-tuple-element.87), channel_id=1, source_target_pairs={{0,24},{8,16},{16,8},{24,0},{1,25},{9,17},{17,9},{25,1},{2,26},{10... | collective-permute-start | bytes 24584 | tf_op jit(solution)/shard_map/ppermute | solution.py:156
  58.8 4.0 %collective-permute-start.17 = (f32[16,128]{1,0:T(8,128)S(1)}, f32[16,128]{1,0:T(8,128)S(1)}, u32[]{:S(2)}, u32[]{:S(2)}) collective-permute-start(f32[16,128]{1,0:T(8,128)S(1)} %get-tuple-element.87), channel_id=1, source_target_pairs={{0,16},{8,24},{16,0},{24,8},{1,17},{9,25},{17,1},{25,9},{2,18},{10... | collective-permute-start | bytes 24584 | tf_op jit(solution)/shard_map/ppermute | solution.py:156
  59.8 9.4 %collective-permute-start.20 = (f32[256,128]{1,0:T(8,128)S(1)}, f32[256,128]{1,0:T(8,128)S(1)}, u32[]{:S(2)}, u32[]{:S(2)}) collective-permute-start(f32[256,128]{1,0:T(8,128)S(1)} %get-tuple-element.94), channel_id=1, source_target_pairs={{1,0},{2,3},{5,4},{6,7},{9,8},{10,11},{13,12},{14,15},{17,16},{18,... | collective-permute-start | bytes 393224 | tf_op jit(solution)/shard_map/ppermute | solution.py:1123
  63.1 10.5 %collective-permute-start.21 = (f32[256,128]{1,0:T(8,128)S(1)}, f32[256,128]{1,0:T(8,128)S(1)}, u32[]{:S(2)}, u32[]{:S(2)}) collective-permute-start(f32[256,128]{1,0:T(8,128)S(1)} %get-tuple-element.95), channel_id=1, source_target_pairs={{0,2},{1,3},{2,0},{3,1},{4,6},{5,7},{6,4},{7,5},{8,10},{9,11},{10,... | collective-permute-start | bytes 393224 | tf_op jit(solution)/shard_map/ppermute | solution.py:162
  64.3 1.2 %collective-permute-start.19 = (f32[16,272]{1,0:T(8,128)S(1)}, f32[16,272]{1,0:T(8,128)S(1)}, u32[]{:S(2)}, u32[]{:S(2)}) collective-permute-start(f32[16,272]{1,0:T(8,128)S(1)} %get-tuple-element.90), channel_id=1, source_target_pairs={{0,4},{4,0},{1,5},{5,1},{2,6},{6,2},{3,7},{7,3},{8,12},{12,8},{9,1... | collective-permute-start | bytes 52232 | tf_op jit(solution)/shard_map/ppermute | solution.py:156
  65.7 3.8 %collective-permute-start.22 = (f32[32,128]{1,0:T(8,128)S(1)}, f32[32,128]{1,0:T(8,128)S(1)}, u32[]{:S(2)}, u32[]{:S(2)}) collective-permute-start(f32[32,128]{1,0:T(8,128)S(1)} %get-tuple-element.96), channel_id=1, source_target_pairs={{0,1},{1,0},{2,3},{3,2},{4,5},{5,4},{6,7},{7,6},{8,9},{9,8},{10,11... | collective-permute-start | bytes 49160 | tf_op jit(solution)/shard_map/ppermute | solution.py:156
  66.1 5.5 %collective-permute-start.24 = (f32[32,128]{1,0:T(8,128)S(1)}, f32[32,128]{1,0:T(8,128)S(1)}, u32[]{:S(2)}, u32[]{:S(2)}) collective-permute-start(f32[32,128]{1,0:T(8,128)S(1)} %get-tuple-element.97), channel_id=1, source_target_pairs={{0,3},{1,2},{2,1},{3,0},{4,7},{5,6},{6,5},{7,4},{8,11},{9,10},{10,... | collective-permute-start | bytes 49160 | tf_op jit(solution)/shard_map/ppermute | solution.py:156
  69.0 4.7 %collective-permute-start.23 = (f32[32,128]{1,0:T(8,128)S(1)}, f32[32,128]{1,0:T(8,128)S(1)}, u32[]{:S(2)}, u32[]{:S(2)}) collective-permute-start(f32[32,128]{1,0:T(8,128)S(1)} %get-tuple-element.97), channel_id=1, source_target_pairs={{0,2},{1,3},{2,0},{3,1},{4,6},{5,7},{6,4},{7,5},{8,10},{9,11},{10,... | collective-permute-start | bytes 49160 | tf_op jit(solution)/shard_map/ppermute | solution.py:156
